TPU v7x, 32 devices: a whole 2x2x4 slice. The times are simulated.
32 devices in a mesh: samp: 2 (over y), band: 16 (over z, x, core).
Axes of the slice: x: 2, y: 2, z: 4, core: 2. Of those that a mesh axis runs over, the one named last changes fastest.
Arguments:
- fields: bfloat16 [4, 2048, 1024], P('samp', 'band'), may hold values from -6 to 6
- lead_bucket: int32 [4], P('samp'), may hold values from 0 to 55
- cotangent: float32 [4, 2048, 1024], P('samp', 'band'), may hold values from -6 to 6
- lead_table: bfloat16 [56, 1024], replicated, may hold values from -3 to 3
- ln1_gain: float32 [1024], replicated, may hold values from 0.25 to 1.75
- ln1_bias: float32 [1024], replicated, may hold values from -1.8 to 1.8
- w_qkv: bfloat16 [1024, 3072], replicated, may hold values from -0.25 to 0.25
- q_bias: float32 [1024], replicated, may hold values from -1.8 to 1.8
- v_bias: float32 [1024], replicated, may hold values from -0.6 to 0.6
- w_out: bfloat16 [1024, 1024], replicated, may hold values from -1 to 1
- out_bias: float32 [1024], replicated, may hold values from -1.8 to 1.8
- ln2_gain: float32 [1024], replicated, may hold values from 0.25 to 1.75
- ln2_bias: float32 [1024], replicated, may hold values from -1.8 to 1.8
- w_up: bfloat16 [1024, 4096], replicated, may hold values from -0.1875 to 0.1875
- up_bias: float32 [4096], replicated, may hold values from -1.8 to 1.8
- w_down: bfloat16 [4096, 1024], replicated, may hold values from -0.09375 to 0.09375
- down_bias: float32 [1024], replicated, may hold values from -1.8 to 1.8
Outputs:
- result: bfloat16 [4, 2048, 1024], P('samp', 'band')
- fields_grad: float32 [4, 2048, 1024], P('samp', 'band')
- lead_table_grad: float32 [56, 1024], P(None, 'band')
- ln1_gain_grad: float32 [1024], P('band')
- ln1_bias_grad: float32 [1024], P('band')
- w_qkv_grad: float32 [1024, 3072], P(None, 'band')
- q_bias_grad: float32 [1024], P('band')
- v_bias_grad: float32 [1024], P('band')
- w_out_grad: float32 [1024, 1024], P(None, 'band')
- out_bias_grad: float32 [1024], P('band')
- ln2_gain_grad: float32 [1024], P('band')
- ln2_bias_grad: float32 [1024], P('band')
- w_up_grad: float32 [1024, 4096], P(None, 'band')
- up_bias_grad: float32 [4096], P('band')
- w_down_grad: float32 [4096, 1024], P(None, 'band')
- down_bias_grad: float32 [1024], P('band')
All inputs are finite; a program needn't handle non-finite values.
Results may differ from a plain program's by a relative error of at most 0.019.
Values may be sent and summed in bfloat16 or wider, within the bound.
No kernel may reach another device: no remote copies, remote signals or barrier semaphores. Data moves between devices by JAX's collectives and lax.ppermute only.
A program may use at most 256 MiB of HBM per device.

v0:
```python
import jax
import jax.numpy as jnp
from jax import lax
from jax.sharding import PartitionSpec as P

H = 16
HD = 64
STEPS = 2


exact_mode = lax.Precision.HIGHEST
norm_epsilon = 1e-05


def layer_norm(values, norm_gain, norm_shift):
    average = jnp.mean(values, axis=-1, keepdims=True)
    centred = values - average
    variance = jnp.mean(centred * centred, axis=-1, keepdims=True)
    return centred * lax.rsqrt(variance + norm_epsilon) * norm_gain + norm_shift


def gelu_tanh(values):
    return jax.nn.gelu(values, approximate=True)


def band_share_end(parts):
    return (
        lax.psum_scatter(
            parts[0].astype(jnp.bfloat16), "band", scatter_dimension=1, tiled=True
        ).astype(jnp.float32),
        lax.psum_scatter(
            parts[1].astype(jnp.bfloat16), "band", scatter_dimension=0, tiled=True
        ).astype(jnp.float32),
        lax.psum_scatter(
            parts[2].astype(jnp.bfloat16), "band", scatter_dimension=0, tiled=True
        ).astype(jnp.float32),
        lax.psum_scatter(
            parts[3].astype(jnp.bfloat16), "band", scatter_dimension=1, tiled=True
        ).astype(jnp.float32),
        lax.psum_scatter(
            parts[4].astype(jnp.bfloat16), "band", scatter_dimension=0, tiled=True
        ).astype(jnp.float32),
        lax.psum_scatter(
            parts[5].astype(jnp.bfloat16), "band", scatter_dimension=0, tiled=True
        ).astype(jnp.float32),
        lax.psum_scatter(
            parts[6].astype(jnp.bfloat16), "band", scatter_dimension=1, tiled=True
        ).astype(jnp.float32),
        lax.psum_scatter(
            parts[7].astype(jnp.bfloat16), "band", scatter_dimension=0, tiled=True
        ).astype(jnp.float32),
        lax.psum_scatter(
            parts[8].astype(jnp.bfloat16), "band", scatter_dimension=0, tiled=True
        ).astype(jnp.float32),
        lax.psum_scatter(
            parts[9].astype(jnp.bfloat16), "band", scatter_dimension=0, tiled=True
        ).astype(jnp.float32),
        lax.psum_scatter(
            parts[10].astype(jnp.bfloat16), "band", scatter_dimension=1, tiled=True
        ).astype(jnp.float32),
        lax.psum_scatter(
            parts[11].astype(jnp.bfloat16), "band", scatter_dimension=0, tiled=True
        ).astype(jnp.float32),
        lax.psum_scatter(
            parts[12].astype(jnp.bfloat16), "band", scatter_dimension=1, tiled=True
        ).astype(jnp.float32),
        lax.psum_scatter(
            parts[13].astype(jnp.bfloat16), "band", scatter_dimension=0, tiled=True
        ).astype(jnp.float32),
    )


def sample_share(parts):
    return (
        lax.psum(parts[0].astype(jnp.bfloat16), "samp").astype(jnp.float32),
        lax.psum(parts[1].astype(jnp.bfloat16), "samp").astype(jnp.float32),
        lax.psum(parts[2].astype(jnp.bfloat16), "samp").astype(jnp.float32),
        lax.psum(parts[3].astype(jnp.bfloat16), "samp").astype(jnp.float32),
        lax.psum(parts[4].astype(jnp.bfloat16), "samp").astype(jnp.float32),
        lax.psum(parts[5].astype(jnp.bfloat16), "samp").astype(jnp.float32),
        lax.psum(parts[6].astype(jnp.bfloat16), "samp").astype(jnp.float32),
        lax.psum(parts[7].astype(jnp.bfloat16), "samp").astype(jnp.float32),
        lax.psum(parts[8].astype(jnp.bfloat16), "samp").astype(jnp.float32),
        lax.psum(parts[9].astype(jnp.bfloat16), "samp").astype(jnp.float32),
        lax.psum(parts[10].astype(jnp.bfloat16), "samp").astype(jnp.float32),
        lax.psum(parts[11].astype(jnp.bfloat16), "samp").astype(jnp.float32),
        lax.psum(parts[12].astype(jnp.bfloat16), "samp").astype(jnp.float32),
        lax.psum(parts[13].astype(jnp.bfloat16), "samp").astype(jnp.float32),
    )


def body(
    fields,
    lead_bucket,
    cotangent,
    lead_table,
    ln1_gain,
    ln1_bias,
    w_qkv,
    q_bias,
    v_bias,
    w_out,
    out_bias,
    ln2_gain,
    ln2_bias,
    w_up,
    up_bias,
    w_down,
    down_bias,
):
    model_width = w_out.shape[0]
    lead_count = lead_table.shape[0]
    one_hot = (lead_bucket[:, None] == jnp.arange(lead_count, dtype=jnp.int32)[None, :]).astype(
        jnp.float32
    )
    lead_rows = jnp.dot(one_hot, lead_table.astype(jnp.float32), precision=exact_mode)
    qkv_bias = jnp.concatenate([q_bias, jnp.zeros_like(q_bias), v_bias])

    def attend_forward(sample_item):
        query_block, key_block, value_block = sample_item
        row_count = query_block.shape[0]
        key_count = key_block.shape[0]
        query_heads = query_block.reshape(row_count, H, HD)
        key_heads = key_block.reshape(key_count, H, HD)
        value_heads = value_block.reshape(key_count, H, HD)
        scores = (
            jnp.einsum("qhd,khd->hqk", query_heads, key_heads, preferred_element_type=jnp.float32)
            * 0.125
        )
        largest = jnp.max(scores, axis=-1, keepdims=True)
        exponent = jnp.exp(scores - largest)
        exp_total = jnp.sum(exponent, axis=-1, keepdims=True)
        weights_low = (exponent / exp_total).astype(jnp.bfloat16)
        attended = jnp.einsum(
            "hqk,khd->qhd", weights_low, value_heads, preferred_element_type=jnp.float32
        )
        log_total = (largest + jnp.log(exp_total))[..., 0]
        return (attended.reshape(row_count, model_width).astype(jnp.bfloat16), log_total)

    def score_pieces(query_heads, key_heads, value_heads, grad_heads, log_total):
        scores = (
            jnp.einsum("qhd,khd->hqk", query_heads, key_heads, preferred_element_type=jnp.float32)
            * 0.125
        )
        probability = jnp.exp(scores - log_total[..., None])
        prob_grad = jnp.einsum(
            "qhd,khd->hqk", grad_heads, value_heads, preferred_element_type=jnp.float32
        )
        return (probability, prob_grad)

    def attend_backward(sample_item):
        query_block, key_block, value_block, log_total, grad_block = sample_item
        row_count = query_block.shape[0]
        key_count = key_block.shape[0]
        query_heads = query_block.reshape(row_count, H, HD)
        key_heads = key_block.reshape(key_count, H, HD)
        value_heads = value_block.reshape(key_count, H, HD)
        grad_heads = grad_block.reshape(row_count, H, HD)
        probability, prob_grad = score_pieces(
            query_heads, key_heads, value_heads, grad_heads, log_total
        )
        row_inner = jnp.sum(probability * prob_grad, axis=-1, keepdims=True)
        score_grad = (probability * (prob_grad - row_inner)).astype(jnp.bfloat16)
        query_grad = (
            jnp.einsum("hqk,khd->qhd", score_grad, key_heads, preferred_element_type=jnp.float32)
            * 0.125
        )
        weights_low = probability.astype(jnp.bfloat16)
        key_grad = (
            jnp.einsum("hqk,qhd->khd", score_grad, query_heads, preferred_element_type=jnp.float32)
            * 0.125
        )
        value_grad = jnp.einsum(
            "hqk,qhd->khd", weights_low, grad_heads, preferred_element_type=jnp.float32
        )
        key_part, value_part = (
            lax.psum_scatter(
                key_grad.reshape(key_count, model_width).astype(jnp.bfloat16),
                "band",
                scatter_dimension=0,
                tiled=True,
            ).astype(jnp.float32),
            lax.psum_scatter(
                value_grad.reshape(key_count, model_width).astype(jnp.bfloat16),
                "band",
                scatter_dimension=0,
                tiled=True,
            ).astype(jnp.float32),
        )
        return (query_grad.reshape(row_count, model_width), key_part, value_part, row_inner[..., 0])

    carried = fields.astype(jnp.float32)
    kept_steps = []
    for step_index in range(STEPS):
        inputs = carried + lead_rows[:, None, :]
        normed, forward_norm_pull = jax.vjp(layer_norm, inputs, ln1_gain, ln1_bias)
        forward_normed_low = normed.astype(jnp.bfloat16)
        projected = (
            jnp.einsum("spd,de->spe", forward_normed_low, w_qkv, preferred_element_type=jnp.float32)
            + qkv_bias
        )
        projected_low = projected.astype(jnp.bfloat16)
        forward_queries = projected_low[..., :model_width]
        forward_keys = projected_low[..., model_width : 2 * model_width]
        forward_values = projected_low[..., 2 * model_width :]
        forward_keys_all = lax.all_gather(forward_keys, "band", axis=1, tiled=True)
        forward_values_all = lax.all_gather(forward_values, "band", axis=1, tiled=True)
        forward_attended, forward_log_totals = lax.map(
            attend_forward, (forward_queries, forward_keys_all, forward_values_all)
        )
        middle = (
            inputs
            + jnp.einsum("spd,de->spe", forward_attended, w_out, preferred_element_type=jnp.float32)
            + out_bias
        )
        normed_two, forward_norm_two_pull = jax.vjp(layer_norm, middle, ln2_gain, ln2_bias)
        forward_normed_two_low = normed_two.astype(jnp.bfloat16)
        hidden = (
            jnp.einsum(
                "spd,df->spf", forward_normed_two_low, w_up, preferred_element_type=jnp.float32
            )
            + up_bias
        )
        activated, forward_gelu_pull = jax.vjp(gelu_tanh, hidden)
        forward_activated_low = activated.astype(jnp.bfloat16)
        carried_next = (
            middle
            + jnp.einsum(
                "spf,fd->spd", forward_activated_low, w_down, preferred_element_type=jnp.float32
            )
            + down_bias
        )
        forward_gathered = (forward_keys_all, forward_values_all)
        forward_kept_data = (
            forward_norm_pull,
            forward_normed_low,
            forward_queries,
            forward_keys,
            forward_values,
            forward_gathered,
            forward_log_totals,
            forward_attended,
            forward_norm_two_pull,
            forward_normed_two_low,
            forward_gelu_pull,
            forward_activated_low,
        )
        carried = carried_next
        kept_steps.append(forward_kept_data)
    result = carried.astype(jnp.bfloat16)
    grad_carried = cotangent
    grad_totals = None
    for step_index in reversed(range(STEPS)):
        (
            norm_pull,
            normed_low,
            queries,
            keys,
            values,
            gathered,
            log_totals,
            backward_attended,
            norm_two_pull,
            normed_two_low,
            gelu_pull,
            activated_low,
        ) = kept_steps[step_index]
        down_grad = grad_carried.astype(jnp.bfloat16)
        w_down_part = jnp.einsum(
            "spf,spd->fd", activated_low, down_grad, preferred_element_type=jnp.float32
        )
        down_bias_part = jnp.sum(down_grad, axis=(0, 1), dtype=jnp.float32)
        activated_grad = jnp.einsum(
            "spd,fd->spf", down_grad, w_down, preferred_element_type=jnp.float32
        )
        (hidden_grad,) = gelu_pull(activated_grad)
        hidden_low = hidden_grad.astype(jnp.bfloat16)
        w_up_part = jnp.einsum(
            "spd,spf->df", normed_two_low, hidden_low, preferred_element_type=jnp.float32
        )
        up_bias_part = jnp.sum(hidden_low, axis=(0, 1), dtype=jnp.float32)
        normed_two_grad = jnp.einsum(
            "spf,df->spd", hidden_low, w_up, preferred_element_type=jnp.float32
        )
        middle_part, ln2_gain_part, ln2_bias_part = norm_two_pull(normed_two_grad)
        middle_grad = grad_carried + middle_part
        branch_grad = middle_grad.astype(jnp.bfloat16)
        w_out_part = jnp.einsum(
            "spd,spe->de", backward_attended, branch_grad, preferred_element_type=jnp.float32
        )
        out_bias_part = jnp.sum(branch_grad, axis=(0, 1), dtype=jnp.float32)
        attended_grad = jnp.einsum(
            "spe,de->spd", branch_grad, w_out, preferred_element_type=jnp.float32
        ).astype(jnp.bfloat16)
        keys_all, values_all = gathered
        backward_query_grad, backward_key_grad, backward_value_grad, row_inners = lax.map(
            attend_backward, (queries, keys_all, values_all, log_totals, attended_grad)
        )
        projected_grad = jnp.concatenate(
            [backward_query_grad, backward_key_grad, backward_value_grad], axis=-1
        ).astype(jnp.bfloat16)
        w_qkv_part = jnp.einsum(
            "spd,spe->de", normed_low, projected_grad, preferred_element_type=jnp.float32
        )
        q_bias_part = jnp.sum(projected_grad[..., :model_width], axis=(0, 1), dtype=jnp.float32)
        v_bias_part = jnp.sum(
            projected_grad[..., 2 * model_width :], axis=(0, 1), dtype=jnp.float32
        )
        normed_grad = jnp.einsum(
            "spe,de->spd", projected_grad, w_qkv, preferred_element_type=jnp.float32
        )
        inputs_part, ln1_gain_part, ln1_bias_part = norm_pull(normed_grad)
        inputs_grad = middle_grad + inputs_part
        per_sample = jnp.sum(inputs_grad, axis=1)
        lead_part = jnp.dot(one_hot.T, per_sample, precision=exact_mode)
        step_grads = (
            lead_part,
            ln1_gain_part,
            ln1_bias_part,
            w_qkv_part,
            q_bias_part,
            v_bias_part,
            w_out_part,
            out_bias_part,
            ln2_gain_part,
            ln2_bias_part,
            w_up_part,
            up_bias_part,
            w_down_part,
            down_bias_part,
        )
        grad_carried, step_grads = (inputs_grad, step_grads)
        if grad_totals is None:
            grad_totals = step_grads
        else:
            grad_totals = jax.tree.map(jnp.add, grad_totals, step_grads)
    grad_totals = band_share_end(grad_totals)
    grad_totals = sample_share(grad_totals)
    return (
        result,
        grad_carried,
        grad_totals[0],
        grad_totals[1],
        grad_totals[2],
        grad_totals[3],
        grad_totals[4],
        grad_totals[5],
        grad_totals[6],
        grad_totals[7],
        grad_totals[8],
        grad_totals[9],
        grad_totals[10],
        grad_totals[11],
        grad_totals[12],
        grad_totals[13],
    )


def solution(mesh):
    in_specs = (
        P("samp", "band", None),
        P("samp"),
        P("samp", "band", None),
        P(),
        P(),
        P(),
        P(),
        P(),
        P(),
        P(),
        P(),
        P(),
        P(),
        P(),
        P(),
        P(),
        P(),
    )
    out_specs = (
        P("samp", "band", None),
        P("samp", "band", None),
        P(None, "band"),
        P("band"),
        P("band"),
        P(None, "band"),
        P("band"),
        P("band"),
        P(None, "band"),
        P("band"),
        P("band"),
        P("band"),
        P(None, "band"),
        P("band"),
        P(None, "band"),
        P("band"),
    )
    return jax.shard_map(body, mesh=mesh, in_specs=in_specs, out_specs=out_specs, check_vma=False)
```

profile of v0, /device:TPU:0, one launch (start us, length us, event | category | flops | bytes accessed | tf_op | source)
XLA Modules:
  0.0 1716.4 jit_solution(16130773027809766441)
XLA Ops:
  19.5 76.7 %all-gather.5.cloned.1.call-done = bf16[2,2048,1024]{2,1,0:T(8,128)(2,1)} async-done(((bf16[2,128,1024]{2,1,0:T(8,128)(2,1)}), bf16[2,2048,1024]{2,1,0:T(8,128)(2,1)}) %all-gather.5.cloned.1.call-update) | async-done | bytes 8388624 | tf_op jit(solution)/shard_map/all_gather | solution.py:207
  96.1 11.8 copy.65
  108.0 64.1 %all-gather.7.cloned.1.call-done = bf16[2,2048,1024]{2,1,0:T(8,128)(2,1)} async-done(((bf16[2,128,1024]{2,1,0:T(8,128)(2,1)}), bf16[2,2048,1024]{2,1,0:T(8,128)(2,1)}) %all-gather.7.cloned.1.call-update) | async-done | bytes 8388624 | tf_op jit(solution)/shard_map/all_gather | solution.py:206
  184.7 35.8 %while.52 = (s32[]{:T(128)}, bf16[2,128,1024]{1,2,0:T(8,128)(2,1)}, f32[2,16,128]{2,1,0:T(8,128)S(1)}, bf16[2,2048,1024]{1,2,0:T(8,128)(2,1)}, bf16[2,128,1024]{...) while((s32[]{:T(128)}, bf16[2,128,1024]{1,2,0:T(8,128)(2,1)}, ...), condition=%wide.region_5.6_spmd, body=%wide.region_2.5_spmd.sunk | while | flops 1111619584 | bytes 98107568 | solution.py:208
  238.4 71.7 %all-gather.9.cloned.1.call-done = bf16[2,2048,1024]{2,1,0:T(8,128)(2,1)} async-done(((bf16[2,128,1024]{2,1,0:T(8,128)(2,1)}), bf16[2,2048,1024]{2,1,0:T(8,128)(2,1)}) %all-gather.9.cloned.1.call-update) | async-done | bytes 8388624 | tf_op jit(solution)/shard_map/all_gather | solution.py:207
  310.1 12.2 copy.69
  322.3 63.6 %all-gather.11.cloned.1.call-done = bf16[2,2048,1024]{2,1,0:T(8,128)(2,1)} async-done(((bf16[2,128,1024]{2,1,0:T(8,128)(2,1)}), bf16[2,2048,1024]{2,1,0:T(8,128)(2,1)}) %all-gather.11.cloned.1.call-update) | async-done | bytes 8388624 | tf_op jit(solution)/shard_map/all_gather | solution.py:206
  398.5 35.8 %while.53 = (s32[]{:T(128)}, bf16[2,128,1024]{1,2,0:T(8,128)(2,1)}, f32[2,16,128]{2,1,0:T(8,128)S(1)}, bf16[2,2048,1024]{1,2,0:T(8,128)(2,1)}, bf16[2,128,1024]{...) while((s32[]{:T(128)}, bf16[2,128,1024]{1,2,0:T(8,128)(2,1)}, ...), condition=%wide.region_13.14_spmd, body=%wide.region_10.13_spmd.sunk | while | flops 1111619584 | bytes 100204752 | solution.py:208
  459.9 364.1 %while.54 = (s32[]{:T(128)}, bf16[2,128,1024]{2,1,0:T(8,128)(2,1)}, bf16[2,128,1024]{2,1,0:T(8,128)(2,1)}, bf16[2,128,1024]{2,1,0:T(8,128)(2,1)}, bf16[2,2048,10...) while((s32[]{:T(128)}, bf16[2,128,1024]{2,1,0:T(8,128)(2,1)}, ...), condition=%wide.region_22.23_spmd, body=%wide.region_18.22_spmd.sunk | while | flops 2741237760 | bytes 249880848 | solution.py:296
  495.8 12.1 multiply_reduce_fusion.22
  507.9 12.4 multiply_convert_fusion.14
  539.9 24.1 %reduce-scatter.38.cloned.1.call-done = bf16[128,1024]{1,0:T(8,128)(2,1)} async-done(((bf16[2048,1024]{1,0:T(8,128)(2,1)}), bf16[128,1024]{1,0:T(8,128)(2,1)}) %reduce-scatter.38.cloned.1.call-update) | async-done | bytes 262160 | tf_op jit(solution)/shard_map/while
  565.2 73.9 %reduce-scatter.40.cloned.1.call-done = bf16[128,1024]{1,0:T(8,128)(2,1)} async-done(((bf16[2048,1024]{1,0:T(8,128)(2,1)}), bf16[128,1024]{1,0:T(8,128)(2,1)}) %reduce-scatter.40.cloned.1.call-update) | async-done | bytes 262160 | tf_op jit(solution)/shard_map/while
  676.9 12.1 multiply_reduce_fusion.22
  688.9 12.5 multiply_convert_fusion.14
  721.1 24.8 %reduce-scatter.38.cloned.1.call-done = bf16[128,1024]{1,0:T(8,128)(2,1)} async-done(((bf16[2048,1024]{1,0:T(8,128)(2,1)}), bf16[128,1024]{1,0:T(8,128)(2,1)}) %reduce-scatter.38.cloned.1.call-update) | async-done | bytes 262160 | tf_op jit(solution)/shard_map/while
  747.2 74.4 %reduce-scatter.40.cloned.1.call-done = bf16[128,1024]{1,0:T(8,128)(2,1)} async-done(((bf16[2048,1024]{1,0:T(8,128)(2,1)}), bf16[128,1024]{1,0:T(8,128)(2,1)}) %reduce-scatter.40.cloned.1.call-update) | async-done | bytes 262160 | tf_op jit(solution)/shard_map/while
  852.2 365.9 %while.55 = (s32[]{:T(128)}, bf16[2,128,1024]{2,1,0:T(8,128)(2,1)}, bf16[2,128,1024]{2,1,0:T(8,128)(2,1)}, bf16[2,128,1024]{2,1,0:T(8,128)(2,1)}, bf16[2,2048,10...) while((s32[]{:T(128)}, bf16[2,128,1024]{2,1,0:T(8,128)(2,1)}, ...), condition=%wide.region_31.32_spmd, body=%wide.region_27.31_spmd.sunk | while | flops 2741237760 | bytes 249880848 | solution.py:296
  888.2 12.0 multiply_reduce_fusion.23
  900.2 12.5 multiply_convert_fusion.16
  932.3 25.3 %reduce-scatter.42.cloned.1.call-done = bf16[128,1024]{1,0:T(8,128)(2,1)} async-done(((bf16[2048,1024]{1,0:T(8,128)(2,1)}), bf16[128,1024]{1,0:T(8,128)(2,1)}) %reduce-scatter.42.cloned.1.call-update) | async-done | bytes 262160 | tf_op jit(solution)/shard_map/while
  958.9 74.3 %reduce-scatter.44.cloned.1.call-done = bf16[128,1024]{1,0:T(8,128)(2,1)} async-done(((bf16[2048,1024]{1,0:T(8,128)(2,1)}), bf16[128,1024]{1,0:T(8,128)(2,1)}) %reduce-scatter.44.cloned.1.call-update) | async-done | bytes 262160 | tf_op jit(solution)/shard_map/while
  1071.1 12.1 multiply_reduce_fusion.23
  1083.1 12.5 multiply_convert_fusion.16
  1115.2 25.1 %reduce-scatter.42.cloned.1.call-done = bf16[128,1024]{1,0:T(8,128)(2,1)} async-done(((bf16[2048,1024]{1,0:T(8,128)(2,1)}), bf16[128,1024]{1,0:T(8,128)(2,1)}) %reduce-scatter.42.cloned.1.call-update) | async-done | bytes 262160 | tf_op jit(solution)/shard_map/while
  1141.6 74.2 %reduce-scatter.44.cloned.1.call-done = bf16[128,1024]{1,0:T(8,128)(2,1)} async-done(((bf16[2048,1024]{1,0:T(8,128)(2,1)}), bf16[128,1024]{1,0:T(8,128)(2,1)}) %reduce-scatter.44.cloned.1.call-update) | async-done | bytes 262160 | tf_op jit(solution)/shard_map/while
  1261.9 13.0 fusion.26
  1291.0 81.0 %reduce-scatter.28.cloned.1.call-done = bf16[1024,192]{0,1:T(8,128)(2,1)} async-done(((bf16[1024,3072]{0,1:T(8,128)(2,1)}), bf16[1024,192]{0,1:T(8,128)(2,1)}) %reduce-scatter.28.cloned.1.call-update) | async-done | bytes 393232 | tf_op jit(solution)/shard_map/reduce_scatter | solution.py:37
  1372.0 108.0 %reduce-scatter.32.cloned.1.call-done = bf16[1024,256]{1,0:T(8,128)(2,1)} async-done(((bf16[1024,4096]{1,0:T(8,128)(2,1)}), bf16[1024,256]{1,0:T(8,128)(2,1)}) %reduce-scatter.32.cloned.1.call-update) | async-done | bytes 524304 | tf_op jit(solution)/shard_map/reduce_scatter | solution.py:58
  1480.0 108.3 %reduce-scatter.34.cloned.1.call-done = bf16[4096,64]{0,1:T(8,128)(2,1)} async-done(((bf16[4096,1024]{0,1:T(8,128)(2,1)}), bf16[4096,64]{0,1:T(8,128)(2,1)}) %reduce-scatter.34.cloned.1.call-update) | async-done | bytes 524304 | tf_op jit(solution)/shard_map/reduce_scatter | solution.py:64
  1589.0 60.7 %all-reduce.9 = (bf16[1024]{0:T(1024)(128)(2,1)S(1)}, bf16[1024]{0:T(1024)(128)(2,1)S(1)}, bf16[1024]{0:T(1024)(128)(2,1)S(1)}, bf16[1024]{0:T(1024)(128)(2,1)S(...) all-reduce(bf16[1024]{0:T(1024)(128)(2,1)S(1)} %get-tuple-element.4, ...), channel_id=7, replica_groups=mesh['samp'=2,'band'=16] {'band'}, use_global_device_ids=true, to_apply=%region_40.41.clone | all-reduce | flops 12288 | bytes 49152
  1673.8 27.5 %all-reduce.14.cloned.1.call-done = (bf16[1024,192]{0,1:T(8,128)(2,1)}, bf16[1024,64]{0,1:T(8,128)(2,1)}, bf16[1024,256]{1,0:T(8,128)(2,1)}, bf16[4096,64]{0,1:T(8,128)(2,1)}) async-done(((bf16[1024,192]{0,1:T(8,128)(2,1)}, bf16[1024,64]{0,1:T(8,128)(2,1)}, bf16[1024,256]{1,0:T(8,128)(2,1)}, bf16[4096,64]{0,1:T(8,128)(2,1)}), (bf16[1024,192]{0,1:T(8,128)(2,1)}, bf16[1024,64]{0,1:T(8,128)(2,1)}, ...) | async-done | bytes 1572880 | tf_op jit(solution)/shard_map/psum | solution.py:78
  (519 shorter events, 504.1 us)
Async XLA Ops:
  7.2 213.4 %copy-start = (bf16[1024,1024]{1,0:T(8,128)(2,1)S(1)}, bf16[1024,1024]{1,0:T(8,128)(2,1)}, u32[]{:S(2)}) copy-start(bf16[1024,1024]{1,0:T(8,128)(2,1)} %param.34) | copy-start | bytes 6291460
  7.2 88.9 %all-gather.5.cloned.1.call-start = ((), (), s32[]{:S(2)}) async-start(), calls=%async_computation.9 | async-start | bytes 8912896 | tf_op jit(solution)/shard_map/all_gather | solution.py:207
  18.4 153.7 %all-gather.7.cloned.1.call-start = ((), (), s32[]{:S(2)}) async-start(), calls=%async_computation.10 | async-start | bytes 8912896 | tf_op jit(solution)/shard_map/all_gather | solution.py:206
  19.1 291.0 %all-gather.9.cloned.1.call-start = ((), (), s32[]{:S(2)}) async-start(), calls=%async_computation.11 | async-start | bytes 8912896 | tf_op jit(solution)/shard_map/all_gather | solution.py:207
  236.8 149.1 %all-gather.11.cloned.1.call-start = ((), (), s32[]{:S(2)}) async-start(), calls=%async_computation.12 | async-start | bytes 8912896 | tf_op jit(solution)/shard_map/all_gather | solution.py:206
  459.9 364.1 %copy-start.47 = (f32[1024]{0:T(1024)S(1)}, f32[1024]{0:T(1024)}, u32[]{:S(2)}) copy-start(f32[1024]{0:T(1024)} %param.29) | copy-start | bytes 12292
  459.9 364.1 %copy-start.66 = (f32[2,128]{1,0:T(2,128)S(1)}, f32[2,128]{1,0:T(2,128)}, u32[]{:S(2)}) copy-start(f32[2,128]{1,0:T(2,128)} %copy-done.65) | copy-start | bytes 3076
  460.1 103.9 %reduce-scatter.38.cloned.1.call-start = ((), (), s32[]{:S(2)}) async-start(), calls=%async_computation.19 | async-start | bytes 4456448 | tf_op jit(solution)/shard_map/while
  493.2 145.9 %reduce-scatter.40.cloned.1.call-start = ((), (), s32[]{:S(2)}) async-start(), calls=%async_computation.20 | async-start | bytes 4456448 | tf_op jit(solution)/shard_map/while
  641.2 104.6 %reduce-scatter.38.cloned.1.call-start = ((), (), s32[]{:S(2)}) async-start(), calls=%async_computation.19 | async-start | bytes 4456448 | tf_op jit(solution)/shard_map/while
  674.3 147.3 %reduce-scatter.40.cloned.1.call-start = ((), (), s32[]{:S(2)}) async-start(), calls=%async_computation.20 | async-start | bytes 4456448 | tf_op jit(solution)/shard_map/while
  852.2 366.8 %copy-start.48 = (f32[1024]{0:T(1024)S(1)}, f32[1024]{0:T(1024)}, u32[]{:S(2)}) copy-start(f32[1024]{0:T(1024)} %param.29) | copy-start | bytes 12292
  852.2 366.8 %copy-start.50 = (f32[1024]{0:T(1024)S(1)}, f32[1024]{0:T(1024)}, u32[]{:S(2)}) copy-start(f32[1024]{0:T(1024)} %param.30) | copy-start | bytes 12292
  852.2 366.8 %copy-start.67 = (f32[2,128]{1,0:T(2,128)S(1)}, f32[2,128]{1,0:T(2,128)}, u32[]{:S(2)}) copy-start(f32[2,128]{1,0:T(2,128)} %copy-done.65) | copy-start | bytes 3076
  852.2 366.8 %copy-start.70 = (f32[2,128]{1,0:T(2,128)S(1)}, f32[2,128]{1,0:T(2,128)}, u32[]{:S(2)}) copy-start(f32[2,128]{1,0:T(2,128)} %copy-done.68) | copy-start | bytes 3076
  852.4 105.2 %reduce-scatter.42.cloned.1.call-start = ((), (), s32[]{:S(2)}) async-start(), calls=%async_computation.21 | async-start | bytes 4456448 | tf_op jit(solution)/shard_map/while
  885.6 147.6 %reduce-scatter.44.cloned.1.call-start = ((), (), s32[]{:S(2)}) async-start(), calls=%async_computation.22 | async-start | bytes 4456448 | tf_op jit(solution)/shard_map/while
  1035.3 105.0 %reduce-scatter.42.cloned.1.call-start = ((), (), s32[]{:S(2)}) async-start(), calls=%async_computation.21 | async-start | bytes 4456448 | tf_op jit(solution)/shard_map/while
  1068.5 147.3 %reduce-scatter.44.cloned.1.call-start = ((), (), s32[]{:S(2)}) async-start(), calls=%async_computation.22 | async-start | bytes 4456448 | tf_op jit(solution)/shard_map/while
  1218.1 72.9 %reduce-scatter.30.cloned.1.call-start = ((), (), s32[]{:S(2)}) async-start(), calls=%async_computation.14 | async-start | bytes 2228224 | tf_op jit(solution)/shard_map/reduce_scatter | solution.py:46
  1218.9 153.1 %reduce-scatter.28.cloned.1.call-start = ((), (), s32[]{:S(2)}) async-start(), calls=%async_computation.13 | async-start | bytes 6684672 | tf_op jit(solution)/shard_map/reduce_scatter | solution.py:37
  1227.6 252.4 %reduce-scatter.32.cloned.1.call-start = ((), (), s32[]{:S(2)}) async-start(), calls=%async_computation.15 | async-start | bytes 8912896 | tf_op jit(solution)/shard_map/reduce_scatter | solution.py:58
  1250.8 337.4 %reduce-scatter.34.cloned.1.call-start = ((), (), s32[]{:S(2)}) async-start(), calls=%async_computation.16 | async-start | bytes 8912896 | tf_op jit(solution)/shard_map/reduce_scatter | solution.py:64
  1274.9 384.1 %reduce-scatter.36.cloned.1.call-start = ((), (), s32[]{:S(2)}) async-start(), calls=%async_computation.17 | async-start | bytes 278528
  1284.5 303.8 %copy-start.88 = (f32[1024]{0:T(1024)S(1)}, f32[1024]{0:T(1024)}, u32[]{:S(2)}) copy-start(f32[1024]{0:T(1024)} %get-tuple-element.258) | copy-start | bytes 12292
  1284.5 303.8 %copy-start.89 = (f32[1024]{0:T(1024)S(1)}, f32[1024]{0:T(1024)}, u32[]{:S(2)}) copy-start(f32[1024]{0:T(1024)} %get-tuple-element.382) | copy-start | bytes 12292
  1284.5 303.8 %copy-start.105 = (f32[1024]{0:T(1024)S(1)}, f32[1024]{0:T(1024)}, u32[]{:S(2)}) copy-start(f32[1024]{0:T(1024)} %get-tuple-element.254) | copy-start | bytes 12292
  1284.5 303.8 %copy-start.106 = (f32[1024]{0:T(1024)S(1)}, f32[1024]{0:T(1024)}, u32[]{:S(2)}) copy-start(f32[1024]{0:T(1024)} %get-tuple-element.261) | copy-start | bytes 12292
  1284.5 304.5 %copy-start.83 = (f32[4096]{0:T(1024)S(1)}, f32[4096]{0:T(1024)}, u32[]{:S(2)}) copy-start(f32[4096]{0:T(1024)} %get-tuple-element.393) | copy-start | bytes 49156
  1284.5 304.5 %copy-start.84 = (f32[4096]{0:T(1024)S(1)}, f32[4096]{0:T(1024)}, u32[]{:S(2)}) copy-start(f32[4096]{0:T(1024)} %get-tuple-element.395) | copy-start | bytes 49156
  1286.1 364.4 %copy-start.16 = (f32[2,128,1024]{2,1,0:T(8,128)S(1)}, f32[2,128,1024]{2,1,0:T(8,128)}, u32[]{:S(2)}) copy-start(f32[2,128,1024]{2,1,0:T(8,128)} %copy-done.15) | copy-start | bytes 3145732
  1290.1 411.1 %all-reduce.14.cloned.1.call-start = ((), (), s32[]{:S(2)}) async-start(), calls=%async_computation.18 | async-start | bytes 3145728 | tf_op jit(solution)/shard_map/psum | solution.py:78
  (118 other events, 768.4 us)
Sparse Core Ops, SparseCore 0:
  18.5 77.6 all-gather.4
  98.9 73.1 all-gather.6
  236.9 73.1 all-gather.8
  312.7 73.1 all-gather.10
  493.4 70.5 reduce-scatter.37
  567.7 71.3 reduce-scatter.39
  674.4 71.3 reduce-scatter.37
  749.7 71.7 reduce-scatter.39
  885.7 71.8 reduce-scatter.41
  961.3 71.8 reduce-scatter.43
  1068.6 71.6 reduce-scatter.41
  1144.1 71.6 reduce-scatter.43
  1222.7 60.6 reduce-scatter.29
  1287.7 84.2 reduce-scatter.27
  1375.9 104.0 reduce-scatter.31
  1483.9 104.3 reduce-scatter.33
  1592.2 55.0 reduce-scatter.35
  1649.6 51.5 all-reduce.13
where the time goes:
time: 1730 us; the launch traced here: 1720 us
  waiting for transfers between devices  999 us (58%)
  matrix products  340 us (20%)
  local copies, waits for them, and re-layouts  197 us (11%)
  other arithmetic  91.3 us (5%)
  blocking collectives  69.3 us (4%)
  between operations  17.5 us (1%)
    while x16, waiting for transfers between devices  396 us
    all_gather x2, waiting for transfers between devices, body(): lax.all_gather(forward_values, 'band', axis=1, tiled=True)  148 us
    all_gather x2, waiting for transfers between devices, body(): forward_keys_all = lax.all_gather(forward_keys, 'band', axis=1, tiled=True)  128 us
    reduce_scatter x1, waiting for transfers between devices, band_share_end(): lax.psum_scatter(parts[12].astype(jnp.bfloat16), 'band', scatter_dimensio...  108 us
    reduce_scatter x1, waiting for transfers between devices, band_share_end(): lax.psum_scatter(parts[10].astype(jnp.bfloat16), 'band', scatter_dimensio...  108 us
    reduce_scatter x1, waiting for transfers between devices, band_share_end(): lax.psum_scatter(parts[3].astype(jnp.bfloat16), 'band', scatter_dimension...  81 us
    while x60, local copies, waits for them, and re-layouts  66.8 us
    unnamed x1, blocking collectives  60.7 us
  transfers between devices with their start and end apart: 18, of which 16 were waited for; matrix products, arithmetic and copies ran while one was open for 17% of the time, Pallas kernels for 0%

commit v1 on v0

v1 whole, which is shorter than its diff:
```python
import functools

import jax
import jax.numpy as jnp
from jax import lax
from jax.experimental import pallas as pl
from jax.experimental.pallas import tpu as pltpu
from jax.sharding import Mesh
from jax.sharding import PartitionSpec as P

HD = 64
STEPS = 2
EPS = 1e-05
EXP_SCALE = 0.125 * 1.4426950408889634
GELU_A = 0.7978845608028654
GELU_B = 0.044715
SWAP = [(0, 1), (1, 0)]
f32 = jnp.float32
bf16 = jnp.bfloat16


def contract(a, b, a_dim, b_dim):
    return lax.dot_general(a, b, (((a_dim,), (b_dim,)), ((), ())), preferred_element_type=f32)


def head_part(x, h, heads):
    if heads == 1:
        return x
    lane = lax.broadcasted_iota(jnp.int32, x.shape, 1)
    return jnp.where(lane // HD == h, x, jnp.zeros_like(x))


def attend_kernel(q_ref, k_ref, v_ref, o_ref, *, heads):
    q, k, v = q_ref[...], k_ref[...], v_ref[...]
    out = None
    for h in range(heads):
        s = contract(head_part(q, h, heads), k, 1, 1)
        top = jnp.max(s, axis=-1, keepdims=True)
        e = jnp.exp2((s - top) * EXP_SCALE)
        total = jnp.sum(e, axis=-1, keepdims=True)
        o = head_part(contract(e.astype(bf16), v, 1, 0) / total, h, heads)
        out = o if out is None else out + o
    o_ref[...] = out.astype(bf16)


def attend(q, k, v):
    rows, width = q.shape
    count = k.shape[0]
    block = 2 * HD
    own = pl.BlockSpec((rows, block), lambda j: (0, j))
    full = pl.BlockSpec((count, block), lambda j: (0, j))
    return pl.pallas_call(
        functools.partial(attend_kernel, heads=block // HD),
        grid=(width // block,),
        in_specs=[own, full, full],
        out_specs=own,
        out_shape=jax.ShapeDtypeStruct((rows, width), bf16),
        compiler_params=pltpu.CompilerParams(vmem_limit_bytes=48 * 2**20),
        cost_estimate=pl.CostEstimate(
            flops=4 * rows * count * width,
            bytes_accessed=4 * (rows + count) * width,
            transcendentals=rows * count * width // HD,
        ),
        name="attend",
    )(q, k, v)


def attend_back_kernel(q_ref, k_ref, v_ref, do_ref, dq_ref, dk_ref, dv_ref, dk_sum, dv_sum, *, heads):
    step = pl.program_id(0)

    @pl.when(step == 0)
    def _():
        dk_sum[...] = jnp.zeros_like(dk_sum)
        dv_sum[...] = jnp.zeros_like(dv_sum)

    q, k, v, do = q_ref[...], k_ref[...], v_ref[...], do_ref[...]
    dq = None
    for h in range(heads):
        qh, doh = head_part(q, h, heads), head_part(do, h, heads)
        s = contract(qh, k, 1, 1)
        dp = contract(doh, v, 1, 1)
        top = jnp.max(s, axis=-1, keepdims=True)
        e = jnp.exp2((s - top) * EXP_SCALE)
        inverse = 1.0 / jnp.sum(e, axis=-1, keepdims=True)
        inner = jnp.sum(e * dp, axis=-1, keepdims=True) * inverse
        p = e * inverse
        ds = (p * (dp - inner)).astype(bf16)
        part = head_part(contract(ds, k, 1, 0), h, heads)
        dq = part if dq is None else dq + part
        dk_sum[...] += contract(ds, qh, 0, 0)
        dv_sum[...] += contract(p.astype(bf16), doh, 0, 0)
    dq_ref[...] = (dq * 0.125).astype(bf16)

    @pl.when(step == pl.num_programs(0) - 1)
    def _():
        dk_ref[...] = (dk_sum[...] * 0.125).astype(bf16)
        dv_ref[...] = dv_sum[...].astype(bf16)


def attend_back(q, k, v, do):
    count, width = q.shape
    rows = 256
    part = pl.BlockSpec((rows, width), lambda i: (i, 0))
    full = pl.BlockSpec((count, width), lambda i: (0, 0))
    out = jax.ShapeDtypeStruct((count, width), bf16)
    return pl.pallas_call(
        functools.partial(attend_back_kernel, heads=width // HD),
        grid=(count // rows,),
        in_specs=[part, full, full, part],
        out_specs=[part, full, full],
        out_shape=[out, out, out],
        scratch_shapes=[pltpu.VMEM((count, width), f32), pltpu.VMEM((count, width), f32)],
        compiler_params=pltpu.CompilerParams(vmem_limit_bytes=48 * 2**20),
        cost_estimate=pl.CostEstimate(
            flops=10 * count * count * width,
            bytes_accessed=14 * count * width,
            transcendentals=count * count * width // HD,
        ),
        name="attend_back",
    )(q, k, v, do)


def norm_parts(v):
    centred = v - jnp.mean(v, axis=-1, keepdims=True)
    r = lax.rsqrt(jnp.mean(centred * centred, axis=-1, keepdims=True) + EPS)
    return centred * r, r


def norm_back(dy, n, r, gain):
    dyg = dy * gain
    mean_one = jnp.mean(dyg, axis=-1, keepdims=True)
    mean_two = jnp.mean(dyg * n, axis=-1, keepdims=True)
    dv = r * (dyg - mean_one - n * mean_two)
    return dv, jnp.sum(dy * n, axis=0), jnp.sum(dy, axis=0)


def gelu(x):
    return 0.5 * x * (1.0 + jnp.tanh(GELU_A * (x + GELU_B * x * x * x)))


def gelu_slope(x):
    t = jnp.tanh(GELU_A * (x + GELU_B * x * x * x))
    return 0.5 * (1.0 + t) + 0.5 * x * (1.0 - t * t) * (GELU_A * (1.0 + 3.0 * GELU_B * x * x))


def dot(a, b):
    return jnp.dot(a, b, preferred_element_type=f32)


def dot_t(a, b):
    return contract(a, b, 1, 1)


def token_dot(pairs):
    a = jnp.concatenate([p[0] for p in pairs])
    b = jnp.concatenate([p[1] for p in pairs])
    return contract(a, b, 0, 0).astype(bf16)


def swap(x, axis):
    return lax.ppermute(x, axis, SWAP)


def half_sum(x, axis, dim):
    me = lax.axis_index(axis)
    there = lax.dynamic_index_in_dim(x, 1 - me, dim, keepdims=False)
    here = lax.dynamic_index_in_dim(x, me, dim, keepdims=False)
    return (here.astype(f32) + swap(there, axis).astype(f32)).astype(bf16)


def add_pair(x, axis):
    return (x.astype(f32) + swap(x, axis).astype(f32)).astype(bf16)


def add_samples(x, two):
    return add_pair(x, "samp") if two else lax.psum(x, "samp")


def body(
    fields,
    lead_bucket,
    cotangent,
    lead_table,
    ln1_gain,
    ln1_bias,
    w_qkv,
    q_bias,
    v_bias,
    w_out,
    out_bias,
    ln2_gain,
    ln2_bias,
    w_up,
    up_bias,
    w_down,
    down_bias,
    *,
    axes,
    x_axes,
    samp_count,
):
    band = tuple(axes)
    low = ("core", "zl") + x_axes[::-1]
    members = 2 ** len(low)
    order = x_axes + ("zl", "core")
    D = w_out.shape[0]
    W = D // members
    half = fields.shape[1]
    rows = 2 * half
    two = samp_count == 2
    zh = lax.axis_index("zh")
    me = lax.axis_index(low)

    def pick(x, i):
        return lax.dynamic_index_in_dim(x, i, 0, keepdims=False)

    def to_sample(x):
        return jnp.concatenate([pick(x, zh), swap(pick(x, 1 - zh), "zh")])

    def to_band(x):
        own = x[:half]
        other = swap(x[half:].astype(bf16), "zh").astype(x.dtype)
        return jnp.where(zh == 0, jnp.stack([own, other]), jnp.stack([other, own]))

    def gather(x):
        if len(x_axes) == 1:
            x_axis = x_axes[0]
            cut = x.shape[0] // 2
            by_x = swap(x, x_axis)
            by_z = swap(x, "zl")
            far = [swap(by_x[:cut], "zl"), swap(by_z[cut:], x_axis)]
            pieces = [(x, 0, 0), (by_x, 1, 0), (by_z, 2, 0), (far[0], 3, 0), (far[1], 3, cut)]
            pieces += [(swap(p, "core"), 4 + k, o) for p, k, o in pieces]
        else:
            pieces = [(x, 0, 0)]
            for bit, axis in enumerate(order):
                pieces += [(swap(p, axis), k + 2**bit, 0) for p, k, _ in pieces]
        out = jnp.zeros((members * rows, D), bf16)
        for piece, k, offset in pieces:
            out = lax.dynamic_update_slice(out, piece, ((me ^ k) * rows + offset, 0))
        return out

    lead_row = pick(lead_table, pick(lead_bucket, zh)).astype(f32)
    kv_bias = jnp.concatenate([jnp.zeros_like(v_bias), v_bias])
    carried = to_sample(fields).astype(f32)
    out_grad = to_sample(cotangent)

    def member_columns(x, block):
        return lax.dynamic_slice_in_dim(x, block * D + me * W, W, x.ndim - 1)

    kept = []
    for _ in range(STEPS):
        inputs = carried + lead_row
        n1, r1 = norm_parts(inputs)
        normed = (n1 * ln1_gain + ln1_bias).astype(bf16)
        normed_all = gather(normed)
        queries = (dot(normed, w_qkv[:, :D]) + q_bias).astype(bf16)
        keys_values = (dot(normed_all, w_qkv[:, D:]) + kv_bias).astype(bf16)
        keys, values = keys_values[:, :D], keys_values[:, D:]
        attended = attend(queries, keys, values)
        q_own = (
            dot(normed_all, member_columns(w_qkv, 0)) + member_columns(q_bias, 0)
        ).astype(bf16)
        k_own = member_columns(keys, 0)
        v_own = member_columns(values, 0)
        middle = inputs + dot(attended, w_out) + out_bias
        n2, r2 = norm_parts(middle)
        normed_two = (n2 * ln2_gain + ln2_bias).astype(bf16)
        hidden = dot(normed_two, w_up) + up_bias
        activated = gelu(hidden).astype(bf16)
        carried = middle + dot(activated, w_down) + down_bias
        kept.append((n1, r1, normed, q_own, k_own, v_own, attended, n2, r2, normed_two, hidden, activated))
    result = to_band(carried.astype(bf16))

    grad = out_grad
    small = None
    pairs = {"qkv": [], "out": [], "up": [], "down": []}
    for n1, r1, normed, q_own, k_own, v_own, attended, n2, r2, normed_two, hidden, activated in kept[::-1]:
        down_grad = grad.astype(bf16)
        hidden_grad = (gelu_slope(hidden) * dot_t(down_grad, w_down)).astype(bf16)
        dv, gain_two, bias_two = norm_back(dot_t(hidden_grad, w_up), n2, r2, ln2_gain)
        middle_grad = grad + dv
        branch_grad = middle_grad.astype(bf16)
        pairs["down"].append((down_grad, activated))
        pairs["up"].append((hidden_grad, normed_two))
        pairs["out"].append((branch_grad, attended))
        attended_grad = dot_t(branch_grad, w_out).astype(bf16)
        sent = attended_grad.reshape(rows, members, W).transpose(1, 0, 2)
        own_grad = lax.all_to_all(sent, low, 0, 0, tiled=True).reshape(members * rows, W)
        dq, dk, dval = attend_back(q_own, k_own, v_own, own_grad)
        sent = jnp.stack([t.reshape(members, rows, W) for t in (dq, dk, dval)], axis=1)
        back = lax.all_to_all(sent, low, 0, 0, tiled=True)
        projected_grad = back.transpose(2, 1, 0, 3).reshape(rows, 3 * D)
        pairs["qkv"].append((projected_grad, normed))
        dv, gain_one, bias_one = norm_back(dot_t(projected_grad, w_qkv), n1, r1, ln1_gain)
        grad = middle_grad + dv
        step_small = (
            gain_one,
            bias_one,
            jnp.sum(projected_grad[:, :D], axis=0, dtype=f32),
            jnp.sum(projected_grad[:, 2 * D :], axis=0, dtype=f32),
            jnp.sum(branch_grad, axis=0, dtype=f32),
            gain_two,
            bias_two,
            jnp.sum(hidden_grad, axis=0, dtype=f32),
            jnp.sum(down_grad, axis=0, dtype=f32),
            jnp.sum(grad, axis=0),
        )
        small = step_small if small is None else tuple(a + b for a, b in zip(small, step_small))
    fields_grad = to_band(grad)

    def blocks(x):
        return x.reshape((2,) * len(axes) + (x.shape[0] // 2 ** len(axes), x.shape[1]))

    def share(x, first_y, turn):
        x = blocks(x)
        left = list(axes)
        x = half_sum(x, "core", left.index("core"))
        left.remove("core")
        if first_y and two:
            x = x.reshape(x.shape[:-2] + (2, x.shape[-2] // 2, x.shape[-1]))
            x = half_sum(x, "samp", len(left))
        for axis in turn:
            x = half_sum(x, axis, left.index(axis))
            left.remove(axis)
        if first_y and two:
            y = lax.axis_index("samp")
            other = swap(x, "samp")
            x = jnp.concatenate([jnp.where(y == 0, x, other), jnp.where(y == 0, other, x)])
        else:
            x = add_samples(x, two)
        return x.astype(f32).T

    x_first = x_axes + ("zl", "zh")
    z_first = ("zl", "zh") + x_axes
    w_down_grad = share(token_dot(pairs["down"]), True, x_first)
    w_up_grad = share(token_dot(pairs["up"]), False, x_first)
    w_out_grad = share(token_dot(pairs["out"]), False, z_first)
    w_qkv_grad = share(token_dot(pairs["qkv"]), True, z_first)

    bands = 2 ** len(axes)
    lead = small[-1]
    leads = [jnp.where(zh == i, lead, 0.0) for i in range(2)]
    vectors = list(small[:-1]) + leads
    packed = jnp.concatenate([v.reshape(bands, -1) for v in vectors], axis=1)
    summed = jnp.sum(lax.all_to_all(packed, band, 0, 0, tiled=True), axis=0)
    widths = [v.shape[0] // bands for v in vectors]
    starts = [sum(widths[:i]) for i in range(len(widths) + 1)]
    lead_sums = summed[starts[-3] :].reshape(2, -1)
    one_hot = (lead_bucket[:, None] == jnp.arange(lead_table.shape[0], dtype=jnp.int32)[None, :]).astype(f32)
    lead_part = jnp.dot(one_hot.T, lead_sums, precision=lax.Precision.HIGHEST)
    joined = jnp.concatenate([summed[: starts[-3]], lead_part.reshape(-1)])
    if two:
        joined = joined + swap(joined, "samp")
    else:
        joined = lax.psum(joined, "samp")
    g = [joined[starts[i] : starts[i + 1]] for i in range(len(widths) - 2)]
    lead_grad = joined[starts[-3] :].reshape(lead_part.shape)
    return (
        result,
        fields_grad,
        lead_grad,
        g[0],
        g[1],
        w_qkv_grad,
        g[2],
        g[3],
        w_out_grad,
        g[4],
        g[5],
        g[6],
        w_up_grad,
        g[7],
        w_down_grad,
        g[8],
    )


def solution(mesh):
    samp_count, band_count = mesh.shape["samp"], mesh.shape["band"]
    x_axes = tuple(f"x{i}" for i in range((band_count // 8).bit_length() - 1))
    axes = ("zh", "zl") + x_axes + ("core",)
    assert 2 ** len(axes) == band_count
    fine = Mesh(mesh.devices.reshape((samp_count,) + (2,) * len(axes)), ("samp",) + axes)
    tokens = P("samp", axes, None)
    columns, vector = P(None, axes), P(axes)
    in_specs = (tokens, P("samp"), tokens) + (P(),) * 14
    out_specs = (
        tokens,
        tokens,
        columns,
        vector,
        vector,
        columns,
        vector,
        vector,
        columns,
        vector,
        vector,
        vector,
        columns,
        vector,
        columns,
        vector,
    )
    run = functools.partial(body, axes=axes, x_axes=x_axes, samp_count=samp_count)
    return jax.shard_map(run, mesh=fine, in_specs=in_specs, out_specs=out_specs, check_vma=False)
```

time: 1730 us -> 635 us (0.37)
  waiting for transfers between devices: 999 us -> 197 us
  matrix products: 340 us -> 118 us
  local copies, waits for them, and re-layouts: 197 us -> 98.7 us
  Pallas kernels: 0 us -> 97.5 us
  blocking collectives: 69.3 us -> 0 us
  starting transfers between devices: 0.94 us -> 63.9 us
  other arithmetic: 91.3 us -> 45.8 us
    while x16 -> x0, waiting for transfers between devices: 396 us -> none
    reduce_scatter x4 -> x0, waiting for transfers between devices: 297 us -> none  [the longest x1 108 us: band_share_end(): lax.psum_scatter(parts[12].astype(jnp.bfloat16), 'band', scatter_dimensio...]
    all_gather x4 -> x0, waiting for transfers between devices: 276 us -> none  [the longest x2 148 us: body(): lax.all_gather(forward_values, 'band', axis=1, tiled=True)]
    dot_general x55 -> x25, matrix products: 340 us -> 118 us  [the longest x12 60.1 us: dot(): return jnp.dot(a, b, preferred_element_type=f32)]
    ppermute x0 -> x45, waiting for transfers between devices: none -> 164 us  [swap(): return lax.ppermute(x, axis, SWAP)]
    while x66 -> x0, local copies, waits for them, and re-layouts: 116 us -> none
    pallas_call x0 -> x4, Pallas kernels: none -> 97.5 us  [the longest x2 62.7 us: attend_back(): pl.pallas_call(functools.partial(attend_back_kernel, heads=width // HD),...]
    unnamed x1 -> x0, blocking collectives: 60.7 us -> none
  transfers between devices with their start and end apart: 18 -> 50, of which waited for: 16 -> 23; matrix products, arithmetic and copies ran while one was open for 17% -> 27% of each run, Pallas kernels for 0% -> 8%
where the time goes in v1:
time: 635 us; the launch traced here: 626 us
  waiting for transfers between devices  197 us (31%)
  matrix products  118 us (19%)
  local copies, waits for them, and re-layouts  98.7 us (16%)
  Pallas kernels  97.5 us (15%)
  starting transfers between devices  63.9 us (10%)
  other arithmetic  45.8 us (7%)
    ppermute x45, waiting for transfers between devices, swap(): return lax.ppermute(x, axis, SWAP)  164 us
    pallas_call x2, Pallas kernels, attend_back(): pl.pallas_call(functools.partial(attend_back_kernel, heads=width // HD),...  62.7 us
    dot_general x12, matrix products, dot(): return jnp.dot(a, b, preferred_element_type=f32)  60.1 us
    dot_general x12, matrix products, contract(): lax.dot_general(a, b, (((a_dim,), (b_dim,)), ((), ())), preferred_element...  58 us
    ppermute x45, starting transfers between devices, swap(): return lax.ppermute(x, axis, SWAP)  43 us
    pallas_call x2, Pallas kernels, attend(): pl.pallas_call(functools.partial(attend_kernel, heads=block // HD), grid=...  34.9 us
    convert_element_type x18, other arithmetic, half_sum(): return (here.astype(f32) + swap(there, axis).astype(f32)).astype(bf16)  23.5 us
    unnamed x165, local copies, waits for them, and re-layouts  21.9 us
  transfers between devices with their start and end apart: 50, of which 23 were waited for; matrix products, arithmetic and copies ran while one was open for 27% of the time, Pallas kernels for 8%

profile of v1, /device:TPU:0, one launch (start us, length us, event | category | flops | bytes accessed | tf_op | source)
XLA Modules:
  0.0 626.3 jit_solution(15180412059228236581)
XLA Ops:
  9.9 8.0 %collective-permute-done = bf16[128,1024]{1,0:T(8,128)(2,1)S(1)} collective-permute-done((bf16[128,1024]{1,0:T(8,128)(2,1)S(1)}, bf16[128,1024]{1,0:T(8,128)(2,1)S(1)}, u32[]{:S(2)}, u32[]{:S(2)}) %collective-permute-start) | collective-permute-done | bytes 262176 | tf_op jit(solution)/shard_map/ppermute | solution.py:161
  25.9 9.7 %collective-permute-done.2 = bf16[256,1024]{1,0:T(8,128)(2,1)S(1)} collective-permute-done((bf16[256,1024]{1,0:T(8,128)(2,1)}, bf16[256,1024]{1,0:T(8,128)(2,1)S(1)}, u32[]{:S(2)}, u32[]{:S(2)}) %collective-permute-start.2) | collective-permute-done | bytes 524320 | tf_op jit(solution)/shard_map/ppermute | solution.py:161
  54.8 11.9 %add_convert_fusion.1 = bf16[2048,2048]{1,0:T(8,128)(2,1)S(1)} fusion(f32[2048]{0:T(1024)S(1)} %concatenate.46, bf16[2048,1024]{1,0:T(8,128)(2,1)} %constant_dynamic-update-slice_fusion.10, bf16[1024,3072]{1,0:T(8,128)(2,1)} %param.23), kind=kOutput, calls=%fused_computation.1 | convolution fusion | flops 8598323200 | bytes 16785408 | tf_op jit(solution)/shard_map/dot_general | solution.py:147
  69.3 17.3 %attend.2 = bf16[256,1024]{1,0:T(8,128)(2,1)S(1)} custom-call(bf16[256,1024]{1,0:T(8,128)(2,1)S(1)} %fusion.56.q_ref, bf16[2048,1024]{1,0:T(8,128)(2,1)S(1)} %get-tuple-element.71.k_ref, bf16[2048,1024]{1,0:T(8,128)(2,1)} %get-tuple-element.70.v_ref), custom_call_target="tpu_custom_call" | custom-call | flops 2147483648 | bytes 9437184 | tf_op jit(solution)/shard_map/attend/pallas_call | solution.py:52
  88.2 9.1 %multiply_convert_fusion.1 = (bf16[256,4096]{1,0:T(8,128)(2,1)S(1)}, f32[256,4096]{1,0:T(8,128)}) fusion(f32[4096]{0:T(1024)S(1)} %copy-done.62, bf16[256,1024]{1,0:T(8,128)(2,1)S(1)} %add_convert_fusion.5, bf16[1024,4096]{1,0:T(8,128)(2,1)} %param.30), kind=kOutput, calls=%fused_computation.47 | convolution fusion | flops 2157969408 | bytes 15220736 | tf_op jit(solution)/shard_map/dot_general | solution.py:147
  103.5 11.3 %collective-permute-done.11 = bf16[256,1024]{1,0:T(8,128)(2,1)S(1)} collective-permute-done((bf16[256,1024]{1,0:T(8,128)(2,1)S(1)}, bf16[256,1024]{1,0:T(8,128)(2,1)S(1)}, u32[]{:S(2)}, u32[]{:S(2)}) %collective-permute-start.11) | collective-permute-done | bytes 524320 | tf_op jit(solution)/shard_map/ppermute | solution.py:161
  126.1 9.3 %add_convert_fusion = bf16[2048,2048]{1,0:T(8,128)(2,1)S(1)} fusion(f32[2048]{0:T(1024)S(1)} %concatenate.46, bf16[2048,1024]{1,0:T(8,128)(2,1)S(1)} %constant_dynamic-update-slice_fusion, bf16[1024,3072]{1,0:T(8,128)(2,1)S(1)} %bitcast.239), kind=kOutput, calls=%fused_computation | convolution fusion | flops 8598323200 | bytes 16785408 | tf_op jit(solution)/shard_map/dot_general | solution.py:147
  137.9 17.6 %attend.3 = bf16[256,1024]{1,0:T(8,128)(2,1)S(1)} custom-call(bf16[256,1024]{1,0:T(8,128)(2,1)S(1)} %fusion.53.q_ref, bf16[2048,1024]{1,0:T(8,128)(2,1)S(1)} %get-tuple-element.69.k_ref, bf16[2048,1024]{1,0:T(8,128)(2,1)} %get-tuple-element.68.v_ref), custom_call_target="tpu_custom_call" | custom-call | flops 2147483648 | bytes 9437184 | tf_op jit(solution)/shard_map/attend/pallas_call | solution.py:52
  156.8 8.2 %multiply_convert_fusion = (bf16[256,4096]{1,0:T(8,128)(2,1)}, f32[256,4096]{1,0:T(8,128)S(1)}) fusion(f32[4096]{0:T(1024)S(1)} %copy-done.62, bf16[256,1024]{1,0:T(8,128)(2,1)S(1)} %add_convert_fusion.3, bf16[1024,4096]{1,0:T(8,128)(2,1)} %param.30), kind=kOutput, calls=%fused_computation.46 | convolution fusion | flops 2157969408 | bytes 15220736 | tf_op jit(solution)/shard_map/dot_general | solution.py:147
  165.1 7.1 %convert_reduce_fusion.1 = (f32[4096]{0:T(1024)S(1)}, bf16[256,4096]{1,0:T(8,128)(2,1)S(1)}) fusion(bf16[256,1024]{1,0:T(8,128)(2,1)S(1)} %get-tuple-element.55, bf16[4096,1024]{1,0:T(8,128)(2,1)} %param.32, f32[256,4096]{1,0:T(8,128)S(1)} %get-tuple-element.103), kind=kOutput, calls=%fused_computation.45 | convolution fusion | flops 2169499648 | bytes 15220736 | tf_op jit(solution)/shard_map/dot_general | solution.py:23
  192.6 31.3 %attend_back.2 = (bf16[2048,128]{1,0:T(8,128)(2,1)S(1)}, bf16[2048,128]{1,0:T(8,128)(2,1)S(1)}, bf16[2048,128]{1,0:T(8,128)(2,1)S(1)}) custom-call(bf16[2048,128]{1,0:T(8,128)(2,1)S(1)} %copy-done.12, bf16[2048,128]{1,0:T(8,128)(2,1)S(1)} %get-tuple-element.115.k_ref, bf16[2048,128]{1,0:T(8,128)(2,1)S(1)} %get-tuple-element.114.v_ref, ...), custom_call_target="tpu_custom_call" | custom-call | flops 5368709120 | bytes 3670016 | tf_op jit(solution)/shard_map/attend_back/pallas_call | solution.py:106
  243.1 14.9 %all-to-all-done.1 = bf16[8,3,256,128]{2,3,1,0:T(8,128)(2,1)} async-done(((bf16[8,3,256,128]{2,3,1,0:T(8,128)(2,1)}), bf16[8,3,256,128]{2,3,1,0:T(8,128)(2,1)}, u32[]{:S(2)}, u32[]{:S(2)}) %all-to-all-start.1) | async-done | bytes 1572896 | tf_op jit(solution)/shard_map/all_to_all | solution.py:292
  259.6 5.9 multiply_reduce_fusion.3
  266.4 6.9 %convert_reduce_fusion = (f32[4096]{0:T(1024)S(1)}, bf16[256,4096]{1,0:T(8,128)(2,1)S(1)}) fusion(bf16[256,1024]{1,0:T(8,128)(2,1)S(1)} %get-tuple-element.53, bf16[4096,1024]{1,0:T(8,128)(2,1)S(1)} %bitcast.237, f32[256,4096]{1,0:T(8,128)} %get-tuple-element.97), kind=kOutput, calls=%fused_computation.44 | convolution fusion | flops 2169499648 | bytes 15220736 | tf_op jit(solution)/shard_map/dot_general | solution.py:23
  280.8 7.2 %convolution_convert_fusion.1 = bf16[4096,1024]{1,0:T(8,128)(2,1)} fusion(bf16[256,4096]{1,0:T(8,128)(2,1)S(1)} %get-tuple-element.111, bf16[256,4096]{1,0:T(8,128)(2,1)S(1)} %copy-done.67, bf16[256,1024]{1,0:T(8,128)(2,1)S(1)} %copy-done.42, bf16[256,1024]{1,0:T(8,128)(2,1)S(1)} %copy-done.44), kind=kOutput, calls=%fused_computation.7 | convolution fusion | flops 4309647360 | bytes 13631488 | tf_op jit(solution)/shard_map/dot_general | solution.py:23
  297.2 8.0 %constant_dynamic-slice_fusion.1 = (bf16[2,2,2,1,256,1024]{5,4,3,2,1,0:T(8,128)(2,1)}, bf16[2,2,2,1,256,1024]{5,4,3,2,1,0:T(8,128)(2,1)}) fusion(bf16[2,2,2,2,256,1024]{5,4,3,2,1,0:T(8,128)(2,1)} %bitcast.208, s32[]{:T(128)S(6)} %select_n.223, s32[]{:T(128)S(6)} %select_n.224), kind=kLoop, calls=%fused_computation.209 | loop fusion | bytes 16777224 | tf_op jit(solution)/shard_map/jit(dynamic_index_in_dim)/dynamic_slice | solution.py:167
  305.2 6.3 %copy.67 = bf16[2,2,2,1,256,1024]{4,5,0,1,2,3:T(8,128)(2,1)} copy(bf16[2,2,2,1,256,1024]{5,4,3,2,1,0:T(8,128)(2,1)} %get-tuple-element.67) | data formatting | bytes 8388608 | tf_op jit(solution)/shard_map/jit(dynamic_index_in_dim)/dynamic_slice | solution.py:166
  311.7 10.5 %convolution_convert_fusion = bf16[1024,4096]{1,0:T(8,128)(2,1)} fusion(bf16[256,4096]{1,0:T(8,128)(2,1)} %copy-done.68, bf16[256,4096]{1,0:T(8,128)(2,1)} %get-tuple-element.102, bf16[256,1024]{1,0:T(8,128)(2,1)} %copy-done.40, bf16[256,1024]{1,0:T(8,128)(2,1)} %copy-done.39), kind=kOutput, calls=%fused_computation.6 | convolution fusion | flops 4309647360 | bytes 13631488 | tf_op jit(solution)/shard_map/dot_general | solution.py:23
  323.2 31.3 %attend_back.3 = (bf16[2048,128]{1,0:T(8,128)(2,1)S(1)}, bf16[2048,128]{1,0:T(8,128)(2,1)S(1)}, bf16[2048,128]{1,0:T(8,128)(2,1)S(1)}) custom-call(bf16[2048,128]{1,0:T(8,128)(2,1)S(1)} %copy-done.11, bf16[2048,128]{1,0:T(8,128)(2,1)S(1)} %get-tuple-element.113.k_ref, bf16[2048,128]{1,0:T(8,128)(2,1)S(1)} %get-tuple-element.112.v_ref, ...), custom_call_target="tpu_custom_call" | custom-call | flops 5368709120 | bytes 3670016 | tf_op jit(solution)/shard_map/attend_back/pallas_call | solution.py:106
  374.1 4.9 dynamic-slice_bitcast_fusion
  379.0 22.6 %collective-permute-done.30 = bf16[2,2,64,1024]{3,2,1,0:T(8,128)(2,1)S(1)} collective-permute-done((bf16[2,2,64,1024]{3,2,1,0:T(8,128)(2,1)S(1)}, bf16[2,2,64,1024]{3,2,1,0:T(8,128)(2,1)S(1)}, u32[]{:S(2)}, u32[]{:S(2)}) %collective-permute-start.30) | collective-permute-done | bytes 524320 | tf_op jit(solution)/shard_map/ppermute | solution.py:161
  402.4 5.8 fusion.52
  410.7 11.3 %collective-permute-done.31 = bf16[2,64,1024]{2,1,0:T(8,128)(2,1)S(1)} collective-permute-done((bf16[2,64,1024]{2,1,0:T(8,128)(2,1)S(1)}, bf16[2,64,1024]{2,1,0:T(8,128)(2,1)S(1)}, u32[]{:S(2)}, u32[]{:S(2)}) %collective-permute-start.31) | collective-permute-done | bytes 262176 | tf_op jit(solution)/shard_map/ppermute | solution.py:161
  428.7 6.2 copy.71
  444.4 5.6 multiply_reduce_fusion.2
  477.3 5.4 convolution_convert_fusion.2
  487.4 15.3 %all-to-all-done.4 = f32[16,1,896]{2,1,0:T(1,128)S(1)} async-done(((f32[16,1,896]{2,1,0:T(1,128)}), f32[16,1,896]{2,1,0:T(1,128)S(1)}, u32[]{:S(2)}, u32[]{:S(2)}) %all-to-all-start.4) | async-done | bytes 57376 | tf_op jit(solution)/shard_map/all_to_all | solution.py:346
  518.7 15.2 %collective-permute-done.36 = bf16[2,256,1024]{1,2,0:T(8,128)(2,1)} collective-permute-done((bf16[2,256,1024]{1,2,0:T(8,128)(2,1)}, bf16[2,256,1024]{1,2,0:T(8,128)(2,1)}, u32[]{:S(2)}, u32[]{:S(2)}) %collective-permute-start.36) | collective-permute-done | bytes 1048608 | tf_op jit(solution)/shard_map/ppermute | solution.py:161
  546.7 14.3 %collective-permute-done.37 = bf16[256,1024]{0,1:T(8,128)(2,1)S(1)} collective-permute-done((bf16[256,1024]{0,1:T(8,128)(2,1)S(1)}, bf16[256,1024]{0,1:T(8,128)(2,1)S(1)}, u32[]{:S(2)}, u32[]{:S(2)}) %collective-permute-start.37) | collective-permute-done | bytes 524320 | tf_op jit(solution)/shard_map/ppermute | solution.py:161
  563.5 19.8 %collective-permute-done.24 = bf16[2,2,2,96,1024]{4,3,2,1,0:T(8,128)(2,1)S(1)} collective-permute-done((bf16[2,2,2,96,1024]{4,3,2,1,0:T(8,128)(2,1)S(1)}, bf16[2,2,2,96,1024]{4,3,2,1,0:T(8,128)(2,1)S(1)}, u32[]{:S(2)}, u32[]{:S(2)}) %collective-permute-start.24) | collective-permute-done | bytes 1572896 | tf_op jit(solution)/shard_map/ppermute | solution.py:161
  586.2 13.9 %collective-permute-done.25 = bf16[2,2,96,1024]{3,2,1,0:T(8,128)(2,1)S(1)} collective-permute-done((bf16[2,2,96,1024]{3,2,1,0:T(8,128)(2,1)S(1)}, bf16[2,2,96,1024]{3,2,1,0:T(8,128)(2,1)S(1)}, u32[]{:S(2)}, u32[]{:S(2)}) %collective-permute-start.25) | collective-permute-done | bytes 786464 | tf_op jit(solution)/shard_map/ppermute | solution.py:161
  600.6 12.8 %collective-permute-done.26 = bf16[2,96,1024]{2,1,0:T(8,128)(2,1)S(1)} collective-permute-done((bf16[2,96,1024]{2,1,0:T(8,128)(2,1)S(1)}, bf16[2,96,1024]{2,1,0:T(8,128)(2,1)S(1)}, u32[]{:S(2)}, u32[]{:S(2)}) %collective-permute-start.26) | collective-permute-done | bytes 393248 | tf_op jit(solution)/shard_map/ppermute | solution.py:161
  (429 shorter events, 236.7 us)
Async XLA Ops:
  1.9 16.0 %collective-permute-start = (bf16[128,1024]{1,0:T(8,128)(2,1)S(1)}, bf16[128,1024]{1,0:T(8,128)(2,1)S(1)}, u32[]{:S(2)}, u32[]{:S(2)}) collective-permute-start(bf16[128,1024]{1,0:T(8,128)(2,1)S(1)} %get-tuple-element.81), channel_id=1, source_target_pairs={{0,8},{8,0},{1,9},{9,1},{2,10},{10,2},{3,11},{11,3},{4,12},{12,4},... | collective-permute-start | bytes 786440 | tf_op jit(solution)/shard_map/ppermute | solution.py:161
  22.3 13.3 %collective-permute-start.2 = (bf16[256,1024]{1,0:T(8,128)(2,1)}, bf16[256,1024]{1,0:T(8,128)(2,1)S(1)}, u32[]{:S(2)}, u32[]{:S(2)}) collective-permute-start(bf16[256,1024]{1,0:T(8,128)(2,1)} %get-tuple-element.65), channel_id=1, source_target_pairs={{0,4},{4,0},{1,5},{5,1},{2,6},{6,2},{3,7},{7,3},{8,12},{12,8},{9,1... | collective-permute-start | bytes 1572872 | tf_op jit(solution)/shard_map/ppermute | solution.py:161
  23.1 13.9 %collective-permute-start.1 = (bf16[256,1024]{1,0:T(8,128)(2,1)}, bf16[256,1024]{1,0:T(8,128)(2,1)}, u32[]{:S(2)}, u32[]{:S(2)}) collective-permute-start(bf16[256,1024]{1,0:T(8,128)(2,1)} %get-tuple-element.65), channel_id=1, source_target_pairs={{0,2},{2,0},{1,3},{3,1},{4,6},{6,4},{5,7},{7,5},{8,10},{10,8},{9,1... | collective-permute-start | bytes 1572872 | tf_op jit(solution)/shard_map/ppermute | solution.py:161
  25.9 24.5 %collective-permute-start.5 = (bf16[256,1024]{1,0:T(8,128)(2,1)}, bf16[256,1024]{1,0:T(8,128)(2,1)S(1)}, u32[]{:S(2)}, u32[]{:S(2)}) collective-permute-start(bf16[256,1024]{1,0:T(8,128)(2,1)} %get-tuple-element.65), channel_id=1, source_target_pairs={{0,1},{1,0},{2,3},{3,2},{4,5},{5,4},{6,7},{7,6},{8,9},{9,8},{10,11... | collective-permute-start | bytes 1572872 | tf_op jit(solution)/shard_map/ppermute | solution.py:161
  45.5 57.2 %collective-permute-start.20 = (f32[128,1024]{1,0:T(8,128)S(1)}, f32[128,1024]{1,0:T(8,128)S(1)}, u32[]{:S(2)}, u32[]{:S(2)}) collective-permute-start(f32[128,1024]{1,0:T(8,128)S(1)} %get-tuple-element.75), channel_id=1, source_target_pairs={{0,8},{8,0},{1,9},{9,1},{2,10},{10,2},{3,11},{11,3},{4,12},{12,4},... | collective-permute-start | bytes 1572872 | tf_op jit(solution)/shard_map/ppermute | solution.py:161
  100.9 13.9 %collective-permute-start.11 = (bf16[256,1024]{1,0:T(8,128)(2,1)S(1)}, bf16[256,1024]{1,0:T(8,128)(2,1)S(1)}, u32[]{:S(2)}, u32[]{:S(2)}) collective-permute-start(bf16[256,1024]{1,0:T(8,128)(2,1)S(1)} %get-tuple-element.63), channel_id=1, source_target_pairs={{0,4},{4,0},{1,5},{5,1},{2,6},{6,2},{3,7},{7,3},{8,12},{12,8},{9,1... | collective-permute-start | bytes 1572872 | tf_op jit(solution)/shard_map/ppermute | solution.py:161
  101.3 14.2 %collective-permute-start.10 = (bf16[256,1024]{1,0:T(8,128)(2,1)S(1)}, bf16[256,1024]{1,0:T(8,128)(2,1)S(1)}, u32[]{:S(2)}, u32[]{:S(2)}) collective-permute-start(bf16[256,1024]{1,0:T(8,128)(2,1)S(1)} %get-tuple-element.63), channel_id=1, source_target_pairs={{0,2},{2,0},{1,3},{3,1},{4,6},{6,4},{5,7},{7,5},{8,10},{10,8},{9,1... | collective-permute-start | bytes 1572872 | tf_op jit(solution)/shard_map/ppermute | solution.py:161
  103.5 19.3 %collective-permute-start.14 = (bf16[256,1024]{1,0:T(8,128)(2,1)S(1)}, bf16[256,1024]{1,0:T(8,128)(2,1)S(1)}, u32[]{:S(2)}, u32[]{:S(2)}) collective-permute-start(bf16[256,1024]{1,0:T(8,128)(2,1)S(1)} %get-tuple-element.63), channel_id=1, source_target_pairs={{0,1},{1,0},{2,3},{3,2},{4,5},{5,4},{6,7},{7,6},{8,9},{9,8},{10,11... | collective-permute-start | bytes 1572872 | tf_op jit(solution)/shard_map/ppermute | solution.py:161
  177.9 13.6 %all-to-all-start = ((bf16[8,256,128]{2,1,0:T(8,128)(2,1)}), bf16[8,256,128]{2,1,0:T(8,128)(2,1)}, u32[]{:S(2)}, u32[]{:S(2)}) async-start(bf16[8,256,128]{2,1,0:T(8,128)(2,1)} %bitcast.192), calls=%async_computation | async-start | bytes 1048576 | tf_op jit(solution)/shard_map/all_to_all | solution.py:289
  233.3 24.8 %all-to-all-start.1 = ((bf16[8,3,256,128]{2,3,1,0:T(8,128)(2,1)}), bf16[8,3,256,128]{2,3,1,0:T(8,128)(2,1)}, u32[]{:S(2)}, u32[]{:S(2)}) async-start(bf16[8,3,256,128]{2,3,1,0:T(8,128)(2,1)} %pad_maximum_fusion), calls=%async_computation.1 | async-start | bytes 3145728 | tf_op jit(solution)/shard_map/all_to_all | solution.py:292
  288.9 33.2 %all-to-all-start.2 = ((bf16[8,256,128]{2,1,0:T(8,128)(2,1)}), bf16[8,256,128]{2,1,0:T(8,128)(2,1)}, u32[]{:S(2)}, u32[]{:S(2)}) async-start(bf16[8,256,128]{2,1,0:T(8,128)(2,1)} %bitcast.219), calls=%async_computation.2 | async-start | bytes 1048576 | tf_op jit(solution)/shard_map/all_to_all | solution.py:289
  296.8 73.5 %collective-permute-start.29 = (bf16[2,2,2,64,1024]{4,3,2,0,1:T(8,128)(2,1)}, bf16[2,2,2,64,1024]{4,3,2,0,1:T(8,128)(2,1)}, u32[]{:S(2)}, u32[]{:S(2)}) collective-permute-start(bf16[2,2,2,64,1024]{4,3,2,0,1:T(8,128)(2,1)} %bitcast.188), channel_id=1, source_target_pairs={{0,1},{1,0},{2,3},{3,2},{4,5},{5,4},{6,7},{7,6},{8,9},{9,8},{10,11... | collective-permute-start | bytes 3145736 | tf_op jit(solution)/shard_map/ppermute | solution.py:161
  311.6 138.5 %collective-permute-start.34 = (bf16[2,2,2,256,1024]{3,4,0,1,2:T(8,128)(2,1)}, bf16[2,2,2,256,1024]{3,4,0,1,2:T(8,128)(2,1)}, u32[]{:S(2)}, u32[]{:S(2)}) collective-permute-start(bf16[2,2,2,256,1024]{3,4,0,1,2:T(8,128)(2,1)} %bitcast.217), channel_id=1, source_target_pairs={{0,1},{1,0},{2,3},{3,2},{4,5},{5,4},{6,7},{7,6},{8,9},{9,8},{10,11... | collective-permute-start | bytes 12582920 | tf_op jit(solution)/shard_map/ppermute | solution.py:161
  365.9 75.3 %all-to-all-start.3 = ((bf16[8,3,256,128]{2,3,1,0:T(8,128)(2,1)}), bf16[8,3,256,128]{2,3,1,0:T(8,128)(2,1)}, u32[]{:S(2)}, u32[]{:S(2)}) async-start(bf16[8,3,256,128]{2,3,1,0:T(8,128)(2,1)} %pad_maximum_fusion.1), calls=%async_computation.3 | async-start | bytes 3145728 | tf_op jit(solution)/shard_map/all_to_all | solution.py:292
  372.0 29.5 %collective-permute-start.30 = (bf16[2,2,64,1024]{3,2,1,0:T(8,128)(2,1)S(1)}, bf16[2,2,64,1024]{3,2,1,0:T(8,128)(2,1)S(1)}, u32[]{:S(2)}, u32[]{:S(2)}) collective-permute-start(bf16[2,2,64,1024]{3,2,1,0:T(8,128)(2,1)S(1)} %dynamic-slice_bitcast_fusion.10), channel_id=1, source_target_pairs={{0,4},{4,0},{1,5},{5,1},{2,6},{6,2},{3,7},{7,3},{8,12},{12,8},{9,1... | collective-permute-start | bytes 1572872 | tf_op jit(solution)/shard_map/ppermute | solution.py:161
  379.0 77.7 %collective-permute-start.39 = (bf16[2,2,2,64,4096]{4,3,2,1,0:T(8,128)(2,1)}, bf16[2,2,2,64,4096]{4,3,2,1,0:T(8,128)(2,1)}, u32[]{:S(2)}, u32[]{:S(2)}) collective-permute-start(bf16[2,2,2,64,4096]{4,3,2,1,0:T(8,128)(2,1)} %dynamic-slice_bitcast_fusion), channel_id=1, source_target_pairs={{0,1},{1,0},{2,3},{3,2},{4,5},{5,4},{6,7},{7,6},{8,9},{9,8},{10,11... | collective-permute-start | bytes 12582920 | tf_op jit(solution)/shard_map/ppermute | solution.py:161
  401.8 20.2 %collective-permute-start.31 = (bf16[2,64,1024]{2,1,0:T(8,128)(2,1)S(1)}, bf16[2,64,1024]{2,1,0:T(8,128)(2,1)S(1)}, u32[]{:S(2)}, u32[]{:S(2)}) collective-permute-start(bf16[2,64,1024]{2,1,0:T(8,128)(2,1)S(1)} %dynamic-slice_bitcast_fusion.15), channel_id=1, source_target_pairs={{0,8},{8,0},{1,9},{9,1},{2,10},{10,2},{3,11},{11,3},{4,12},{12,4},... | collective-permute-start | bytes 786440 | tf_op jit(solution)/shard_map/ppermute | solution.py:161
  408.2 19.3 %collective-permute-start.19 = (bf16[128,1024]{1,0:T(8,128)(2,1)S(1)}, bf16[128,1024]{1,0:T(8,128)(2,1)S(1)}, u32[]{:S(2)}, u32[]{:S(2)}) collective-permute-start(bf16[128,1024]{1,0:T(8,128)(2,1)S(1)} %get-tuple-element.79), channel_id=1, source_target_pairs={{0,8},{8,0},{1,9},{9,1},{2,10},{10,2},{3,11},{11,3},{4,12},{12,4},... | collective-permute-start | bytes 786440 | tf_op jit(solution)/shard_map/ppermute | solution.py:161
  455.2 49.6 %collective-permute-start.35 = (bf16[2,2,256,1024]{2,3,0,1:T(8,128)(2,1)}, bf16[2,2,256,1024]{2,3,0,1:T(8,128)(2,1)}, u32[]{:S(2)}, u32[]{:S(2)}) collective-permute-start(bf16[2,2,256,1024]{2,3,0,1:T(8,128)(2,1)} %dynamic-slice_bitcast_fusion.3), channel_id=1, source_target_pairs={{0,2},{2,0},{1,3},{3,1},{4,6},{6,4},{5,7},{7,5},{8,10},{10,8},{9,1... | collective-permute-start | bytes 6291464 | tf_op jit(solution)/shard_map/ppermute | solution.py:161
  463.9 47.0 %collective-permute-start.40 = (bf16[2,2,2,32,4096]{4,3,2,1,0:T(8,128)(2,1)}, bf16[2,2,2,32,4096]{4,3,2,1,0:T(8,128)(2,1)}, u32[]{:S(2)}, u32[]{:S(2)}) collective-permute-start(bf16[2,2,2,32,4096]{4,3,2,1,0:T(8,128)(2,1)} %dynamic-slice_bitcast_fusion.2), channel_id=1, source_target_pairs={{0,16},{16,0},{1,17},{17,1},{2,18},{18,2},{3,19},{19,3},{4,20},{20... | collective-permute-start | bytes 6291464 | tf_op jit(solution)/shard_map/ppermute | solution.py:161
  467.9 34.8 %all-to-all-start.4 = ((f32[16,1,896]{2,1,0:T(1,128)}), f32[16,1,896]{2,1,0:T(1,128)S(1)}, u32[]{:S(2)}, u32[]{:S(2)}) async-start(f32[16,1,896]{2,1,0:T(1,128)} %all_to_all.22), calls=%async_computation.4 | async-start | bytes 114688 | tf_op jit(solution)/shard_map/all_to_all | solution.py:346
  473.4 44.2 %collective-permute-start.21 = (bf16[128,1024]{1,0:T(8,128)(2,1)}, bf16[128,1024]{1,0:T(8,128)(2,1)S(1)}, u32[]{:S(2)}, u32[]{:S(2)}) collective-permute-start(bf16[128,1024]{1,0:T(8,128)(2,1)} %slice.191), channel_id=1, source_target_pairs={{0,8},{8,0},{1,9},{9,1},{2,10},{10,2},{3,11},{11,3},{4,12},{12,4},... | collective-permute-start | bytes 786440 | tf_op jit(solution)/shard_map/ppermute | solution.py:161
  487.4 54.0 %collective-permute-start.23 = (bf16[2,2,2,192,1024]{4,3,2,1,0:T(8,128)(2,1)}, bf16[2,2,2,192,1024]{4,3,2,1,0:T(8,128)(2,1)}, u32[]{:S(2)}, u32[]{:S(2)}) collective-permute-start(bf16[2,2,2,192,1024]{4,3,2,1,0:T(8,128)(2,1)} %dynamic-slice_bitcast_fusion.1), channel_id=1, source_target_pairs={{0,1},{1,0},{2,3},{3,2},{4,5},{5,4},{6,7},{7,6},{8,9},{9,8},{10,11... | collective-permute-start | bytes 9437192 | tf_op jit(solution)/shard_map/ppermute | solution.py:161
  508.6 25.3 %collective-permute-start.36 = (bf16[2,256,1024]{1,2,0:T(8,128)(2,1)}, bf16[2,256,1024]{1,2,0:T(8,128)(2,1)}, u32[]{:S(2)}, u32[]{:S(2)}) collective-permute-start(bf16[2,256,1024]{1,2,0:T(8,128)(2,1)} %dynamic-slice_bitcast_fusion.6), channel_id=1, source_target_pairs={{0,4},{4,0},{1,5},{5,1},{2,6},{6,2},{3,7},{7,3},{8,12},{12,8},{9,1... | collective-permute-start | bytes 3145736 | tf_op jit(solution)/shard_map/ppermute | solution.py:161
  514.9 23.1 %collective-permute-start.41 = (bf16[2,2,32,4096]{3,2,1,0:T(8,128)(2,1)}, bf16[2,2,32,4096]{3,2,1,0:T(8,128)(2,1)}, u32[]{:S(2)}, u32[]{:S(2)}) collective-permute-start(bf16[2,2,32,4096]{3,2,1,0:T(8,128)(2,1)} %dynamic-slice_bitcast_fusion.5), channel_id=1, source_target_pairs={{0,2},{2,0},{1,3},{3,1},{4,6},{6,4},{5,7},{7,5},{8,10},{10,8},{9,1... | collective-permute-start | bytes 3145736 | tf_op jit(solution)/shard_map/ppermute | solution.py:161
  535.8 25.2 %collective-permute-start.37 = (bf16[256,1024]{0,1:T(8,128)(2,1)S(1)}, bf16[256,1024]{0,1:T(8,128)(2,1)S(1)}, u32[]{:S(2)}, u32[]{:S(2)}) collective-permute-start(bf16[256,1024]{0,1:T(8,128)(2,1)S(1)} %dynamic-slice_bitcast_fusion.9), channel_id=1, source_target_pairs={{0,8},{8,0},{1,9},{9,1},{2,10},{10,2},{3,11},{11,3},{4,12},{12,4},... | collective-permute-start | bytes 1572872 | tf_op jit(solution)/shard_map/ppermute | solution.py:161
  539.6 23.7 %collective-permute-start.42 = (bf16[2,32,4096]{2,1,0:T(8,128)(2,1)S(1)}, bf16[2,32,4096]{2,1,0:T(8,128)(2,1)S(1)}, u32[]{:S(2)}, u32[]{:S(2)}) collective-permute-start(bf16[2,32,4096]{2,1,0:T(8,128)(2,1)S(1)} %dynamic-slice_bitcast_fusion.8), channel_id=1, source_target_pairs={{0,4},{4,0},{1,5},{5,1},{2,6},{6,2},{3,7},{7,3},{8,12},{12,8},{9,1... | collective-permute-start | bytes 1572872 | tf_op jit(solution)/shard_map/ppermute | solution.py:161
  546.0 37.4 %collective-permute-start.24 = (bf16[2,2,2,96,1024]{4,3,2,1,0:T(8,128)(2,1)S(1)}, bf16[2,2,2,96,1024]{4,3,2,1,0:T(8,128)(2,1)S(1)}, u32[]{:S(2)}, u32[]{:S(2)}) collective-permute-start(bf16[2,2,2,96,1024]{4,3,2,1,0:T(8,128)(2,1)S(1)} %dynamic-slice_bitcast_fusion.4), channel_id=1, source_target_pairs={{0,16},{16,0},{1,17},{17,1},{2,18},{18,2},{3,19},{19,3},{4,20},{20... | collective-permute-start | bytes 4718600 | tf_op jit(solution)/shard_map/ppermute | solution.py:161
  561.1 59.3 %collective-permute-start.38 = (bf16[256,1024]{0,1:T(8,128)(2,1)S(1)}, bf16[256,1024]{0,1:T(8,128)(2,1)S(1)}, u32[]{:S(2)}, u32[]{:S(2)}) collective-permute-start(bf16[256,1024]{0,1:T(8,128)(2,1)S(1)} %fusion.77), channel_id=1, source_target_pairs={{0,16},{16,0},{1,17},{17,1},{2,18},{18,2},{3,19},{19,3},{4,20},{20... | collective-permute-start | bytes 1572872 | tf_op jit(solution)/shard_map/ppermute | solution.py:161
  563.4 21.1 %collective-permute-start.43 = (bf16[32,4096]{1,0:T(8,128)(2,1)S(1)}, bf16[32,4096]{1,0:T(8,128)(2,1)S(1)}, u32[]{:S(2)}, u32[]{:S(2)}) collective-permute-start(bf16[32,4096]{1,0:T(8,128)(2,1)S(1)} %dynamic-slice_bitcast_fusion.14), channel_id=1, source_target_pairs={{0,8},{8,0},{1,9},{9,1},{2,10},{10,2},{3,11},{11,3},{4,12},{12,4},... | collective-permute-start | bytes 786440 | tf_op jit(solution)/shard_map/ppermute | solution.py:161
  584.1 15.9 %collective-permute-start.25 = (bf16[2,2,96,1024]{3,2,1,0:T(8,128)(2,1)S(1)}, bf16[2,2,96,1024]{3,2,1,0:T(8,128)(2,1)S(1)}, u32[]{:S(2)}, u32[]{:S(2)}) collective-permute-start(bf16[2,2,96,1024]{3,2,1,0:T(8,128)(2,1)S(1)} %dynamic-slice_bitcast_fusion.7), channel_id=1, source_target_pairs={{0,4},{4,0},{1,5},{5,1},{2,6},{6,2},{3,7},{7,3},{8,12},{12,8},{9,1... | collective-permute-start | bytes 2359304 | tf_op jit(solution)/shard_map/ppermute | solution.py:161
  584.6 15.9 %collective-permute-start.44 = (bf16[32,4096]{1,0:T(8,128)(2,1)S(1)}, bf16[32,4096]{1,0:T(8,128)(2,1)S(1)}, u32[]{:S(2)}, u32[]{:S(2)}) collective-permute-start(bf16[32,4096]{1,0:T(8,128)(2,1)S(1)} %fusion.84), channel_id=1, source_target_pairs={{0,16},{16,0},{1,17},{17,1},{2,18},{18,2},{3,19},{19,3},{4,20},{20... | collective-permute-start | bytes 786440 | tf_op jit(solution)/shard_map/ppermute | solution.py:161
  (100 other events, 1270.1 us)

commit v2 on v1

v2 whole, which is shorter than its diff:
```python
import functools
import math

import jax
import jax.numpy as jnp
import numpy as np
from jax import lax
from jax.experimental import pallas as pl
from jax.experimental.pallas import tpu as pltpu
from jax.sharding import Mesh
from jax.sharding import PartitionSpec as P

HD = 64
STEPS = 2
EPS = 1e-05
EXP_SCALE = 0.125 * 1.4426950408889634
GELU_A = 0.7978845608028654
GELU_B = 0.044715
MIB = 2**20
SWAP = [(0, 1), (1, 0)]
f32 = jnp.float32
bf16 = jnp.bfloat16


def cost(us):
    return pl.CostEstimate(flops=int(us * 1.15e9), bytes_accessed=1000, transcendentals=0)


def contract(a, b, a_dim, b_dim):
    return lax.dot_general(a, b, (((a_dim,), (b_dim,)), ((), ())), preferred_element_type=f32)


def head_part(x, h, heads):
    if heads == 1:
        return x
    lane = lax.broadcasted_iota(jnp.int32, x.shape, 1)
    return jnp.where(lane // HD == h, x, jnp.zeros_like(x))


def attend_kernel(q_ref, n_ref, wk_ref, wv_ref, b_ref, o_ref):
    normed = n_ref[...]
    keys = contract(normed, wk_ref[...], 1, 0).astype(bf16)
    values = (contract(normed, wv_ref[...], 1, 0) + b_ref[...]).astype(bf16)
    pair = 2 * HD
    for start in range(0, q_ref.shape[1], pair):
        q, k, v = q_ref[:, start : start + pair], keys[:, start : start + pair], values[:, start : start + pair]
        out = None
        for h in range(2):
            s = contract(head_part(q, h, 2), k, 1, 1)
            top = jnp.max(s, axis=-1, keepdims=True)
            e = jnp.exp2((s - top) * EXP_SCALE)
            total = jnp.sum(e, axis=-1, keepdims=True)
            o = head_part(contract(e.astype(bf16), v, 1, 0) / total, h, 2)
            out = o if out is None else out + o
        o_ref[:, start : start + pair] = out.astype(bf16)


def attend(q, normed_all, w_qkv, v_bias):
    rows, width = q.shape
    count = normed_all.shape[0]
    block = 4 * HD
    own = spec((rows, block), lambda j: (0, j))
    shift = width // block
    return pl.pallas_call(
        attend_kernel,
        grid=(width // block,),
        in_specs=[
            own,
            spec((count, width), lambda j: (0, 0)),
            spec((width, block), lambda j: (0, shift + j)),
            spec((width, block), lambda j: (0, 2 * shift + j)),
            spec((1, block), lambda j: (0, j)),
        ],
        out_specs=own,
        out_shape=jax.ShapeDtypeStruct((rows, width), bf16),
        compiler_params=pltpu.CompilerParams(vmem_limit_bytes=40 * MIB),
        cost_estimate=cost(24),
        name="attend",
    )(q, normed_all, w_qkv, w_qkv, v_bias.reshape(1, width))


def attend_back_kernel(q_ref, k_ref, v_ref, do_ref, *rest, heads, some):
    out_ref, dk_sum, dv_sum = rest[-3:]
    step = pl.program_id(0)
    rows = q_ref.shape[0]

    @pl.when(step == 0)
    def _():
        dk_sum[...] = jnp.zeros_like(dk_sum)
        dv_sum[...] = jnp.zeros_like(dv_sum)

    q, k, v, do = q_ref[...], k_ref[...], v_ref[...], do_ref[...]
    dq = None
    for h in some:
        qh, doh = head_part(q, h, heads), head_part(do, h, heads)
        s = contract(qh, k, 1, 1)
        dp = contract(doh, v, 1, 1)
        top = jnp.max(s, axis=-1, keepdims=True)
        e = jnp.exp2((s - top) * EXP_SCALE)
        inverse = 1.0 / jnp.sum(e, axis=-1, keepdims=True)
        inner = jnp.sum(e * dp, axis=-1, keepdims=True) * inverse
        p = e * inverse
        ds = (p * (dp - inner)).astype(bf16)
        part = head_part(contract(ds, k, 1, 0), h, heads)
        dq = part if dq is None else dq + part
        dk_sum[...] += contract(ds, qh, 0, 0)
        dv_sum[...] += contract(p.astype(bf16), doh, 0, 0)

    def put(m, i, x):
        if len(rest) == 4:
            x = x + rest[0][m, i].astype(f32)
        out_ref[m, i] = x.astype(bf16)

    put(step, 0, dq * 0.125)

    @pl.when(step == pl.num_programs(0) - 1)
    def _():
        for m in range(out_ref.shape[0]):
            put(m, 1, dk_sum[m * rows : (m + 1) * rows, :] * 0.125)
            put(m, 2, dv_sum[m * rows : (m + 1) * rows, :])


def attend_back(q, k, v, do, members, some=None, add=None):
    count, width = q.shape
    rows = count // members
    heads = width // HD
    part = pl.BlockSpec((rows, width), lambda i: (i, 0))
    full = pl.BlockSpec((count, width), lambda i: (0, 0))
    shape = (members, 3, rows, width)
    out = pl.BlockSpec(shape, lambda i: (0, 0, 0, 0))
    extra = [] if add is None else [add]
    return pl.pallas_call(
        functools.partial(attend_back_kernel, heads=heads, some=some or range(heads)),
        grid=(members,),
        in_specs=[part, full, full, part] + [out] * len(extra),
        out_specs=out,
        out_shape=jax.ShapeDtypeStruct(shape, bf16),
        scratch_shapes=[pltpu.VMEM((count, width), f32), pltpu.VMEM((count, width), f32)],
        compiler_params=pltpu.CompilerParams(vmem_limit_bytes=60 * MIB),
        cost_estimate=cost(33 if some is None else 17),
        name="attend_back",
    )(q, k, v, do, *extra)


def spec(block, index):
    return pl.BlockSpec(block, index)


def grad_rows_kernel(c_ref, l1, l0, r1, r0, other_ref, own_ref, sums):
    sums[...] = contract(l1[...], r1[...], 0, 0) + contract(l0[...], r0[...], 0, 0)
    count, n, _ = own_ref.shape
    for j in range(count):
        for ref, core in ((other_ref, 1 - c_ref[0]), (own_ref, c_ref[0])):
            ref[j] = sums[pl.ds(pl.multiple_of((2 * j + core) * n, n), n), :].astype(bf16)


def grad_rows(core, left, right, bands, part, parts):
    tokens, m = left[0].shape
    n = right[0].shape[1] // parts
    block = min(n, 512)
    first = part * (n // block)
    out = spec((bands // 2, m // bands, block), lambda j, c: (0, 0, j))
    whole = spec((tokens, m), lambda j, c: (0, 0))
    part = spec((tokens, block), lambda j, c: (0, first + j))
    return pl.pallas_call(
        grad_rows_kernel,
        grid_spec=pltpu.PrefetchScalarGridSpec(
            num_scalar_prefetch=1,
            grid=(n // block,),
            in_specs=[whole, whole, part, part],
            out_specs=[out, out],
            scratch_shapes=[pltpu.VMEM((m, block), f32)],
        ),
        out_shape=[jax.ShapeDtypeStruct((bands // 2, m // bands, n), bf16)] * 2,
        compiler_params=pltpu.CompilerParams(vmem_limit_bytes=16 * MIB),
        cost_estimate=cost(8),
        name="grad_rows",
    )(core.reshape(1), *left, *right)


def block_forward_kernel(
    x_ref, a_ref, wo_ref, bo_ref, g_ref, b_ref, wu_ref, bu_ref, wd_ref, bd_ref, lead_ref, g1_ref, b1_ref,
    n2_ref, r2_ref, low2_ref, hidden_ref, act_ref, *rest, last
):
    total = rest[-1]
    step = pl.program_id(0)

    @pl.when(step == 0)
    def _():
        middle = x_ref[...] + contract(a_ref[...], wo_ref[...], 1, 0) + bo_ref[...]
        n, r = norm_parts(middle)
        n2_ref[...] = n
        r2_ref[...] = r
        low2_ref[...] = (n * g_ref[...] + b_ref[...]).astype(bf16)
        total[...] = middle + bd_ref[...]

    hidden = contract(low2_ref[...], wu_ref[...], 1, 0) + bu_ref[...]
    hidden_ref[...] = hidden
    act = gelu(hidden).astype(bf16)
    act_ref[...] = act
    total[...] += contract(act, wd_ref[...], 1, 0)

    @pl.when(step == pl.num_programs(0) - 1)
    def _():
        carried = total[...]
        if last:
            rest[0][...] = carried.astype(bf16)
        else:
            x = carried + lead_ref[...]
            n, r = norm_parts(x)
            rest[0][...] = x
            rest[1][...] = n
            rest[2][...] = r
            rest[3][...] = (n * g1_ref[...] + b1_ref[...]).astype(bf16)


def block_forward(inputs, attended, weights, last):
    w_out, out_bias, ln2_gain, ln2_bias, w_up, up_bias, w_down, down_bias, lead, ln1_gain, ln1_bias = weights
    t, d = inputs.shape
    f = w_up.shape[1]
    block = 512
    row = lambda v: v.reshape(1, -1)
    full = spec((t, d), lambda i: (0, 0))
    vec = spec((1, d), lambda i: (0, 0))
    one = spec((t, 1), lambda i: (0, 0))
    wide = spec((t, block), lambda i: (0, i))
    shape = jax.ShapeDtypeStruct
    outs = [full, one, full, wide, wide] + ([full] if last else [full, full, one, full])
    shapes = [shape((t, d), f32), shape((t, 1), f32), shape((t, d), bf16), shape((t, f), f32), shape((t, f), bf16)]
    shapes += [shape((t, d), bf16)] if last else [
        shape((t, d), f32), shape((t, d), f32), shape((t, 1), f32), shape((t, d), bf16)
    ]
    return pl.pallas_call(
        functools.partial(block_forward_kernel, last=last),
        grid=(f // block,),
        in_specs=[
            full, full, spec((d, d), lambda i: (0, 0)), vec, vec, vec,
            spec((d, block), lambda i: (0, i)), spec((1, block), lambda i: (0, i)),
            spec((block, d), lambda i: (i, 0)), vec, vec, vec, vec,
        ],
        out_specs=outs,
        out_shape=shapes,
        scratch_shapes=[pltpu.VMEM((t, d), f32)],
        compiler_params=pltpu.CompilerParams(vmem_limit_bytes=40 * MIB),
        cost_estimate=cost(12),
        name="block_forward",
    )(
        inputs, attended, w_out, row(out_bias), row(ln2_gain), row(ln2_bias), w_up, row(up_bias), w_down,
        row(down_bias), row(lead), row(ln1_gain), row(ln1_bias),
    )


def put_sums(ref, *sums):
    for i, v in enumerate(sums):
        ref[i : i + 1, :] = v


def column_sum(x):
    return jnp.sum(x.astype(f32), axis=0, keepdims=True)


def block_backward_kernel(c_ref, grad_ref, h_ref, wd_ref, wu_ref, wo_ref, n_ref, r_ref, g_ref, *rest, grads, bands):
    if grads:
        l1_ref, x1_ref, x0_ref = rest[:3]
        z_other, x_other, z_own, x_own = rest[9:13]
        sums, rest = rest[14], rest[3:9] + rest[13:14]
    hg_ref, hsum_ref, middle_ref, branch_ref, sent_ref, sums_ref, total = rest
    step = pl.program_id(0)
    down = grad_ref[...].astype(bf16)
    low = (gelu_slope(h_ref[...]) * contract(down, wd_ref[...], 1, 1)).astype(bf16)
    hg_ref[...] = low
    hsum_ref[...] = column_sum(low)
    part = contract(low, wu_ref[...], 1, 1)
    if grads:
        sums[...] = contract(l1_ref[...], x1_ref[...], 0, 0) + contract(low, x0_ref[...], 0, 0)
        pairs = z_own.shape[0]
        n = sums.shape[0] // (2 * pairs)
        for q in range(pairs):
            for z, x, core in ((z_other, x_other, 1 - c_ref[0]), (z_own, x_own, c_ref[0])):
                start = pl.multiple_of((2 * q + core) * n, n)
                z[q] = sums[pl.ds(start, n // 2), :].astype(bf16)
                x[q] = sums[pl.ds(start + n // 2, n // 2), :].astype(bf16)

    @pl.when(step == 0)
    def _():
        total[...] = part

    @pl.when(step > 0)
    def _():
        total[...] += part

    @pl.when(step == pl.num_programs(0) - 1)
    def _():
        dv, gain, bias = norm_back(total[...], n_ref[...], r_ref[...], g_ref[...])
        middle = grad_ref[...] + dv
        middle_ref[...] = middle
        branch = middle.astype(bf16)
        branch_ref[...] = branch
        put_sums(sums_ref, gain, bias, column_sum(branch), column_sum(down))
        w = sent_ref.shape[2]
        attended = contract(branch, wo_ref[...], 1, 1).astype(bf16)
        for m in range(sent_ref.shape[0]):
            sent_ref[m] = attended[:, m * w : (m + 1) * w]


def block_backward(core, grad, hidden, w_down, w_up, w_out, n2, r2, gain, members, grads=()):
    t, d = grad.shape
    f = hidden.shape[1]
    block = 512
    bands = 2 * members
    full = spec((t, d), lambda i, c: (0, 0))
    wide = spec((t, block), lambda i, c: (0, i))
    sent = (members, t, d // members)
    shape = jax.ShapeDtypeStruct
    outs = [
        wide, spec((1, block), lambda i, c: (0, i)), full, full,
        spec(sent, lambda i, c: (0, 0, 0)), spec((8, d), lambda i, c: (0, 0)),
    ]
    shapes = [
        shape((t, f), bf16), shape((1, f), f32), shape((t, d), f32), shape((t, d), bf16),
        shape(sent, bf16), shape((8, d), f32),
    ]
    scratch = [pltpu.VMEM((t, d), f32)]
    if grads:
        n = f // bands
        pairs = block // (2 * n)
        part = spec((pairs, n // 2, d), lambda i, c: (i, 0, 0))
        outs += [part] * 4
        shapes += [shape((bands // 2, n // 2, d), bf16), shape((bands // 2, n // 2 + d // bands, d), bf16)] * 2
        scratch += [pltpu.VMEM((block, d), f32)]
    return pl.pallas_call(
        functools.partial(block_backward_kernel, grads=bool(grads), bands=bands),
        grid_spec=pltpu.PrefetchScalarGridSpec(
            num_scalar_prefetch=1,
            grid=(f // block,),
            in_specs=[
                full, wide, spec((block, d), lambda i, c: (i, 0)), spec((d, block), lambda i, c: (0, i)),
                spec((d, d), lambda i, c: (0, 0)), full, spec((t, 1), lambda i, c: (0, 0)),
                spec((1, d), lambda i, c: (0, 0)),
            ] + [wide, full, full][: len(grads)],
            out_specs=outs,
            scratch_shapes=scratch,
        ),
        out_shape=shapes,
        compiler_params=pltpu.CompilerParams(vmem_limit_bytes=48 * MIB),
        cost_estimate=cost(18 if grads else 14),
        name="block_backward",
    )(core.reshape(1), grad, hidden, w_down, w_up, w_out, n2, r2, gain.reshape(1, d), *grads)


def grad_out_kernel(c_ref, l1, l0, r1, r0, _, __, other_ref, own_ref, sums, *, pairs):
    sums[...] = contract(l1[...], r1[...], 0, 0) + contract(l0[...], r0[...], 0, 0)
    n = own_ref.shape[1]
    for q in range(pairs):
        for ref, core in ((other_ref, 1 - c_ref[0]), (own_ref, c_ref[0])):
            ref[q] = sums[pl.ds(pl.multiple_of((2 * q + core) * n, n), n), :].astype(bf16)


def grad_out(core, left, right, bands, other, own):
    tokens, m = left[0].shape
    count, height, d = own.shape
    n = m // bands
    pairs = max(1, 256 // (2 * n))
    columns = spec((tokens, 2 * n * pairs), lambda j, c: (0, j))
    whole = spec((tokens, d), lambda j, c: (0, 0))
    out = spec((pairs, n, d), lambda j, c: (j, height // n - 1, 0))
    anywhere = pl.BlockSpec(memory_space=pl.ANY)
    return pl.pallas_call(
        functools.partial(grad_out_kernel, pairs=pairs),
        grid_spec=pltpu.PrefetchScalarGridSpec(
            num_scalar_prefetch=1,
            grid=(count // pairs,),
            in_specs=[columns, columns, whole, whole, anywhere, anywhere],
            out_specs=[out, out],
            scratch_shapes=[pltpu.VMEM((2 * n * pairs, d), f32)],
        ),
        out_shape=[jax.ShapeDtypeStruct(own.shape, bf16)] * 2,
        input_output_aliases={5: 0, 6: 1},
        compiler_params=pltpu.CompilerParams(vmem_limit_bytes=16 * MIB),
        cost_estimate=cost(3),
        name="grad_out",
    )(core.reshape(1), *left, *right, other, own)


def qkv_backward_kernel(b_ref, wq_ref, wk_ref, wv_ref, m_ref, n_ref, r_ref, g_ref, grad_ref, low_ref, sums_ref, qv_ref, total):
    step = pl.program_id(0)
    w = b_ref.shape[3]
    part = None
    for m in range(b_ref.shape[0]):
        for i, ref in enumerate((wq_ref, wk_ref, wv_ref)):
            x = contract(b_ref[m, i], ref[:, m * w : (m + 1) * w], 1, 1)
            part = x if part is None else part + x
        qv_ref[0:1, m * w : (m + 1) * w] = column_sum(b_ref[m, 0])
        qv_ref[1:2, m * w : (m + 1) * w] = column_sum(b_ref[m, 2])

    @pl.when(step == 0)
    def _():
        total[...] = part

    @pl.when(step > 0)
    def _():
        total[...] += part

    @pl.when(step == pl.num_programs(0) - 1)
    def _():
        dv, gain, bias = norm_back(total[...], n_ref[...], r_ref[...], g_ref[...])
        grad = m_ref[...] + dv
        grad_ref[...] = grad
        half = low_ref.shape[1]
        low_ref[0] = grad[:half].astype(bf16)
        low_ref[1] = grad[half:].astype(bf16)
        put_sums(sums_ref, gain, bias, column_sum(grad))


def qkv_backward(back, w_qkv, middle_grad, n1, r1, gain):
    members, _, t, w = back.shape
    d = members * w
    at_once = max(2, 128 // w)
    block = at_once * w
    shift = d // block
    full = spec((t, d), lambda i: (0, 0))
    weight = [spec((d, block), lambda i, s=s: (0, s * shift + i)) for s in range(3)]
    shape = jax.ShapeDtypeStruct
    return pl.pallas_call(
        qkv_backward_kernel,
        grid=(members // at_once,),
        in_specs=[spec((at_once, 3, t, w), lambda i: (i, 0, 0, 0))] + weight + [
            full, full, spec((t, 1), lambda i: (0, 0)), spec((1, d), lambda i: (0, 0)),
        ],
        out_specs=[
            full, spec((2, t // 2, d), lambda i: (0, 0, 0)), spec((8, d), lambda i: (0, 0)),
            spec((8, block), lambda i: (0, i)),
        ],
        out_shape=[
            shape((t, d), f32), shape((2, t // 2, d), bf16), shape((8, d), f32), shape((8, d), f32),
        ],
        scratch_shapes=[pltpu.VMEM((t, d), f32)],
        compiler_params=pltpu.CompilerParams(vmem_limit_bytes=40 * MIB),
        cost_estimate=cost(6),
        name="qkv_backward",
    )(back, w_qkv, w_qkv, w_qkv, middle_grad, n1, r1, gain.reshape(1, d))


def grad_heads_kernel(d_ref, n_ref, *rest):
    out_ref = rest[-1]
    rows = d_ref.shape[2]
    for i in range(3):
        total = rest[0][i] if len(rest) == 2 else jnp.zeros(out_ref.shape[1:], f32)
        for m in range(d_ref.shape[0]):
            total += contract(d_ref[m, i], n_ref[m * rows : (m + 1) * rows, :], 0, 0)
        out_ref[i] = total.astype(out_ref.dtype)


def grad_heads(d, normed_all, add, kind):
    members, _, rows, width = d.shape
    dim = normed_all.shape[1]
    shape = (3, width, dim)
    out = spec((3, width, dim // 4), lambda i: (0, 0, i))
    extra = [] if add is None else [add]
    return pl.pallas_call(
        grad_heads_kernel,
        grid=(4,),
        in_specs=[
            spec(d.shape, lambda i: (0, 0, 0, 0)),
            spec((members * rows, dim // 4), lambda i: (0, i)),
        ]
        + [out] * len(extra),
        out_specs=out,
        out_shape=jax.ShapeDtypeStruct(shape, kind),
        compiler_params=pltpu.CompilerParams(vmem_limit_bytes=16 * MIB),
        cost_estimate=cost(5),
        name="grad_heads",
    )(d, normed_all, *extra)


def take_kernel(table, *refs):
    for i in range(refs[-1].shape[0]):
        total = refs[0][table[i]].astype(f32)
        for r in refs[1:-1]:
            total = total + r[table[i]].astype(f32)
        refs[-1][i] = total.astype(bf16)


def take(terms, table):
    shape = terms[0].shape
    count = table.shape[0]
    return pl.pallas_call(
        take_kernel,
        grid_spec=pltpu.PrefetchScalarGridSpec(
            num_scalar_prefetch=1,
            grid=(1,),
            in_specs=[spec(shape, lambda i, t: (0, 0, 0))] * len(terms),
            out_specs=spec((count,) + shape[1:], lambda i, t: (0, 0, 0)),
        ),
        out_shape=jax.ShapeDtypeStruct((count,) + shape[1:], bf16),
        compiler_params=pltpu.CompilerParams(vmem_limit_bytes=8 * MIB),
        cost_estimate=cost(3),
        name="take",
    )(table, *terms)


def unit_tables(bands, x_count, width, dim):
    members = bands // 2
    unit = math.gcd(HD, 3 * dim // bands)
    per_band = 3 * dim // bands // unit
    made, slots, place = [], [], {}
    for g in range(members):
        units = [(b * dim + g * width) // unit + i for b in range(3) for i in range(width // unit)]
        by_low = [[] for _ in range(members)]
        for local, u in enumerate(units):
            band = u // per_band
            core, x, zl = band % 2, band // 2 % x_count, band // (2 * x_count) % 2
            low = (core * 2 + zl) * x_count + x
            place[u] = (g, len(by_low[low]))
            by_low[low].append(local)
        made.append(by_low)
    most = max(len(l) for by_low in made for l in by_low)
    send = np.zeros((members, members * most), np.int32)
    for g, by_low in enumerate(made):
        for low, locals_ in enumerate(by_low):
            for m, local in enumerate(locals_):
                send[g, low * most + m] = local
    keep = np.zeros((members, 2, per_band), np.int32)
    for u, (g, m) in place.items():
        band = u // per_band
        core, x, zl = band % 2, band // 2 % x_count, band // (2 * x_count) % 2
        low = (core * 2 + zl) * x_count + x
        keep[low, band // members, u % per_band] = g * most + m
    return unit, send, keep


def norm_parts(v):
    centred = v - jnp.mean(v, axis=-1, keepdims=True)
    r = lax.rsqrt(jnp.mean(centred * centred, axis=-1, keepdims=True) + EPS)
    return centred * r, r


def norm_back(dy, n, r, gain):
    dyg = dy * gain
    mean_one = jnp.mean(dyg, axis=-1, keepdims=True)
    mean_two = jnp.mean(dyg * n, axis=-1, keepdims=True)
    dv = r * (dyg - mean_one - n * mean_two)
    return dv, jnp.sum(dy * n, axis=0, keepdims=True), jnp.sum(dy, axis=0, keepdims=True)


def gelu(x):
    return 0.5 * x * (1.0 + jnp.tanh(GELU_A * (x + GELU_B * x * x * x)))


def gelu_slope(x):
    t = jnp.tanh(GELU_A * (x + GELU_B * x * x * x))
    return 0.5 * (1.0 + t) + 0.5 * x * (1.0 - t * t) * (GELU_A * (1.0 + 3.0 * GELU_B * x * x))


def dot(a, b):
    return jnp.dot(a, b, preferred_element_type=f32)


def dot_t(a, b):
    return contract(a, b, 1, 1)


def swap(x, axis):
    return lax.ppermute(x, axis, SWAP)


def pin(x, *first):
    return lax.optimization_barrier((x,) + first)[0]


def total(terms):
    out = terms[0].astype(f32)
    for t in terms[1:]:
        out = out + t.astype(f32)
    return out


class Share:
    def __init__(self, terms, names):
        self.terms = list(terms)
        self.names = list(names)

    def halve(self, axis, *first):
        if axis not in self.names:
            return self.terms[-1]
        dim = self.names.index(axis)
        i = lax.axis_index(axis)
        terms = [pin(t, *first) if first else t for t in self.terms[-1:]] + self.terms[:-1]
        there = [lax.dynamic_index_in_dim(t, 1 - i, dim, keepdims=False) for t in terms]
        self.terms = [lax.dynamic_index_in_dim(t, i, dim, keepdims=False) for t in terms]
        self.names.remove(axis)
        sent = total(there).astype(bf16)
        self.terms.append(swap(sent, axis))
        return sent


def body(
    fields,
    lead_bucket,
    cotangent,
    lead_table,
    ln1_gain,
    ln1_bias,
    w_qkv,
    q_bias,
    v_bias,
    w_out,
    out_bias,
    ln2_gain,
    ln2_bias,
    w_up,
    up_bias,
    w_down,
    down_bias,
    *,
    axes,
    x_axes,
    samp_count,
):
    band = tuple(axes)
    low = ("core", "zl") + x_axes[::-1]
    members = 2 ** len(low)
    order = x_axes + ("zl", "core")
    D = w_out.shape[0]
    W = D // members
    half = fields.shape[1]
    rows = 2 * half
    two = samp_count == 2
    zh = lax.axis_index("zh")
    me = lax.axis_index(low)

    def pick(x, i):
        return lax.dynamic_index_in_dim(x, i, 0, keepdims=False)

    def to_sample(x):
        return jnp.concatenate([pick(x, zh), swap(pick(x, 1 - zh), "zh")])

    def to_band(x):
        own = x[:half]
        other = swap(x[half:].astype(bf16), "zh").astype(x.dtype)
        return jnp.where(zh == 0, jnp.stack([own, other]), jnp.stack([other, own]))

    def gather(x):
        if len(x_axes) == 1:
            x_axis = x_axes[0]
            cut = x.shape[0] // 2
            by_x = swap(x, x_axis)
            by_z = swap(x, "zl")
            far = [swap(by_x[:cut], "zl"), swap(by_z[cut:], x_axis)]
            pieces = [(x, 0, 0), (by_x, 1, 0), (by_z, 2, 0), (far[0], 3, 0), (far[1], 3, cut)]
            pieces += [(swap(p, "core"), 4 + k, o) for p, k, o in pieces]
        else:
            pieces = [(x, 0, 0)]
            for bit, axis in enumerate(order):
                pieces += [(swap(p, axis), k + 2**bit, 0) for p, k, _ in pieces]
        out = jnp.zeros((members * rows, D), bf16)
        for piece, k, offset in pieces:
            out = lax.dynamic_update_slice(out, piece, ((me ^ k) * rows + offset, 0))
        return out

    lead_row = pick(lead_table, pick(lead_bucket, zh)).astype(f32)
    carried = to_sample(fields).astype(f32)

    def member_columns(x, block):
        return lax.dynamic_slice_in_dim(x, block * D + me * W, W, x.ndim - 1)

    kept = []
    inputs = carried + lead_row
    n1, r1 = norm_parts(inputs)
    normed = (n1 * ln1_gain + ln1_bias).astype(bf16)
    weights = (w_out, out_bias, ln2_gain, ln2_bias, w_up, up_bias, w_down, down_bias, lead_row, ln1_gain, ln1_bias)
    for index in range(STEPS):
        normed_all = gather(normed)
        queries = (dot(normed, w_qkv[:, :D]) + q_bias).astype(bf16)
        if index == 0:
            out_grad = to_sample(pin(cotangent, normed_all))
        attended = attend(queries, normed_all, w_qkv, v_bias)
        if index == 0:
            attended, out_grad = pin((attended, out_grad))
        last = index == STEPS - 1
        n2, r2, normed_two, hidden, activated, *after = block_forward(inputs, attended, weights, last)
        kept.append((n1, r1, normed_all, attended, n2, r2, normed_two, hidden, activated))
        if not last:
            inputs, n1, r1, normed = after
    carried = after[0]
    result = to_band(carried)

    grad = out_grad
    small = None
    core = lax.axis_index("core")
    y = lax.axis_index("samp")
    bands = 2 ** len(axes)
    names = axes[:-1]
    cube = (2,) * len(names)
    later = None
    w_heads = None
    unit, send_table, keep_table = unit_tables(bands, 2 ** len(x_axes), W, D)
    def split_rows(x, rows_two):
        n, r, c = x.shape
        return x.reshape(cube + ((2, r // 2) if rows_two else (r,)) + (c,))

    own_weight = jnp.concatenate([member_columns(w_qkv, i) for i in range(3)], axis=1)
    own_bias = jnp.concatenate([member_columns(q_bias, 0), jnp.zeros((W,), f32), member_columns(v_bias, 0)])

    def own_part(index):
        own = (dot(kept[index][2], own_weight) + own_bias).astype(bf16)
        return own[:, :W], own[:, W : 2 * W], own[:, 2 * W :]

    owns = {}
    for index in reversed(range(STEPS)):
        n1, r1, normed_all, attended, n2, r2, normed_two, hidden, activated = kept[index]
        last = index == 0
        if last:
            left, right = (later[0], down_grad), (later[1], activated)
            y_other, y_own = grad_rows(core, left, right, bands, 0, 2)
            y_core = swap(y_other, "core")
            right = (later[1], pin(activated, y_other))
            x_other, x_own = grad_rows(core, left, right, bands, 1, 2)
            x_core = swap(x_other, "core")
            grad = pin(grad, x_other)
            grads = (later[2], later[3], normed_two)
        else:
            down_grad = grad.astype(bf16)
            grads = ()
        hidden_grad, hidden_sum, middle_grad, branch_grad, sent, sums_two, *ups = block_backward(
            core, grad, hidden, w_down, w_up, w_out, n2, r2, ln2_gain, members, grads
        )
        if last:
            (y_own, y_core), (x_own, x_core) = pin(((y_own, y_core), (x_own, x_core)), hidden_grad)
            down_y = Share([split_rows(y_own, two), split_rows(y_core, two)], names + ("samp",) * two)
            down_x = Share([split_rows(x_own, two), split_rows(x_core, two)], names + ("samp",) * two)
            first = (down_y.halve("samp"), down_x.halve(x_axes[0]))
            sent = pin(sent, *first)
        own_grad = lax.all_to_all(sent, low, 0, 0, tiled=True).reshape(members * rows, W)
        if last:
            z_other, x_other, z_own, x_own = ups
            z_core = swap(z_other, "core")
            x_other, x_own = grad_out(
                core, (later[4], pin(branch_grad, sent)), (later[5], attended), bands, x_other, x_own
            )
            x_core = swap(x_other, "core")
            own_grad, z_own, z_core = pin((own_grad, z_own, z_core), x_other)
            z_share = Share([split_rows(z_own, two), split_rows(z_core, two)], names + ("samp",) * two)
            x_share = Share([split_rows(t, two) for t in (x_own, x_core)], names + ("samp",) * two)
            sent = [z_share.halve("zh"), x_share.halve(x_axes[0])]
            own_grad = pin(own_grad, *sent)
            heads = W // HD
            d_heads = attend_back(*owns[0], own_grad, members, range((heads + 1) // 2))
            waits = pin((own_grad, d_heads, down_y.terms[-1], down_x.terms[-1]))
            own_grad, d_heads, down_y.terms[-1], down_x.terms[-1] = waits
            sent = [down_y.halve("zl"), down_x.halve("samp")]
            if heads > 1:
                own_grad, d_heads = pin((own_grad, d_heads), *sent)
                d_heads = attend_back(*owns[0], own_grad, members, range(heads // 2, heads), d_heads)
            waits = pin((d_heads, z_share.terms[-1], x_share.terms[-1], down_y.terms[-1], down_x.terms[-1]))
            d_heads, z_share.terms[-1], x_share.terms[-1], down_y.terms[-1], down_x.terms[-1] = waits
            sent = [x_share.halve("samp"), z_share.halve("samp")] + [down_y.halve(a) for a in x_axes]
            sent += [down_x.halve(a) for a in x_axes[1:] + ("zl",)]
            d_heads = pin(d_heads, *sent)
        else:
            own_grad = pin(own_grad, result)
            later = (down_grad, activated, hidden_grad, normed_two, branch_grad, attended)
            owns[index] = own_part(index)
            d_heads = attend_back(*owns[index], own_grad, members)
        back = lax.all_to_all(d_heads, low, 0, 0, tiled=True)
        w_heads = grad_heads(d_heads, normed_all, w_heads, bf16 if last else f32)
        if last:
            units = w_heads.reshape(-1, unit, D)
            if two:
                there = lax.dynamic_slice_in_dim(units, (1 - y) * (D // 2), D // 2, 2)
                here = lax.dynamic_slice_in_dim(units, y * (D // 2), D // 2, 2)
                units = [here, swap(there, "samp")]
            else:
                there, units = units, [units]
            back = pin(back, there)
            waits = pin((x_share.terms[-1], z_share.terms[-1], down_y.terms[-1], down_x.terms[-1]), back)
            x_share.terms[-1], z_share.terms[-1], down_y.terms[-1], down_x.terms[-1] = waits
            sent = [x_share.halve(a) for a in x_axes[1:] + ("zl",)] + [z_share.halve("zl")]
            sent += [down_y.halve("zh"), down_x.halve("zh")]
            units[-1] = pin(units[-1], *sent)
            outgoing = take(units, pick(jnp.asarray(send_table), me))
            incoming = lax.all_to_all(outgoing, low, 0, 0, tiled=True)
            back = pin(back, outgoing)
        else:
            owns[0] = own_part(0)
            back = pin(back, w_heads, *owns[0])
        grad, low_grad, sums_one, sums_qv = qkv_backward(back, w_qkv, middle_grad, n1, r1, ln1_gain)
        down_grad = low_grad.reshape(rows, D)
        step_small = (sums_one[:3], sums_qv[:2], sums_two[:4], hidden_sum)
        small = step_small if small is None else tuple(a + b for a, b in zip(small, step_small))
    fields_own = grad[:half]
    fields_sent = low_grad[1]
    fields_other = swap(fields_sent, "zh")
    one, qv, two_sums, up_sum = small
    samples = 2 * samp_count
    slot = 2 * y + zh
    mine = lax.broadcasted_iota(jnp.int32, (samples, 1), 0) == slot
    leads = jnp.where(mine, one[2:3], 0.0)
    lane = lax.broadcasted_iota(jnp.int32, (bands, 1, D // bands), 2) == slot
    bucket = jnp.where(lane & (me == 0) & (zh == slot % 2), pick(lead_bucket, zh).astype(f32), 0.0)
    vectors = jnp.concatenate([one[:2], qv, two_sums, leads])
    vectors = vectors.reshape(-1, bands, D // bands).transpose(1, 0, 2)
    ups = up_sum.reshape(bands, -1, D // bands)
    vectors = jnp.concatenate([vectors, ups, bucket], axis=1)
    incoming, vectors = pin((incoming, vectors), fields_sent)
    vectors = lax.all_to_all(vectors, band, 0, 0, tiled=True)

    def both(x):
        x = x.astype(bf16)
        if not two:
            return lax.psum(x, "samp").astype(f32)
        other = swap(x, "samp")
        return jnp.concatenate([jnp.where(y == 0, x, other), jnp.where(y == 0, other, x)]).astype(f32)

    def both_cut(x, n):
        if not two:
            x = both(x)
            return x[:n], x[n:]
        x = x.astype(bf16)
        other = swap(x, "samp")
        first, second = jnp.where(y == 0, x, other), jnp.where(y == 0, other, x)
        x = jnp.concatenate([first, second]).astype(f32)
        return x[:n], x[n:]

    waits = pin((z_share.terms[-1], x_share.terms[-1], down_y.terms[-1], down_x.terms[-1], incoming), fields_sent)
    z_share.terms[-1], x_share.terms[-1], down_y.terms[-1], down_x.terms[-1], incoming = waits
    sent = [x_share.halve("zh")] + [z_share.halve(a) for a in x_axes]
    down = jnp.concatenate([total(down_y.terms), total(down_x.terms)], axis=1).astype(bf16)
    incoming, fields_other, x_share.terms[-1], z_share.terms[-1], vectors = pin(
        (incoming, fields_other, x_share.terms[-1], z_share.terms[-1], vectors), down, *sent
    )
    vectors = jnp.sum(vectors, axis=0)
    vectors = vectors + swap(vectors, "samp") if two else lax.psum(vectors, "samp")
    keep_table = pick(jnp.asarray(keep_table), me)
    other = swap(take([incoming], pick(keep_table, 1 - zh)), "zh")
    own = take([incoming], pick(keep_table, zh))
    own = total([own, other]).astype(bf16).reshape(3 * D // bands, -1)
    if two:
        other = swap(own, "samp")
        own = jnp.concatenate([jnp.where(y == 0, own, other), jnp.where(y == 0, other, own)], axis=1)
    else:
        own = lax.psum(own, "samp")
    w_qkv_grad = own.astype(f32).T

    w_down_grad = both(down).T
    n_up = w_up.shape[1] // bands
    bottom = both_cut(total(x_share.terms), n_up // 2)
    w_out_grad = bottom[1].T
    w_up_grad = jnp.concatenate([both(total(z_share.terms)), bottom[0]]).T
    fields_other = fields_other.astype(f32)
    fields_grad = jnp.where(
        zh == 0, jnp.stack([fields_own, fields_other]), jnp.stack([fields_other, fields_own])
    )

    leads = vectors[8 : 8 + samples]
    up_grad = vectors[8 + samples : -1].reshape(-1)
    buckets = vectors[-1, :samples].astype(jnp.int32)
    one_hot = (buckets[:, None] == jnp.arange(lead_table.shape[0], dtype=jnp.int32)[None, :]).astype(f32)
    lead_grad = jnp.dot(one_hot.T, leads, precision=lax.Precision.HIGHEST)
    g = [vectors[i] for i in (0, 1, 2, 3, 6, 4, 5)] + [up_grad, vectors[7]]
    return (
        result,
        fields_grad,
        lead_grad,
        g[0],
        g[1],
        w_qkv_grad,
        g[2],
        g[3],
        w_out_grad,
        g[4],
        g[5],
        g[6],
        w_up_grad,
        g[7],
        w_down_grad,
        g[8],
    )


def solution(mesh):
    samp_count, band_count = mesh.shape["samp"], mesh.shape["band"]
    x_axes = tuple(f"x{i}" for i in range((band_count // 8).bit_length() - 1))
    axes = ("zh", "zl") + x_axes + ("core",)
    assert 2 ** len(axes) == band_count
    fine = Mesh(mesh.devices.reshape((samp_count,) + (2,) * len(axes)), ("samp",) + axes)
    tokens = P("samp", axes, None)
    columns, vector = P(None, axes), P(axes)
    in_specs = (tokens, P("samp"), tokens) + (P(),) * 14
    out_specs = (
        tokens,
        tokens,
        columns,
        vector,
        vector,
        columns,
        vector,
        vector,
        columns,
        vector,
        vector,
        vector,
        columns,
        vector,
        columns,
        vector,
    )
    run = functools.partial(body, axes=axes, x_axes=x_axes, samp_count=samp_count)
    return jax.shard_map(run, mesh=fine, in_specs=in_specs, out_specs=out_specs, check_vma=False)
```

time: 635 us -> 530 us (0.83)
  Pallas kernels: 97.5 us -> 219 us
  waiting for transfers between devices: 197 us -> 82.5 us
  matrix products: 118 us -> 15.1 us
  local copies, waits for them, and re-layouts: 98.7 us -> 59.5 us
  other arithmetic: 45.8 us -> 64.8 us
  starting transfers between devices: 63.9 us -> 77.9 us
    pallas_call x4 -> x19, Pallas kernels: 97.5 us -> 219 us  [the longest x3 70.5 us: attend_back(): pl.pallas_call(functools.partial(attend_back_kernel, heads=heads, some=so...]
    ppermute x45 -> x49, waiting for transfers between devices: 164 us -> 60.3 us  [swap(): return lax.ppermute(x, axis, SWAP)]
    dot_general x13 -> x1, matrix products: 58.3 us -> 0.9 us  [body(): lead_grad = jnp.dot(one_hot.T, leads, precision=lax.Precision.HIGHEST)]
    dot_general x12 -> x4, matrix products: 60.1 us -> 14.2 us  [dot(): return jnp.dot(a, b, preferred_element_type=f32)]
    convert_element_type x20 -> x24, other arithmetic: 24 us -> 43.6 us  [the longest x16 38.3 us: halve(): sent = total(there).astype(bf16)]
    dynamic_slice x4 -> x1, local copies, waits for them, and re-layouts: 18.1 us -> 0.86 us  [body(): here = lax.dynamic_slice_in_dim(units, y * (D // 2), D // 2, 2)]
    all_to_all x3 -> x4, waiting for transfers between devices: 30.2 us -> 15.6 us  [the longest x2 8.71 us: body(): back = lax.all_to_all(d_heads, low, 0, 0, tiled=True)]
    squeeze x16 -> x2, local copies, waits for them, and re-layouts: 12.7 us -> 1.26 us  [the longest x1 0.72 us: body(): fields_sent = low_grad[1]]
  transfers between devices with their start and end apart: 50 -> 55, of which waited for: 23 -> 20; matrix products, arithmetic and copies ran while one was open for 27% -> 16% of each run, Pallas kernels for 8% -> 24%
where the time goes in v2:
time: 530 us; the launch traced here: 524 us
  Pallas kernels  219 us (41%)
  waiting for transfers between devices  82.5 us (16%)
  starting transfers between devices  77.9 us (15%)
  other arithmetic  64.8 us (12%)
  local copies, waits for them, and re-layouts  59.5 us (11%)
  matrix products  15.1 us (3%)
    pallas_call x3, Pallas kernels, attend_back(): pl.pallas_call(functools.partial(attend_back_kernel, heads=heads, some=so...  70.5 us
    ppermute x49, waiting for transfers between devices, swap(): return lax.ppermute(x, axis, SWAP)  60.3 us
    ppermute x49, starting transfers between devices, swap(): return lax.ppermute(x, axis, SWAP)  52.6 us
    pallas_call x2, Pallas kernels, attend(): pl.pallas_call(attend_kernel, grid=(width // block,), in_specs=[own, spec...  48.2 us
    convert_element_type x16, other arithmetic, halve(): sent = total(there).astype(bf16)  38.3 us
    pallas_call x2, Pallas kernels, block_backward(): pl.pallas_call(functools.partial(block_backward_kernel, grads=bool(grads)...  38.1 us
    unnamed x154, local copies, waits for them, and re-layouts  32.3 us
    pallas_call x2, Pallas kernels, block_forward(): pl.pallas_call(functools.partial(block_forward_kernel, last=last), grid=(...  25.2 us
  transfers between devices with their start and end apart: 55, of which 20 were waited for; matrix products, arithmetic and copies ran while one was open for 16% of the time, Pallas kernels for 24%

profile of v2, /device:TPU:0, one launch (start us, length us, event | category | flops | bytes accessed | tf_op | source)
XLA Modules:
  0.0 523.8 jit_solution(11288189001609214440)
XLA Ops:
  1.8 4.1 collective-permute-start
  9.8 8.0 %collective-permute-done = bf16[128,1024]{1,0:T(8,128)(2,1)S(1)} collective-permute-done((bf16[128,1024]{1,0:T(8,128)(2,1)S(1)}, bf16[128,1024]{1,0:T(8,128)(2,1)S(1)}, u32[]{:S(2)}, u32[]{:S(2)}) %collective-permute-start) | collective-permute-done | bytes 262176 | tf_op jit(solution)/shard_map/ppermute | solution.py:564
  26.8 8.2 %collective-permute-done.1 = bf16[256,1024]{1,0:T(8,128)(2,1)S(1)} collective-permute-done((bf16[256,1024]{1,0:T(8,128)(2,1)S(1)}, bf16[256,1024]{1,0:T(8,128)(2,1)S(1)}, u32[]{:S(2)}, u32[]{:S(2)}) %collective-permute-start.1) | collective-permute-done | bytes 524320 | tf_op jit(solution)/shard_map/ppermute | solution.py:564
  52.7 25.3 %attend.2.a_ref.r0 = bf16[256,1024]{1,0:T(8,128)(2,1)S(1)} custom-call(bf16[256,1024]{1,0:T(8,128)(2,1)S(1)} %fusion.15.q_ref, bf16[2048,1024]{1,0:T(8,128)(2,1)} %constant_dynamic-update-slice_fusion.10.n_ref, bf16[1024,3072]{1,0:T(8,128)(2,1)S(1)} %bitcast.354, bf16[1024,3072]{1,0:T(8,128)(2,1)S(1)} %bitcast.354, f32[1,1024]{1,0:T(1,128)S(1)} %bitcast.365), custom_call_target="tpu_custom_call" | custom-call | flops 27599998976 | bytes 1000 | tf_op jit(solution)/shard_map/attend/pallas_call | solution.py:64
  78.2 12.7 %block_forward.2 = (f32[256,1024]{1,0:T(8,128)S(1)}, f32[256,1]{1,0:T(8,128)S(1)}, bf16[256,1024]{1,0:T(8,128)(2,1)S(1)}, f32[256,4096]{1,0:T(8,128)S(1)}, bf16[...) custom-call(f32[256,1024]{1,0:T(8,128)S(1)} %get-tuple-element.264.x, ...), custom_call_target="tpu_custom_call" | custom-call | flops 13799999488 | bytes 1000 | tf_op jit(solution)/shard_map/block_forward/pallas_call | solution.py:233
  99.7 7.4 %collective-permute-done.11 = bf16[256,1024]{1,0:T(8,128)(2,1)S(1)} collective-permute-done((bf16[256,1024]{1,0:T(8,128)(2,1)S(1)}, bf16[256,1024]{1,0:T(8,128)(2,1)S(1)}, u32[]{:S(2)}, u32[]{:S(2)}) %collective-permute-start.11) | collective-permute-done | bytes 524320 | tf_op jit(solution)/shard_map/ppermute | solution.py:564
  110.3 4.5 collective-permute-done.13
  117.3 23.0 %attend.3.a_ref.r1 = bf16[256,1024]{1,0:T(8,128)(2,1)S(1)} custom-call(bf16[256,1024]{1,0:T(8,128)(2,1)S(1)} %fusion.12.q_ref, bf16[2048,1024]{1,0:T(8,128)(2,1)S(1)} %constant_dynamic-update-slice_fusion.n_ref, bf16[1024,3072]{1,0:T(8,128)(2,1)S(1)} %bitcast.356, bf16[1024,3072]{1,0:T(8,128)(2,1)S(1)} %bitcast.356, f32[1,1024]{1,0:T(1,128)S(1)} %bitcast.366), custom_call_target="tpu_custom_call" | custom-call | flops 27599998976 | bytes 1000 | tf_op jit(solution)/shard_map/attend/pallas_call | solution.py:64
  140.3 12.5 %block_forward.3 = (f32[256,1024]{1,0:T(8,128)S(1)}, f32[256,1]{1,0:T(8,128)S(1)}, bf16[256,1024]{1,0:T(8,128)(2,1)S(1)}, f32[256,4096]{1,0:T(8,128)S(1)}, bf16[...) custom-call(f32[256,1024]{1,0:T(8,128)S(1)} %get-tuple-element.110.x_ref, bf16[256,1024]{1,0:T(8,128)(2,1)S(1)} %attend.3.a_ref.r1, ...), custom_call_target="tpu_custom_call" | custom-call | flops 13799999488 | bytes 1000 | tf_op jit(solution)/shard_map/block_forward/pallas_call | solution.py:233
  157.7 16.5 %block_backward.2 = (bf16[256,4096]{1,0:T(8,128)(2,1)}, f32[1,4096]{1,0:T(1,128)S(1)}, f32[256,1024]{1,0:T(8,128)S(1)}, bf16[256,1024]{1,0:T(8,128)(2,1)S(1)}, b...) custom-call(s32[1]{0:T(128)} %bitcast.16.c_ref, f32[256,1024]{1,0:T(8,128)S(1)} %pad_maximum_fusion.grad_ref, ...), custom_call_target="tpu_custom_call" | custom-call | flops 16099999744 | bytes 1000 | tf_op jit(solution)/shard_map/block_backward/pallas_call | solution.py:331
  176.0 4.5 all-to-all-start
  180.5 4.6 add_convert_fusion.1
  189.8 32.9 %attend_back.3.d_ref = bf16[8,3,256,128]{3,2,1,0:T(8,128)(2,1)} custom-call(bf16[2048,128]{1,0:T(8,128)(2,1)} %get-tuple-element.258.q_ref, bf16[2048,128]{1,0:T(8,128)(2,1)} %get-tuple-element.257.k_ref, bf16[2048,128]{1,0:T(8,128)(2,1)} %get-tuple-element.256.v_ref, bf16[2048,128]{1,0:T(8,128)(2,1)} %bitcast.17.do_ref), custom_call_target="tpu_custom_call" | custom-call | flops 37950001152 | bytes 1000 | tf_op jit(solution)/shard_map/attend_back/pallas_call | solution.py:132
  222.7 3.9 all-to-all-start.1
  226.6 4.7 add_convert_fusion.2
  238.6 8.5 %all-to-all-done.1.b_ref = bf16[8,3,256,128]{3,2,1,0:T(8,128)(2,1)S(1)} async-done(((bf16[8,3,256,128]{3,2,1,0:T(8,128)(2,1)}), bf16[8,3,256,128]{3,2,1,0:T(8,128)(2,1)S(1)}, u32[]{:S(2)}, u32[]{:S(2)}) %all-to-all-start.1) | async-done | bytes 1572896 | tf_op jit(solution)/shard_map/all_to_all | solution.py:765
  251.1 5.8 %qkv_backward.2 = (f32[256,1024]{1,0:T(8,128)S(1)}, bf16[2,128,1024]{2,1,0:T(8,128)(2,1)S(1)}, f32[8,1024]{1,0:T(8,128)S(1)}, f32[8,1024]{1,0:T(8,128)S(1)}) custom-call(bf16[8,3,256,128]{3,2,1,0:T(8,128)(2,1)S(1)} %all-to-all-done.1.b_ref, bf16[1024,3072]{1,0:T(8,128)(2,1)S(1)} %copy-done.13, bf16[1024,3072]{1,0:T(8,128)(2,1)S(1)} %copy-done.13, ...), custom_call_target="tpu_custom_call" | custom-call | flops 6899999744 | bytes 1000 | tf_op jit(solution)/shard_map/qkv_backward/pallas_call | solution.py:424
  256.9 3.9 grad_rows.2
  262.5 4.6 grad_rows.3
  272.2 21.6 %block_backward.3 = (bf16[256,4096]{1,0:T(8,128)(2,1)}, f32[1,4096]{1,0:T(1,128)S(1)}, f32[256,1024]{1,0:T(8,128)S(1)}, bf16[256,1024]{1,0:T(8,128)(2,1)S(1)}, b...) custom-call(s32[1]{0:T(128)} %bitcast.16.c_ref, ...), custom_call_target="tpu_custom_call" | custom-call | flops 20700000256 | bytes 1000 | tf_op jit(solution)/shard_map/block_backward/pallas_call | solution.py:331
  303.4 4.4 all-to-all-start.2
  311.9 5.2 %all-to-all-done.2 = bf16[8,256,128]{2,1,0:T(8,128)(2,1)} async-done(((bf16[8,256,128]{2,1,0:T(8,128)(2,1)}), bf16[8,256,128]{2,1,0:T(8,128)(2,1)}, u32[]{:S(2)}, u32[]{:S(2)}) %all-to-all-start.2) | async-done | bytes 524320 | tf_op jit(solution)/shard_map/all_to_all | solution.py:734
  325.8 18.5 %attend_back.4.rest_0_ = bf16[8,3,256,128]{3,2,1,0:T(8,128)(2,1)} custom-call(bf16[2048,128]{1,0:T(8,128)(2,1)} %get-tuple-element.255.q_ref, bf16[2048,128]{1,0:T(8,128)(2,1)} %get-tuple-element.254.k_ref, bf16[2048,128]{1,0:T(8,128)(2,1)} %get-tuple-element.253.v_ref, bf16[2048,128]{1,0:T(8,128)(2,1)} %bitcast.25.do_ref), custom_call_target="tpu_custom_call" | custom-call | flops 19549999104 | bytes 1000 | tf_op jit(solution)/shard_map/attend_back/pallas_call | solution.py:132
  351.9 19.1 %attend_back.5.d_ref = bf16[8,3,256,128]{3,2,1,0:T(8,128)(2,1)} custom-call(bf16[2048,128]{1,0:T(8,128)(2,1)} %get-tuple-element.255.q_ref, bf16[2048,128]{1,0:T(8,128)(2,1)} %get-tuple-element.254.k_ref, bf16[2048,128]{1,0:T(8,128)(2,1)} %get-tuple-element.253.v_ref, bf16[2048,128]{1,0:T(8,128)(2,1)} %bitcast.25.do_ref, ...), custom_call_target="tpu_custom_call" | custom-call | flops 19549999104 | bytes 1000 | tf_op jit(solution)/shard_map/attend_back/pallas_call | solution.py:132
  371.0 9.3 %collective-permute-done.29 = bf16[2,2,32,2048]{3,2,1,0:T(8,128)(2,1)S(1)} collective-permute-done((bf16[2,2,32,2048]{3,2,1,0:T(8,128)(2,1)}, bf16[2,2,32,2048]{3,2,1,0:T(8,128)(2,1)S(1)}, u32[]{:S(2)}, u32[]{:S(2)}) %collective-permute-start.29) | collective-permute-done | bytes 524320 | tf_op jit(solution)/shard_map/ppermute | solution.py:564
  389.5 4.3 all-to-all-start.3
  407.3 4.5 grad_heads.3
  414.4 5.1 collective-permute-done.34
  419.6 10.9 %collective-permute-done.33 = bf16[2,2,64,1024]{3,2,1,0:T(8,128)(2,1)} collective-permute-done((bf16[2,2,64,1024]{3,2,1,0:T(8,128)(2,1)}, bf16[2,2,64,1024]{3,2,1,0:T(8,128)(2,1)}, u32[]{:S(2)}, u32[]{:S(2)}) %collective-permute-start.33) | collective-permute-done | bytes 524320 | tf_op jit(solution)/shard_map/ppermute | solution.py:564
  446.3 4.5 all-to-all-start.4
  456.9 6.4 %qkv_backward.3 = (f32[256,1024]{1,0:T(8,128)S(1)}, bf16[2,128,1024]{2,1,0:T(8,128)(2,1)S(1)}, f32[8,1024]{1,0:T(8,128)S(1)}, f32[8,1024]{1,0:T(8,128)S(1)}) custom-call(bf16[8,3,256,128]{3,2,1,0:T(8,128)(2,1)} %all-to-all-done.3.b_ref, bf16[1024,3072]{1,0:T(8,128)(2,1)S(1)} %copy-done.14, bf16[1024,3072]{1,0:T(8,128)(2,1)S(1)} %copy-done.14, ...), custom_call_target="tpu_custom_call" | custom-call | flops 6899999744 | bytes 1000 | tf_op jit(solution)/shard_map/qkv_backward/pallas_call | solution.py:424
  483.5 6.9 %all-to-all-done.5 = f32[16,1,1088]{2,1,0:T(1,128)S(1)} async-done(((f32[16,1,1088]{2,1,0:T(1,128)}), f32[16,1,1088]{2,1,0:T(1,128)S(1)}, u32[]{:S(2)}, u32[]{:S(2)}) %all-to-all-start.5) | async-done | bytes 69664 | tf_op jit(solution)/shard_map/all_to_all | solution.py:806
  (367 shorter events, 202.8 us)
Async XLA Ops:
  1.8 16.0 %collective-permute-start = (bf16[128,1024]{1,0:T(8,128)(2,1)S(1)}, bf16[128,1024]{1,0:T(8,128)(2,1)S(1)}, u32[]{:S(2)}, u32[]{:S(2)}) collective-permute-start(bf16[128,1024]{1,0:T(8,128)(2,1)S(1)} %get-tuple-element.270), channel_id=1, source_target_pairs={{0,8},{8,0},{1,9},{9,1},{2,10},{10,2},{3,11},{11,3},{4,12},{12,4},... | collective-permute-start | bytes 786440 | tf_op jit(solution)/shard_map/ppermute | solution.py:564
  24.2 21.0 %collective-permute-start.5 = (bf16[256,1024]{1,0:T(8,128)(2,1)S(1)}, bf16[256,1024]{1,0:T(8,128)(2,1)S(1)}, u32[]{:S(2)}, u32[]{:S(2)}) collective-permute-start(bf16[256,1024]{1,0:T(8,128)(2,1)S(1)} %get-tuple-element.249), channel_id=1, source_target_pairs={{0,1},{1,0},{2,3},{3,2},{4,5},{5,4},{6,7},{7,6},{8,9},{9,8},{10,11... | collective-permute-start | bytes 1572872 | tf_op jit(solution)/shard_map/ppermute | solution.py:564
  49.2 28.8 %collective-permute-start.10 = (f32[128,1024]{1,0:T(8,128)S(1)}, f32[128,1024]{1,0:T(8,128)S(1)}, u32[]{:S(2)}, u32[]{:S(2)}) collective-permute-start(f32[128,1024]{1,0:T(8,128)S(1)} %get-tuple-element.260), channel_id=1, source_target_pairs={{0,8},{8,0},{1,9},{9,1},{2,10},{10,2},{3,11},{11,3},{4,12},{12,4},... | collective-permute-start | bytes 1572872 | tf_op jit(solution)/shard_map/ppermute | solution.py:564
  97.2 18.5 %collective-permute-start.15 = (bf16[256,1024]{1,0:T(8,128)(2,1)S(1)}, bf16[256,1024]{1,0:T(8,128)(2,1)S(1)}, u32[]{:S(2)}, u32[]{:S(2)}) collective-permute-start(bf16[256,1024]{1,0:T(8,128)(2,1)S(1)} %get-tuple-element.111), channel_id=1, source_target_pairs={{0,1},{1,0},{2,3},{3,2},{4,5},{5,4},{6,7},{7,6},{8,9},{9,8},{10,11... | collective-permute-start | bytes 1572872 | tf_op jit(solution)/shard_map/ppermute | solution.py:564
  157.1 29.4 %collective-permute-start.20 = (bf16[128,1024]{1,0:T(8,128)(2,1)}, bf16[128,1024]{1,0:T(8,128)(2,1)}, u32[]{:S(2)}, u32[]{:S(2)}) collective-permute-start(bf16[128,1024]{1,0:T(8,128)(2,1)} %get-tuple-element.268), channel_id=1, source_target_pairs={{0,8},{8,0},{1,9},{9,1},{2,10},{10,2},{3,11},{11,3},{4,12},{12,4},... | collective-permute-start | bytes 786440 | tf_op jit(solution)/shard_map/ppermute | solution.py:564
  222.7 24.3 %all-to-all-start.1 = ((bf16[8,3,256,128]{3,2,1,0:T(8,128)(2,1)}), bf16[8,3,256,128]{3,2,1,0:T(8,128)(2,1)S(1)}, u32[]{:S(2)}, u32[]{:S(2)}) async-start(bf16[8,3,256,128]{3,2,1,0:T(8,128)(2,1)} %attend_back.3.d_ref), calls=%async_computation.1 | async-start | bytes 3145728 | tf_op jit(solution)/shard_map/all_to_all | solution.py:765
  262.2 31.6 %collective-permute-start.21 = (bf16[8,64,2048]{2,1,0:T(8,128)(2,1)S(1)}, bf16[8,64,2048]{2,1,0:T(8,128)(2,1)}, u32[]{:S(2)}, u32[]{:S(2)}) collective-permute-start(bf16[8,64,2048]{2,1,0:T(8,128)(2,1)S(1)} %get-tuple-element.127), channel_id=1, source_target_pairs={{0,1},{1,0},{2,3},{3,2},{4,5},{5,4},{6,7},{7,6},{8,9},{9,8},{10,11... | collective-permute-start | bytes 6291464 | tf_op jit(solution)/shard_map/ppermute | solution.py:564
  268.5 25.4 %collective-permute-start.22 = (bf16[8,64,2048]{2,1,0:T(8,128)(2,1)}, bf16[8,64,2048]{2,1,0:T(8,128)(2,1)}, u32[]{:S(2)}, u32[]{:S(2)}) collective-permute-start(bf16[8,64,2048]{2,1,0:T(8,128)(2,1)} %get-tuple-element.129), channel_id=1, source_target_pairs={{0,1},{1,0},{2,3},{3,2},{4,5},{5,4},{6,7},{7,6},{8,9},{9,8},{10,11... | collective-permute-start | bytes 6291464 | tf_op jit(solution)/shard_map/ppermute | solution.py:564
  302.9 19.5 %collective-permute-start.24 = (bf16[8,192,1024]{2,1,0:T(8,128)(2,1)}, bf16[8,192,1024]{2,1,0:T(8,128)(2,1)}, u32[]{:S(2)}, u32[]{:S(2)}) collective-permute-start(bf16[8,192,1024]{2,1,0:T(8,128)(2,1)} %get-tuple-element.152), channel_id=1, source_target_pairs={{0,1},{1,0},{2,3},{3,2},{4,5},{5,4},{6,7},{7,6},{8,9},{9,8},{10,11... | collective-permute-start | bytes 9437192 | tf_op jit(solution)/shard_map/ppermute | solution.py:564
  307.8 36.5 %collective-permute-start.25 = (bf16[2,2,2,32,2048]{4,3,2,1,0:T(8,128)(2,1)}, bf16[2,2,2,32,2048]{4,3,2,1,0:T(8,128)(2,1)}, u32[]{:S(2)}, u32[]{:S(2)}) collective-permute-start(bf16[2,2,2,32,2048]{4,3,2,1,0:T(8,128)(2,1)} %fusion.18), channel_id=1, source_target_pairs={{0,16},{16,0},{1,17},{17,1},{2,18},{18,2},{3,19},{19,3},{4,20},{20... | collective-permute-start | bytes 3145736 | tf_op jit(solution)/shard_map/ppermute | solution.py:564
  309.3 35.0 %collective-permute-start.26 = (bf16[2,2,2,32,2048]{4,3,2,1,0:T(8,128)(2,1)}, bf16[2,2,2,32,2048]{4,3,2,1,0:T(8,128)(2,1)}, u32[]{:S(2)}, u32[]{:S(2)}) collective-permute-start(bf16[2,2,2,32,2048]{4,3,2,1,0:T(8,128)(2,1)} %fusion.19), channel_id=1, source_target_pairs={{0,2},{2,0},{1,3},{3,1},{4,6},{6,4},{5,7},{7,5},{8,10},{10,8},{9,1... | collective-permute-start | bytes 3145736 | tf_op jit(solution)/shard_map/ppermute | solution.py:564
  320.1 50.9 %collective-permute-start.27 = (bf16[2,2,2,64,1024]{4,3,2,1,0:T(8,128)(2,1)}, bf16[2,2,2,64,1024]{4,3,2,1,0:T(8,128)(2,1)}, u32[]{:S(2)}, u32[]{:S(2)}) collective-permute-start(bf16[2,2,2,64,1024]{4,3,2,1,0:T(8,128)(2,1)} %fusion.20), channel_id=1, source_target_pairs={{0,8},{8,0},{1,9},{9,1},{2,10},{10,2},{3,11},{11,3},{4,12},{12,4},... | collective-permute-start | bytes 3145736 | tf_op jit(solution)/shard_map/ppermute | solution.py:564
  325.7 54.6 %collective-permute-start.28 = (bf16[2,2,2,96,1024]{4,3,2,1,0:T(8,128)(2,1)}, bf16[2,2,2,96,1024]{4,3,2,1,0:T(8,128)(2,1)}, u32[]{:S(2)}, u32[]{:S(2)}) collective-permute-start(bf16[2,2,2,96,1024]{4,3,2,1,0:T(8,128)(2,1)} %fusion.4), channel_id=1, source_target_pairs={{0,2},{2,0},{1,3},{3,1},{4,6},{6,4},{5,7},{7,5},{8,10},{10,8},{9,1... | collective-permute-start | bytes 4718600 | tf_op jit(solution)/shard_map/ppermute | solution.py:564
  346.7 33.5 %collective-permute-start.29 = (bf16[2,2,32,2048]{3,2,1,0:T(8,128)(2,1)}, bf16[2,2,32,2048]{3,2,1,0:T(8,128)(2,1)S(1)}, u32[]{:S(2)}, u32[]{:S(2)}) collective-permute-start(bf16[2,2,32,2048]{3,2,1,0:T(8,128)(2,1)} %fusion.23), channel_id=1, source_target_pairs={{0,4},{4,0},{1,5},{5,1},{2,6},{6,2},{3,7},{7,3},{8,12},{12,8},{9,1... | collective-permute-start | bytes 1572872 | tf_op jit(solution)/shard_map/ppermute | solution.py:564
  350.4 29.8 %collective-permute-start.30 = (bf16[2,2,32,2048]{3,2,1,0:T(8,128)(2,1)}, bf16[2,2,32,2048]{3,2,1,0:T(8,128)(2,1)}, u32[]{:S(2)}, u32[]{:S(2)}) collective-permute-start(bf16[2,2,32,2048]{3,2,1,0:T(8,128)(2,1)} %fusion.22), channel_id=1, source_target_pairs={{0,16},{16,0},{1,17},{17,1},{2,18},{18,2},{3,19},{19,3},{4,20},{20... | collective-permute-start | bytes 1572872 | tf_op jit(solution)/shard_map/ppermute | solution.py:564
  389.5 24.9 %all-to-all-start.3 = ((bf16[8,3,256,128]{3,2,1,0:T(8,128)(2,1)}), bf16[8,3,256,128]{3,2,1,0:T(8,128)(2,1)}, u32[]{:S(2)}, u32[]{:S(2)}) async-start(bf16[8,3,256,128]{3,2,1,0:T(8,128)(2,1)} %attend_back.5.d_ref), calls=%async_computation.3 | async-start | bytes 3145728 | tf_op jit(solution)/shard_map/all_to_all | solution.py:765
  398.5 31.9 %collective-permute-start.32 = (bf16[2,2,96,1024]{3,2,1,0:T(8,128)(2,1)}, bf16[2,2,96,1024]{3,2,1,0:T(8,128)(2,1)}, u32[]{:S(2)}, u32[]{:S(2)}) collective-permute-start(bf16[2,2,96,1024]{3,2,1,0:T(8,128)(2,1)} %fusion.5), channel_id=1, source_target_pairs={{0,16},{16,0},{1,17},{17,1},{2,18},{18,2},{3,19},{19,3},{4,20},{20... | collective-permute-start | bytes 2359304 | tf_op jit(solution)/shard_map/ppermute | solution.py:564
  400.7 29.8 %collective-permute-start.33 = (bf16[2,2,64,1024]{3,2,1,0:T(8,128)(2,1)}, bf16[2,2,64,1024]{3,2,1,0:T(8,128)(2,1)}, u32[]{:S(2)}, u32[]{:S(2)}) collective-permute-start(bf16[2,2,64,1024]{3,2,1,0:T(8,128)(2,1)} %fusion.21), channel_id=1, source_target_pairs={{0,16},{16,0},{1,17},{17,1},{2,18},{18,2},{3,19},{19,3},{4,20},{20... | collective-permute-start | bytes 1572872 | tf_op jit(solution)/shard_map/ppermute | solution.py:564
  401.2 18.3 %collective-permute-start.34 = (bf16[2,32,2048]{2,1,0:T(8,128)(2,1)}, bf16[2,32,2048]{2,1,0:T(8,128)(2,1)}, u32[]{:S(2)}, u32[]{:S(2)}) collective-permute-start(bf16[2,32,2048]{2,1,0:T(8,128)(2,1)} %fusion.28), channel_id=1, source_target_pairs={{0,2},{2,0},{1,3},{3,1},{4,6},{6,4},{5,7},{7,5},{8,10},{10,8},{9,1... | collective-permute-start | bytes 786440 | tf_op jit(solution)/shard_map/ppermute | solution.py:564
  403.1 16.5 %collective-permute-start.35 = (bf16[2,32,2048]{2,1,0:T(8,128)(2,1)}, bf16[2,32,2048]{2,1,0:T(8,128)(2,1)}, u32[]{:S(2)}, u32[]{:S(2)}) collective-permute-start(bf16[2,32,2048]{2,1,0:T(8,128)(2,1)} %fusion.27), channel_id=1, source_target_pairs={{0,4},{4,0},{1,5},{5,1},{2,6},{6,2},{3,7},{7,3},{8,12},{12,8},{9,1... | collective-permute-start | bytes 786440 | tf_op jit(solution)/shard_map/ppermute | solution.py:564
  412.7 30.8 %collective-permute-start.31 = (bf16[6,64,512]{2,1,0:T(8,128)(2,1)}, bf16[6,64,512]{2,1,0:T(8,128)(2,1)}, u32[]{:S(2)}, u32[]{:S(2)}) collective-permute-start(bf16[6,64,512]{2,1,0:T(8,128)(2,1)} %get-tuple-element.262), channel_id=1, source_target_pairs={{0,16},{16,0},{1,17},{17,1},{2,18},{18,2},{3,19},{19,3},{4,20},{20... | collective-permute-start | bytes 1179656 | tf_op jit(solution)/shard_map/ppermute | solution.py:564
  432.5 35.0 %collective-permute-start.36 = (bf16[2,64,1024]{2,1,0:T(8,128)(2,1)}, bf16[2,64,1024]{2,1,0:T(8,128)(2,1)}, u32[]{:S(2)}, u32[]{:S(2)}) collective-permute-start(bf16[2,64,1024]{2,1,0:T(8,128)(2,1)} %fusion.26), channel_id=1, source_target_pairs={{0,4},{4,0},{1,5},{5,1},{2,6},{6,2},{3,7},{7,3},{8,12},{12,8},{9,1... | collective-permute-start | bytes 786440 | tf_op jit(solution)/shard_map/ppermute | solution.py:564
  436.7 30.9 %collective-permute-start.37 = (bf16[2,96,1024]{2,1,0:T(8,128)(2,1)}, bf16[2,96,1024]{2,1,0:T(8,128)(2,1)}, u32[]{:S(2)}, u32[]{:S(2)}) collective-permute-start(bf16[2,96,1024]{2,1,0:T(8,128)(2,1)} %fusion.24), channel_id=1, source_target_pairs={{0,4},{4,0},{1,5},{5,1},{2,6},{6,2},{3,7},{7,3},{8,12},{12,8},{9,1... | collective-permute-start | bytes 1179656 | tf_op jit(solution)/shard_map/ppermute | solution.py:564
  438.7 28.8 %collective-permute-start.38 = (bf16[32,2048]{1,0:T(8,128)(2,1)}, bf16[32,2048]{1,0:T(8,128)(2,1)}, u32[]{:S(2)}, u32[]{:S(2)}) collective-permute-start(bf16[32,2048]{1,0:T(8,128)(2,1)} %fusion.41), channel_id=1, source_target_pairs={{0,8},{8,0},{1,9},{9,1},{2,10},{10,2},{3,11},{11,3},{4,12},{12,4},... | collective-permute-start | bytes 393224 | tf_op jit(solution)/shard_map/ppermute | solution.py:564
  442.0 25.5 %collective-permute-start.39 = (bf16[32,2048]{1,0:T(8,128)(2,1)}, bf16[32,2048]{1,0:T(8,128)(2,1)}, u32[]{:S(2)}, u32[]{:S(2)}) collective-permute-start(bf16[32,2048]{1,0:T(8,128)(2,1)} %fusion.40), channel_id=1, source_target_pairs={{0,8},{8,0},{1,9},{9,1},{2,10},{10,2},{3,11},{11,3},{4,12},{12,4},... | collective-permute-start | bytes 393224 | tf_op jit(solution)/shard_map/ppermute | solution.py:564
  446.3 21.2 %all-to-all-start.4 = ((bf16[16,64,512]{2,1,0:T(8,128)(2,1)}), bf16[16,64,512]{2,1,0:T(8,128)(2,1)}, u32[]{:S(2)}, u32[]{:S(2)}) async-start(bf16[16,64,512]{2,1,0:T(8,128)(2,1)} %copy-done.10), calls=%async_computation.4 | async-start | bytes 2097152 | tf_op jit(solution)/shard_map/all_to_all | solution.py:782
  464.1 29.8 %collective-permute-start.40 = (bf16[128,1024]{1,0:T(8,128)(2,1)}, bf16[128,1024]{1,0:T(8,128)(2,1)}, u32[]{:S(2)}, u32[]{:S(2)}) collective-permute-start(bf16[128,1024]{1,0:T(8,128)(2,1)} %slice_bitcast_fusion.1), channel_id=1, source_target_pairs={{0,8},{8,0},{1,9},{9,1},{2,10},{10,2},{3,11},{11,3},{4,12},{12,4},... | collective-permute-start | bytes 786440 | tf_op jit(solution)/shard_map/ppermute | solution.py:564
  469.6 24.3 %collective-permute-start.41 = (bf16[96,1024]{1,0:T(8,128)(2,1)}, bf16[96,1024]{1,0:T(8,128)(2,1)}, u32[]{:S(2)}, u32[]{:S(2)}) collective-permute-start(bf16[96,1024]{1,0:T(8,128)(2,1)} %fusion.31), channel_id=1, source_target_pairs={{0,8},{8,0},{1,9},{9,1},{2,10},{10,2},{3,11},{11,3},{4,12},{12,4},... | collective-permute-start | bytes 589832 | tf_op jit(solution)/shard_map/ppermute | solution.py:564
  473.0 20.9 %collective-permute-start.42 = (bf16[64,1024]{1,0:T(8,128)(2,1)}, bf16[64,1024]{1,0:T(8,128)(2,1)}, u32[]{:S(2)}, u32[]{:S(2)}) collective-permute-start(bf16[64,1024]{1,0:T(8,128)(2,1)} %fusion.39), channel_id=1, source_target_pairs={{0,2},{2,0},{1,3},{3,1},{4,6},{6,4},{5,7},{7,5},{8,10},{10,8},{9,1... | collective-permute-start | bytes 393224 | tf_op jit(solution)/shard_map/ppermute | solution.py:564
  475.7 14.6 %all-to-all-start.5 = ((f32[16,1,1088]{2,1,0:T(1,128)}), f32[16,1,1088]{2,1,0:T(1,128)S(1)}, u32[]{:S(2)}, u32[]{:S(2)}) async-start(f32[16,1,1088]{2,1,0:T(1,128)} %reshape.567), calls=%async_computation.5 | async-start | bytes 147456 | tf_op jit(solution)/shard_map/all_to_all | solution.py:806
  481.9 31.7 %collective-permute-start.48 = (bf16[32,4096]{1,0:T(8,128)(2,1)}, bf16[32,4096]{1,0:T(8,128)(2,1)}, u32[]{:S(2)}, u32[]{:S(2)}) collective-permute-start(bf16[32,4096]{1,0:T(8,128)(2,1)} %pad_maximum_fusion.6), channel_id=1, source_target_pairs={{0,16},{16,0},{1,17},{17,1},{2,18},{18,2},{3,19},{19,3},{4,20},{20... | collective-permute-start | bytes 786440 | tf_op jit(solution)/shard_map/ppermute | solution.py:564
  500.6 15.2 %collective-permute-start.44 = (bf16[3,64,512]{2,1,0:T(8,128)(2,1)S(1)}, bf16[3,64,512]{2,1,0:T(8,128)(2,1)}, u32[]{:S(2)}, u32[]{:S(2)}) collective-permute-start(bf16[3,64,512]{2,1,0:T(8,128)(2,1)S(1)} %take.5), channel_id=1, source_target_pairs={{0,8},{8,0},{1,9},{9,1},{2,10},{10,2},{3,11},{11,3},{4,12},{12,4},... | collective-permute-start | bytes 589832 | tf_op jit(solution)/shard_map/ppermute | solution.py:564
  (99 other events, 932.8 us)

commit v3 on v2

--- a/solution.py
+++ b/solution.py
@@ -406,13 +406,11 @@
         dv, gain, bias = norm_back(total[...], n_ref[...], r_ref[...], g_ref[...])
         grad = m_ref[...] + dv
         grad_ref[...] = grad
-        half = low_ref.shape[1]
-        low_ref[0] = grad[:half].astype(bf16)
-        low_ref[1] = grad[half:].astype(bf16)
+        low_ref[...] = grad[grad.shape[0] - low_ref.shape[0] :].astype(bf16)
         put_sums(sums_ref, gain, bias, column_sum(grad))
 
 
-def qkv_backward(back, w_qkv, middle_grad, n1, r1, gain):
+def qkv_backward(back, w_qkv, middle_grad, n1, r1, gain, low):
     members, _, t, w = back.shape
     d = members * w
     at_once = max(2, 128 // w)
@@ -428,15 +426,15 @@
             full, full, spec((t, 1), lambda i: (0, 0)), spec((1, d), lambda i: (0, 0)),
         ],
         out_specs=[
-            full, spec((2, t // 2, d), lambda i: (0, 0, 0)), spec((8, d), lambda i: (0, 0)),
+            full, spec((low, d), lambda i: (0, 0)), spec((8, d), lambda i: (0, 0)),
             spec((8, block), lambda i: (0, i)),
         ],
         out_shape=[
-            shape((t, d), f32), shape((2, t // 2, d), bf16), shape((8, d), f32), shape((8, d), f32),
+            shape((t, d), f32), shape((low, d), bf16), shape((8, d), f32), shape((8, d), f32),
         ],
         scratch_shapes=[pltpu.VMEM((t, d), f32)],
-        compiler_params=pltpu.CompilerParams(vmem_limit_bytes=40 * MIB),
-        cost_estimate=cost(6),
+        compiler_params=pltpu.CompilerParams(vmem_limit_bytes=60 * MIB),
+        cost_estimate=cost(12),
         name="qkv_backward",
     )(back, w_qkv, w_qkv, w_qkv, middle_grad, n1, r1, gain.reshape(1, d))
 
@@ -497,6 +495,30 @@
         cost_estimate=cost(3),
         name="take",
     )(table, *terms)
+
+
+def join_kernel(i_ref, own_ref, other_ref, out_ref):
+    half = other_ref.shape[0]
+    out_ref[i_ref[0]] = own_ref[:half]
+    out_ref[1 - i_ref[0]] = other_ref[...].astype(f32)
+
+
+def join(index, own, other):
+    half, d = other.shape
+    full = spec((half, d), lambda i, c: (0, 0))
+    return pl.pallas_call(
+        join_kernel,
+        grid_spec=pltpu.PrefetchScalarGridSpec(
+            num_scalar_prefetch=1,
+            grid=(1,),
+            in_specs=[full, full],
+            out_specs=spec((2, half, d), lambda i, c: (0, 0, 0)),
+        ),
+        out_shape=jax.ShapeDtypeStruct((2, half, d), f32),
+        compiler_params=pltpu.CompilerParams(vmem_limit_bytes=8 * MIB),
+        cost_estimate=cost(2),
+        name="join",
+    )(index.reshape(1), own, other)
 
 
 def unit_tables(bands, x_count, width, dim):
@@ -695,6 +717,8 @@
     later = None
     w_heads = None
     unit, send_table, keep_table = unit_tables(bands, 2 ** len(x_axes), W, D)
+    send_row, keep_row = pick(jnp.asarray(send_table), me), pick(jnp.asarray(keep_table), me)
+    keep_rows = pick(keep_row, zh), pick(keep_row, 1 - zh)
     def split_rows(x, rows_two):
         n, r, c = x.shape
         return x.reshape(cube + ((2, r // 2) if rows_two else (r,)) + (c,))
@@ -711,13 +735,6 @@
         n1, r1, normed_all, attended, n2, r2, normed_two, hidden, activated = kept[index]
         last = index == 0
         if last:
-            left, right = (later[0], down_grad), (later[1], activated)
-            y_other, y_own = grad_rows(core, left, right, bands, 0, 2)
-            y_core = swap(y_other, "core")
-            right = (later[1], pin(activated, y_other))
-            x_other, x_own = grad_rows(core, left, right, bands, 1, 2)
-            x_core = swap(x_other, "core")
-            grad = pin(grad, x_other)
             grads = (later[2], later[3], normed_two)
         else:
             down_grad = grad.astype(bf16)
@@ -725,12 +742,6 @@
         hidden_grad, hidden_sum, middle_grad, branch_grad, sent, sums_two, *ups = block_backward(
             core, grad, hidden, w_down, w_up, w_out, n2, r2, ln2_gain, members, grads
         )
-        if last:
-            (y_own, y_core), (x_own, x_core) = pin(((y_own, y_core), (x_own, x_core)), hidden_grad)
-            down_y = Share([split_rows(y_own, two), split_rows(y_core, two)], names + ("samp",) * two)
-            down_x = Share([split_rows(x_own, two), split_rows(x_core, two)], names + ("samp",) * two)
-            first = (down_y.halve("samp"), down_x.halve(x_axes[0]))
-            sent = pin(sent, *first)
         own_grad = lax.all_to_all(sent, low, 0, 0, tiled=True).reshape(members * rows, W)
         if last:
             z_other, x_other, z_own, x_own = ups
@@ -739,26 +750,39 @@
                 core, (later[4], pin(branch_grad, sent)), (later[5], attended), bands, x_other, x_own
             )
             x_core = swap(x_other, "core")
-            own_grad, z_own, z_core = pin((own_grad, z_own, z_core), x_other)
-            z_share = Share([split_rows(z_own, two), split_rows(z_core, two)], names + ("samp",) * two)
-            x_share = Share([split_rows(t, two) for t in (x_own, x_core)], names + ("samp",) * two)
-            sent = [z_share.halve("zh"), x_share.halve(x_axes[0])]
-            own_grad = pin(own_grad, *sent)
+            left, right = (later[0], pin(down_grad, x_other)), (later[1], activated)
+            one_other, one_own = grad_rows(core, left, right, bands, 0, 2)
+            one_core = swap(one_other, "core")
+            samp = ("samp",) * two
+            z_terms = pin((z_own, z_core), one_other)
+            z_share = Share([split_rows(t, two) for t in z_terms], names + samp)
+            left = (later[0], pin(down_grad, z_share.halve("zl")))
+            two_other, two_own = grad_rows(core, left, right, bands, 1, 2)
+            two_core = swap(two_other, "core")
+            x_terms = pin((x_own, x_core), two_other)
+            x_share = Share([split_rows(t, two) for t in x_terms], names + samp)
+            own_grad, one_own = pin((own_grad, one_own), x_share.halve(x_axes[0]))
+            down_one = Share([split_rows(t, two) for t in (one_own, one_core)], names + samp)
+            own_grad = pin(own_grad, down_one.halve("samp"))
             heads = W // HD
             d_heads = attend_back(*owns[0], own_grad, members, range((heads + 1) // 2))
-            waits = pin((own_grad, d_heads, down_y.terms[-1], down_x.terms[-1]))
-            own_grad, d_heads, down_y.terms[-1], down_x.terms[-1] = waits
-            sent = [down_y.halve("zl"), down_x.halve("samp")]
+            waits = pin((own_grad, d_heads, z_share.terms[-1], down_one.terms[-1], two_own, two_core))
+            own_grad, d_heads, z_share.terms[-1], down_one.terms[-1], two_own, two_core = waits
+            down_two = Share([split_rows(t, two) for t in (two_own, two_core)], names + samp)
+            sent = [z_share.halve("zh"), down_one.halve("zl"), down_two.halve("samp")]
             if heads > 1:
                 own_grad, d_heads = pin((own_grad, d_heads), *sent)
                 d_heads = attend_back(*owns[0], own_grad, members, range(heads // 2, heads), d_heads)
-            waits = pin((d_heads, z_share.terms[-1], x_share.terms[-1], down_y.terms[-1], down_x.terms[-1]))
-            d_heads, z_share.terms[-1], x_share.terms[-1], down_y.terms[-1], down_x.terms[-1] = waits
-            sent = [x_share.halve("samp"), z_share.halve("samp")] + [down_y.halve(a) for a in x_axes]
-            sent += [down_x.halve(a) for a in x_axes[1:] + ("zl",)]
+            shares = (z_share, x_share, down_one, down_two)
+            waits = pin((d_heads, *(t.terms[-1] for t in shares)))
+            d_heads = waits[0]
+            for t, value in zip(shares, waits[1:]):
+                t.terms[-1] = value
+            sent = [x_share.halve("samp"), down_two.halve("zh"), z_share.halve("samp")]
+            sent += [down_one.halve(a) for a in x_axes]
             d_heads = pin(d_heads, *sent)
         else:
-            own_grad = pin(own_grad, result)
+            own_grad, send_row, keep_rows = pin((own_grad, send_row, keep_rows), result)
             later = (down_grad, activated, hidden_grad, normed_two, branch_grad, attended)
             owns[index] = own_part(index)
             d_heads = attend_back(*owns[index], own_grad, members)
@@ -773,35 +797,38 @@
             else:
                 there, units = units, [units]
             back = pin(back, there)
-            waits = pin((x_share.terms[-1], z_share.terms[-1], down_y.terms[-1], down_x.terms[-1]), back)
-            x_share.terms[-1], z_share.terms[-1], down_y.terms[-1], down_x.terms[-1] = waits
-            sent = [x_share.halve(a) for a in x_axes[1:] + ("zl",)] + [z_share.halve("zl")]
-            sent += [down_y.halve("zh"), down_x.halve("zh")]
+            waits = pin(tuple(t.terms[-1] for t in shares), back)
+            for t, value in zip(shares, waits):
+                t.terms[-1] = value
+            sent = [x_share.halve(a) for a in x_axes[1:] + ("zl",)]
+            sent += [down_one.halve("zh")] + [t.halve(a) for t in (down_two, z_share) for a in x_axes]
             units[-1] = pin(units[-1], *sent)
-            outgoing = take(units, pick(jnp.asarray(send_table), me))
+            outgoing = take(units, send_row)
             incoming = lax.all_to_all(outgoing, low, 0, 0, tiled=True)
             back = pin(back, outgoing)
         else:
             owns[0] = own_part(0)
             back = pin(back, w_heads, *owns[0])
-        grad, low_grad, sums_one, sums_qv = qkv_backward(back, w_qkv, middle_grad, n1, r1, ln1_gain)
-        down_grad = low_grad.reshape(rows, D)
+        grad, low_grad, sums_one, sums_qv = qkv_backward(
+            back, w_qkv, middle_grad, n1, r1, ln1_gain, half if last else rows
+        )
+        down_grad = low_grad
         step_small = (sums_one[:3], sums_qv[:2], sums_two[:4], hidden_sum)
         small = step_small if small is None else tuple(a + b for a, b in zip(small, step_small))
-    fields_own = grad[:half]
-    fields_sent = low_grad[1]
+    fields_sent = low_grad
     fields_other = swap(fields_sent, "zh")
-    one, qv, two_sums, up_sum = small
+    x_share.terms[-1] = pin(x_share.terms[-1], fields_sent)
+    x_sent = x_share.halve("zh")
+    one, qv, two_sums, up_sum = pin(small, x_sent)
     samples = 2 * samp_count
     slot = 2 * y + zh
     mine = lax.broadcasted_iota(jnp.int32, (samples, 1), 0) == slot
     leads = jnp.where(mine, one[2:3], 0.0)
-    lane = lax.broadcasted_iota(jnp.int32, (bands, 1, D // bands), 2) == slot
-    bucket = jnp.where(lane & (me == 0) & (zh == slot % 2), pick(lead_bucket, zh).astype(f32), 0.0)
+    lane = lax.broadcasted_iota(jnp.int32, (bands, D // bands), 1) == slot
+    bucket = jnp.where(lane & (me == 0), pick(lead_bucket, zh).astype(f32), 0.0)
     vectors = jnp.concatenate([one[:2], qv, two_sums, leads])
-    vectors = vectors.reshape(-1, bands, D // bands).transpose(1, 0, 2)
-    ups = up_sum.reshape(bands, -1, D // bands)
-    vectors = jnp.concatenate([vectors, ups, bucket], axis=1)
+    vectors = vectors.reshape(-1, bands, D // bands).transpose(1, 0, 2).reshape(bands, -1)
+    vectors = jnp.concatenate([vectors, up_sum.reshape(bands, -1), bucket], axis=1)
     incoming, vectors = pin((incoming, vectors), fields_sent)
     vectors = lax.all_to_all(vectors, band, 0, 0, tiled=True)
 
@@ -822,18 +849,17 @@
         x = jnp.concatenate([first, second]).astype(f32)
         return x[:n], x[n:]
 
-    waits = pin((z_share.terms[-1], x_share.terms[-1], down_y.terms[-1], down_x.terms[-1], incoming), fields_sent)
-    z_share.terms[-1], x_share.terms[-1], down_y.terms[-1], down_x.terms[-1], incoming = waits
-    sent = [x_share.halve("zh")] + [z_share.halve(a) for a in x_axes]
-    down = jnp.concatenate([total(down_y.terms), total(down_x.terms)], axis=1).astype(bf16)
-    incoming, fields_other, x_share.terms[-1], z_share.terms[-1], vectors = pin(
-        (incoming, fields_other, x_share.terms[-1], z_share.terms[-1], vectors), down, *sent
-    )
+    incoming, down_two.terms[-1] = pin((incoming, down_two.terms[-1]), x_sent)
+    sent = down_two.halve("zl")
+    waits = pin((incoming, fields_other, vectors, *(t.terms[-1] for t in shares)), sent)
+    incoming, fields_other, vectors = waits[:3]
+    for t, value in zip(shares, waits[3:]):
+        t.terms[-1] = value
+    down = jnp.concatenate([total(down_one.terms), total(down_two.terms)], axis=1)
     vectors = jnp.sum(vectors, axis=0)
     vectors = vectors + swap(vectors, "samp") if two else lax.psum(vectors, "samp")
-    keep_table = pick(jnp.asarray(keep_table), me)
-    other = swap(take([incoming], pick(keep_table, 1 - zh)), "zh")
-    own = take([incoming], pick(keep_table, zh))
+    other = swap(take([incoming], keep_rows[1]), "zh")
+    own = take([incoming], keep_rows[0])
     own = total([own, other]).astype(bf16).reshape(3 * D // bands, -1)
     if two:
         other = swap(own, "samp")
@@ -847,17 +873,16 @@
     bottom = both_cut(total(x_share.terms), n_up // 2)
     w_out_grad = bottom[1].T
     w_up_grad = jnp.concatenate([both(total(z_share.terms)), bottom[0]]).T
-    fields_other = fields_other.astype(f32)
-    fields_grad = jnp.where(
-        zh == 0, jnp.stack([fields_own, fields_other]), jnp.stack([fields_other, fields_own])
-    )
-
-    leads = vectors[8 : 8 + samples]
-    up_grad = vectors[8 + samples : -1].reshape(-1)
-    buckets = vectors[-1, :samples].astype(jnp.int32)
+    fields_grad = join(zh, grad, fields_other)
+
+    w = D // bands
+    leads = vectors[8 * w : (8 + samples) * w].reshape(samples, w)
+    up_grad = vectors[(8 + samples) * w : -w]
+    buckets = vectors[-w:][:samples].astype(jnp.int32)
     one_hot = (buckets[:, None] == jnp.arange(lead_table.shape[0], dtype=jnp.int32)[None, :]).astype(f32)
     lead_grad = jnp.dot(one_hot.T, leads, precision=lax.Precision.HIGHEST)
-    g = [vectors[i] for i in (0, 1, 2, 3, 6, 4, 5)] + [up_grad, vectors[7]]
+    rows_of = lambda i: vectors[i * w : (i + 1) * w]
+    g = [rows_of(i) for i in (0, 1, 2, 3, 6, 4, 5)] + [up_grad, rows_of(7)]
     return (
         result,
         fields_grad,

time: 530 us -> 527 us (level)
  waiting for transfers between devices: 82.5 us -> 91.5 us
  other arithmetic: 64.8 us -> 56.1 us
  local copies, waits for them, and re-layouts: 59.5 us -> 50.9 us
    all_to_all x2, waiting for transfers between devices: 8.71 us -> 20.1 us  [body(): back = lax.all_to_all(d_heads, low, 0, 0, tiled=True)]
    dynamic_update_slice x19, local copies, waits for them, and re-layouts: 7.4 us -> 0.67 us  [gather(): out = lax.dynamic_update_slice(out, piece, ((me ^ k) * rows + offset, 0))]
    pallas_call x2, Pallas kernels: 12.2 us -> 18 us  [qkv_backward(): pl.pallas_call(qkv_backward_kernel, grid=(members // at_once,), in_specs=...]
    unnamed x154 -> x148, local copies, waits for them, and re-layouts: 32.3 us -> 30.7 us
  transfers between devices with their start and end apart: 55 -> 55, of which waited for: 20 -> 20; matrix products, arithmetic and copies ran while one was open for 16% -> 14% of each run, Pallas kernels for 24% -> 21%
where the time goes in v3:
time: 527 us; the launch traced here: 521 us
  Pallas kernels  223 us (42%)
  waiting for transfers between devices  91.5 us (17%)
  starting transfers between devices  80.7 us (15%)
  other arithmetic  56.1 us (11%)
  local copies, waits for them, and re-layouts  50.9 us (10%)
  matrix products  13.5 us (3%)
    pallas_call x3, Pallas kernels, attend_back(): pl.pallas_call(functools.partial(attend_back_kernel, heads=heads, some=so...  70.6 us
    ppermute x49, waiting for transfers between devices, swap(): return lax.ppermute(x, axis, SWAP)  63 us
    ppermute x49, starting transfers between devices, swap(): return lax.ppermute(x, axis, SWAP)  50.5 us
    pallas_call x2, Pallas kernels, attend(): pl.pallas_call(attend_kernel, grid=(width // block,), in_specs=[own, spec...  46.2 us
    pallas_call x2, Pallas kernels, block_backward(): pl.pallas_call(functools.partial(block_backward_kernel, grads=bool(grads)...  38.1 us
    convert_element_type x16, other arithmetic, halve(): sent = total(there).astype(bf16)  37.3 us
    unnamed x148, local copies, waits for them, and re-layouts  30.7 us
    pallas_call x2, Pallas kernels, block_forward(): pl.pallas_call(functools.partial(block_forward_kernel, last=last), grid=(...  25.3 us
  transfers between devices with their start and end apart: 55, of which 20 were waited for; matrix products, arithmetic and copies ran while one was open for 14% of the time, Pallas kernels for 21%

profile of v3, /device:TPU:0, one launch (start us, length us, event | category | flops | bytes accessed | tf_op | source)
XLA Modules:
  0.0 520.7 jit_solution(7725264613638049603)
XLA Ops:
  1.8 4.1 collective-permute-start
  11.3 6.5 %collective-permute-done = bf16[128,1024]{1,0:T(8,128)(2,1)S(1)} collective-permute-done((bf16[128,1024]{1,0:T(8,128)(2,1)S(1)}, bf16[128,1024]{1,0:T(8,128)(2,1)S(1)}, u32[]{:S(2)}, u32[]{:S(2)}) %collective-permute-start) | collective-permute-done | bytes 262176 | tf_op jit(solution)/shard_map/ppermute | solution.py:586
  23.0 9.3 %collective-permute-done.2 = bf16[256,1024]{1,0:T(8,128)(2,1)S(1)} collective-permute-done((bf16[256,1024]{1,0:T(8,128)(2,1)S(1)}, bf16[256,1024]{1,0:T(8,128)(2,1)S(1)}, u32[]{:S(2)}, u32[]{:S(2)}) %collective-permute-start.2) | collective-permute-done | bytes 524320 | tf_op jit(solution)/shard_map/ppermute | solution.py:586
  42.5 3.8 collective-permute-start.10
  46.3 23.3 %attend.2.a_ref.r0 = bf16[256,1024]{1,0:T(8,128)(2,1)S(1)} custom-call(bf16[256,1024]{1,0:T(8,128)(2,1)S(1)} %fusion.15.q_ref, bf16[2048,1024]{1,0:T(8,128)(2,1)S(1)} %constant_dynamic-update-slice_fusion.10.n_ref, bf16[1024,3072]{1,0:T(8,128)(2,1)S(1)} %copy-done.15, bf16[1024,3072]{1,0:T(8,128)(2,1)S(1)} %copy-done.15, f32[1,1024]{1,0:T(1,128)S(1)} %bitcast.341), custom_call_target="tpu_custom_call" | custom-call | flops 27599998976 | bytes 1000 | tf_op jit(solution)/shard_map/attend/pallas_call | solution.py:64
  69.9 12.7 %block_forward.2 = (f32[256,1024]{1,0:T(8,128)S(1)}, f32[256,1]{1,0:T(8,128)S(1)}, bf16[256,1024]{1,0:T(8,128)(2,1)S(1)}, f32[256,4096]{1,0:T(8,128)S(1)}, bf16[...) custom-call(f32[256,1024]{1,0:T(8,128)S(1)} %get-tuple-element.278.x, ...), custom_call_target="tpu_custom_call" | custom-call | flops 13799999488 | bytes 1000 | tf_op jit(solution)/shard_map/block_forward/pallas_call | solution.py:233
  93.5 6.5 %collective-permute-done.12 = bf16[256,1024]{1,0:T(8,128)(2,1)S(1)} collective-permute-done((bf16[256,1024]{1,0:T(8,128)(2,1)S(1)}, bf16[256,1024]{1,0:T(8,128)(2,1)S(1)}, u32[]{:S(2)}, u32[]{:S(2)}) %collective-permute-start.12) | collective-permute-done | bytes 524320 | tf_op jit(solution)/shard_map/ppermute | solution.py:586
  103.5 3.8 collective-permute-done.14
  109.8 22.9 %attend.3.a_ref.r1 = bf16[256,1024]{1,0:T(8,128)(2,1)S(1)} custom-call(bf16[256,1024]{1,0:T(8,128)(2,1)S(1)} %fusion.12.q_ref, bf16[2048,1024]{1,0:T(8,128)(2,1)S(1)} %constant_dynamic-update-slice_fusion.n_ref, bf16[1024,3072]{1,0:T(8,128)(2,1)S(1)} %bitcast.332, bf16[1024,3072]{1,0:T(8,128)(2,1)S(1)} %bitcast.332, f32[1,1024]{1,0:T(1,128)S(1)} %bitcast.342), custom_call_target="tpu_custom_call" | custom-call | flops 27599998976 | bytes 1000 | tf_op jit(solution)/shard_map/attend/pallas_call | solution.py:64
  132.8 12.6 %block_forward.3 = (f32[256,1024]{1,0:T(8,128)S(1)}, f32[256,1]{1,0:T(8,128)S(1)}, bf16[256,1024]{1,0:T(8,128)(2,1)S(1)}, f32[256,4096]{1,0:T(8,128)S(1)}, bf16[...) custom-call(f32[256,1024]{1,0:T(8,128)S(1)} %copy-done.47, bf16[256,1024]{1,0:T(8,128)(2,1)S(1)} %attend.3.a_ref.r1, ...), custom_call_target="tpu_custom_call" | custom-call | flops 13799999488 | bytes 1000 | tf_op jit(solution)/shard_map/block_forward/pallas_call | solution.py:233
  151.1 16.5 %block_backward.2 = (bf16[256,4096]{1,0:T(8,128)(2,1)}, f32[1,4096]{1,0:T(1,128)S(1)}, f32[256,1024]{1,0:T(8,128)S(1)}, bf16[256,1024]{1,0:T(8,128)(2,1)S(1)}, b...) custom-call(s32[1]{0:T(128)} %bitcast.17.c_ref, f32[256,1024]{1,0:T(8,128)S(1)} %pad_maximum_fusion.grad_ref, ...), custom_call_target="tpu_custom_call" | custom-call | flops 16099999744 | bytes 1000 | tf_op jit(solution)/shard_map/block_backward/pallas_call | solution.py:331
  168.6 4.4 all-to-all-start
  172.9 4.7 add_convert_fusion.1
  182.2 33.0 %attend_back.3.d_ref = bf16[8,3,256,128]{3,2,1,0:T(8,128)(2,1)} custom-call(bf16[2048,128]{1,0:T(8,128)(2,1)} %get-tuple-element.269.q_ref, bf16[2048,128]{1,0:T(8,128)(2,1)} %get-tuple-element.268.k_ref, bf16[2048,128]{1,0:T(8,128)(2,1)} %get-tuple-element.267.v_ref, bf16[2048,128]{1,0:T(8,128)(2,1)} %bitcast.18.do_ref), custom_call_target="tpu_custom_call" | custom-call | flops 37950001152 | bytes 1000 | tf_op jit(solution)/shard_map/attend_back/pallas_call | solution.py:132
  215.2 4.7 all-to-all-start.1
  219.9 4.7 add_convert_fusion.2
  231.0 9.4 %all-to-all-done.1.b_ref = bf16[8,3,256,128]{3,2,1,0:T(8,128)(2,1)} async-done(((bf16[8,3,256,128]{3,2,1,0:T(8,128)(2,1)}), bf16[8,3,256,128]{3,2,1,0:T(8,128)(2,1)}, u32[]{:S(2)}, u32[]{:S(2)}) %all-to-all-start.1) | async-done | bytes 1572896 | tf_op jit(solution)/shard_map/all_to_all | solution.py:789
  240.4 9.1 %qkv_backward.2 = (f32[256,1024]{1,0:T(8,128)}, bf16[256,1024]{1,0:T(8,128)(2,1)}, f32[8,1024]{1,0:T(8,128)}, f32[8,1024]{1,0:T(8,128)}) custom-call(bf16[8,3,256,128]{3,2,1,0:T(8,128)(2,1)} %all-to-all-done.1.b_ref, bf16[1024,3072]{1,0:T(8,128)(2,1)} %wv_ref.7, bf16[1024,3072]{1,0:T(8,128)(2,1)} %wv_ref.7, bf16[1024,3072]{1,0:T(8,128)(2,1)} %wv_ref.7, ...), custom_call_target="tpu_custom_call" | custom-call | flops 13799999488 | bytes 1000 | tf_op jit(solution)/shard_map/qkv_backward/pallas_call | solution.py:422
  252.0 21.7 %block_backward.3 = (bf16[256,4096]{1,0:T(8,128)(2,1)}, f32[1,4096]{1,0:T(1,128)S(1)}, f32[256,1024]{1,0:T(8,128)S(1)}, bf16[256,1024]{1,0:T(8,128)(2,1)S(1)}, b...) custom-call(s32[1]{0:T(128)} %bitcast.17.c_ref, ...), custom_call_target="tpu_custom_call" | custom-call | flops 20700000256 | bytes 1000 | tf_op jit(solution)/shard_map/block_backward/pallas_call | solution.py:331
  281.3 4.6 grad_rows.2
  287.6 4.6 all-to-all-start.2
  301.1 4.6 grad_rows.3
  316.2 18.5 %attend_back.4.rest_0_ = bf16[8,3,256,128]{3,2,1,0:T(8,128)(2,1)} custom-call(bf16[2048,128]{1,0:T(8,128)(2,1)} %get-tuple-element.272.q_ref, bf16[2048,128]{1,0:T(8,128)(2,1)} %get-tuple-element.271.k_ref, bf16[2048,128]{1,0:T(8,128)(2,1)} %get-tuple-element.270.v_ref, bf16[2048,128]{1,0:T(8,128)(2,1)} %bitcast.22.do_ref), custom_call_target="tpu_custom_call" | custom-call | flops 19549999104 | bytes 1000 | tf_op jit(solution)/shard_map/attend_back/pallas_call | solution.py:132
  334.7 5.6 %collective-permute-done.25 = bf16[2,2,2,32,2048]{4,3,2,1,0:T(8,128)(2,1)} collective-permute-done((bf16[2,2,2,32,2048]{4,3,2,1,0:T(8,128)(2,1)}, bf16[2,2,2,32,2048]{4,3,2,1,0:T(8,128)(2,1)}, u32[]{:S(2)}, u32[]{:S(2)}) %collective-permute-start.25) | collective-permute-done | bytes 1048608 | tf_op jit(solution)/shard_map/ppermute | solution.py:586
  350.3 19.1 %attend_back.5.d_ref = bf16[8,3,256,128]{3,2,1,0:T(8,128)(2,1)} custom-call(bf16[2048,128]{1,0:T(8,128)(2,1)} %get-tuple-element.272.q_ref, bf16[2048,128]{1,0:T(8,128)(2,1)} %get-tuple-element.271.k_ref, bf16[2048,128]{1,0:T(8,128)(2,1)} %get-tuple-element.270.v_ref, bf16[2048,128]{1,0:T(8,128)(2,1)} %bitcast.22.do_ref, ...), custom_call_target="tpu_custom_call" | custom-call | flops 19549999104 | bytes 1000 | tf_op jit(solution)/shard_map/attend_back/pallas_call | solution.py:132
  382.2 4.5 all-to-all-start.3
  407.7 10.7 %all-to-all-done.3.b_ref = bf16[8,3,256,128]{3,2,1,0:T(8,128)(2,1)} async-done(((bf16[8,3,256,128]{3,2,1,0:T(8,128)(2,1)}), bf16[8,3,256,128]{3,2,1,0:T(8,128)(2,1)}, u32[]{:S(2)}, u32[]{:S(2)}) %all-to-all-start.3) | async-done | bytes 1572896 | tf_op jit(solution)/shard_map/all_to_all | solution.py:789
  432.2 6.1 %all-to-all-start.4 = ((bf16[16,64,512]{2,1,0:T(8,128)(2,1)}), bf16[16,64,512]{2,1,0:T(8,128)(2,1)}, u32[]{:S(2)}, u32[]{:S(2)}) async-start(bf16[16,64,512]{2,1,0:T(8,128)(2,1)} %copy-done.12), calls=%async_computation.4 | async-start | bytes 2097152 | tf_op jit(solution)/shard_map/all_to_all | solution.py:807
  441.3 8.9 %qkv_backward.3 = (f32[256,1024]{1,0:T(8,128)}, bf16[128,1024]{1,0:T(8,128)(2,1)}, f32[8,1024]{1,0:T(8,128)}, f32[8,1024]{1,0:T(8,128)}) custom-call(bf16[8,3,256,128]{3,2,1,0:T(8,128)(2,1)} %all-to-all-done.3.b_ref, bf16[1024,3072]{1,0:T(8,128)(2,1)} %wv_ref.7, bf16[1024,3072]{1,0:T(8,128)(2,1)} %wv_ref.7, bf16[1024,3072]{1,0:T(8,128)(2,1)} %wv_ref.7, ...), custom_call_target="tpu_custom_call" | custom-call | flops 13799999488 | bytes 1000 | tf_op jit(solution)/shard_map/qkv_backward/pallas_call | solution.py:422
  451.9 15.0 %collective-permute-done.36 = bf16[2,96,1024]{2,1,0:T(8,128)(2,1)S(1)} collective-permute-done((bf16[2,96,1024]{2,1,0:T(8,128)(2,1)}, bf16[2,96,1024]{2,1,0:T(8,128)(2,1)S(1)}, u32[]{:S(2)}, u32[]{:S(2)}) %collective-permute-start.36) | collective-permute-done | bytes 393248 | tf_op jit(solution)/shard_map/ppermute | solution.py:586
  478.0 6.0 %all-to-all-start.5 = ((f32[16,1,1088]{2,1,0:T(1,128)}), f32[16,1,1088]{2,1,0:T(1,128)S(1)}, u32[]{:S(2)}, u32[]{:S(2)}) async-start(f32[16,1,1088]{2,1,0:T(1,128)} %copy.154), calls=%async_computation.5 | async-start | bytes 147456 | tf_op jit(solution)/shard_map/all_to_all | solution.py:833
  484.0 7.0 %all-to-all-done.5 = f32[16,1,1088]{2,1,0:T(1,128)S(1)} async-done(((f32[16,1,1088]{2,1,0:T(1,128)}), f32[16,1,1088]{2,1,0:T(1,128)S(1)}, u32[]{:S(2)}, u32[]{:S(2)}) %all-to-all-start.5) | async-done | bytes 69664 | tf_op jit(solution)/shard_map/all_to_all | solution.py:833
  (357 shorter events, 187.4 us)
Async XLA Ops:
  1.8 16.0 %collective-permute-start = (bf16[128,1024]{1,0:T(8,128)(2,1)S(1)}, bf16[128,1024]{1,0:T(8,128)(2,1)S(1)}, u32[]{:S(2)}, u32[]{:S(2)}) collective-permute-start(bf16[128,1024]{1,0:T(8,128)(2,1)S(1)} %get-tuple-element.284), channel_id=1, source_target_pairs={{0,8},{8,0},{1,9},{9,1},{2,10},{10,2},{3,11},{11,3},{4,12},{12,4},... | collective-permute-start | bytes 786440 | tf_op jit(solution)/shard_map/ppermute | solution.py:586
  19.9 13.7 %collective-permute-start.1 = (bf16[256,1024]{1,0:T(8,128)(2,1)S(1)}, bf16[256,1024]{1,0:T(8,128)(2,1)S(1)}, u32[]{:S(2)}, u32[]{:S(2)}) collective-permute-start(bf16[256,1024]{1,0:T(8,128)(2,1)S(1)} %get-tuple-element.263), channel_id=1, source_target_pairs={{0,2},{2,0},{1,3},{3,1},{4,6},{6,4},{5,7},{7,5},{8,10},{10,8},{9,1... | collective-permute-start | bytes 1572872 | tf_op jit(solution)/shard_map/ppermute | solution.py:586
  22.2 18.7 %collective-permute-start.5 = (bf16[256,1024]{1,0:T(8,128)(2,1)S(1)}, bf16[256,1024]{1,0:T(8,128)(2,1)S(1)}, u32[]{:S(2)}, u32[]{:S(2)}) collective-permute-start(bf16[256,1024]{1,0:T(8,128)(2,1)S(1)} %get-tuple-element.263), channel_id=1, source_target_pairs={{0,1},{1,0},{2,3},{3,2},{4,5},{5,4},{6,7},{7,6},{8,9},{9,8},{10,11... | collective-permute-start | bytes 1572872 | tf_op jit(solution)/shard_map/ppermute | solution.py:586
  42.5 27.2 %collective-permute-start.10 = (f32[128,1024]{1,0:T(8,128)S(1)}, f32[128,1024]{1,0:T(8,128)S(1)}, u32[]{:S(2)}, u32[]{:S(2)}) collective-permute-start(f32[128,1024]{1,0:T(8,128)S(1)} %get-tuple-element.274), channel_id=1, source_target_pairs={{0,8},{8,0},{1,9},{9,1},{2,10},{10,2},{3,11},{11,3},{4,12},{12,4},... | collective-permute-start | bytes 1572872 | tf_op jit(solution)/shard_map/ppermute | solution.py:586
  86.4 13.6 %collective-permute-start.12 = (bf16[256,1024]{1,0:T(8,128)(2,1)S(1)}, bf16[256,1024]{1,0:T(8,128)(2,1)S(1)}, u32[]{:S(2)}, u32[]{:S(2)}) collective-permute-start(bf16[256,1024]{1,0:T(8,128)(2,1)S(1)} %get-tuple-element.118), channel_id=1, source_target_pairs={{0,4},{4,0},{1,5},{5,1},{2,6},{6,2},{3,7},{7,3},{8,12},{12,8},{9,1... | collective-permute-start | bytes 1572872 | tf_op jit(solution)/shard_map/ppermute | solution.py:586
  91.1 17.1 %collective-permute-start.15 = (bf16[256,1024]{1,0:T(8,128)(2,1)S(1)}, bf16[256,1024]{1,0:T(8,128)(2,1)S(1)}, u32[]{:S(2)}, u32[]{:S(2)}) collective-permute-start(bf16[256,1024]{1,0:T(8,128)(2,1)S(1)} %get-tuple-element.118), channel_id=1, source_target_pairs={{0,1},{1,0},{2,3},{3,2},{4,5},{5,4},{6,7},{7,6},{8,9},{9,8},{10,11... | collective-permute-start | bytes 1572872 | tf_op jit(solution)/shard_map/ppermute | solution.py:586
  148.2 30.7 %collective-permute-start.20 = (bf16[128,1024]{1,0:T(8,128)(2,1)}, bf16[128,1024]{1,0:T(8,128)(2,1)}, u32[]{:S(2)}, u32[]{:S(2)}) collective-permute-start(bf16[128,1024]{1,0:T(8,128)(2,1)} %get-tuple-element.282), channel_id=1, source_target_pairs={{0,8},{8,0},{1,9},{9,1},{2,10},{10,2},{3,11},{11,3},{4,12},{12,4},... | collective-permute-start | bytes 786440 | tf_op jit(solution)/shard_map/ppermute | solution.py:586
  215.2 25.2 %all-to-all-start.1 = ((bf16[8,3,256,128]{3,2,1,0:T(8,128)(2,1)}), bf16[8,3,256,128]{3,2,1,0:T(8,128)(2,1)}, u32[]{:S(2)}, u32[]{:S(2)}) async-start(bf16[8,3,256,128]{3,2,1,0:T(8,128)(2,1)} %attend_back.3.d_ref), calls=%async_computation.1 | async-start | bytes 3145728 | tf_op jit(solution)/shard_map/all_to_all | solution.py:789
  280.7 26.3 %collective-permute-start.21 = (bf16[8,192,1024]{2,1,0:T(8,128)(2,1)}, bf16[8,192,1024]{2,1,0:T(8,128)(2,1)}, u32[]{:S(2)}, u32[]{:S(2)}) collective-permute-start(bf16[8,192,1024]{2,1,0:T(8,128)(2,1)} %get-tuple-element.144), channel_id=1, source_target_pairs={{0,1},{1,0},{2,3},{3,2},{4,5},{5,4},{6,7},{7,6},{8,9},{9,8},{10,11... | collective-permute-start | bytes 9437192 | tf_op jit(solution)/shard_map/ppermute | solution.py:586
  287.3 24.5 %collective-permute-start.23 = (bf16[8,64,2048]{2,1,0:T(8,128)(2,1)}, bf16[8,64,2048]{2,1,0:T(8,128)(2,1)}, u32[]{:S(2)}, u32[]{:S(2)}) collective-permute-start(bf16[8,64,2048]{2,1,0:T(8,128)(2,1)} %get-tuple-element.152), channel_id=1, source_target_pairs={{0,1},{1,0},{2,3},{3,2},{4,5},{5,4},{6,7},{7,6},{8,9},{9,8},{10,11... | collective-permute-start | bytes 6291464 | tf_op jit(solution)/shard_map/ppermute | solution.py:586
  287.6 24.2 %all-to-all-start.2 = ((bf16[8,256,128]{2,1,0:T(8,128)(2,1)}), bf16[8,256,128]{2,1,0:T(8,128)(2,1)}, u32[]{:S(2)}, u32[]{:S(2)}) async-start(bf16[8,256,128]{2,1,0:T(8,128)(2,1)} %get-tuple-element.137), calls=%async_computation.2 | async-start | bytes 1048576 | tf_op jit(solution)/shard_map/all_to_all | solution.py:745
  294.9 39.9 %collective-permute-start.24 = (bf16[2,2,2,64,1024]{4,3,2,1,0:T(8,128)(2,1)}, bf16[2,2,2,64,1024]{4,3,2,1,0:T(8,128)(2,1)}, u32[]{:S(2)}, u32[]{:S(2)}) collective-permute-start(bf16[2,2,2,64,1024]{4,3,2,1,0:T(8,128)(2,1)} %fusion.18), channel_id=1, source_target_pairs={{0,4},{4,0},{1,5},{5,1},{2,6},{6,2},{3,7},{7,3},{8,12},{12,8},{9,1... | collective-permute-start | bytes 3145736 | tf_op jit(solution)/shard_map/ppermute | solution.py:586
  307.0 33.3 %collective-permute-start.26 = (bf16[8,64,2048]{2,1,0:T(8,128)(2,1)}, bf16[8,64,2048]{2,1,0:T(8,128)(2,1)}, u32[]{:S(2)}, u32[]{:S(2)}) collective-permute-start(bf16[8,64,2048]{2,1,0:T(8,128)(2,1)} %get-tuple-element.156), channel_id=1, source_target_pairs={{0,1},{1,0},{2,3},{3,2},{4,5},{5,4},{6,7},{7,6},{8,9},{9,8},{10,11... | collective-permute-start | bytes 6291464 | tf_op jit(solution)/shard_map/ppermute | solution.py:586
  310.3 59.1 %collective-permute-start.28 = (bf16[2,2,2,96,1024]{4,3,2,1,0:T(8,128)(2,1)}, bf16[2,2,2,96,1024]{4,3,2,1,0:T(8,128)(2,1)}, u32[]{:S(2)}, u32[]{:S(2)}) collective-permute-start(bf16[2,2,2,96,1024]{4,3,2,1,0:T(8,128)(2,1)} %fusion.4), channel_id=1, source_target_pairs={{0,2},{2,0},{1,3},{3,1},{4,6},{6,4},{5,7},{7,5},{8,10},{10,8},{9,1... | collective-permute-start | bytes 4718600 | tf_op jit(solution)/shard_map/ppermute | solution.py:586
  314.7 25.6 %collective-permute-start.25 = (bf16[2,2,2,32,2048]{4,3,2,1,0:T(8,128)(2,1)}, bf16[2,2,2,32,2048]{4,3,2,1,0:T(8,128)(2,1)}, u32[]{:S(2)}, u32[]{:S(2)}) collective-permute-start(bf16[2,2,2,32,2048]{4,3,2,1,0:T(8,128)(2,1)} %fusion.19), channel_id=1, source_target_pairs={{0,16},{16,0},{1,17},{17,1},{2,18},{18,2},{3,19},{19,3},{4,20},{20... | collective-permute-start | bytes 3145736 | tf_op jit(solution)/shard_map/ppermute | solution.py:586
  342.7 26.7 %collective-permute-start.29 = (bf16[2,2,32,2048]{3,2,1,0:T(8,128)(2,1)}, bf16[2,2,32,2048]{3,2,1,0:T(8,128)(2,1)}, u32[]{:S(2)}, u32[]{:S(2)}) collective-permute-start(bf16[2,2,32,2048]{3,2,1,0:T(8,128)(2,1)} %fusion.22), channel_id=1, source_target_pairs={{0,4},{4,0},{1,5},{5,1},{2,6},{6,2},{3,7},{7,3},{8,12},{12,8},{9,1... | collective-permute-start | bytes 1572872 | tf_op jit(solution)/shard_map/ppermute | solution.py:586
  346.0 25.3 %collective-permute-start.27 = (bf16[2,2,64,1024]{3,2,1,0:T(8,128)(2,1)}, bf16[2,2,64,1024]{3,2,1,0:T(8,128)(2,1)S(1)}, u32[]{:S(2)}, u32[]{:S(2)}) collective-permute-start(bf16[2,2,64,1024]{3,2,1,0:T(8,128)(2,1)} %fusion.23), channel_id=1, source_target_pairs={{0,8},{8,0},{1,9},{9,1},{2,10},{10,2},{3,11},{11,3},{4,12},{12,4},... | collective-permute-start | bytes 1572872 | tf_op jit(solution)/shard_map/ppermute | solution.py:586
  348.8 24.3 %collective-permute-start.30 = (bf16[2,2,2,32,2048]{4,3,2,1,0:T(8,128)(2,1)}, bf16[2,2,2,32,2048]{4,3,2,1,0:T(8,128)(2,1)}, u32[]{:S(2)}, u32[]{:S(2)}) collective-permute-start(bf16[2,2,2,32,2048]{4,3,2,1,0:T(8,128)(2,1)} %fusion.20), channel_id=1, source_target_pairs={{0,16},{16,0},{1,17},{17,1},{2,18},{18,2},{3,19},{19,3},{4,20},{20... | collective-permute-start | bytes 3145736 | tf_op jit(solution)/shard_map/ppermute | solution.py:586
  382.2 36.2 %all-to-all-start.3 = ((bf16[8,3,256,128]{3,2,1,0:T(8,128)(2,1)}), bf16[8,3,256,128]{3,2,1,0:T(8,128)(2,1)}, u32[]{:S(2)}, u32[]{:S(2)}) async-start(bf16[8,3,256,128]{3,2,1,0:T(8,128)(2,1)} %attend_back.5.d_ref), calls=%async_computation.3 | async-start | bytes 3145728 | tf_op jit(solution)/shard_map/all_to_all | solution.py:789
  389.9 28.6 %collective-permute-start.33 = (bf16[2,2,96,1024]{3,2,1,0:T(8,128)(2,1)}, bf16[2,2,96,1024]{3,2,1,0:T(8,128)(2,1)}, u32[]{:S(2)}, u32[]{:S(2)}) collective-permute-start(bf16[2,2,96,1024]{3,2,1,0:T(8,128)(2,1)} %fusion.5), channel_id=1, source_target_pairs={{0,16},{16,0},{1,17},{17,1},{2,18},{18,2},{3,19},{19,3},{4,20},{20... | collective-permute-start | bytes 2359304 | tf_op jit(solution)/shard_map/ppermute | solution.py:586
  392.0 26.4 %collective-permute-start.34 = (bf16[2,32,2048]{2,1,0:T(8,128)(2,1)}, bf16[2,32,2048]{2,1,0:T(8,128)(2,1)}, u32[]{:S(2)}, u32[]{:S(2)}) collective-permute-start(bf16[2,32,2048]{2,1,0:T(8,128)(2,1)} %fusion.27), channel_id=1, source_target_pairs={{0,2},{2,0},{1,3},{3,1},{4,6},{6,4},{5,7},{7,5},{8,10},{10,8},{9,1... | collective-permute-start | bytes 786440 | tf_op jit(solution)/shard_map/ppermute | solution.py:586
  393.9 24.5 %collective-permute-start.32 = (bf16[2,64,1024]{2,1,0:T(8,128)(2,1)}, bf16[2,64,1024]{2,1,0:T(8,128)(2,1)}, u32[]{:S(2)}, u32[]{:S(2)}) collective-permute-start(bf16[2,64,1024]{2,1,0:T(8,128)(2,1)} %fusion.28), channel_id=1, source_target_pairs={{0,16},{16,0},{1,17},{17,1},{2,18},{18,2},{3,19},{19,3},{4,20},{20... | collective-permute-start | bytes 786440 | tf_op jit(solution)/shard_map/ppermute | solution.py:586
  394.4 24.0 %collective-permute-start.35 = (bf16[2,2,32,2048]{3,2,1,0:T(8,128)(2,1)}, bf16[2,2,32,2048]{3,2,1,0:T(8,128)(2,1)}, u32[]{:S(2)}, u32[]{:S(2)}) collective-permute-start(bf16[2,2,32,2048]{3,2,1,0:T(8,128)(2,1)} %fusion.21), channel_id=1, source_target_pairs={{0,8},{8,0},{1,9},{9,1},{2,10},{10,2},{3,11},{11,3},{4,12},{12,4},... | collective-permute-start | bytes 1572872 | tf_op jit(solution)/shard_map/ppermute | solution.py:586
  406.2 23.3 %collective-permute-start.31 = (bf16[6,64,512]{2,1,0:T(8,128)(2,1)}, bf16[6,64,512]{2,1,0:T(8,128)(2,1)}, u32[]{:S(2)}, u32[]{:S(2)}) collective-permute-start(bf16[6,64,512]{2,1,0:T(8,128)(2,1)} %get-tuple-element.276), channel_id=1, source_target_pairs={{0,16},{16,0},{1,17},{17,1},{2,18},{18,2},{3,19},{19,3},{4,20},{20... | collective-permute-start | bytes 1179656 | tf_op jit(solution)/shard_map/ppermute | solution.py:586
  422.3 69.4 %collective-permute-start.39 = (bf16[64,1024]{1,0:T(8,128)(2,1)}, bf16[64,1024]{1,0:T(8,128)(2,1)}, u32[]{:S(2)}, u32[]{:S(2)}) collective-permute-start(bf16[64,1024]{1,0:T(8,128)(2,1)} %fusion.40), channel_id=1, source_target_pairs={{0,2},{2,0},{1,3},{3,1},{4,6},{6,4},{5,7},{7,5},{8,10},{10,8},{9,1... | collective-permute-start | bytes 393224 | tf_op jit(solution)/shard_map/ppermute | solution.py:586
  422.3 69.4 %collective-permute-start.41 = (bf16[32,2048]{1,0:T(8,128)(2,1)}, bf16[32,2048]{1,0:T(8,128)(2,1)}, u32[]{:S(2)}, u32[]{:S(2)}) collective-permute-start(bf16[32,2048]{1,0:T(8,128)(2,1)} %fusion.41), channel_id=1, source_target_pairs={{0,8},{8,0},{1,9},{9,1},{2,10},{10,2},{3,11},{11,3},{4,12},{12,4},... | collective-permute-start | bytes 393224 | tf_op jit(solution)/shard_map/ppermute | solution.py:586
  426.9 47.9 %collective-permute-start.37 = (bf16[2,32,2048]{2,1,0:T(8,128)(2,1)}, bf16[2,32,2048]{2,1,0:T(8,128)(2,1)}, u32[]{:S(2)}, u32[]{:S(2)}) collective-permute-start(bf16[2,32,2048]{2,1,0:T(8,128)(2,1)} %fusion.26), channel_id=1, source_target_pairs={{0,2},{2,0},{1,3},{3,1},{4,6},{6,4},{5,7},{7,5},{8,10},{10,8},{9,1... | collective-permute-start | bytes 786440 | tf_op jit(solution)/shard_map/ppermute | solution.py:586
  432.2 42.6 %all-to-all-start.4 = ((bf16[16,64,512]{2,1,0:T(8,128)(2,1)}), bf16[16,64,512]{2,1,0:T(8,128)(2,1)}, u32[]{:S(2)}, u32[]{:S(2)}) async-start(bf16[16,64,512]{2,1,0:T(8,128)(2,1)} %copy-done.12), calls=%async_computation.4 | async-start | bytes 2097152 | tf_op jit(solution)/shard_map/all_to_all | solution.py:807
  438.3 28.6 %collective-permute-start.36 = (bf16[2,96,1024]{2,1,0:T(8,128)(2,1)}, bf16[2,96,1024]{2,1,0:T(8,128)(2,1)S(1)}, u32[]{:S(2)}, u32[]{:S(2)}) collective-permute-start(bf16[2,96,1024]{2,1,0:T(8,128)(2,1)} %fusion.24), channel_id=1, source_target_pairs={{0,4},{4,0},{1,5},{5,1},{2,6},{6,2},{3,7},{7,3},{8,12},{12,8},{9,1... | collective-permute-start | bytes 1179656 | tf_op jit(solution)/shard_map/ppermute | solution.py:586
  450.3 41.4 %collective-permute-start.38 = (bf16[128,1024]{1,0:T(8,128)(2,1)}, bf16[128,1024]{1,0:T(8,128)(2,1)S(1)}, u32[]{:S(2)}, u32[]{:S(2)}) collective-permute-start(bf16[128,1024]{1,0:T(8,128)(2,1)} %get-tuple-element.195), channel_id=1, source_target_pairs={{0,8},{8,0},{1,9},{9,1},{2,10},{10,2},{3,11},{11,3},{4,12},{12,4},... | collective-permute-start | bytes 786440 | tf_op jit(solution)/shard_map/ppermute | solution.py:586
  469.6 22.1 %collective-permute-start.40 = (bf16[96,1024]{1,0:T(8,128)(2,1)}, bf16[96,1024]{1,0:T(8,128)(2,1)}, u32[]{:S(2)}, u32[]{:S(2)}) collective-permute-start(bf16[96,1024]{1,0:T(8,128)(2,1)} %fusion.31), channel_id=1, source_target_pairs={{0,8},{8,0},{1,9},{9,1},{2,10},{10,2},{3,11},{11,3},{4,12},{12,4},... | collective-permute-start | bytes 589832 | tf_op jit(solution)/shard_map/ppermute | solution.py:586
  476.7 15.0 %collective-permute-start.42 = (bf16[32,2048]{1,0:T(8,128)(2,1)}, bf16[32,2048]{1,0:T(8,128)(2,1)}, u32[]{:S(2)}, u32[]{:S(2)}) collective-permute-start(bf16[32,2048]{1,0:T(8,128)(2,1)} %fusion.39), channel_id=1, source_target_pairs={{0,4},{4,0},{1,5},{5,1},{2,6},{6,2},{3,7},{7,3},{8,12},{12,8},{9,1... | collective-permute-start | bytes 393224 | tf_op jit(solution)/shard_map/ppermute | solution.py:586
  (96 other events, 904.3 us)

commit v4 on v3

--- a/solution.py
+++ b/solution.py
@@ -90,21 +90,23 @@
         dv_sum[...] = jnp.zeros_like(dv_sum)
 
     q, k, v, do = q_ref[...], k_ref[...], v_ref[...], do_ref[...]
-    dq = None
-    for h in some:
-        qh, doh = head_part(q, h, heads), head_part(do, h, heads)
-        s = contract(qh, k, 1, 1)
-        dp = contract(doh, v, 1, 1)
+    queries = [head_part(q, h, heads) for h in some]
+    grads = [head_part(do, h, heads) for h in some]
+    scores = [contract(x, k, 1, 1) for x in queries]
+    prob_grads = [contract(x, v, 1, 1) for x in grads]
+    dq = dk = dv = 0.0
+    for h, qh, doh, s, dp in zip(some, queries, grads, scores, prob_grads):
         top = jnp.max(s, axis=-1, keepdims=True)
         e = jnp.exp2((s - top) * EXP_SCALE)
         inverse = 1.0 / jnp.sum(e, axis=-1, keepdims=True)
         inner = jnp.sum(e * dp, axis=-1, keepdims=True) * inverse
         p = e * inverse
         ds = (p * (dp - inner)).astype(bf16)
-        part = head_part(contract(ds, k, 1, 0), h, heads)
-        dq = part if dq is None else dq + part
-        dk_sum[...] += contract(ds, qh, 0, 0)
-        dv_sum[...] += contract(p.astype(bf16), doh, 0, 0)
+        dq = dq + head_part(contract(ds, k, 1, 0), h, heads)
+        dk = dk + contract(ds, qh, 0, 0)
+        dv = dv + contract(p.astype(bf16), doh, 0, 0)
+    dk_sum[...] += dk
+    dv_sum[...] += dv
 
     def put(m, i, x):
         if len(rest) == 4:
@@ -172,7 +174,7 @@
             scratch_shapes=[pltpu.VMEM((m, block), f32)],
         ),
         out_shape=[jax.ShapeDtypeStruct((bands // 2, m // bands, n), bf16)] * 2,
-        compiler_params=pltpu.CompilerParams(vmem_limit_bytes=16 * MIB),
+        compiler_params=pltpu.CompilerParams(vmem_limit_bytes=60 * MIB),
         cost_estimate=cost(8),
         name="grad_rows",
     )(core.reshape(1), *left, *right)
@@ -342,7 +344,7 @@
             scratch_shapes=scratch,
         ),
         out_shape=shapes,
-        compiler_params=pltpu.CompilerParams(vmem_limit_bytes=48 * MIB),
+        compiler_params=pltpu.CompilerParams(vmem_limit_bytes=(60 if grads else 48) * MIB),
         cost_estimate=cost(18 if grads else 14),
         name="block_backward",
     )(core.reshape(1), grad, hidden, w_down, w_up, w_out, n2, r2, gain.reshape(1, d), *grads)
@@ -376,7 +378,7 @@
         ),
         out_shape=[jax.ShapeDtypeStruct(own.shape, bf16)] * 2,
         input_output_aliases={5: 0, 6: 1},
-        compiler_params=pltpu.CompilerParams(vmem_limit_bytes=16 * MIB),
+        compiler_params=pltpu.CompilerParams(vmem_limit_bytes=60 * MIB),
         cost_estimate=cost(3),
         name="grad_out",
     )(core.reshape(1), *left, *right, other, own)
@@ -465,7 +467,7 @@
         + [out] * len(extra),
         out_specs=out,
         out_shape=jax.ShapeDtypeStruct(shape, kind),
-        compiler_params=pltpu.CompilerParams(vmem_limit_bytes=16 * MIB),
+        compiler_params=pltpu.CompilerParams(vmem_limit_bytes=60 * MIB),
         cost_estimate=cost(5),
         name="grad_heads",
     )(d, normed_all, *extra)
@@ -491,7 +493,7 @@
             out_specs=spec((count,) + shape[1:], lambda i, t: (0, 0, 0)),
         ),
         out_shape=jax.ShapeDtypeStruct((count,) + shape[1:], bf16),
-        compiler_params=pltpu.CompilerParams(vmem_limit_bytes=8 * MIB),
+        compiler_params=pltpu.CompilerParams(vmem_limit_bytes=60 * MIB),
         cost_estimate=cost(3),
         name="take",
     )(table, *terms)
@@ -746,40 +748,34 @@
         if last:
             z_other, x_other, z_own, x_own = ups
             z_core = swap(z_other, "core")
+            left, right = (later[0], pin(down_grad, sent)), (later[1], activated)
+            d_other, d_own = grad_rows(core, left, right, bands, 0, 1)
+            d_core = swap(d_other, "core")
             x_other, x_own = grad_out(
-                core, (later[4], pin(branch_grad, sent)), (later[5], attended), bands, x_other, x_own
+                core, (later[4], pin(branch_grad, d_other)), (later[5], attended), bands, x_other, x_own
             )
             x_core = swap(x_other, "core")
-            left, right = (later[0], pin(down_grad, x_other)), (later[1], activated)
-            one_other, one_own = grad_rows(core, left, right, bands, 0, 2)
-            one_core = swap(one_other, "core")
             samp = ("samp",) * two
-            z_terms = pin((z_own, z_core), one_other)
+            z_terms = pin((z_own, z_core), x_other)
             z_share = Share([split_rows(t, two) for t in z_terms], names + samp)
-            left = (later[0], pin(down_grad, z_share.halve("zl")))
-            two_other, two_own = grad_rows(core, left, right, bands, 1, 2)
-            two_core = swap(two_other, "core")
-            x_terms = pin((x_own, x_core), two_other)
+            d_terms = pin((d_own, d_core), z_share.halve("zl"))
+            down_share = Share([split_rows(t, two) for t in d_terms], names + samp)
+            x_terms = pin((x_own, x_core), down_share.halve("samp"))
             x_share = Share([split_rows(t, two) for t in x_terms], names + samp)
-            own_grad, one_own = pin((own_grad, one_own), x_share.halve(x_axes[0]))
-            down_one = Share([split_rows(t, two) for t in (one_own, one_core)], names + samp)
-            own_grad = pin(own_grad, down_one.halve("samp"))
+            own_grad = pin(own_grad, x_share.halve(x_axes[0]))
             heads = W // HD
             d_heads = attend_back(*owns[0], own_grad, members, range((heads + 1) // 2))
-            waits = pin((own_grad, d_heads, z_share.terms[-1], down_one.terms[-1], two_own, two_core))
-            own_grad, d_heads, z_share.terms[-1], down_one.terms[-1], two_own, two_core = waits
-            down_two = Share([split_rows(t, two) for t in (two_own, two_core)], names + samp)
-            sent = [z_share.halve("zh"), down_one.halve("zl"), down_two.halve("samp")]
+            own_grad, d_heads, z_share.terms[-1] = pin((own_grad, d_heads, z_share.terms[-1]))
+            sent = z_share.halve("zh")
             if heads > 1:
-                own_grad, d_heads = pin((own_grad, d_heads), *sent)
+                own_grad, d_heads = pin((own_grad, d_heads), sent)
                 d_heads = attend_back(*owns[0], own_grad, members, range(heads // 2, heads), d_heads)
-            shares = (z_share, x_share, down_one, down_two)
+            shares = (z_share, x_share, down_share)
             waits = pin((d_heads, *(t.terms[-1] for t in shares)))
             d_heads = waits[0]
             for t, value in zip(shares, waits[1:]):
                 t.terms[-1] = value
-            sent = [x_share.halve("samp"), down_two.halve("zh"), z_share.halve("samp")]
-            sent += [down_one.halve(a) for a in x_axes]
+            sent = [x_share.halve("samp"), z_share.halve("samp")] + [down_share.halve(a) for a in x_axes]
             d_heads = pin(d_heads, *sent)
         else:
             own_grad, send_row, keep_rows = pin((own_grad, send_row, keep_rows), result)
@@ -797,15 +793,13 @@
             else:
                 there, units = units, [units]
             back = pin(back, there)
-            waits = pin(tuple(t.terms[-1] for t in shares), back)
-            for t, value in zip(shares, waits):
-                t.terms[-1] = value
-            sent = [x_share.halve(a) for a in x_axes[1:] + ("zl",)]
-            sent += [down_one.halve("zh")] + [t.halve(a) for t in (down_two, z_share) for a in x_axes]
+            x_share.terms[-1], z_share.terms[-1] = pin((x_share.terms[-1], z_share.terms[-1]), back)
+            sent = [x_share.halve(a) for a in x_axes[1:] + ("zl",)] + [z_share.halve(a) for a in x_axes]
             units[-1] = pin(units[-1], *sent)
             outgoing = take(units, send_row)
             incoming = lax.all_to_all(outgoing, low, 0, 0, tiled=True)
-            back = pin(back, outgoing)
+            down_share.terms[-1] = pin(down_share.terms[-1], outgoing)
+            back = pin(back, down_share.halve("zl"))
         else:
             owns[0] = own_part(0)
             back = pin(back, w_heads, *owns[0])
@@ -818,8 +812,10 @@
     fields_sent = low_grad
     fields_other = swap(fields_sent, "zh")
     x_share.terms[-1] = pin(x_share.terms[-1], fields_sent)
-    x_sent = x_share.halve("zh")
-    one, qv, two_sums, up_sum = pin(small, x_sent)
+    incoming = pin(incoming, x_share.halve("zh"))
+    there = take([incoming], keep_rows[1])
+    other = swap(there, "zh")
+    one, qv, two_sums, up_sum = pin(small, there)
     samples = 2 * samp_count
     slot = 2 * y + zh
     mine = lax.broadcasted_iota(jnp.int32, (samples, 1), 0) == slot
@@ -829,7 +825,7 @@
     vectors = jnp.concatenate([one[:2], qv, two_sums, leads])
     vectors = vectors.reshape(-1, bands, D // bands).transpose(1, 0, 2).reshape(bands, -1)
     vectors = jnp.concatenate([vectors, up_sum.reshape(bands, -1), bucket], axis=1)
-    incoming, vectors = pin((incoming, vectors), fields_sent)
+    sums = vectors
     vectors = lax.all_to_all(vectors, band, 0, 0, tiled=True)
 
     def both(x):
@@ -849,17 +845,15 @@
         x = jnp.concatenate([first, second]).astype(f32)
         return x[:n], x[n:]
 
-    incoming, down_two.terms[-1] = pin((incoming, down_two.terms[-1]), x_sent)
-    sent = down_two.halve("zl")
-    waits = pin((incoming, fields_other, vectors, *(t.terms[-1] for t in shares)), sent)
-    incoming, fields_other, vectors = waits[:3]
-    for t, value in zip(shares, waits[3:]):
-        t.terms[-1] = value
-    down = jnp.concatenate([total(down_one.terms), total(down_two.terms)], axis=1)
+    incoming, down_share.terms[-1], z_share.terms[-1] = pin((incoming, down_share.terms[-1], z_share.terms[-1]), sums)
+    sent = down_share.halve("zh")
+    own = take([incoming], keep_rows[0])
+    up_first = total(z_share.terms).astype(bf16)
+    late = (vectors, fields_other, other, down_share.terms[-1], x_share.terms[-1])
+    late = pin(late, sent, own, up_first)
+    vectors, fields_other, other, down_share.terms[-1], x_share.terms[-1] = late
     vectors = jnp.sum(vectors, axis=0)
     vectors = vectors + swap(vectors, "samp") if two else lax.psum(vectors, "samp")
-    other = swap(take([incoming], keep_rows[1]), "zh")
-    own = take([incoming], keep_rows[0])
     own = total([own, other]).astype(bf16).reshape(3 * D // bands, -1)
     if two:
         other = swap(own, "samp")
@@ -868,11 +862,11 @@
         own = lax.psum(own, "samp")
     w_qkv_grad = own.astype(f32).T
 
-    w_down_grad = both(down).T
+    w_down_grad = both(total(down_share.terms)).T
     n_up = w_up.shape[1] // bands
     bottom = both_cut(total(x_share.terms), n_up // 2)
     w_out_grad = bottom[1].T
-    w_up_grad = jnp.concatenate([both(total(z_share.terms)), bottom[0]]).T
+    w_up_grad = jnp.concatenate([both(up_first), bottom[0]]).T
     fields_grad = join(zh, grad, fields_other)
 
     w = D // bands

time: 527 us -> 498 us (0.945)
  local copies, waits for them, and re-layouts: 50.9 us -> 29.9 us
  Pallas kernels: 223 us -> 235 us
  starting transfers between devices: 80.7 us -> 70.2 us
  other arithmetic: 56.1 us -> 46.8 us
    unnamed x148 -> x96, local copies, waits for them, and re-layouts: 30.7 us -> 12.7 us
    all_to_all x2, waiting for transfers between devices: 20.1 us -> 12.8 us  [body(): back = lax.all_to_all(d_heads, low, 0, 0, tiled=True)]
    convert_element_type x16 -> x12, other arithmetic: 37.3 us -> 30.2 us  [halve(): sent = total(there).astype(bf16)]
    ppermute x49 -> x44, starting transfers between devices: 50.5 us -> 44.1 us  [swap(): return lax.ppermute(x, axis, SWAP)]
    all_to_all x1, waiting for transfers between devices: 7.01 us -> 13.2 us  [body(): vectors = lax.all_to_all(vectors, band, 0, 0, tiled=True)]
    pallas_call x2, Pallas kernels: 6.5 us -> 11.9 us  [grad_heads(): pl.pallas_call(grad_heads_kernel, grid=(4,), in_specs=[spec(d.shape, lamb...]
    ppermute x49 -> x44, waiting for transfers between devices: 63 us -> 65.4 us  [swap(): return lax.ppermute(x, axis, SWAP)]
    pallas_call x2 -> x1, Pallas kernels: 9.19 us -> 10.9 us  [grad_rows(): pl.pallas_call(grad_rows_kernel, grid_spec=pltpu.PrefetchScalarGridSpec(n...]
  transfers between devices with their start and end apart: 55 -> 50, of which waited for: 20 -> 21; matrix products, arithmetic and copies ran while one was open for 14% -> 13% of each run, Pallas kernels for 21% -> 23%
where the time goes in v4:
time: 498 us; the launch traced here: 492 us
  Pallas kernels  235 us (47%)
  waiting for transfers between devices  93.9 us (19%)
  starting transfers between devices  70.2 us (14%)
  other arithmetic  46.8 us (9%)
  local copies, waits for them, and re-layouts  29.9 us (6%)
  matrix products  11.4 us (2%)
    pallas_call x3, Pallas kernels, attend_back(): pl.pallas_call(functools.partial(attend_back_kernel, heads=heads, some=so...  69.5 us
    ppermute x44, waiting for transfers between devices, swap(): return lax.ppermute(x, axis, SWAP)  65.4 us
    pallas_call x2, Pallas kernels, attend(): pl.pallas_call(attend_kernel, grid=(width // block,), in_specs=[own, spec...  46.5 us
    ppermute x44, starting transfers between devices, swap(): return lax.ppermute(x, axis, SWAP)  44.1 us
    pallas_call x2, Pallas kernels, block_backward(): pl.pallas_call(functools.partial(block_backward_kernel, grads=bool(grads)...  39.4 us
    convert_element_type x12, other arithmetic, halve(): sent = total(there).astype(bf16)  30.2 us
    pallas_call x2, Pallas kernels, block_forward(): pl.pallas_call(functools.partial(block_forward_kernel, last=last), grid=(...  25.3 us
    pallas_call x2, Pallas kernels, qkv_backward(): pl.pallas_call(qkv_backward_kernel, grid=(members // at_once,), in_specs=...  17.9 us
  transfers between devices with their start and end apart: 50, of which 21 were waited for; matrix products, arithmetic and copies ran while one was open for 13% of the time, Pallas kernels for 23%

profile of v4, /device:TPU:0, one launch (start us, length us, event | category | flops | bytes accessed | tf_op | source)
XLA Modules:
  0.0 492.1 jit_solution(11979552442191367479)
XLA Ops:
  11.3 6.5 %collective-permute-done = bf16[128,1024]{1,0:T(8,128)(2,1)S(1)} collective-permute-done((bf16[128,1024]{1,0:T(8,128)(2,1)S(1)}, bf16[128,1024]{1,0:T(8,128)(2,1)S(1)}, u32[]{:S(2)}, u32[]{:S(2)}) %collective-permute-start) | collective-permute-done | bytes 262176 | tf_op jit(solution)/shard_map/ppermute | solution.py:588
  23.5 8.8 %collective-permute-done.2 = bf16[256,1024]{1,0:T(8,128)(2,1)S(1)} collective-permute-done((bf16[256,1024]{1,0:T(8,128)(2,1)S(1)}, bf16[256,1024]{1,0:T(8,128)(2,1)S(1)}, u32[]{:S(2)}, u32[]{:S(2)}) %collective-permute-start.2) | collective-permute-done | bytes 524320 | tf_op jit(solution)/shard_map/ppermute | solution.py:588
  46.3 23.4 %attend.2.a_ref.r0 = bf16[256,1024]{1,0:T(8,128)(2,1)S(1)} custom-call(bf16[256,1024]{1,0:T(8,128)(2,1)S(1)} %fusion.17.q_ref, bf16[2048,1024]{1,0:T(8,128)(2,1)S(1)} %constant_dynamic-update-slice_fusion.10.n_ref, bf16[1024,3072]{1,0:T(8,128)(2,1)S(1)} %copy-done.2, bf16[1024,3072]{1,0:T(8,128)(2,1)S(1)} %copy-done.2, f32[1,1024]{1,0:T(1,128)S(1)} %bitcast.257), custom_call_target="tpu_custom_call" | custom-call | flops 27599998976 | bytes 1000 | tf_op jit(solution)/shard_map/attend/pallas_call | solution.py:64
  70.0 12.8 %block_forward.2 = (f32[256,1024]{1,0:T(8,128)S(1)}, f32[256,1]{1,0:T(8,128)S(1)}, bf16[256,1024]{1,0:T(8,128)(2,1)S(1)}, f32[256,4096]{1,0:T(8,128)S(1)}, bf16[...) custom-call(f32[256,1024]{1,0:T(8,128)S(1)} %get-tuple-element.258.x, ...), custom_call_target="tpu_custom_call" | custom-call | flops 13799999488 | bytes 1000 | tf_op jit(solution)/shard_map/block_forward/pallas_call | solution.py:235
  90.8 9.4 %collective-permute-done.12 = bf16[256,1024]{1,0:T(8,128)(2,1)S(1)} collective-permute-done((bf16[256,1024]{1,0:T(8,128)(2,1)S(1)}, bf16[256,1024]{1,0:T(8,128)(2,1)S(1)}, u32[]{:S(2)}, u32[]{:S(2)}) %collective-permute-start.12) | collective-permute-done | bytes 524320 | tf_op jit(solution)/shard_map/ppermute | solution.py:588
  110.0 23.0 %attend.3.a_ref.r1 = bf16[256,1024]{1,0:T(8,128)(2,1)S(1)} custom-call(bf16[256,1024]{1,0:T(8,128)(2,1)S(1)} %fusion.14.q_ref, bf16[2048,1024]{1,0:T(8,128)(2,1)S(1)} %constant_dynamic-update-slice_fusion.n_ref, bf16[1024,3072]{1,0:T(8,128)(2,1)S(1)} %copy-done.2, bf16[1024,3072]{1,0:T(8,128)(2,1)S(1)} %copy-done.2, f32[1,1024]{1,0:T(1,128)S(1)} %bitcast.258), custom_call_target="tpu_custom_call" | custom-call | flops 27599998976 | bytes 1000 | tf_op jit(solution)/shard_map/attend/pallas_call | solution.py:64
  133.1 12.6 %block_forward.3 = (f32[256,1024]{1,0:T(8,128)S(1)}, f32[256,1]{1,0:T(8,128)S(1)}, bf16[256,1024]{1,0:T(8,128)(2,1)S(1)}, f32[256,4096]{1,0:T(8,128)S(1)}, bf16[...) custom-call(f32[256,1024]{1,0:T(8,128)S(1)} %copy-done.24, bf16[256,1024]{1,0:T(8,128)(2,1)S(1)} %attend.3.a_ref.r1, ...), custom_call_target="tpu_custom_call" | custom-call | flops 13799999488 | bytes 1000 | tf_op jit(solution)/shard_map/block_forward/pallas_call | solution.py:235
  151.5 16.5 %block_backward.2 = (bf16[256,4096]{1,0:T(8,128)(2,1)}, f32[1,4096]{1,0:T(1,128)S(1)}, f32[256,1024]{1,0:T(8,128)S(1)}, bf16[256,1024]{1,0:T(8,128)(2,1)S(1)}, b...) custom-call(s32[1]{0:T(128)} %bitcast.17.c_ref, f32[256,1024]{1,0:T(8,128)S(1)} %pad_maximum_fusion.grad_ref, ...), custom_call_target="tpu_custom_call" | custom-call | flops 16099999744 | bytes 1000 | tf_op jit(solution)/shard_map/block_backward/pallas_call | solution.py:333
  173.6 4.5 add_convert_fusion.2
  183.6 31.9 %attend_back.3.d_ref = bf16[8,3,256,128]{3,2,1,0:T(8,128)(2,1)} custom-call(bf16[2048,128]{1,0:T(8,128)(2,1)} %get-tuple-element.249.q_ref, bf16[2048,128]{1,0:T(8,128)(2,1)} %get-tuple-element.248.k_ref, bf16[2048,128]{1,0:T(8,128)(2,1)} %get-tuple-element.247.v_ref, bf16[2048,128]{1,0:T(8,128)(2,1)} %bitcast.292), custom_call_target="tpu_custom_call" | custom-call | flops 37950001152 | bytes 1000 | tf_op jit(solution)/shard_map/attend_back/pallas_call | solution.py:134
  219.3 4.5 add_convert_fusion.3
  226.0 5.9 %grad_heads.2.rest_0_ = f32[3,128,1024]{2,1,0:T(8,128)} custom-call(bf16[8,3,256,128]{3,2,1,0:T(8,128)(2,1)} %attend_back.3.d_ref, bf16[2048,1024]{1,0:T(8,128)(2,1)} %copy-done.1), custom_call_target="tpu_custom_call" | custom-call | flops 5750000128 | bytes 1000 | tf_op jit(solution)/shard_map/grad_heads/pallas_call | solution.py:460
  231.9 7.8 %all-to-all-done.1.b_ref = bf16[8,3,256,128]{3,2,1,0:T(8,128)(2,1)S(1)} async-done(((bf16[8,3,256,128]{3,2,1,0:T(8,128)(2,1)}), bf16[8,3,256,128]{3,2,1,0:T(8,128)(2,1)S(1)}, u32[]{:S(2)}, u32[]{:S(2)}) %all-to-all-start.1) | async-done | bytes 1572896 | tf_op jit(solution)/shard_map/all_to_all | solution.py:785
  240.9 9.0 %qkv_backward.2 = (f32[256,1024]{1,0:T(8,128)}, bf16[256,1024]{1,0:T(8,128)(2,1)}, f32[8,1024]{1,0:T(8,128)}, f32[8,1024]{1,0:T(8,128)}) custom-call(bf16[8,3,256,128]{3,2,1,0:T(8,128)(2,1)} %copy-done.31, bf16[1024,3072]{1,0:T(8,128)(2,1)} %wv_ref.7, bf16[1024,3072]{1,0:T(8,128)(2,1)} %wv_ref.7, bf16[1024,3072]{1,0:T(8,128)(2,1)} %wv_ref.7, ...), custom_call_target="tpu_custom_call" | custom-call | flops 13799999488 | bytes 1000 | tf_op jit(solution)/shard_map/qkv_backward/pallas_call | solution.py:424
  249.9 22.8 %block_backward.3 = (bf16[256,4096]{1,0:T(8,128)(2,1)}, f32[1,4096]{1,0:T(1,128)}, f32[256,1024]{1,0:T(8,128)}, bf16[256,1024]{1,0:T(8,128)(2,1)}, bf16[8,256,12...) custom-call(s32[1]{0:T(128)} %bitcast.17.c_ref, ...), custom_call_target="tpu_custom_call" | custom-call | flops 20700000256 | bytes 1000 | tf_op jit(solution)/shard_map/block_backward/pallas_call | solution.py:333
  272.7 10.9 %grad_rows.1 = (bf16[8,64,4096]{2,1,0:T(8,128)(2,1)}, bf16[8,64,4096]{2,1,0:T(8,128)(2,1)}) custom-call(s32[1]{0:T(128)} %bitcast.17.c_ref, bf16[256,1024]{1,0:T(8,128)(2,1)} %convert_element_type.449.l1, bf16[256,1024]{1,0:T(8,128)(2,1)} %get-tuple-element.131.l0, bf16[256,4096]{1,0:T(8,128)(2,1)} %copy-done.19, bf16[256,4096]{1,0:T(8,128)(2,1)} %copy-done.18), custom_call_target="tpu_custom_call" | custom-call | flops 9200000000 | bytes 1000 | tf_op jit(solution)/shard_map/grad_rows/pallas_call | solution.py:167
  283.9 5.0 %grad_out.1 = (bf16[8,192,1024]{2,1,0:T(8,128)(2,1)}, bf16[8,192,1024]{2,1,0:T(8,128)(2,1)}) custom-call(s32[1]{0:T(128)} %bitcast.17.c_ref, bf16[256,1024]{1,0:T(8,128)(2,1)} %copy-done.15, bf16[256,1024]{1,0:T(8,128)(2,1)} %get-tuple-element.135.l0, bf16[256,1024]{1,0:T(8,128)(2,1)} %copy-done.14, ...), custom_call_target="tpu_custom_call", output_to_operand_aliasing={{0}: (5, {}), {1}: (6, {})} | custom-call | flops 3449999872 | bytes 1000 | tf_op jit(solution)/shard_map/grad_out/pallas_call | solution.py:370
  289.4 4.6 all-to-all-start.2
  301.1 4.5 fusion
  309.6 18.5 %attend_back.4.rest_0_ = bf16[8,3,256,128]{3,2,1,0:T(8,128)(2,1)} custom-call(bf16[2048,128]{1,0:T(8,128)(2,1)} %get-tuple-element.252.q_ref, bf16[2048,128]{1,0:T(8,128)(2,1)} %get-tuple-element.251.k_ref, bf16[2048,128]{1,0:T(8,128)(2,1)} %get-tuple-element.250.v_ref, bf16[2048,128]{1,0:T(8,128)(2,1)} %bitcast.22.do_ref), custom_call_target="tpu_custom_call" | custom-call | flops 19549999104 | bytes 1000 | tf_op jit(solution)/shard_map/attend_back/pallas_call | solution.py:134
  331.2 19.1 %attend_back.5.d_ref = bf16[8,3,256,128]{3,2,1,0:T(8,128)(2,1)} custom-call(bf16[2048,128]{1,0:T(8,128)(2,1)} %get-tuple-element.252.q_ref, bf16[2048,128]{1,0:T(8,128)(2,1)} %get-tuple-element.251.k_ref, bf16[2048,128]{1,0:T(8,128)(2,1)} %get-tuple-element.250.v_ref, bf16[2048,128]{1,0:T(8,128)(2,1)} %bitcast.22.do_ref, ...), custom_call_target="tpu_custom_call" | custom-call | flops 19549999104 | bytes 1000 | tf_op jit(solution)/shard_map/attend_back/pallas_call | solution.py:134
  350.3 5.7 %collective-permute-done.25 = bf16[2,2,64,1024]{3,2,1,0:T(8,128)(2,1)S(1)} collective-permute-done((bf16[2,2,64,1024]{3,2,1,0:T(8,128)(2,1)}, bf16[2,2,64,1024]{3,2,1,0:T(8,128)(2,1)S(1)}, u32[]{:S(2)}, u32[]{:S(2)}) %collective-permute-start.25) | collective-permute-done | bytes 524320 | tf_op jit(solution)/shard_map/ppermute | solution.py:588
  364.9 4.3 all-to-all-start.3
  375.7 6.0 %grad_heads.3 = bf16[3,128,1024]{2,1,0:T(8,128)(2,1)} custom-call(bf16[8,3,256,128]{3,2,1,0:T(8,128)(2,1)} %attend_back.5.d_ref, bf16[2048,1024]{1,0:T(8,128)(2,1)} %copy-done, f32[3,128,1024]{2,1,0:T(8,128)} %grad_heads.2.rest_0_), custom_call_target="tpu_custom_call" | custom-call | flops 5750000128 | bytes 1000 | tf_op jit(solution)/shard_map/grad_heads/pallas_call | solution.py:460
  384.8 5.0 %all-to-all-done.3.b_ref = bf16[8,3,256,128]{3,2,1,0:T(8,128)(2,1)} async-done(((bf16[8,3,256,128]{3,2,1,0:T(8,128)(2,1)}), bf16[8,3,256,128]{3,2,1,0:T(8,128)(2,1)}, u32[]{:S(2)}, u32[]{:S(2)}) %all-to-all-start.3) | async-done | bytes 1572896 | tf_op jit(solution)/shard_map/all_to_all | solution.py:785
  389.8 8.3 %collective-permute-done.30 = bf16[2,2,96,1024]{3,2,1,0:T(8,128)(2,1)} collective-permute-done((bf16[2,2,96,1024]{3,2,1,0:T(8,128)(2,1)}, bf16[2,2,96,1024]{3,2,1,0:T(8,128)(2,1)}, u32[]{:S(2)}, u32[]{:S(2)}) %collective-permute-start.30) | collective-permute-done | bytes 786464 | tf_op jit(solution)/shard_map/ppermute | solution.py:588
  409.0 4.4 all-to-all-start.4
  418.0 8.9 %qkv_backward.3 = (f32[256,1024]{1,0:T(8,128)}, bf16[128,1024]{1,0:T(8,128)(2,1)}, f32[8,1024]{1,0:T(8,128)}, f32[8,1024]{1,0:T(8,128)}) custom-call(bf16[8,3,256,128]{3,2,1,0:T(8,128)(2,1)} %all-to-all-done.3.b_ref, bf16[1024,3072]{1,0:T(8,128)(2,1)} %wv_ref.7, bf16[1024,3072]{1,0:T(8,128)(2,1)} %wv_ref.7, bf16[1024,3072]{1,0:T(8,128)(2,1)} %wv_ref.7, ...), custom_call_target="tpu_custom_call" | custom-call | flops 13799999488 | bytes 1000 | tf_op jit(solution)/shard_map/qkv_backward/pallas_call | solution.py:424
  439.7 5.2 %all-to-all-start.5 = ((f32[16,1,1088]{2,1,0:T(1,128)}), f32[16,1,1088]{2,1,0:T(1,128)S(1)}, u32[]{:S(2)}, u32[]{:S(2)}) async-start(f32[16,1,1088]{2,1,0:T(1,128)} %copy.130), calls=%async_computation.5 | async-start | bytes 147456 | tf_op jit(solution)/shard_map/all_to_all | solution.py:829
  453.6 13.2 %all-to-all-done.5 = f32[16,1,1088]{2,1,0:T(1,128)S(1)} async-done(((f32[16,1,1088]{2,1,0:T(1,128)}), f32[16,1,1088]{2,1,0:T(1,128)S(1)}, u32[]{:S(2)}, u32[]{:S(2)}) %all-to-all-start.5) | async-done | bytes 69664 | tf_op jit(solution)/shard_map/all_to_all | solution.py:829
  466.8 4.6 collective-permute-done.37
  481.9 5.2 %collective-permute-done.41 = bf16[96,1024]{1,0:T(8,128)(2,1)S(1)} collective-permute-done((bf16[96,1024]{1,0:T(8,128)(2,1)S(1)}, bf16[96,1024]{1,0:T(8,128)(2,1)S(1)}, u32[]{:S(2)}, u32[]{:S(2)}) %collective-permute-start.41) | collective-permute-done | bytes 196640 | tf_op jit(solution)/shard_map/ppermute | solution.py:588
  (289 shorter events, 154.8 us)
Async XLA Ops:
  1.8 16.0 %collective-permute-start = (bf16[128,1024]{1,0:T(8,128)(2,1)S(1)}, bf16[128,1024]{1,0:T(8,128)(2,1)S(1)}, u32[]{:S(2)}, u32[]{:S(2)}) collective-permute-start(bf16[128,1024]{1,0:T(8,128)(2,1)S(1)} %get-tuple-element.264), channel_id=1, source_target_pairs={{0,8},{8,0},{1,9},{9,1},{2,10},{10,2},{3,11},{11,3},{4,12},{12,4},... | collective-permute-start | bytes 786440 | tf_op jit(solution)/shard_map/ppermute | solution.py:588
  19.9 13.7 %collective-permute-start.1 = (bf16[256,1024]{1,0:T(8,128)(2,1)S(1)}, bf16[256,1024]{1,0:T(8,128)(2,1)S(1)}, u32[]{:S(2)}, u32[]{:S(2)}) collective-permute-start(bf16[256,1024]{1,0:T(8,128)(2,1)S(1)} %get-tuple-element.243), channel_id=1, source_target_pairs={{0,2},{2,0},{1,3},{3,1},{4,6},{6,4},{5,7},{7,5},{8,10},{10,8},{9,1... | collective-permute-start | bytes 1572872 | tf_op jit(solution)/shard_map/ppermute | solution.py:588
  22.7 18.2 %collective-permute-start.5 = (bf16[256,1024]{1,0:T(8,128)(2,1)S(1)}, bf16[256,1024]{1,0:T(8,128)(2,1)S(1)}, u32[]{:S(2)}, u32[]{:S(2)}) collective-permute-start(bf16[256,1024]{1,0:T(8,128)(2,1)S(1)} %get-tuple-element.243), channel_id=1, source_target_pairs={{0,1},{1,0},{2,3},{3,2},{4,5},{5,4},{6,7},{7,6},{8,9},{9,8},{10,11... | collective-permute-start | bytes 1572872 | tf_op jit(solution)/shard_map/ppermute | solution.py:588
  42.5 27.2 %collective-permute-start.10 = (f32[128,1024]{1,0:T(8,128)S(1)}, f32[128,1024]{1,0:T(8,128)S(1)}, u32[]{:S(2)}, u32[]{:S(2)}) collective-permute-start(f32[128,1024]{1,0:T(8,128)S(1)} %get-tuple-element.254), channel_id=1, source_target_pairs={{0,8},{8,0},{1,9},{9,1},{2,10},{10,2},{3,11},{11,3},{4,12},{12,4},... | collective-permute-start | bytes 1572872 | tf_op jit(solution)/shard_map/ppermute | solution.py:588
  86.5 13.7 %collective-permute-start.12 = (bf16[256,1024]{1,0:T(8,128)(2,1)S(1)}, bf16[256,1024]{1,0:T(8,128)(2,1)S(1)}, u32[]{:S(2)}, u32[]{:S(2)}) collective-permute-start(bf16[256,1024]{1,0:T(8,128)(2,1)S(1)} %get-tuple-element.108), channel_id=1, source_target_pairs={{0,4},{4,0},{1,5},{5,1},{2,6},{6,2},{3,7},{7,3},{8,12},{12,8},{9,1... | collective-permute-start | bytes 1572872 | tf_op jit(solution)/shard_map/ppermute | solution.py:588
  88.0 13.4 %collective-permute-start.11 = (bf16[256,1024]{1,0:T(8,128)(2,1)S(1)}, bf16[256,1024]{1,0:T(8,128)(2,1)S(1)}, u32[]{:S(2)}, u32[]{:S(2)}) collective-permute-start(bf16[256,1024]{1,0:T(8,128)(2,1)S(1)} %get-tuple-element.108), channel_id=1, source_target_pairs={{0,2},{2,0},{1,3},{3,1},{4,6},{6,4},{5,7},{7,5},{8,10},{10,8},{9,1... | collective-permute-start | bytes 1572872 | tf_op jit(solution)/shard_map/ppermute | solution.py:588
  90.0 18.4 %collective-permute-start.15 = (bf16[256,1024]{1,0:T(8,128)(2,1)S(1)}, bf16[256,1024]{1,0:T(8,128)(2,1)S(1)}, u32[]{:S(2)}, u32[]{:S(2)}) collective-permute-start(bf16[256,1024]{1,0:T(8,128)(2,1)S(1)} %get-tuple-element.108), channel_id=1, source_target_pairs={{0,1},{1,0},{2,3},{3,2},{4,5},{5,4},{6,7},{7,6},{8,9},{9,8},{10,11... | collective-permute-start | bytes 1572872 | tf_op jit(solution)/shard_map/ppermute | solution.py:588
  148.6 30.7 %collective-permute-start.20 = (bf16[128,1024]{1,0:T(8,128)(2,1)S(1)}, bf16[128,1024]{1,0:T(8,128)(2,1)S(1)}, u32[]{:S(2)}, u32[]{:S(2)}) collective-permute-start(bf16[128,1024]{1,0:T(8,128)(2,1)S(1)} %get-tuple-element.262), channel_id=1, source_target_pairs={{0,8},{8,0},{1,9},{9,1},{2,10},{10,2},{3,11},{11,3},{4,12},{12,4},... | collective-permute-start | bytes 786440 | tf_op jit(solution)/shard_map/ppermute | solution.py:588
  215.5 24.3 %all-to-all-start.1 = ((bf16[8,3,256,128]{3,2,1,0:T(8,128)(2,1)}), bf16[8,3,256,128]{3,2,1,0:T(8,128)(2,1)S(1)}, u32[]{:S(2)}, u32[]{:S(2)}) async-start(bf16[8,3,256,128]{3,2,1,0:T(8,128)(2,1)} %attend_back.3.d_ref), calls=%async_computation.1 | async-start | bytes 3145728 | tf_op jit(solution)/shard_map/all_to_all | solution.py:785
  283.7 17.5 %collective-permute-start.22 = (bf16[8,64,4096]{2,1,0:T(8,128)(2,1)}, bf16[8,64,4096]{2,1,0:T(8,128)(2,1)}, u32[]{:S(2)}, u32[]{:S(2)}) collective-permute-start(bf16[8,64,4096]{2,1,0:T(8,128)(2,1)} %get-tuple-element.134), channel_id=1, source_target_pairs={{0,1},{1,0},{2,3},{3,2},{4,5},{5,4},{6,7},{7,6},{8,9},{9,8},{10,11... | collective-permute-start | bytes 12582920 | tf_op jit(solution)/shard_map/ppermute | solution.py:588
  288.9 18.2 %collective-permute-start.21 = (bf16[8,192,1024]{2,1,0:T(8,128)(2,1)}, bf16[8,192,1024]{2,1,0:T(8,128)(2,1)S(1)}, u32[]{:S(2)}, u32[]{:S(2)}) collective-permute-start(bf16[8,192,1024]{2,1,0:T(8,128)(2,1)} %get-tuple-element.139), channel_id=1, source_target_pairs={{0,1},{1,0},{2,3},{3,2},{4,5},{5,4},{6,7},{7,6},{8,9},{9,8},{10,11... | collective-permute-start | bytes 9437192 | tf_op jit(solution)/shard_map/ppermute | solution.py:588
  289.4 20.2 %all-to-all-start.2 = ((bf16[8,256,128]{2,1,0:T(8,128)(2,1)}), bf16[8,256,128]{2,1,0:T(8,128)(2,1)}, u32[]{:S(2)}, u32[]{:S(2)}) async-start(bf16[8,256,128]{2,1,0:T(8,128)(2,1)} %get-tuple-element.127), calls=%async_computation.2 | async-start | bytes 1048576 | tf_op jit(solution)/shard_map/all_to_all | solution.py:747
  300.1 28.0 %collective-permute-start.24 = (bf16[2,2,2,64,1024]{4,3,2,1,0:T(8,128)(2,1)}, bf16[2,2,2,64,1024]{4,3,2,1,0:T(8,128)(2,1)}, u32[]{:S(2)}, u32[]{:S(2)}) collective-permute-start(bf16[2,2,2,64,1024]{4,3,2,1,0:T(8,128)(2,1)} %fusion.20), channel_id=1, source_target_pairs={{0,4},{4,0},{1,5},{5,1},{2,6},{6,2},{3,7},{7,3},{8,12},{12,8},{9,1... | collective-permute-start | bytes 3145736 | tf_op jit(solution)/shard_map/ppermute | solution.py:588
  305.6 50.4 %collective-permute-start.27 = (bf16[2,2,2,32,4096]{4,3,2,1,0:T(8,128)(2,1)}, bf16[2,2,2,32,4096]{4,3,2,1,0:T(8,128)(2,1)}, u32[]{:S(2)}, u32[]{:S(2)}) collective-permute-start(bf16[2,2,2,32,4096]{4,3,2,1,0:T(8,128)(2,1)} %fusion), channel_id=1, source_target_pairs={{0,16},{16,0},{1,17},{17,1},{2,18},{18,2},{3,19},{19,3},{4,20},{20... | collective-permute-start | bytes 6291464 | tf_op jit(solution)/shard_map/ppermute | solution.py:588
  309.3 46.7 %collective-permute-start.26 = (bf16[2,2,2,96,1024]{4,3,2,1,0:T(8,128)(2,1)}, bf16[2,2,2,96,1024]{4,3,2,1,0:T(8,128)(2,1)}, u32[]{:S(2)}, u32[]{:S(2)}) collective-permute-start(bf16[2,2,2,96,1024]{4,3,2,1,0:T(8,128)(2,1)} %fusion.6), channel_id=1, source_target_pairs={{0,2},{2,0},{1,3},{3,1},{4,6},{6,4},{5,7},{7,5},{8,10},{10,8},{9,1... | collective-permute-start | bytes 4718600 | tf_op jit(solution)/shard_map/ppermute | solution.py:588
  330.5 25.5 %collective-permute-start.25 = (bf16[2,2,64,1024]{3,2,1,0:T(8,128)(2,1)}, bf16[2,2,64,1024]{3,2,1,0:T(8,128)(2,1)S(1)}, u32[]{:S(2)}, u32[]{:S(2)}) collective-permute-start(bf16[2,2,64,1024]{3,2,1,0:T(8,128)(2,1)} %fusion.22), channel_id=1, source_target_pairs={{0,8},{8,0},{1,9},{9,1},{2,10},{10,2},{3,11},{11,3},{4,12},{12,4},... | collective-permute-start | bytes 1572872 | tf_op jit(solution)/shard_map/ppermute | solution.py:588
  364.9 24.9 %all-to-all-start.3 = ((bf16[8,3,256,128]{3,2,1,0:T(8,128)(2,1)}), bf16[8,3,256,128]{3,2,1,0:T(8,128)(2,1)}, u32[]{:S(2)}, u32[]{:S(2)}) async-start(bf16[8,3,256,128]{3,2,1,0:T(8,128)(2,1)} %attend_back.5.d_ref), calls=%async_computation.3 | async-start | bytes 3145728 | tf_op jit(solution)/shard_map/all_to_all | solution.py:785
  371.8 18.0 %collective-permute-start.31 = (bf16[2,64,1024]{2,1,0:T(8,128)(2,1)}, bf16[2,64,1024]{2,1,0:T(8,128)(2,1)}, u32[]{:S(2)}, u32[]{:S(2)}) collective-permute-start(bf16[2,64,1024]{2,1,0:T(8,128)(2,1)} %fusion.28), channel_id=1, source_target_pairs={{0,16},{16,0},{1,17},{17,1},{2,18},{18,2},{3,19},{19,3},{4,20},{20... | collective-permute-start | bytes 786440 | tf_op jit(solution)/shard_map/ppermute | solution.py:588
  372.2 25.9 %collective-permute-start.30 = (bf16[2,2,96,1024]{3,2,1,0:T(8,128)(2,1)}, bf16[2,2,96,1024]{3,2,1,0:T(8,128)(2,1)}, u32[]{:S(2)}, u32[]{:S(2)}) collective-permute-start(bf16[2,2,96,1024]{3,2,1,0:T(8,128)(2,1)} %fusion.7), channel_id=1, source_target_pairs={{0,16},{16,0},{1,17},{17,1},{2,18},{18,2},{3,19},{19,3},{4,20},{20... | collective-permute-start | bytes 2359304 | tf_op jit(solution)/shard_map/ppermute | solution.py:588
  373.8 39.6 %collective-permute-start.28 = (bf16[2,2,32,4096]{3,2,1,0:T(8,128)(2,1)}, bf16[2,2,32,4096]{3,2,1,0:T(8,128)(2,1)}, u32[]{:S(2)}, u32[]{:S(2)}) collective-permute-start(bf16[2,2,32,4096]{3,2,1,0:T(8,128)(2,1)} %fusion.1), channel_id=1, source_target_pairs={{0,2},{2,0},{1,3},{3,1},{4,6},{6,4},{5,7},{7,5},{8,10},{10,8},{9,1... | collective-permute-start | bytes 3145736 | tf_op jit(solution)/shard_map/ppermute | solution.py:588
  383.7 22.2 %collective-permute-start.29 = (bf16[6,64,512]{2,1,0:T(8,128)(2,1)}, bf16[6,64,512]{2,1,0:T(8,128)(2,1)}, u32[]{:S(2)}, u32[]{:S(2)}) collective-permute-start(bf16[6,64,512]{2,1,0:T(8,128)(2,1)} %get-tuple-element.256), channel_id=1, source_target_pairs={{0,16},{16,0},{1,17},{17,1},{2,18},{18,2},{3,19},{19,3},{4,20},{20... | collective-permute-start | bytes 1179656 | tf_op jit(solution)/shard_map/ppermute | solution.py:588
  400.0 44.9 %collective-permute-start.36 = (bf16[64,1024]{1,0:T(8,128)(2,1)}, bf16[64,1024]{1,0:T(8,128)(2,1)S(1)}, u32[]{:S(2)}, u32[]{:S(2)}) collective-permute-start(bf16[64,1024]{1,0:T(8,128)(2,1)} %fusion.35), channel_id=1, source_target_pairs={{0,2},{2,0},{1,3},{3,1},{4,6},{6,4},{5,7},{7,5},{8,10},{10,8},{9,1... | collective-permute-start | bytes 393224 | tf_op jit(solution)/shard_map/ppermute | solution.py:588
  404.1 25.6 %collective-permute-start.32 = (bf16[2,96,1024]{2,1,0:T(8,128)(2,1)}, bf16[2,96,1024]{2,1,0:T(8,128)(2,1)}, u32[]{:S(2)}, u32[]{:S(2)}) collective-permute-start(bf16[2,96,1024]{2,1,0:T(8,128)(2,1)} %fusion.23), channel_id=1, source_target_pairs={{0,4},{4,0},{1,5},{5,1},{2,6},{6,2},{3,7},{7,3},{8,12},{12,8},{9,1... | collective-permute-start | bytes 1179656 | tf_op jit(solution)/shard_map/ppermute | solution.py:588
  409.0 25.8 %all-to-all-start.4 = ((bf16[16,64,512]{2,1,0:T(8,128)(2,1)}), bf16[16,64,512]{2,1,0:T(8,128)(2,1)}, u32[]{:S(2)}, u32[]{:S(2)}) async-start(bf16[16,64,512]{2,1,0:T(8,128)(2,1)} %take.3), calls=%async_computation.4 | async-start | bytes 2097152 | tf_op jit(solution)/shard_map/all_to_all | solution.py:800
  416.0 31.0 %collective-permute-start.35 = (bf16[2,32,4096]{2,1,0:T(8,128)(2,1)}, bf16[2,32,4096]{2,1,0:T(8,128)(2,1)}, u32[]{:S(2)}, u32[]{:S(2)}) collective-permute-start(bf16[2,32,4096]{2,1,0:T(8,128)(2,1)} %fusion.21), channel_id=1, source_target_pairs={{0,4},{4,0},{1,5},{5,1},{2,6},{6,2},{3,7},{7,3},{8,12},{12,8},{9,1... | collective-permute-start | bytes 1572872 | tf_op jit(solution)/shard_map/ppermute | solution.py:588
  426.9 39.9 %collective-permute-start.33 = (bf16[128,1024]{1,0:T(8,128)(2,1)}, bf16[128,1024]{1,0:T(8,128)(2,1)S(1)}, u32[]{:S(2)}, u32[]{:S(2)}) collective-permute-start(bf16[128,1024]{1,0:T(8,128)(2,1)} %get-tuple-element.178), channel_id=1, source_target_pairs={{0,8},{8,0},{1,9},{9,1},{2,10},{10,2},{3,11},{11,3},{4,12},{12,4},... | collective-permute-start | bytes 786440 | tf_op jit(solution)/shard_map/ppermute | solution.py:588
  431.8 35.0 %collective-permute-start.38 = (bf16[96,1024]{1,0:T(8,128)(2,1)}, bf16[96,1024]{1,0:T(8,128)(2,1)S(1)}, u32[]{:S(2)}, u32[]{:S(2)}) collective-permute-start(bf16[96,1024]{1,0:T(8,128)(2,1)} %fusion.31), channel_id=1, source_target_pairs={{0,8},{8,0},{1,9},{9,1},{2,10},{10,2},{3,11},{11,3},{4,12},{12,4},... | collective-permute-start | bytes 589832 | tf_op jit(solution)/shard_map/ppermute | solution.py:588
  437.3 29.5 %collective-permute-start.34 = (bf16[3,64,512]{2,1,0:T(8,128)(2,1)}, bf16[3,64,512]{2,1,0:T(8,128)(2,1)S(1)}, u32[]{:S(2)}, u32[]{:S(2)}) collective-permute-start(bf16[3,64,512]{2,1,0:T(8,128)(2,1)} %take.4), channel_id=1, source_target_pairs={{0,8},{8,0},{1,9},{9,1},{2,10},{10,2},{3,11},{11,3},{4,12},{12,4},... | collective-permute-start | bytes 589832 | tf_op jit(solution)/shard_map/ppermute | solution.py:588
  439.7 27.0 %all-to-all-start.5 = ((f32[16,1,1088]{2,1,0:T(1,128)}), f32[16,1,1088]{2,1,0:T(1,128)S(1)}, u32[]{:S(2)}, u32[]{:S(2)}) async-start(f32[16,1,1088]{2,1,0:T(1,128)} %copy.130), calls=%async_computation.5 | async-start | bytes 147456 | tf_op jit(solution)/shard_map/all_to_all | solution.py:829
  448.3 18.4 %collective-permute-start.42 = (bf16[64,1024]{1,0:T(8,128)(2,1)S(1)}, bf16[64,1024]{1,0:T(8,128)(2,1)S(1)}, u32[]{:S(2)}, u32[]{:S(2)}) collective-permute-start(bf16[64,1024]{1,0:T(8,128)(2,1)S(1)} %fusion.34), channel_id=1, source_target_pairs={{0,16},{16,0},{1,17},{17,1},{2,18},{18,2},{3,19},{19,3},{4,20},{20... | collective-permute-start | bytes 393224 | tf_op jit(solution)/shard_map/ppermute | solution.py:588
  450.3 21.2 %collective-permute-start.37 = (bf16[32,4096]{1,0:T(8,128)(2,1)S(1)}, bf16[32,4096]{1,0:T(8,128)(2,1)S(1)}, u32[]{:S(2)}, u32[]{:S(2)}) collective-permute-start(bf16[32,4096]{1,0:T(8,128)(2,1)S(1)} %fusion.27), channel_id=1, source_target_pairs={{0,8},{8,0},{1,9},{9,1},{2,10},{10,2},{3,11},{11,3},{4,12},{12,4},... | collective-permute-start | bytes 786440 | tf_op jit(solution)/shard_map/ppermute | solution.py:588
  477.0 13.8 %collective-permute-start.43 = (bf16[32,4096]{1,0:T(8,128)(2,1)S(1)}, bf16[32,4096]{1,0:T(8,128)(2,1)S(1)}, u32[]{:S(2)}, u32[]{:S(2)}) collective-permute-start(bf16[32,4096]{1,0:T(8,128)(2,1)S(1)} %fusion.26), channel_id=1, source_target_pairs={{0,16},{16,0},{1,17},{17,1},{2,18},{18,2},{3,19},{19,3},{4,20},{20... | collective-permute-start | bytes 786440 | tf_op jit(solution)/shard_map/ppermute | solution.py:588
  (66 other events, 778.3 us)

commit v5 on v4

--- a/solution.py
+++ b/solution.py
@@ -775,7 +775,7 @@
             d_heads = waits[0]
             for t, value in zip(shares, waits[1:]):
                 t.terms[-1] = value
-            sent = [x_share.halve("samp"), z_share.halve("samp")] + [down_share.halve(a) for a in x_axes]
+            sent = [x_share.halve("samp"), z_share.halve("samp")] + [down_share.halve("zh")]
             d_heads = pin(d_heads, *sent)
         else:
             own_grad, send_row, keep_rows = pin((own_grad, send_row, keep_rows), result)
@@ -799,7 +799,7 @@
             outgoing = take(units, send_row)
             incoming = lax.all_to_all(outgoing, low, 0, 0, tiled=True)
             down_share.terms[-1] = pin(down_share.terms[-1], outgoing)
-            back = pin(back, down_share.halve("zl"))
+            back = pin(back, *[down_share.halve(a) for a in x_axes])
         else:
             owns[0] = own_part(0)
             back = pin(back, w_heads, *owns[0])
@@ -846,7 +846,7 @@
         return x[:n], x[n:]
 
     incoming, down_share.terms[-1], z_share.terms[-1] = pin((incoming, down_share.terms[-1], z_share.terms[-1]), sums)
-    sent = down_share.halve("zh")
+    sent = down_share.halve("zl")
     own = take([incoming], keep_rows[0])
     up_first = total(z_share.terms).astype(bf16)
     late = (vectors, fields_other, other, down_share.terms[-1], x_share.terms[-1])

time: 498 us -> 499 us (level)
  waiting for transfers between devices: 93.9 us -> 99.2 us
    all_to_all x2, waiting for transfers between devices: 12.8 us -> 25.6 us  [body(): back = lax.all_to_all(d_heads, low, 0, 0, tiled=True)]
    all_to_all x1, waiting for transfers between devices: 13.2 us -> 5.42 us  [body(): vectors = lax.all_to_all(vectors, band, 0, 0, tiled=True)]
  transfers between devices with their start and end apart: 50 -> 50, of which waited for: 21 -> 20; matrix products, arithmetic and copies ran while one was open for 13% -> 13% of each run, Pallas kernels for 23% -> 23%
where the time goes in v5:
time: 499 us; the launch traced here: 493 us
  Pallas kernels  235 us (47%)
  waiting for transfers between devices  99.2 us (20%)
  starting transfers between devices  65.6 us (13%)
  other arithmetic  46.8 us (9%)
  local copies, waits for them, and re-layouts  29.9 us (6%)
  matrix products  11.4 us (2%)
    pallas_call x3, Pallas kernels, attend_back(): pl.pallas_call(functools.partial(attend_back_kernel, heads=heads, some=so...  69.5 us
    ppermute x44, waiting for transfers between devices, swap(): return lax.ppermute(x, axis, SWAP)  65.6 us
    pallas_call x2, Pallas kernels, attend(): pl.pallas_call(attend_kernel, grid=(width // block,), in_specs=[own, spec...  46.5 us
    ppermute x44, starting transfers between devices, swap(): return lax.ppermute(x, axis, SWAP)  40.5 us
    pallas_call x2, Pallas kernels, block_backward(): pl.pallas_call(functools.partial(block_backward_kernel, grads=bool(grads)...  39.4 us
    convert_element_type x12, other arithmetic, halve(): sent = total(there).astype(bf16)  30.2 us
    all_to_all x2, waiting for transfers between devices, body(): back = lax.all_to_all(d_heads, low, 0, 0, tiled=True)  25.6 us
    pallas_call x2, Pallas kernels, block_forward(): pl.pallas_call(functools.partial(block_forward_kernel, last=last), grid=(...  25.3 us
  transfers between devices with their start and end apart: 50, of which 20 were waited for; matrix products, arithmetic and copies ran while one was open for 13% of the time, Pallas kernels for 23%

profile of v5, /device:TPU:0, one launch (start us, length us, event | category | flops | bytes accessed | tf_op | source)
XLA Modules:
  0.0 492.9 jit_solution(2431690550939815113)
XLA Ops:
  11.3 6.5 %collective-permute-done = bf16[128,1024]{1,0:T(8,128)(2,1)S(1)} collective-permute-done((bf16[128,1024]{1,0:T(8,128)(2,1)S(1)}, bf16[128,1024]{1,0:T(8,128)(2,1)S(1)}, u32[]{:S(2)}, u32[]{:S(2)}) %collective-permute-start) | collective-permute-done | bytes 262176 | tf_op jit(solution)/shard_map/ppermute | solution.py:588
  23.5 8.8 %collective-permute-done.2 = bf16[256,1024]{1,0:T(8,128)(2,1)S(1)} collective-permute-done((bf16[256,1024]{1,0:T(8,128)(2,1)S(1)}, bf16[256,1024]{1,0:T(8,128)(2,1)S(1)}, u32[]{:S(2)}, u32[]{:S(2)}) %collective-permute-start.2) | collective-permute-done | bytes 524320 | tf_op jit(solution)/shard_map/ppermute | solution.py:588
  46.3 23.4 %attend.2.a_ref.r0 = bf16[256,1024]{1,0:T(8,128)(2,1)S(1)} custom-call(bf16[256,1024]{1,0:T(8,128)(2,1)S(1)} %fusion.17.q_ref, bf16[2048,1024]{1,0:T(8,128)(2,1)S(1)} %constant_dynamic-update-slice_fusion.10.n_ref, bf16[1024,3072]{1,0:T(8,128)(2,1)S(1)} %copy-done.2, bf16[1024,3072]{1,0:T(8,128)(2,1)S(1)} %copy-done.2, f32[1,1024]{1,0:T(1,128)S(1)} %bitcast.257), custom_call_target="tpu_custom_call" | custom-call | flops 27599998976 | bytes 1000 | tf_op jit(solution)/shard_map/attend/pallas_call | solution.py:64
  70.0 12.8 %block_forward.2 = (f32[256,1024]{1,0:T(8,128)S(1)}, f32[256,1]{1,0:T(8,128)S(1)}, bf16[256,1024]{1,0:T(8,128)(2,1)S(1)}, f32[256,4096]{1,0:T(8,128)S(1)}, bf16[...) custom-call(f32[256,1024]{1,0:T(8,128)S(1)} %get-tuple-element.258.x, ...), custom_call_target="tpu_custom_call" | custom-call | flops 13799999488 | bytes 1000 | tf_op jit(solution)/shard_map/block_forward/pallas_call | solution.py:235
  90.8 9.4 %collective-permute-done.12 = bf16[256,1024]{1,0:T(8,128)(2,1)S(1)} collective-permute-done((bf16[256,1024]{1,0:T(8,128)(2,1)S(1)}, bf16[256,1024]{1,0:T(8,128)(2,1)S(1)}, u32[]{:S(2)}, u32[]{:S(2)}) %collective-permute-start.12) | collective-permute-done | bytes 524320 | tf_op jit(solution)/shard_map/ppermute | solution.py:588
  110.0 23.0 %attend.3.a_ref.r1 = bf16[256,1024]{1,0:T(8,128)(2,1)S(1)} custom-call(bf16[256,1024]{1,0:T(8,128)(2,1)S(1)} %fusion.14.q_ref, bf16[2048,1024]{1,0:T(8,128)(2,1)S(1)} %constant_dynamic-update-slice_fusion.n_ref, bf16[1024,3072]{1,0:T(8,128)(2,1)S(1)} %copy-done.2, bf16[1024,3072]{1,0:T(8,128)(2,1)S(1)} %copy-done.2, f32[1,1024]{1,0:T(1,128)S(1)} %bitcast.258), custom_call_target="tpu_custom_call" | custom-call | flops 27599998976 | bytes 1000 | tf_op jit(solution)/shard_map/attend/pallas_call | solution.py:64
  133.1 12.6 %block_forward.3 = (f32[256,1024]{1,0:T(8,128)S(1)}, f32[256,1]{1,0:T(8,128)S(1)}, bf16[256,1024]{1,0:T(8,128)(2,1)S(1)}, f32[256,4096]{1,0:T(8,128)S(1)}, bf16[...) custom-call(f32[256,1024]{1,0:T(8,128)S(1)} %copy-done.24, bf16[256,1024]{1,0:T(8,128)(2,1)S(1)} %attend.3.a_ref.r1, ...), custom_call_target="tpu_custom_call" | custom-call | flops 13799999488 | bytes 1000 | tf_op jit(solution)/shard_map/block_forward/pallas_call | solution.py:235
  151.5 16.5 %block_backward.2 = (bf16[256,4096]{1,0:T(8,128)(2,1)}, f32[1,4096]{1,0:T(1,128)S(1)}, f32[256,1024]{1,0:T(8,128)S(1)}, bf16[256,1024]{1,0:T(8,128)(2,1)S(1)}, b...) custom-call(s32[1]{0:T(128)} %bitcast.17.c_ref, f32[256,1024]{1,0:T(8,128)S(1)} %pad_maximum_fusion.grad_ref, ...), custom_call_target="tpu_custom_call" | custom-call | flops 16099999744 | bytes 1000 | tf_op jit(solution)/shard_map/block_backward/pallas_call | solution.py:333
  173.6 4.5 add_convert_fusion.2
  183.6 31.9 %attend_back.3.d_ref = bf16[8,3,256,128]{3,2,1,0:T(8,128)(2,1)} custom-call(bf16[2048,128]{1,0:T(8,128)(2,1)} %get-tuple-element.249.q_ref, bf16[2048,128]{1,0:T(8,128)(2,1)} %get-tuple-element.248.k_ref, bf16[2048,128]{1,0:T(8,128)(2,1)} %get-tuple-element.247.v_ref, bf16[2048,128]{1,0:T(8,128)(2,1)} %bitcast.292), custom_call_target="tpu_custom_call" | custom-call | flops 37950001152 | bytes 1000 | tf_op jit(solution)/shard_map/attend_back/pallas_call | solution.py:134
  219.3 4.5 add_convert_fusion.3
  226.0 5.9 %grad_heads.2.rest_0_ = f32[3,128,1024]{2,1,0:T(8,128)} custom-call(bf16[8,3,256,128]{3,2,1,0:T(8,128)(2,1)} %attend_back.3.d_ref, bf16[2048,1024]{1,0:T(8,128)(2,1)} %copy-done.1), custom_call_target="tpu_custom_call" | custom-call | flops 5750000128 | bytes 1000 | tf_op jit(solution)/shard_map/grad_heads/pallas_call | solution.py:460
  231.9 7.8 %all-to-all-done.1.b_ref = bf16[8,3,256,128]{3,2,1,0:T(8,128)(2,1)S(1)} async-done(((bf16[8,3,256,128]{3,2,1,0:T(8,128)(2,1)}), bf16[8,3,256,128]{3,2,1,0:T(8,128)(2,1)S(1)}, u32[]{:S(2)}, u32[]{:S(2)}) %all-to-all-start.1) | async-done | bytes 1572896 | tf_op jit(solution)/shard_map/all_to_all | solution.py:785
  240.9 9.0 %qkv_backward.2 = (f32[256,1024]{1,0:T(8,128)}, bf16[256,1024]{1,0:T(8,128)(2,1)}, f32[8,1024]{1,0:T(8,128)}, f32[8,1024]{1,0:T(8,128)}) custom-call(bf16[8,3,256,128]{3,2,1,0:T(8,128)(2,1)} %copy-done.31, bf16[1024,3072]{1,0:T(8,128)(2,1)} %wv_ref.7, bf16[1024,3072]{1,0:T(8,128)(2,1)} %wv_ref.7, bf16[1024,3072]{1,0:T(8,128)(2,1)} %wv_ref.7, ...), custom_call_target="tpu_custom_call" | custom-call | flops 13799999488 | bytes 1000 | tf_op jit(solution)/shard_map/qkv_backward/pallas_call | solution.py:424
  249.9 22.8 %block_backward.3 = (bf16[256,4096]{1,0:T(8,128)(2,1)}, f32[1,4096]{1,0:T(1,128)}, f32[256,1024]{1,0:T(8,128)}, bf16[256,1024]{1,0:T(8,128)(2,1)}, bf16[8,256,12...) custom-call(s32[1]{0:T(128)} %bitcast.17.c_ref, ...), custom_call_target="tpu_custom_call" | custom-call | flops 20700000256 | bytes 1000 | tf_op jit(solution)/shard_map/block_backward/pallas_call | solution.py:333
  272.7 10.9 %grad_rows.1 = (bf16[8,64,4096]{2,1,0:T(8,128)(2,1)}, bf16[8,64,4096]{2,1,0:T(8,128)(2,1)}) custom-call(s32[1]{0:T(128)} %bitcast.17.c_ref, bf16[256,1024]{1,0:T(8,128)(2,1)} %convert_element_type.449.l1, bf16[256,1024]{1,0:T(8,128)(2,1)} %get-tuple-element.131.l0, bf16[256,4096]{1,0:T(8,128)(2,1)} %copy-done.19, bf16[256,4096]{1,0:T(8,128)(2,1)} %copy-done.18), custom_call_target="tpu_custom_call" | custom-call | flops 9200000000 | bytes 1000 | tf_op jit(solution)/shard_map/grad_rows/pallas_call | solution.py:167
  283.9 5.0 %grad_out.1 = (bf16[8,192,1024]{2,1,0:T(8,128)(2,1)}, bf16[8,192,1024]{2,1,0:T(8,128)(2,1)}) custom-call(s32[1]{0:T(128)} %bitcast.17.c_ref, bf16[256,1024]{1,0:T(8,128)(2,1)} %copy-done.15, bf16[256,1024]{1,0:T(8,128)(2,1)} %get-tuple-element.135.l0, bf16[256,1024]{1,0:T(8,128)(2,1)} %copy-done.14, ...), custom_call_target="tpu_custom_call", output_to_operand_aliasing={{0}: (5, {}), {1}: (6, {})} | custom-call | flops 3449999872 | bytes 1000 | tf_op jit(solution)/shard_map/grad_out/pallas_call | solution.py:370
  289.4 4.6 all-to-all-start.2
  301.1 4.5 fusion
  309.6 18.5 %attend_back.4.rest_0_ = bf16[8,3,256,128]{3,2,1,0:T(8,128)(2,1)} custom-call(bf16[2048,128]{1,0:T(8,128)(2,1)} %get-tuple-element.252.q_ref, bf16[2048,128]{1,0:T(8,128)(2,1)} %get-tuple-element.251.k_ref, bf16[2048,128]{1,0:T(8,128)(2,1)} %get-tuple-element.250.v_ref, bf16[2048,128]{1,0:T(8,128)(2,1)} %bitcast.22.do_ref), custom_call_target="tpu_custom_call" | custom-call | flops 19549999104 | bytes 1000 | tf_op jit(solution)/shard_map/attend_back/pallas_call | solution.py:134
  331.2 19.1 %attend_back.5.d_ref = bf16[8,3,256,128]{3,2,1,0:T(8,128)(2,1)} custom-call(bf16[2048,128]{1,0:T(8,128)(2,1)} %get-tuple-element.252.q_ref, bf16[2048,128]{1,0:T(8,128)(2,1)} %get-tuple-element.251.k_ref, bf16[2048,128]{1,0:T(8,128)(2,1)} %get-tuple-element.250.v_ref, bf16[2048,128]{1,0:T(8,128)(2,1)} %bitcast.22.do_ref, ...), custom_call_target="tpu_custom_call" | custom-call | flops 19549999104 | bytes 1000 | tf_op jit(solution)/shard_map/attend_back/pallas_call | solution.py:134
  350.3 5.7 %collective-permute-done.25 = bf16[2,2,64,1024]{3,2,1,0:T(8,128)(2,1)S(1)} collective-permute-done((bf16[2,2,64,1024]{3,2,1,0:T(8,128)(2,1)}, bf16[2,2,64,1024]{3,2,1,0:T(8,128)(2,1)S(1)}, u32[]{:S(2)}, u32[]{:S(2)}) %collective-permute-start.25) | collective-permute-done | bytes 524320 | tf_op jit(solution)/shard_map/ppermute | solution.py:588
  364.9 4.3 all-to-all-start.3
  373.8 6.0 %grad_heads.3 = bf16[3,128,1024]{2,1,0:T(8,128)(2,1)} custom-call(bf16[8,3,256,128]{3,2,1,0:T(8,128)(2,1)} %attend_back.5.d_ref, bf16[2048,1024]{1,0:T(8,128)(2,1)} %copy-done, f32[3,128,1024]{2,1,0:T(8,128)} %grad_heads.2.rest_0_), custom_call_target="tpu_custom_call" | custom-call | flops 5750000128 | bytes 1000 | tf_op jit(solution)/shard_map/grad_heads/pallas_call | solution.py:460
  382.9 17.8 %all-to-all-done.3.b_ref = bf16[8,3,256,128]{3,2,1,0:T(8,128)(2,1)} async-done(((bf16[8,3,256,128]{3,2,1,0:T(8,128)(2,1)}), bf16[8,3,256,128]{3,2,1,0:T(8,128)(2,1)}, u32[]{:S(2)}, u32[]{:S(2)}) %all-to-all-start.3) | async-done | bytes 1572896 | tf_op jit(solution)/shard_map/all_to_all | solution.py:785
  409.0 4.4 all-to-all-start.4
  413.4 9.1 %collective-permute-done.28 = bf16[2,2,32,4096]{3,2,1,0:T(8,128)(2,1)} collective-permute-done((bf16[2,2,32,4096]{3,2,1,0:T(8,128)(2,1)}, bf16[2,2,32,4096]{3,2,1,0:T(8,128)(2,1)}, u32[]{:S(2)}, u32[]{:S(2)}) %collective-permute-start.28) | collective-permute-done | bytes 1048608 | tf_op jit(solution)/shard_map/ppermute | solution.py:588
  426.7 8.9 %qkv_backward.3 = (f32[256,1024]{1,0:T(8,128)}, bf16[128,1024]{1,0:T(8,128)(2,1)}, f32[8,1024]{1,0:T(8,128)}, f32[8,1024]{1,0:T(8,128)}) custom-call(bf16[8,3,256,128]{3,2,1,0:T(8,128)(2,1)} %all-to-all-done.3.b_ref, bf16[1024,3072]{1,0:T(8,128)(2,1)} %wv_ref.7, bf16[1024,3072]{1,0:T(8,128)(2,1)} %wv_ref.7, bf16[1024,3072]{1,0:T(8,128)(2,1)} %wv_ref.7, ...), custom_call_target="tpu_custom_call" | custom-call | flops 13799999488 | bytes 1000 | tf_op jit(solution)/shard_map/qkv_backward/pallas_call | solution.py:424
  448.5 4.3 all-to-all-start.5
  460.6 5.4 %all-to-all-done.5 = f32[16,1,1088]{2,1,0:T(1,128)S(1)} async-done(((f32[16,1,1088]{2,1,0:T(1,128)}), f32[16,1,1088]{2,1,0:T(1,128)S(1)}, u32[]{:S(2)}, u32[]{:S(2)}) %all-to-all-start.5) | async-done | bytes 69664 | tf_op jit(solution)/shard_map/all_to_all | solution.py:829
  466.1 5.5 %collective-permute-done.37 = bf16[32,4096]{1,0:T(8,128)(2,1)S(1)} collective-permute-done((bf16[32,4096]{1,0:T(8,128)(2,1)S(1)}, bf16[32,4096]{1,0:T(8,128)(2,1)S(1)}, u32[]{:S(2)}, u32[]{:S(2)}) %collective-permute-start.37) | collective-permute-done | bytes 262176 | tf_op jit(solution)/shard_map/ppermute | solution.py:588
  482.0 5.1 %collective-permute-done.41 = bf16[96,1024]{1,0:T(8,128)(2,1)S(1)} collective-permute-done((bf16[96,1024]{1,0:T(8,128)(2,1)S(1)}, bf16[96,1024]{1,0:T(8,128)(2,1)S(1)}, u32[]{:S(2)}, u32[]{:S(2)}) %collective-permute-start.41) | collective-permute-done | bytes 196640 | tf_op jit(solution)/shard_map/ppermute | solution.py:588
  (289 shorter events, 149.7 us)
Async XLA Ops:
  1.8 16.0 %collective-permute-start = (bf16[128,1024]{1,0:T(8,128)(2,1)S(1)}, bf16[128,1024]{1,0:T(8,128)(2,1)S(1)}, u32[]{:S(2)}, u32[]{:S(2)}) collective-permute-start(bf16[128,1024]{1,0:T(8,128)(2,1)S(1)} %get-tuple-element.264), channel_id=1, source_target_pairs={{0,8},{8,0},{1,9},{9,1},{2,10},{10,2},{3,11},{11,3},{4,12},{12,4},... | collective-permute-start | bytes 786440 | tf_op jit(solution)/shard_map/ppermute | solution.py:588
  19.1 13.2 %collective-permute-start.2 = (bf16[256,1024]{1,0:T(8,128)(2,1)S(1)}, bf16[256,1024]{1,0:T(8,128)(2,1)S(1)}, u32[]{:S(2)}, u32[]{:S(2)}) collective-permute-start(bf16[256,1024]{1,0:T(8,128)(2,1)S(1)} %get-tuple-element.243), channel_id=1, source_target_pairs={{0,4},{4,0},{1,5},{5,1},{2,6},{6,2},{3,7},{7,3},{8,12},{12,8},{9,1... | collective-permute-start | bytes 1572872 | tf_op jit(solution)/shard_map/ppermute | solution.py:588
  19.9 13.7 %collective-permute-start.1 = (bf16[256,1024]{1,0:T(8,128)(2,1)S(1)}, bf16[256,1024]{1,0:T(8,128)(2,1)S(1)}, u32[]{:S(2)}, u32[]{:S(2)}) collective-permute-start(bf16[256,1024]{1,0:T(8,128)(2,1)S(1)} %get-tuple-element.243), channel_id=1, source_target_pairs={{0,2},{2,0},{1,3},{3,1},{4,6},{6,4},{5,7},{7,5},{8,10},{10,8},{9,1... | collective-permute-start | bytes 1572872 | tf_op jit(solution)/shard_map/ppermute | solution.py:588
  22.7 18.2 %collective-permute-start.5 = (bf16[256,1024]{1,0:T(8,128)(2,1)S(1)}, bf16[256,1024]{1,0:T(8,128)(2,1)S(1)}, u32[]{:S(2)}, u32[]{:S(2)}) collective-permute-start(bf16[256,1024]{1,0:T(8,128)(2,1)S(1)} %get-tuple-element.243), channel_id=1, source_target_pairs={{0,1},{1,0},{2,3},{3,2},{4,5},{5,4},{6,7},{7,6},{8,9},{9,8},{10,11... | collective-permute-start | bytes 1572872 | tf_op jit(solution)/shard_map/ppermute | solution.py:588
  42.5 27.2 %collective-permute-start.10 = (f32[128,1024]{1,0:T(8,128)S(1)}, f32[128,1024]{1,0:T(8,128)S(1)}, u32[]{:S(2)}, u32[]{:S(2)}) collective-permute-start(f32[128,1024]{1,0:T(8,128)S(1)} %get-tuple-element.254), channel_id=1, source_target_pairs={{0,8},{8,0},{1,9},{9,1},{2,10},{10,2},{3,11},{11,3},{4,12},{12,4},... | collective-permute-start | bytes 1572872 | tf_op jit(solution)/shard_map/ppermute | solution.py:588
  86.5 13.7 %collective-permute-start.12 = (bf16[256,1024]{1,0:T(8,128)(2,1)S(1)}, bf16[256,1024]{1,0:T(8,128)(2,1)S(1)}, u32[]{:S(2)}, u32[]{:S(2)}) collective-permute-start(bf16[256,1024]{1,0:T(8,128)(2,1)S(1)} %get-tuple-element.108), channel_id=1, source_target_pairs={{0,4},{4,0},{1,5},{5,1},{2,6},{6,2},{3,7},{7,3},{8,12},{12,8},{9,1... | collective-permute-start | bytes 1572872 | tf_op jit(solution)/shard_map/ppermute | solution.py:588
  88.0 13.4 %collective-permute-start.11 = (bf16[256,1024]{1,0:T(8,128)(2,1)S(1)}, bf16[256,1024]{1,0:T(8,128)(2,1)S(1)}, u32[]{:S(2)}, u32[]{:S(2)}) collective-permute-start(bf16[256,1024]{1,0:T(8,128)(2,1)S(1)} %get-tuple-element.108), channel_id=1, source_target_pairs={{0,2},{2,0},{1,3},{3,1},{4,6},{6,4},{5,7},{7,5},{8,10},{10,8},{9,1... | collective-permute-start | bytes 1572872 | tf_op jit(solution)/shard_map/ppermute | solution.py:588
  90.0 18.4 %collective-permute-start.15 = (bf16[256,1024]{1,0:T(8,128)(2,1)S(1)}, bf16[256,1024]{1,0:T(8,128)(2,1)S(1)}, u32[]{:S(2)}, u32[]{:S(2)}) collective-permute-start(bf16[256,1024]{1,0:T(8,128)(2,1)S(1)} %get-tuple-element.108), channel_id=1, source_target_pairs={{0,1},{1,0},{2,3},{3,2},{4,5},{5,4},{6,7},{7,6},{8,9},{9,8},{10,11... | collective-permute-start | bytes 1572872 | tf_op jit(solution)/shard_map/ppermute | solution.py:588
  148.6 30.7 %collective-permute-start.20 = (bf16[128,1024]{1,0:T(8,128)(2,1)S(1)}, bf16[128,1024]{1,0:T(8,128)(2,1)S(1)}, u32[]{:S(2)}, u32[]{:S(2)}) collective-permute-start(bf16[128,1024]{1,0:T(8,128)(2,1)S(1)} %get-tuple-element.262), channel_id=1, source_target_pairs={{0,8},{8,0},{1,9},{9,1},{2,10},{10,2},{3,11},{11,3},{4,12},{12,4},... | collective-permute-start | bytes 786440 | tf_op jit(solution)/shard_map/ppermute | solution.py:588
  215.5 24.3 %all-to-all-start.1 = ((bf16[8,3,256,128]{3,2,1,0:T(8,128)(2,1)}), bf16[8,3,256,128]{3,2,1,0:T(8,128)(2,1)S(1)}, u32[]{:S(2)}, u32[]{:S(2)}) async-start(bf16[8,3,256,128]{3,2,1,0:T(8,128)(2,1)} %attend_back.3.d_ref), calls=%async_computation.1 | async-start | bytes 3145728 | tf_op jit(solution)/shard_map/all_to_all | solution.py:785
  283.7 17.5 %collective-permute-start.22 = (bf16[8,64,4096]{2,1,0:T(8,128)(2,1)}, bf16[8,64,4096]{2,1,0:T(8,128)(2,1)}, u32[]{:S(2)}, u32[]{:S(2)}) collective-permute-start(bf16[8,64,4096]{2,1,0:T(8,128)(2,1)} %get-tuple-element.134), channel_id=1, source_target_pairs={{0,1},{1,0},{2,3},{3,2},{4,5},{5,4},{6,7},{7,6},{8,9},{9,8},{10,11... | collective-permute-start | bytes 12582920 | tf_op jit(solution)/shard_map/ppermute | solution.py:588
  288.9 18.2 %collective-permute-start.21 = (bf16[8,192,1024]{2,1,0:T(8,128)(2,1)}, bf16[8,192,1024]{2,1,0:T(8,128)(2,1)S(1)}, u32[]{:S(2)}, u32[]{:S(2)}) collective-permute-start(bf16[8,192,1024]{2,1,0:T(8,128)(2,1)} %get-tuple-element.139), channel_id=1, source_target_pairs={{0,1},{1,0},{2,3},{3,2},{4,5},{5,4},{6,7},{7,6},{8,9},{9,8},{10,11... | collective-permute-start | bytes 9437192 | tf_op jit(solution)/shard_map/ppermute | solution.py:588
  289.4 20.2 %all-to-all-start.2 = ((bf16[8,256,128]{2,1,0:T(8,128)(2,1)}), bf16[8,256,128]{2,1,0:T(8,128)(2,1)}, u32[]{:S(2)}, u32[]{:S(2)}) async-start(bf16[8,256,128]{2,1,0:T(8,128)(2,1)} %get-tuple-element.127), calls=%async_computation.2 | async-start | bytes 1048576 | tf_op jit(solution)/shard_map/all_to_all | solution.py:747
  300.1 28.0 %collective-permute-start.24 = (bf16[2,2,2,64,1024]{4,3,2,1,0:T(8,128)(2,1)}, bf16[2,2,2,64,1024]{4,3,2,1,0:T(8,128)(2,1)}, u32[]{:S(2)}, u32[]{:S(2)}) collective-permute-start(bf16[2,2,2,64,1024]{4,3,2,1,0:T(8,128)(2,1)} %fusion.20), channel_id=1, source_target_pairs={{0,4},{4,0},{1,5},{5,1},{2,6},{6,2},{3,7},{7,3},{8,12},{12,8},{9,1... | collective-permute-start | bytes 3145736 | tf_op jit(solution)/shard_map/ppermute | solution.py:588
  305.6 50.4 %collective-permute-start.27 = (bf16[2,2,2,32,4096]{4,3,2,1,0:T(8,128)(2,1)}, bf16[2,2,2,32,4096]{4,3,2,1,0:T(8,128)(2,1)}, u32[]{:S(2)}, u32[]{:S(2)}) collective-permute-start(bf16[2,2,2,32,4096]{4,3,2,1,0:T(8,128)(2,1)} %fusion), channel_id=1, source_target_pairs={{0,16},{16,0},{1,17},{17,1},{2,18},{18,2},{3,19},{19,3},{4,20},{20... | collective-permute-start | bytes 6291464 | tf_op jit(solution)/shard_map/ppermute | solution.py:588
  309.3 46.7 %collective-permute-start.26 = (bf16[2,2,2,96,1024]{4,3,2,1,0:T(8,128)(2,1)}, bf16[2,2,2,96,1024]{4,3,2,1,0:T(8,128)(2,1)}, u32[]{:S(2)}, u32[]{:S(2)}) collective-permute-start(bf16[2,2,2,96,1024]{4,3,2,1,0:T(8,128)(2,1)} %fusion.6), channel_id=1, source_target_pairs={{0,2},{2,0},{1,3},{3,1},{4,6},{6,4},{5,7},{7,5},{8,10},{10,8},{9,1... | collective-permute-start | bytes 4718600 | tf_op jit(solution)/shard_map/ppermute | solution.py:588
  330.5 25.5 %collective-permute-start.25 = (bf16[2,2,64,1024]{3,2,1,0:T(8,128)(2,1)}, bf16[2,2,64,1024]{3,2,1,0:T(8,128)(2,1)S(1)}, u32[]{:S(2)}, u32[]{:S(2)}) collective-permute-start(bf16[2,2,64,1024]{3,2,1,0:T(8,128)(2,1)} %fusion.22), channel_id=1, source_target_pairs={{0,8},{8,0},{1,9},{9,1},{2,10},{10,2},{3,11},{11,3},{4,12},{12,4},... | collective-permute-start | bytes 1572872 | tf_op jit(solution)/shard_map/ppermute | solution.py:588
  364.9 35.9 %all-to-all-start.3 = ((bf16[8,3,256,128]{3,2,1,0:T(8,128)(2,1)}), bf16[8,3,256,128]{3,2,1,0:T(8,128)(2,1)}, u32[]{:S(2)}, u32[]{:S(2)}) async-start(bf16[8,3,256,128]{3,2,1,0:T(8,128)(2,1)} %attend_back.5.d_ref), calls=%async_computation.3 | async-start | bytes 3145728 | tf_op jit(solution)/shard_map/all_to_all | solution.py:785
  371.8 29.0 %collective-permute-start.31 = (bf16[2,64,1024]{2,1,0:T(8,128)(2,1)}, bf16[2,64,1024]{2,1,0:T(8,128)(2,1)}, u32[]{:S(2)}, u32[]{:S(2)}) collective-permute-start(bf16[2,64,1024]{2,1,0:T(8,128)(2,1)} %fusion.28), channel_id=1, source_target_pairs={{0,16},{16,0},{1,17},{17,1},{2,18},{18,2},{3,19},{19,3},{4,20},{20... | collective-permute-start | bytes 786440 | tf_op jit(solution)/shard_map/ppermute | solution.py:588
  372.2 28.5 %collective-permute-start.30 = (bf16[2,2,96,1024]{3,2,1,0:T(8,128)(2,1)}, bf16[2,2,96,1024]{3,2,1,0:T(8,128)(2,1)}, u32[]{:S(2)}, u32[]{:S(2)}) collective-permute-start(bf16[2,2,96,1024]{3,2,1,0:T(8,128)(2,1)} %fusion.7), channel_id=1, source_target_pairs={{0,16},{16,0},{1,17},{17,1},{2,18},{18,2},{3,19},{19,3},{4,20},{20... | collective-permute-start | bytes 2359304 | tf_op jit(solution)/shard_map/ppermute | solution.py:588
  373.8 48.7 %collective-permute-start.28 = (bf16[2,2,32,4096]{3,2,1,0:T(8,128)(2,1)}, bf16[2,2,32,4096]{3,2,1,0:T(8,128)(2,1)}, u32[]{:S(2)}, u32[]{:S(2)}) collective-permute-start(bf16[2,2,32,4096]{3,2,1,0:T(8,128)(2,1)} %fusion.1), channel_id=1, source_target_pairs={{0,8},{8,0},{1,9},{9,1},{2,10},{10,2},{3,11},{11,3},{4,12},{12,4},... | collective-permute-start | bytes 3145736 | tf_op jit(solution)/shard_map/ppermute | solution.py:588
  381.9 24.1 %collective-permute-start.29 = (bf16[6,64,512]{2,1,0:T(8,128)(2,1)}, bf16[6,64,512]{2,1,0:T(8,128)(2,1)}, u32[]{:S(2)}, u32[]{:S(2)}) collective-permute-start(bf16[6,64,512]{2,1,0:T(8,128)(2,1)} %get-tuple-element.256), channel_id=1, source_target_pairs={{0,16},{16,0},{1,17},{17,1},{2,18},{18,2},{3,19},{19,3},{4,20},{20... | collective-permute-start | bytes 1179656 | tf_op jit(solution)/shard_map/ppermute | solution.py:588
  402.6 50.1 %collective-permute-start.36 = (bf16[64,1024]{1,0:T(8,128)(2,1)}, bf16[64,1024]{1,0:T(8,128)(2,1)S(1)}, u32[]{:S(2)}, u32[]{:S(2)}) collective-permute-start(bf16[64,1024]{1,0:T(8,128)(2,1)} %fusion.35), channel_id=1, source_target_pairs={{0,2},{2,0},{1,3},{3,1},{4,6},{6,4},{5,7},{7,5},{8,10},{10,8},{9,1... | collective-permute-start | bytes 393224 | tf_op jit(solution)/shard_map/ppermute | solution.py:588
  404.9 33.6 %collective-permute-start.32 = (bf16[2,96,1024]{2,1,0:T(8,128)(2,1)}, bf16[2,96,1024]{2,1,0:T(8,128)(2,1)}, u32[]{:S(2)}, u32[]{:S(2)}) collective-permute-start(bf16[2,96,1024]{2,1,0:T(8,128)(2,1)} %fusion.23), channel_id=1, source_target_pairs={{0,4},{4,0},{1,5},{5,1},{2,6},{6,2},{3,7},{7,3},{8,12},{12,8},{9,1... | collective-permute-start | bytes 1179656 | tf_op jit(solution)/shard_map/ppermute | solution.py:588
  409.0 34.5 %all-to-all-start.4 = ((bf16[16,64,512]{2,1,0:T(8,128)(2,1)}), bf16[16,64,512]{2,1,0:T(8,128)(2,1)}, u32[]{:S(2)}, u32[]{:S(2)}) async-start(bf16[16,64,512]{2,1,0:T(8,128)(2,1)} %take.3), calls=%async_computation.4 | async-start | bytes 2097152 | tf_op jit(solution)/shard_map/all_to_all | solution.py:800
  425.1 27.7 %collective-permute-start.35 = (bf16[2,32,4096]{2,1,0:T(8,128)(2,1)}, bf16[2,32,4096]{2,1,0:T(8,128)(2,1)}, u32[]{:S(2)}, u32[]{:S(2)}) collective-permute-start(bf16[2,32,4096]{2,1,0:T(8,128)(2,1)} %fusion.21), channel_id=1, source_target_pairs={{0,2},{2,0},{1,3},{3,1},{4,6},{6,4},{5,7},{7,5},{8,10},{10,8},{9,1... | collective-permute-start | bytes 1572872 | tf_op jit(solution)/shard_map/ppermute | solution.py:588
  435.6 30.4 %collective-permute-start.33 = (bf16[128,1024]{1,0:T(8,128)(2,1)}, bf16[128,1024]{1,0:T(8,128)(2,1)S(1)}, u32[]{:S(2)}, u32[]{:S(2)}) collective-permute-start(bf16[128,1024]{1,0:T(8,128)(2,1)} %get-tuple-element.178), channel_id=1, source_target_pairs={{0,8},{8,0},{1,9},{9,1},{2,10},{10,2},{3,11},{11,3},{4,12},{12,4},... | collective-permute-start | bytes 786440 | tf_op jit(solution)/shard_map/ppermute | solution.py:588
  440.5 25.5 %collective-permute-start.38 = (bf16[96,1024]{1,0:T(8,128)(2,1)}, bf16[96,1024]{1,0:T(8,128)(2,1)S(1)}, u32[]{:S(2)}, u32[]{:S(2)}) collective-permute-start(bf16[96,1024]{1,0:T(8,128)(2,1)} %fusion.31), channel_id=1, source_target_pairs={{0,8},{8,0},{1,9},{9,1},{2,10},{10,2},{3,11},{11,3},{4,12},{12,4},... | collective-permute-start | bytes 589832 | tf_op jit(solution)/shard_map/ppermute | solution.py:588
  446.1 20.0 %collective-permute-start.34 = (bf16[3,64,512]{2,1,0:T(8,128)(2,1)}, bf16[3,64,512]{2,1,0:T(8,128)(2,1)S(1)}, u32[]{:S(2)}, u32[]{:S(2)}) collective-permute-start(bf16[3,64,512]{2,1,0:T(8,128)(2,1)} %take.4), channel_id=1, source_target_pairs={{0,8},{8,0},{1,9},{9,1},{2,10},{10,2},{3,11},{11,3},{4,12},{12,4},... | collective-permute-start | bytes 589832 | tf_op jit(solution)/shard_map/ppermute | solution.py:588
  448.5 17.5 %all-to-all-start.5 = ((f32[16,1,1088]{2,1,0:T(1,128)}), f32[16,1,1088]{2,1,0:T(1,128)S(1)}, u32[]{:S(2)}, u32[]{:S(2)}) async-start(f32[16,1,1088]{2,1,0:T(1,128)} %copy.127), calls=%async_computation.5 | async-start | bytes 147456 | tf_op jit(solution)/shard_map/all_to_all | solution.py:829
  456.0 15.6 %collective-permute-start.37 = (bf16[32,4096]{1,0:T(8,128)(2,1)S(1)}, bf16[32,4096]{1,0:T(8,128)(2,1)S(1)}, u32[]{:S(2)}, u32[]{:S(2)}) collective-permute-start(bf16[32,4096]{1,0:T(8,128)(2,1)S(1)} %fusion.27), channel_id=1, source_target_pairs={{0,4},{4,0},{1,5},{5,1},{2,6},{6,2},{3,7},{7,3},{8,12},{12,8},{9,1... | collective-permute-start | bytes 786440 | tf_op jit(solution)/shard_map/ppermute | solution.py:588
  477.1 14.5 %collective-permute-start.43 = (bf16[32,4096]{1,0:T(8,128)(2,1)S(1)}, bf16[32,4096]{1,0:T(8,128)(2,1)S(1)}, u32[]{:S(2)}, u32[]{:S(2)}) collective-permute-start(bf16[32,4096]{1,0:T(8,128)(2,1)S(1)} %fusion.26), channel_id=1, source_target_pairs={{0,16},{16,0},{1,17},{17,1},{2,18},{18,2},{3,19},{19,3},{4,20},{20... | collective-permute-start | bytes 786440 | tf_op jit(solution)/shard_map/ppermute | solution.py:588
  (66 other events, 768.2 us)

commit v6 on v5

--- a/solution.py
+++ b/solution.py
@@ -659,9 +659,7 @@
     def to_sample(x):
         return jnp.concatenate([pick(x, zh), swap(pick(x, 1 - zh), "zh")])
 
-    def to_band(x):
-        own = x[:half]
-        other = swap(x[half:].astype(bf16), "zh").astype(x.dtype)
+    def by_band(own, other):
         return jnp.where(zh == 0, jnp.stack([own, other]), jnp.stack([other, own]))
 
     def gather(x):
@@ -707,7 +705,6 @@
         if not last:
             inputs, n1, r1, normed = after
     carried = after[0]
-    result = to_band(carried)
 
     grad = out_grad
     small = None
@@ -756,11 +753,11 @@
             )
             x_core = swap(x_other, "core")
             samp = ("samp",) * two
-            z_terms = pin((z_own, z_core), x_other)
+            d_terms = pin((d_own, d_core), x_other)
+            down_share = Share([split_rows(t, two) for t in d_terms], names + samp)
+            z_terms = pin((z_own, z_core), down_share.halve("samp"))
             z_share = Share([split_rows(t, two) for t in z_terms], names + samp)
-            d_terms = pin((d_own, d_core), z_share.halve("zl"))
-            down_share = Share([split_rows(t, two) for t in d_terms], names + samp)
-            x_terms = pin((x_own, x_core), down_share.halve("samp"))
+            x_terms = pin((x_own, x_core), z_share.halve("zl"))
             x_share = Share([split_rows(t, two) for t in x_terms], names + samp)
             own_grad = pin(own_grad, x_share.halve(x_axes[0]))
             heads = W // HD
@@ -778,10 +775,12 @@
             sent = [x_share.halve("samp"), z_share.halve("samp")] + [down_share.halve("zh")]
             d_heads = pin(d_heads, *sent)
         else:
-            own_grad, send_row, keep_rows = pin((own_grad, send_row, keep_rows), result)
+            result = swap(pin(carried[half:], sent), "zh")
+            own_grad, send_row, keep_rows = pin((own_grad, send_row, keep_rows))
             later = (down_grad, activated, hidden_grad, normed_two, branch_grad, attended)
             owns[index] = own_part(index)
-            d_heads = attend_back(*owns[index], own_grad, members)
+            d_heads, result = pin((attend_back(*owns[index], own_grad, members), result))
+            result = by_band(carried[:half], result)
         back = lax.all_to_all(d_heads, low, 0, 0, tiled=True)
         w_heads = grad_heads(d_heads, normed_all, w_heads, bf16 if last else f32)
         if last:
@@ -802,7 +801,7 @@
             back = pin(back, *[down_share.halve(a) for a in x_axes])
         else:
             owns[0] = own_part(0)
-            back = pin(back, w_heads, *owns[0])
+            back = pin(back, w_heads, result, *owns[0])
         grad, low_grad, sums_one, sums_qv = qkv_backward(
             back, w_qkv, middle_grad, n1, r1, ln1_gain, half if last else rows
         )

time: 499 us -> 503 us (level)
    unnamed x96 -> x104, local copies, waits for them, and re-layouts: 12.7 us -> 13.3 us
  transfers between devices with their start and end apart: 50 -> 50, of which waited for: 20 -> 20; matrix products, arithmetic and copies ran while one was open for 13% -> 12% of each run, Pallas kernels for 23% -> 26%
where the time goes in v6:
time: 503 us; the launch traced here: 497 us
  Pallas kernels  236 us (47%)
  waiting for transfers between devices  101 us (20%)
  starting transfers between devices  67.6 us (13%)
  other arithmetic  46.4 us (9%)
  local copies, waits for them, and re-layouts  30.5 us (6%)
  matrix products  11.4 us (2%)
    pallas_call x3, Pallas kernels, attend_back(): pl.pallas_call(functools.partial(attend_back_kernel, heads=heads, some=so...  69.6 us
    ppermute x44, waiting for transfers between devices, swap(): return lax.ppermute(x, axis, SWAP)  64.9 us
    pallas_call x2, Pallas kernels, attend(): pl.pallas_call(attend_kernel, grid=(width // block,), in_specs=[own, spec...  46.4 us
    ppermute x44, starting transfers between devices, swap(): return lax.ppermute(x, axis, SWAP)  42.4 us
    pallas_call x2, Pallas kernels, block_backward(): pl.pallas_call(functools.partial(block_backward_kernel, grads=bool(grads)...  40.1 us
    convert_element_type x12, other arithmetic, halve(): sent = total(there).astype(bf16)  29.8 us
    pallas_call x2, Pallas kernels, block_forward(): pl.pallas_call(functools.partial(block_forward_kernel, last=last), grid=(...  25.3 us
    all_to_all x2, waiting for transfers between devices, body(): back = lax.all_to_all(d_heads, low, 0, 0, tiled=True)  24.3 us
  transfers between devices with their start and end apart: 50, of which 20 were waited for; matrix products, arithmetic and copies ran while one was open for 12% of the time, Pallas kernels for 26%

profile of v6, /device:TPU:0, one launch (start us, length us, event | category | flops | bytes accessed | tf_op | source)
XLA Modules:
  0.0 497.4 jit_solution(5559595271518107532)
XLA Ops:
  11.3 6.5 %collective-permute-done = bf16[128,1024]{1,0:T(8,128)(2,1)S(1)} collective-permute-done((bf16[128,1024]{1,0:T(8,128)(2,1)S(1)}, bf16[128,1024]{1,0:T(8,128)(2,1)S(1)}, u32[]{:S(2)}, u32[]{:S(2)}) %collective-permute-start) | collective-permute-done | bytes 262176 | tf_op jit(solution)/shard_map/ppermute | solution.py:588
  23.5 8.8 %collective-permute-done.2 = bf16[256,1024]{1,0:T(8,128)(2,1)S(1)} collective-permute-done((bf16[256,1024]{1,0:T(8,128)(2,1)S(1)}, bf16[256,1024]{1,0:T(8,128)(2,1)S(1)}, u32[]{:S(2)}, u32[]{:S(2)}) %collective-permute-start.2) | collective-permute-done | bytes 524320 | tf_op jit(solution)/shard_map/ppermute | solution.py:588
  46.3 23.4 %attend.2.a_ref.r0 = bf16[256,1024]{1,0:T(8,128)(2,1)S(1)} custom-call(bf16[256,1024]{1,0:T(8,128)(2,1)S(1)} %fusion.17.q_ref, bf16[2048,1024]{1,0:T(8,128)(2,1)S(1)} %constant_dynamic-update-slice_fusion.10.n_ref, bf16[1024,3072]{1,0:T(8,128)(2,1)S(1)} %copy-done.2, bf16[1024,3072]{1,0:T(8,128)(2,1)S(1)} %copy-done.2, f32[1,1024]{1,0:T(1,128)S(1)} %bitcast.257), custom_call_target="tpu_custom_call" | custom-call | flops 27599998976 | bytes 1000 | tf_op jit(solution)/shard_map/attend/pallas_call | solution.py:64
  70.0 12.8 %block_forward.2 = (f32[256,1024]{1,0:T(8,128)S(1)}, f32[256,1]{1,0:T(8,128)S(1)}, bf16[256,1024]{1,0:T(8,128)(2,1)S(1)}, f32[256,4096]{1,0:T(8,128)S(1)}, bf16[...) custom-call(f32[256,1024]{1,0:T(8,128)S(1)} %get-tuple-element.264.x, ...), custom_call_target="tpu_custom_call" | custom-call | flops 13799999488 | bytes 1000 | tf_op jit(solution)/shard_map/block_forward/pallas_call | solution.py:235
  90.8 9.4 %collective-permute-done.12 = bf16[256,1024]{1,0:T(8,128)(2,1)S(1)} collective-permute-done((bf16[256,1024]{1,0:T(8,128)(2,1)S(1)}, bf16[256,1024]{1,0:T(8,128)(2,1)S(1)}, u32[]{:S(2)}, u32[]{:S(2)}) %collective-permute-start.12) | collective-permute-done | bytes 524320 | tf_op jit(solution)/shard_map/ppermute | solution.py:588
  110.0 23.0 %attend.3.a_ref.r1 = bf16[256,1024]{1,0:T(8,128)(2,1)S(1)} custom-call(bf16[256,1024]{1,0:T(8,128)(2,1)S(1)} %fusion.14.q_ref, bf16[2048,1024]{1,0:T(8,128)(2,1)S(1)} %constant_dynamic-update-slice_fusion.n_ref, bf16[1024,3072]{1,0:T(8,128)(2,1)S(1)} %copy-done.2, bf16[1024,3072]{1,0:T(8,128)(2,1)S(1)} %copy-done.2, f32[1,1024]{1,0:T(1,128)S(1)} %bitcast.258), custom_call_target="tpu_custom_call" | custom-call | flops 27599998976 | bytes 1000 | tf_op jit(solution)/shard_map/attend/pallas_call | solution.py:64
  133.0 12.6 %block_forward.3 = (f32[256,1024]{1,0:T(8,128)S(1)}, f32[256,1]{1,0:T(8,128)S(1)}, bf16[256,1024]{1,0:T(8,128)(2,1)S(1)}, f32[256,4096]{1,0:T(8,128)S(1)}, bf16[...) custom-call(f32[256,1024]{1,0:T(8,128)S(1)} %copy-done.24, bf16[256,1024]{1,0:T(8,128)(2,1)S(1)} %attend.3.a_ref.r1, ...), custom_call_target="tpu_custom_call" | custom-call | flops 13799999488 | bytes 1000 | tf_op jit(solution)/shard_map/block_forward/pallas_call | solution.py:235
  148.6 17.4 %block_backward.2 = (bf16[256,4096]{1,0:T(8,128)(2,1)}, f32[1,4096]{1,0:T(1,128)S(1)}, f32[256,1024]{1,0:T(8,128)S(1)}, bf16[256,1024]{1,0:T(8,128)(2,1)S(1)}, b...) custom-call(s32[1]{0:T(128)} %bitcast.15.c_ref, f32[256,1024]{1,0:T(8,128)S(1)} %pad_maximum_fusion.grad_ref, ...), custom_call_target="tpu_custom_call" | custom-call | flops 16099999744 | bytes 1000 | tf_op jit(solution)/shard_map/block_backward/pallas_call | solution.py:333
  174.3 4.5 add_convert_fusion.3
  180.1 6.1 %all-to-all-done = bf16[8,256,128]{2,1,0:T(8,128)(2,1)S(1)} async-done(((bf16[8,256,128]{2,1,0:T(8,128)(2,1)}), bf16[8,256,128]{2,1,0:T(8,128)(2,1)S(1)}, u32[]{:S(2)}, u32[]{:S(2)}) %all-to-all-start) | async-done | bytes 524320 | tf_op jit(solution)/shard_map/all_to_all | solution.py:744
  187.0 31.9 %attend_back.3.d_ref = bf16[8,3,256,128]{3,2,1,0:T(8,128)(2,1)} custom-call(bf16[2048,128]{1,0:T(8,128)(2,1)} %get-tuple-element.258.q_ref, bf16[2048,128]{1,0:T(8,128)(2,1)} %get-tuple-element.257.k_ref, bf16[2048,128]{1,0:T(8,128)(2,1)} %get-tuple-element.256.v_ref, bf16[2048,128]{1,0:T(8,128)(2,1)} %bitcast.292), custom_call_target="tpu_custom_call" | custom-call | flops 37950001152 | bytes 1000 | tf_op jit(solution)/shard_map/attend_back/pallas_call | solution.py:134
  223.5 4.6 add_convert_fusion.2
  231.1 5.9 %grad_heads.2.rest_0_ = f32[3,128,1024]{2,1,0:T(8,128)} custom-call(bf16[8,3,256,128]{3,2,1,0:T(8,128)(2,1)} %attend_back.3.d_ref, bf16[2048,1024]{1,0:T(8,128)(2,1)} %copy-done.1), custom_call_target="tpu_custom_call" | custom-call | flops 5750000128 | bytes 1000 | tf_op jit(solution)/shard_map/grad_heads/pallas_call | solution.py:460
  237.0 6.9 %all-to-all-done.1.b_ref = bf16[8,3,256,128]{3,2,1,0:T(8,128)(2,1)S(1)} async-done(((bf16[8,3,256,128]{3,2,1,0:T(8,128)(2,1)}), bf16[8,3,256,128]{3,2,1,0:T(8,128)(2,1)S(1)}, u32[]{:S(2)}, u32[]{:S(2)}) %all-to-all-start.1) | async-done | bytes 1572896 | tf_op jit(solution)/shard_map/all_to_all | solution.py:784
  245.1 9.0 %qkv_backward.2 = (f32[256,1024]{1,0:T(8,128)}, bf16[256,1024]{1,0:T(8,128)(2,1)}, f32[8,1024]{1,0:T(8,128)}, f32[8,1024]{1,0:T(8,128)}) custom-call(bf16[8,3,256,128]{3,2,1,0:T(8,128)(2,1)} %copy-done.32, bf16[1024,3072]{1,0:T(8,128)(2,1)} %wv_ref.7, bf16[1024,3072]{1,0:T(8,128)(2,1)} %wv_ref.7, bf16[1024,3072]{1,0:T(8,128)(2,1)} %wv_ref.7, ...), custom_call_target="tpu_custom_call" | custom-call | flops 13799999488 | bytes 1000 | tf_op jit(solution)/shard_map/qkv_backward/pallas_call | solution.py:424
  254.1 22.8 %block_backward.3 = (bf16[256,4096]{1,0:T(8,128)(2,1)}, f32[1,4096]{1,0:T(1,128)}, f32[256,1024]{1,0:T(8,128)}, bf16[256,1024]{1,0:T(8,128)(2,1)}, bf16[8,256,12...) custom-call(s32[1]{0:T(128)} %bitcast.15.c_ref, ...), custom_call_target="tpu_custom_call" | custom-call | flops 20700000256 | bytes 1000 | tf_op jit(solution)/shard_map/block_backward/pallas_call | solution.py:333
  276.9 10.9 %grad_rows.1 = (bf16[8,64,4096]{2,1,0:T(8,128)(2,1)}, bf16[8,64,4096]{2,1,0:T(8,128)(2,1)}) custom-call(s32[1]{0:T(128)} %bitcast.15.c_ref, bf16[256,1024]{1,0:T(8,128)(2,1)} %convert_element_type.449.l1, bf16[256,1024]{1,0:T(8,128)(2,1)} %get-tuple-element.137.l0, bf16[256,4096]{1,0:T(8,128)(2,1)} %copy-done.19, bf16[256,4096]{1,0:T(8,128)(2,1)} %copy-done.18), custom_call_target="tpu_custom_call" | custom-call | flops 9200000000 | bytes 1000 | tf_op jit(solution)/shard_map/grad_rows/pallas_call | solution.py:167
  288.0 5.0 %grad_out.1 = (bf16[8,192,1024]{2,1,0:T(8,128)(2,1)}, bf16[8,192,1024]{2,1,0:T(8,128)(2,1)}) custom-call(s32[1]{0:T(128)} %bitcast.15.c_ref, bf16[256,1024]{1,0:T(8,128)(2,1)} %copy-done.15, bf16[256,1024]{1,0:T(8,128)(2,1)} %get-tuple-element.141.l0, bf16[256,1024]{1,0:T(8,128)(2,1)} %copy-done.14, ...), custom_call_target="tpu_custom_call", output_to_operand_aliasing={{0}: (5, {}), {1}: (6, {})} | custom-call | flops 3449999872 | bytes 1000 | tf_op jit(solution)/shard_map/grad_out/pallas_call | solution.py:370
  293.5 4.6 all-to-all-start.2
  298.2 4.5 fusion
  312.4 18.5 %attend_back.4.rest_0_ = bf16[8,3,256,128]{3,2,1,0:T(8,128)(2,1)} custom-call(bf16[2048,128]{1,0:T(8,128)(2,1)} %get-tuple-element.255.q_ref, bf16[2048,128]{1,0:T(8,128)(2,1)} %get-tuple-element.254.k_ref, bf16[2048,128]{1,0:T(8,128)(2,1)} %get-tuple-element.253.v_ref, bf16[2048,128]{1,0:T(8,128)(2,1)} %bitcast.22.do_ref), custom_call_target="tpu_custom_call" | custom-call | flops 19549999104 | bytes 1000 | tf_op jit(solution)/shard_map/attend_back/pallas_call | solution.py:134
  334.8 19.1 %attend_back.5.d_ref = bf16[8,3,256,128]{3,2,1,0:T(8,128)(2,1)} custom-call(bf16[2048,128]{1,0:T(8,128)(2,1)} %get-tuple-element.255.q_ref, bf16[2048,128]{1,0:T(8,128)(2,1)} %get-tuple-element.254.k_ref, bf16[2048,128]{1,0:T(8,128)(2,1)} %get-tuple-element.253.v_ref, bf16[2048,128]{1,0:T(8,128)(2,1)} %bitcast.22.do_ref, ...), custom_call_target="tpu_custom_call" | custom-call | flops 19549999104 | bytes 1000 | tf_op jit(solution)/shard_map/attend_back/pallas_call | solution.py:134
  353.9 6.4 %collective-permute-done.25 = bf16[2,2,64,1024]{3,2,1,0:T(8,128)(2,1)S(1)} collective-permute-done((bf16[2,2,64,1024]{3,2,1,0:T(8,128)(2,1)}, bf16[2,2,64,1024]{3,2,1,0:T(8,128)(2,1)S(1)}, u32[]{:S(2)}, u32[]{:S(2)}) %collective-permute-start.25) | collective-permute-done | bytes 524320 | tf_op jit(solution)/shard_map/ppermute | solution.py:588
  378.1 6.0 %grad_heads.3 = bf16[3,128,1024]{2,1,0:T(8,128)(2,1)} custom-call(bf16[8,3,256,128]{3,2,1,0:T(8,128)(2,1)} %attend_back.5.d_ref, bf16[2048,1024]{1,0:T(8,128)(2,1)} %copy-done, f32[3,128,1024]{2,1,0:T(8,128)} %grad_heads.2.rest_0_), custom_call_target="tpu_custom_call" | custom-call | flops 5750000128 | bytes 1000 | tf_op jit(solution)/shard_map/grad_heads/pallas_call | solution.py:460
  387.3 17.4 %all-to-all-done.3.b_ref = bf16[8,3,256,128]{3,2,1,0:T(8,128)(2,1)} async-done(((bf16[8,3,256,128]{3,2,1,0:T(8,128)(2,1)}), bf16[8,3,256,128]{3,2,1,0:T(8,128)(2,1)}, u32[]{:S(2)}, u32[]{:S(2)}) %all-to-all-start.3) | async-done | bytes 1572896 | tf_op jit(solution)/shard_map/all_to_all | solution.py:784
  413.2 4.4 all-to-all-start.4
  417.6 9.1 %collective-permute-done.28 = bf16[2,2,32,4096]{3,2,1,0:T(8,128)(2,1)} collective-permute-done((bf16[2,2,32,4096]{3,2,1,0:T(8,128)(2,1)}, bf16[2,2,32,4096]{3,2,1,0:T(8,128)(2,1)}, u32[]{:S(2)}, u32[]{:S(2)}) %collective-permute-start.28) | collective-permute-done | bytes 1048608 | tf_op jit(solution)/shard_map/ppermute | solution.py:588
  431.0 8.9 %qkv_backward.3 = (f32[256,1024]{1,0:T(8,128)}, bf16[128,1024]{1,0:T(8,128)(2,1)}, f32[8,1024]{1,0:T(8,128)}, f32[8,1024]{1,0:T(8,128)}) custom-call(bf16[8,3,256,128]{3,2,1,0:T(8,128)(2,1)} %all-to-all-done.3.b_ref, bf16[1024,3072]{1,0:T(8,128)(2,1)} %wv_ref.7, bf16[1024,3072]{1,0:T(8,128)(2,1)} %wv_ref.7, bf16[1024,3072]{1,0:T(8,128)(2,1)} %wv_ref.7, ...), custom_call_target="tpu_custom_call" | custom-call | flops 13799999488 | bytes 1000 | tf_op jit(solution)/shard_map/qkv_backward/pallas_call | solution.py:424
  452.7 4.3 all-to-all-start.5
  465.0 5.3 %all-to-all-done.5 = f32[16,1,1088]{2,1,0:T(1,128)S(1)} async-done(((f32[16,1,1088]{2,1,0:T(1,128)}), f32[16,1,1088]{2,1,0:T(1,128)S(1)}, u32[]{:S(2)}, u32[]{:S(2)}) %all-to-all-start.5) | async-done | bytes 69664 | tf_op jit(solution)/shard_map/all_to_all | solution.py:828
  470.3 5.5 %collective-permute-done.37 = bf16[32,4096]{1,0:T(8,128)(2,1)S(1)} collective-permute-done((bf16[32,4096]{1,0:T(8,128)(2,1)S(1)}, bf16[32,4096]{1,0:T(8,128)(2,1)S(1)}, u32[]{:S(2)}, u32[]{:S(2)}) %collective-permute-start.37) | collective-permute-done | bytes 262176 | tf_op jit(solution)/shard_map/ppermute | solution.py:588
  486.3 5.3 %collective-permute-done.41 = bf16[96,1024]{1,0:T(8,128)(2,1)S(1)} collective-permute-done((bf16[96,1024]{1,0:T(8,128)(2,1)S(1)}, bf16[96,1024]{1,0:T(8,128)(2,1)S(1)}, u32[]{:S(2)}, u32[]{:S(2)}) %collective-permute-start.41) | collective-permute-done | bytes 196640 | tf_op jit(solution)/shard_map/ppermute | solution.py:588
  (297 shorter events, 152.1 us)
Async XLA Ops:
  1.8 16.0 %collective-permute-start = (bf16[128,1024]{1,0:T(8,128)(2,1)S(1)}, bf16[128,1024]{1,0:T(8,128)(2,1)S(1)}, u32[]{:S(2)}, u32[]{:S(2)}) collective-permute-start(bf16[128,1024]{1,0:T(8,128)(2,1)S(1)} %get-tuple-element.270), channel_id=1, source_target_pairs={{0,8},{8,0},{1,9},{9,1},{2,10},{10,2},{3,11},{11,3},{4,12},{12,4},... | collective-permute-start | bytes 786440 | tf_op jit(solution)/shard_map/ppermute | solution.py:588
  19.1 13.2 %collective-permute-start.2 = (bf16[256,1024]{1,0:T(8,128)(2,1)S(1)}, bf16[256,1024]{1,0:T(8,128)(2,1)S(1)}, u32[]{:S(2)}, u32[]{:S(2)}) collective-permute-start(bf16[256,1024]{1,0:T(8,128)(2,1)S(1)} %get-tuple-element.249), channel_id=1, source_target_pairs={{0,4},{4,0},{1,5},{5,1},{2,6},{6,2},{3,7},{7,3},{8,12},{12,8},{9,1... | collective-permute-start | bytes 1572872 | tf_op jit(solution)/shard_map/ppermute | solution.py:588
  19.9 13.7 %collective-permute-start.1 = (bf16[256,1024]{1,0:T(8,128)(2,1)S(1)}, bf16[256,1024]{1,0:T(8,128)(2,1)S(1)}, u32[]{:S(2)}, u32[]{:S(2)}) collective-permute-start(bf16[256,1024]{1,0:T(8,128)(2,1)S(1)} %get-tuple-element.249), channel_id=1, source_target_pairs={{0,2},{2,0},{1,3},{3,1},{4,6},{6,4},{5,7},{7,5},{8,10},{10,8},{9,1... | collective-permute-start | bytes 1572872 | tf_op jit(solution)/shard_map/ppermute | solution.py:588
  22.7 18.2 %collective-permute-start.5 = (bf16[256,1024]{1,0:T(8,128)(2,1)S(1)}, bf16[256,1024]{1,0:T(8,128)(2,1)S(1)}, u32[]{:S(2)}, u32[]{:S(2)}) collective-permute-start(bf16[256,1024]{1,0:T(8,128)(2,1)S(1)} %get-tuple-element.249), channel_id=1, source_target_pairs={{0,1},{1,0},{2,3},{3,2},{4,5},{5,4},{6,7},{7,6},{8,9},{9,8},{10,11... | collective-permute-start | bytes 1572872 | tf_op jit(solution)/shard_map/ppermute | solution.py:588
  42.5 27.2 %collective-permute-start.10 = (f32[128,1024]{1,0:T(8,128)S(1)}, f32[128,1024]{1,0:T(8,128)S(1)}, u32[]{:S(2)}, u32[]{:S(2)}) collective-permute-start(f32[128,1024]{1,0:T(8,128)S(1)} %get-tuple-element.260), channel_id=1, source_target_pairs={{0,8},{8,0},{1,9},{9,1},{2,10},{10,2},{3,11},{11,3},{4,12},{12,4},... | collective-permute-start | bytes 1572872 | tf_op jit(solution)/shard_map/ppermute | solution.py:588
  86.5 13.7 %collective-permute-start.12 = (bf16[256,1024]{1,0:T(8,128)(2,1)S(1)}, bf16[256,1024]{1,0:T(8,128)(2,1)S(1)}, u32[]{:S(2)}, u32[]{:S(2)}) collective-permute-start(bf16[256,1024]{1,0:T(8,128)(2,1)S(1)} %get-tuple-element.111), channel_id=1, source_target_pairs={{0,4},{4,0},{1,5},{5,1},{2,6},{6,2},{3,7},{7,3},{8,12},{12,8},{9,1... | collective-permute-start | bytes 1572872 | tf_op jit(solution)/shard_map/ppermute | solution.py:588
  88.0 13.4 %collective-permute-start.11 = (bf16[256,1024]{1,0:T(8,128)(2,1)S(1)}, bf16[256,1024]{1,0:T(8,128)(2,1)S(1)}, u32[]{:S(2)}, u32[]{:S(2)}) collective-permute-start(bf16[256,1024]{1,0:T(8,128)(2,1)S(1)} %get-tuple-element.111), channel_id=1, source_target_pairs={{0,2},{2,0},{1,3},{3,1},{4,6},{6,4},{5,7},{7,5},{8,10},{10,8},{9,1... | collective-permute-start | bytes 1572872 | tf_op jit(solution)/shard_map/ppermute | solution.py:588
  90.0 18.4 %collective-permute-start.15 = (bf16[256,1024]{1,0:T(8,128)(2,1)S(1)}, bf16[256,1024]{1,0:T(8,128)(2,1)S(1)}, u32[]{:S(2)}, u32[]{:S(2)}) collective-permute-start(bf16[256,1024]{1,0:T(8,128)(2,1)S(1)} %get-tuple-element.111), channel_id=1, source_target_pairs={{0,1},{1,0},{2,3},{3,2},{4,5},{5,4},{6,7},{7,6},{8,9},{9,8},{10,11... | collective-permute-start | bytes 1572872 | tf_op jit(solution)/shard_map/ppermute | solution.py:588
  167.7 18.5 %all-to-all-start = ((bf16[8,256,128]{2,1,0:T(8,128)(2,1)}), bf16[8,256,128]{2,1,0:T(8,128)(2,1)S(1)}, u32[]{:S(2)}, u32[]{:S(2)}) async-start(bf16[8,256,128]{2,1,0:T(8,128)(2,1)} %get-tuple-element.117), calls=%async_computation | async-start | bytes 1048576 | tf_op jit(solution)/shard_map/all_to_all | solution.py:744
  171.4 47.5 %collective-permute-start.20 = (bf16[128,1024]{1,0:T(8,128)(2,1)S(1)}, bf16[128,1024]{1,0:T(8,128)(2,1)S(1)}, u32[]{:S(2)}, u32[]{:S(2)}) collective-permute-start(bf16[128,1024]{1,0:T(8,128)(2,1)S(1)} %get-tuple-element.119), channel_id=1, source_target_pairs={{0,8},{8,0},{1,9},{9,1},{2,10},{10,2},{3,11},{11,3},{4,12},{12,4},... | collective-permute-start | bytes 786440 | tf_op jit(solution)/shard_map/ppermute | solution.py:588
  219.6 24.3 %all-to-all-start.1 = ((bf16[8,3,256,128]{3,2,1,0:T(8,128)(2,1)}), bf16[8,3,256,128]{3,2,1,0:T(8,128)(2,1)S(1)}, u32[]{:S(2)}, u32[]{:S(2)}) async-start(bf16[8,3,256,128]{3,2,1,0:T(8,128)(2,1)} %attend_back.3.d_ref), calls=%async_computation.1 | async-start | bytes 3145728 | tf_op jit(solution)/shard_map/all_to_all | solution.py:784
  293.0 15.8 %collective-permute-start.21 = (bf16[8,192,1024]{2,1,0:T(8,128)(2,1)}, bf16[8,192,1024]{2,1,0:T(8,128)(2,1)S(1)}, u32[]{:S(2)}, u32[]{:S(2)}) collective-permute-start(bf16[8,192,1024]{2,1,0:T(8,128)(2,1)} %get-tuple-element.145), channel_id=1, source_target_pairs={{0,1},{1,0},{2,3},{3,2},{4,5},{5,4},{6,7},{7,6},{8,9},{9,8},{10,11... | collective-permute-start | bytes 9437192 | tf_op jit(solution)/shard_map/ppermute | solution.py:588
  293.5 18.9 %all-to-all-start.2 = ((bf16[8,256,128]{2,1,0:T(8,128)(2,1)}), bf16[8,256,128]{2,1,0:T(8,128)(2,1)}, u32[]{:S(2)}, u32[]{:S(2)}) async-start(bf16[8,256,128]{2,1,0:T(8,128)(2,1)} %get-tuple-element.133), calls=%async_computation.2 | async-start | bytes 1048576 | tf_op jit(solution)/shard_map/all_to_all | solution.py:744
  302.7 57.7 %collective-permute-start.27 = (bf16[2,2,2,32,4096]{4,3,2,1,0:T(8,128)(2,1)}, bf16[2,2,2,32,4096]{4,3,2,1,0:T(8,128)(2,1)}, u32[]{:S(2)}, u32[]{:S(2)}) collective-permute-start(bf16[2,2,2,32,4096]{4,3,2,1,0:T(8,128)(2,1)} %fusion), channel_id=1, source_target_pairs={{0,16},{16,0},{1,17},{17,1},{2,18},{18,2},{3,19},{19,3},{4,20},{20... | collective-permute-start | bytes 6291464 | tf_op jit(solution)/shard_map/ppermute | solution.py:588
  306.8 25.6 %collective-permute-start.24 = (bf16[2,2,2,64,1024]{4,3,2,1,0:T(8,128)(2,1)}, bf16[2,2,2,64,1024]{4,3,2,1,0:T(8,128)(2,1)}, u32[]{:S(2)}, u32[]{:S(2)}) collective-permute-start(bf16[2,2,2,64,1024]{4,3,2,1,0:T(8,128)(2,1)} %fusion.20), channel_id=1, source_target_pairs={{0,4},{4,0},{1,5},{5,1},{2,6},{6,2},{3,7},{7,3},{8,12},{12,8},{9,1... | collective-permute-start | bytes 3145736 | tf_op jit(solution)/shard_map/ppermute | solution.py:588
  310.9 49.4 %collective-permute-start.26 = (bf16[2,2,2,96,1024]{4,3,2,1,0:T(8,128)(2,1)}, bf16[2,2,2,96,1024]{4,3,2,1,0:T(8,128)(2,1)}, u32[]{:S(2)}, u32[]{:S(2)}) collective-permute-start(bf16[2,2,2,96,1024]{4,3,2,1,0:T(8,128)(2,1)} %fusion.6), channel_id=1, source_target_pairs={{0,2},{2,0},{1,3},{3,1},{4,6},{6,4},{5,7},{7,5},{8,10},{10,8},{9,1... | collective-permute-start | bytes 4718600 | tf_op jit(solution)/shard_map/ppermute | solution.py:588
  334.8 25.5 %collective-permute-start.25 = (bf16[2,2,64,1024]{3,2,1,0:T(8,128)(2,1)}, bf16[2,2,64,1024]{3,2,1,0:T(8,128)(2,1)S(1)}, u32[]{:S(2)}, u32[]{:S(2)}) collective-permute-start(bf16[2,2,64,1024]{3,2,1,0:T(8,128)(2,1)} %fusion.22), channel_id=1, source_target_pairs={{0,8},{8,0},{1,9},{9,1},{2,10},{10,2},{3,11},{11,3},{4,12},{12,4},... | collective-permute-start | bytes 1572872 | tf_op jit(solution)/shard_map/ppermute | solution.py:588
  369.1 35.6 %all-to-all-start.3 = ((bf16[8,3,256,128]{3,2,1,0:T(8,128)(2,1)}), bf16[8,3,256,128]{3,2,1,0:T(8,128)(2,1)}, u32[]{:S(2)}, u32[]{:S(2)}) async-start(bf16[8,3,256,128]{3,2,1,0:T(8,128)(2,1)} %attend_back.5.d_ref), calls=%async_computation.3 | async-start | bytes 3145728 | tf_op jit(solution)/shard_map/all_to_all | solution.py:784
  376.0 28.7 %collective-permute-start.31 = (bf16[2,64,1024]{2,1,0:T(8,128)(2,1)}, bf16[2,64,1024]{2,1,0:T(8,128)(2,1)}, u32[]{:S(2)}, u32[]{:S(2)}) collective-permute-start(bf16[2,64,1024]{2,1,0:T(8,128)(2,1)} %fusion.28), channel_id=1, source_target_pairs={{0,16},{16,0},{1,17},{17,1},{2,18},{18,2},{3,19},{19,3},{4,20},{20... | collective-permute-start | bytes 786440 | tf_op jit(solution)/shard_map/ppermute | solution.py:588
  376.6 28.1 %collective-permute-start.30 = (bf16[2,2,96,1024]{3,2,1,0:T(8,128)(2,1)}, bf16[2,2,96,1024]{3,2,1,0:T(8,128)(2,1)}, u32[]{:S(2)}, u32[]{:S(2)}) collective-permute-start(bf16[2,2,96,1024]{3,2,1,0:T(8,128)(2,1)} %fusion.7), channel_id=1, source_target_pairs={{0,16},{16,0},{1,17},{17,1},{2,18},{18,2},{3,19},{19,3},{4,20},{20... | collective-permute-start | bytes 2359304 | tf_op jit(solution)/shard_map/ppermute | solution.py:588
  378.1 48.7 %collective-permute-start.28 = (bf16[2,2,32,4096]{3,2,1,0:T(8,128)(2,1)}, bf16[2,2,32,4096]{3,2,1,0:T(8,128)(2,1)}, u32[]{:S(2)}, u32[]{:S(2)}) collective-permute-start(bf16[2,2,32,4096]{3,2,1,0:T(8,128)(2,1)} %fusion.1), channel_id=1, source_target_pairs={{0,8},{8,0},{1,9},{9,1},{2,10},{10,2},{3,11},{11,3},{4,12},{12,4},... | collective-permute-start | bytes 3145736 | tf_op jit(solution)/shard_map/ppermute | solution.py:588
  386.2 24.0 %collective-permute-start.29 = (bf16[6,64,512]{2,1,0:T(8,128)(2,1)}, bf16[6,64,512]{2,1,0:T(8,128)(2,1)}, u32[]{:S(2)}, u32[]{:S(2)}) collective-permute-start(bf16[6,64,512]{2,1,0:T(8,128)(2,1)} %get-tuple-element.262), channel_id=1, source_target_pairs={{0,16},{16,0},{1,17},{17,1},{2,18},{18,2},{3,19},{19,3},{4,20},{20... | collective-permute-start | bytes 1179656 | tf_op jit(solution)/shard_map/ppermute | solution.py:588
  406.6 50.4 %collective-permute-start.36 = (bf16[64,1024]{1,0:T(8,128)(2,1)}, bf16[64,1024]{1,0:T(8,128)(2,1)S(1)}, u32[]{:S(2)}, u32[]{:S(2)}) collective-permute-start(bf16[64,1024]{1,0:T(8,128)(2,1)} %fusion.35), channel_id=1, source_target_pairs={{0,2},{2,0},{1,3},{3,1},{4,6},{6,4},{5,7},{7,5},{8,10},{10,8},{9,1... | collective-permute-start | bytes 393224 | tf_op jit(solution)/shard_map/ppermute | solution.py:588
  408.9 33.8 %collective-permute-start.32 = (bf16[2,96,1024]{2,1,0:T(8,128)(2,1)}, bf16[2,96,1024]{2,1,0:T(8,128)(2,1)}, u32[]{:S(2)}, u32[]{:S(2)}) collective-permute-start(bf16[2,96,1024]{2,1,0:T(8,128)(2,1)} %fusion.23), channel_id=1, source_target_pairs={{0,4},{4,0},{1,5},{5,1},{2,6},{6,2},{3,7},{7,3},{8,12},{12,8},{9,1... | collective-permute-start | bytes 1179656 | tf_op jit(solution)/shard_map/ppermute | solution.py:588
  413.2 34.6 %all-to-all-start.4 = ((bf16[16,64,512]{2,1,0:T(8,128)(2,1)}), bf16[16,64,512]{2,1,0:T(8,128)(2,1)}, u32[]{:S(2)}, u32[]{:S(2)}) async-start(bf16[16,64,512]{2,1,0:T(8,128)(2,1)} %take.3), calls=%async_computation.4 | async-start | bytes 2097152 | tf_op jit(solution)/shard_map/all_to_all | solution.py:799
  429.3 27.7 %collective-permute-start.35 = (bf16[2,32,4096]{2,1,0:T(8,128)(2,1)}, bf16[2,32,4096]{2,1,0:T(8,128)(2,1)}, u32[]{:S(2)}, u32[]{:S(2)}) collective-permute-start(bf16[2,32,4096]{2,1,0:T(8,128)(2,1)} %fusion.21), channel_id=1, source_target_pairs={{0,2},{2,0},{1,3},{3,1},{4,6},{6,4},{5,7},{7,5},{8,10},{10,8},{9,1... | collective-permute-start | bytes 1572872 | tf_op jit(solution)/shard_map/ppermute | solution.py:588
  439.9 30.4 %collective-permute-start.33 = (bf16[128,1024]{1,0:T(8,128)(2,1)}, bf16[128,1024]{1,0:T(8,128)(2,1)S(1)}, u32[]{:S(2)}, u32[]{:S(2)}) collective-permute-start(bf16[128,1024]{1,0:T(8,128)(2,1)} %get-tuple-element.184), channel_id=1, source_target_pairs={{0,8},{8,0},{1,9},{9,1},{2,10},{10,2},{3,11},{11,3},{4,12},{12,4},... | collective-permute-start | bytes 786440 | tf_op jit(solution)/shard_map/ppermute | solution.py:588
  444.8 25.5 %collective-permute-start.38 = (bf16[96,1024]{1,0:T(8,128)(2,1)}, bf16[96,1024]{1,0:T(8,128)(2,1)S(1)}, u32[]{:S(2)}, u32[]{:S(2)}) collective-permute-start(bf16[96,1024]{1,0:T(8,128)(2,1)} %fusion.31), channel_id=1, source_target_pairs={{0,8},{8,0},{1,9},{9,1},{2,10},{10,2},{3,11},{11,3},{4,12},{12,4},... | collective-permute-start | bytes 589832 | tf_op jit(solution)/shard_map/ppermute | solution.py:588
  450.4 19.9 %collective-permute-start.34 = (bf16[3,64,512]{2,1,0:T(8,128)(2,1)}, bf16[3,64,512]{2,1,0:T(8,128)(2,1)S(1)}, u32[]{:S(2)}, u32[]{:S(2)}) collective-permute-start(bf16[3,64,512]{2,1,0:T(8,128)(2,1)} %take.4), channel_id=1, source_target_pairs={{0,8},{8,0},{1,9},{9,1},{2,10},{10,2},{3,11},{11,3},{4,12},{12,4},... | collective-permute-start | bytes 589832 | tf_op jit(solution)/shard_map/ppermute | solution.py:588
  452.7 17.5 %all-to-all-start.5 = ((f32[16,1,1088]{2,1,0:T(1,128)}), f32[16,1,1088]{2,1,0:T(1,128)S(1)}, u32[]{:S(2)}, u32[]{:S(2)}) async-start(f32[16,1,1088]{2,1,0:T(1,128)} %copy.127), calls=%async_computation.5 | async-start | bytes 147456 | tf_op jit(solution)/shard_map/all_to_all | solution.py:828
  460.4 15.5 %collective-permute-start.37 = (bf16[32,4096]{1,0:T(8,128)(2,1)S(1)}, bf16[32,4096]{1,0:T(8,128)(2,1)S(1)}, u32[]{:S(2)}, u32[]{:S(2)}) collective-permute-start(bf16[32,4096]{1,0:T(8,128)(2,1)S(1)} %fusion.27), channel_id=1, source_target_pairs={{0,4},{4,0},{1,5},{5,1},{2,6},{6,2},{3,7},{7,3},{8,12},{12,8},{9,1... | collective-permute-start | bytes 786440 | tf_op jit(solution)/shard_map/ppermute | solution.py:588
  481.6 14.5 %collective-permute-start.43 = (bf16[32,4096]{1,0:T(8,128)(2,1)S(1)}, bf16[32,4096]{1,0:T(8,128)(2,1)S(1)}, u32[]{:S(2)}, u32[]{:S(2)}) collective-permute-start(bf16[32,4096]{1,0:T(8,128)(2,1)S(1)} %fusion.26), channel_id=1, source_target_pairs={{0,16},{16,0},{1,17},{17,1},{2,18},{18,2},{3,19},{19,3},{4,20},{20... | collective-permute-start | bytes 786440 | tf_op jit(solution)/shard_map/ppermute | solution.py:588
  (70 other events, 863.0 us)

commit v7 on v4

--- a/solution.py
+++ b/solution.py
@@ -756,11 +756,11 @@
             )
             x_core = swap(x_other, "core")
             samp = ("samp",) * two
-            z_terms = pin((z_own, z_core), x_other)
+            d_terms = pin((d_own, d_core), x_other)
+            down_share = Share([split_rows(t, two) for t in d_terms], names + samp)
+            z_terms = pin((z_own, z_core), down_share.halve("samp"))
             z_share = Share([split_rows(t, two) for t in z_terms], names + samp)
-            d_terms = pin((d_own, d_core), z_share.halve("zl"))
-            down_share = Share([split_rows(t, two) for t in d_terms], names + samp)
-            x_terms = pin((x_own, x_core), down_share.halve("samp"))
+            x_terms = pin((x_own, x_core), z_share.halve("zl"))
             x_share = Share([split_rows(t, two) for t in x_terms], names + samp)
             own_grad = pin(own_grad, x_share.halve(x_axes[0]))
             heads = W // HD

time: 498 us -> 498 us (level)
    unnamed x96 -> x98, local copies, waits for them, and re-layouts: 12.7 us -> 12.5 us
  transfers between devices with their start and end apart: 50 -> 50, of which waited for: 21 -> 21; matrix products, arithmetic and copies ran while one was open for 13% -> 12% of each run, Pallas kernels for 23% -> 23%
where the time goes in v7:
time: 498 us; the launch traced here: 492 us
  Pallas kernels  235 us (47%)
  waiting for transfers between devices  92.4 us (19%)
  starting transfers between devices  72.4 us (15%)
  other arithmetic  46.4 us (9%)
  local copies, waits for them, and re-layouts  29.6 us (6%)
  matrix products  11.4 us (2%)
    pallas_call x3, Pallas kernels, attend_back(): pl.pallas_call(functools.partial(attend_back_kernel, heads=heads, some=so...  69.5 us
    ppermute x44, waiting for transfers between devices, swap(): return lax.ppermute(x, axis, SWAP)  64.1 us
    pallas_call x2, Pallas kernels, attend(): pl.pallas_call(attend_kernel, grid=(width // block,), in_specs=[own, spec...  46.5 us
    ppermute x44, starting transfers between devices, swap(): return lax.ppermute(x, axis, SWAP)  46.4 us
    pallas_call x2, Pallas kernels, block_backward(): pl.pallas_call(functools.partial(block_backward_kernel, grads=bool(grads)...  39.4 us
    convert_element_type x12, other arithmetic, halve(): sent = total(there).astype(bf16)  29.8 us
    pallas_call x2, Pallas kernels, block_forward(): pl.pallas_call(functools.partial(block_forward_kernel, last=last), grid=(...  25.3 us
    pallas_call x2, Pallas kernels, qkv_backward(): pl.pallas_call(qkv_backward_kernel, grid=(members // at_once,), in_specs=...  17.9 us
  transfers between devices with their start and end apart: 50, of which 21 were waited for; matrix products, arithmetic and copies ran while one was open for 12% of the time, Pallas kernels for 23%

profile of v7, /device:TPU:0, one launch (start us, length us, event | category | flops | bytes accessed | tf_op | source)
XLA Modules:
  0.0 492.3 jit_solution(10661046151228910834)
XLA Ops:
  11.3 6.5 %collective-permute-done = bf16[128,1024]{1,0:T(8,128)(2,1)S(1)} collective-permute-done((bf16[128,1024]{1,0:T(8,128)(2,1)S(1)}, bf16[128,1024]{1,0:T(8,128)(2,1)S(1)}, u32[]{:S(2)}, u32[]{:S(2)}) %collective-permute-start) | collective-permute-done | bytes 262176 | tf_op jit(solution)/shard_map/ppermute | solution.py:588
  23.5 8.8 %collective-permute-done.2 = bf16[256,1024]{1,0:T(8,128)(2,1)S(1)} collective-permute-done((bf16[256,1024]{1,0:T(8,128)(2,1)S(1)}, bf16[256,1024]{1,0:T(8,128)(2,1)S(1)}, u32[]{:S(2)}, u32[]{:S(2)}) %collective-permute-start.2) | collective-permute-done | bytes 524320 | tf_op jit(solution)/shard_map/ppermute | solution.py:588
  46.3 23.4 %attend.2.a_ref.r0 = bf16[256,1024]{1,0:T(8,128)(2,1)S(1)} custom-call(bf16[256,1024]{1,0:T(8,128)(2,1)S(1)} %fusion.17.q_ref, bf16[2048,1024]{1,0:T(8,128)(2,1)S(1)} %constant_dynamic-update-slice_fusion.10.n_ref, bf16[1024,3072]{1,0:T(8,128)(2,1)S(1)} %copy-done.2, bf16[1024,3072]{1,0:T(8,128)(2,1)S(1)} %copy-done.2, f32[1,1024]{1,0:T(1,128)S(1)} %bitcast.257), custom_call_target="tpu_custom_call" | custom-call | flops 27599998976 | bytes 1000 | tf_op jit(solution)/shard_map/attend/pallas_call | solution.py:64
  70.0 12.8 %block_forward.2 = (f32[256,1024]{1,0:T(8,128)S(1)}, f32[256,1]{1,0:T(8,128)S(1)}, bf16[256,1024]{1,0:T(8,128)(2,1)S(1)}, f32[256,4096]{1,0:T(8,128)S(1)}, bf16[...) custom-call(f32[256,1024]{1,0:T(8,128)S(1)} %get-tuple-element.258.x, ...), custom_call_target="tpu_custom_call" | custom-call | flops 13799999488 | bytes 1000 | tf_op jit(solution)/shard_map/block_forward/pallas_call | solution.py:235
  90.8 9.4 %collective-permute-done.12 = bf16[256,1024]{1,0:T(8,128)(2,1)S(1)} collective-permute-done((bf16[256,1024]{1,0:T(8,128)(2,1)S(1)}, bf16[256,1024]{1,0:T(8,128)(2,1)S(1)}, u32[]{:S(2)}, u32[]{:S(2)}) %collective-permute-start.12) | collective-permute-done | bytes 524320 | tf_op jit(solution)/shard_map/ppermute | solution.py:588
  110.0 23.0 %attend.3.a_ref.r1 = bf16[256,1024]{1,0:T(8,128)(2,1)S(1)} custom-call(bf16[256,1024]{1,0:T(8,128)(2,1)S(1)} %fusion.14.q_ref, bf16[2048,1024]{1,0:T(8,128)(2,1)S(1)} %constant_dynamic-update-slice_fusion.n_ref, bf16[1024,3072]{1,0:T(8,128)(2,1)S(1)} %copy-done.2, bf16[1024,3072]{1,0:T(8,128)(2,1)S(1)} %copy-done.2, f32[1,1024]{1,0:T(1,128)S(1)} %bitcast.258), custom_call_target="tpu_custom_call" | custom-call | flops 27599998976 | bytes 1000 | tf_op jit(solution)/shard_map/attend/pallas_call | solution.py:64
  133.1 12.6 %block_forward.3 = (f32[256,1024]{1,0:T(8,128)S(1)}, f32[256,1]{1,0:T(8,128)S(1)}, bf16[256,1024]{1,0:T(8,128)(2,1)S(1)}, f32[256,4096]{1,0:T(8,128)S(1)}, bf16[...) custom-call(f32[256,1024]{1,0:T(8,128)S(1)} %copy-done.24, bf16[256,1024]{1,0:T(8,128)(2,1)S(1)} %attend.3.a_ref.r1, ...), custom_call_target="tpu_custom_call" | custom-call | flops 13799999488 | bytes 1000 | tf_op jit(solution)/shard_map/block_forward/pallas_call | solution.py:235
  151.4 16.6 %block_backward.2 = (bf16[256,4096]{1,0:T(8,128)(2,1)}, f32[1,4096]{1,0:T(1,128)S(1)}, f32[256,1024]{1,0:T(8,128)S(1)}, bf16[256,1024]{1,0:T(8,128)(2,1)S(1)}, b...) custom-call(s32[1]{0:T(128)} %bitcast.17.c_ref, f32[256,1024]{1,0:T(8,128)S(1)} %pad_maximum_fusion.grad_ref, ...), custom_call_target="tpu_custom_call" | custom-call | flops 16099999744 | bytes 1000 | tf_op jit(solution)/shard_map/block_backward/pallas_call | solution.py:333
  173.4 4.5 add_convert_fusion.2
  183.4 31.9 %attend_back.3.d_ref = bf16[8,3,256,128]{3,2,1,0:T(8,128)(2,1)} custom-call(bf16[2048,128]{1,0:T(8,128)(2,1)} %get-tuple-element.249.q_ref, bf16[2048,128]{1,0:T(8,128)(2,1)} %get-tuple-element.248.k_ref, bf16[2048,128]{1,0:T(8,128)(2,1)} %get-tuple-element.247.v_ref, bf16[2048,128]{1,0:T(8,128)(2,1)} %bitcast.292), custom_call_target="tpu_custom_call" | custom-call | flops 37950001152 | bytes 1000 | tf_op jit(solution)/shard_map/attend_back/pallas_call | solution.py:134
  219.2 4.5 add_convert_fusion.3
  225.8 5.9 %grad_heads.2.rest_0_ = f32[3,128,1024]{2,1,0:T(8,128)} custom-call(bf16[8,3,256,128]{3,2,1,0:T(8,128)(2,1)} %attend_back.3.d_ref, bf16[2048,1024]{1,0:T(8,128)(2,1)} %copy-done.1), custom_call_target="tpu_custom_call" | custom-call | flops 5750000128 | bytes 1000 | tf_op jit(solution)/shard_map/grad_heads/pallas_call | solution.py:460
  231.7 7.9 %all-to-all-done.1.b_ref = bf16[8,3,256,128]{3,2,1,0:T(8,128)(2,1)S(1)} async-done(((bf16[8,3,256,128]{3,2,1,0:T(8,128)(2,1)}), bf16[8,3,256,128]{3,2,1,0:T(8,128)(2,1)S(1)}, u32[]{:S(2)}, u32[]{:S(2)}) %all-to-all-start.1) | async-done | bytes 1572896 | tf_op jit(solution)/shard_map/all_to_all | solution.py:785
  240.8 9.0 %qkv_backward.2 = (f32[256,1024]{1,0:T(8,128)}, bf16[256,1024]{1,0:T(8,128)(2,1)}, f32[8,1024]{1,0:T(8,128)}, f32[8,1024]{1,0:T(8,128)}) custom-call(bf16[8,3,256,128]{3,2,1,0:T(8,128)(2,1)} %copy-done.32, bf16[1024,3072]{1,0:T(8,128)(2,1)} %wv_ref.7, bf16[1024,3072]{1,0:T(8,128)(2,1)} %wv_ref.7, bf16[1024,3072]{1,0:T(8,128)(2,1)} %wv_ref.7, ...), custom_call_target="tpu_custom_call" | custom-call | flops 13799999488 | bytes 1000 | tf_op jit(solution)/shard_map/qkv_backward/pallas_call | solution.py:424
  249.8 22.8 %block_backward.3 = (bf16[256,4096]{1,0:T(8,128)(2,1)}, f32[1,4096]{1,0:T(1,128)}, f32[256,1024]{1,0:T(8,128)}, bf16[256,1024]{1,0:T(8,128)(2,1)}, bf16[8,256,12...) custom-call(s32[1]{0:T(128)} %bitcast.17.c_ref, ...), custom_call_target="tpu_custom_call" | custom-call | flops 20700000256 | bytes 1000 | tf_op jit(solution)/shard_map/block_backward/pallas_call | solution.py:333
  272.6 10.9 %grad_rows.1 = (bf16[8,64,4096]{2,1,0:T(8,128)(2,1)}, bf16[8,64,4096]{2,1,0:T(8,128)(2,1)}) custom-call(s32[1]{0:T(128)} %bitcast.17.c_ref, bf16[256,1024]{1,0:T(8,128)(2,1)} %convert_element_type.449.l1, bf16[256,1024]{1,0:T(8,128)(2,1)} %get-tuple-element.131.l0, bf16[256,4096]{1,0:T(8,128)(2,1)} %copy-done.19, bf16[256,4096]{1,0:T(8,128)(2,1)} %copy-done.18), custom_call_target="tpu_custom_call" | custom-call | flops 9200000000 | bytes 1000 | tf_op jit(solution)/shard_map/grad_rows/pallas_call | solution.py:167
  283.8 5.0 %grad_out.1 = (bf16[8,192,1024]{2,1,0:T(8,128)(2,1)}, bf16[8,192,1024]{2,1,0:T(8,128)(2,1)}) custom-call(s32[1]{0:T(128)} %bitcast.17.c_ref, bf16[256,1024]{1,0:T(8,128)(2,1)} %copy-done.15, bf16[256,1024]{1,0:T(8,128)(2,1)} %get-tuple-element.135.l0, bf16[256,1024]{1,0:T(8,128)(2,1)} %copy-done.14, ...), custom_call_target="tpu_custom_call", output_to_operand_aliasing={{0}: (5, {}), {1}: (6, {})} | custom-call | flops 3449999872 | bytes 1000 | tf_op jit(solution)/shard_map/grad_out/pallas_call | solution.py:370
  289.3 4.6 all-to-all-start.2
  293.9 4.5 fusion
  308.1 18.5 %attend_back.4.rest_0_ = bf16[8,3,256,128]{3,2,1,0:T(8,128)(2,1)} custom-call(bf16[2048,128]{1,0:T(8,128)(2,1)} %get-tuple-element.252.q_ref, bf16[2048,128]{1,0:T(8,128)(2,1)} %get-tuple-element.251.k_ref, bf16[2048,128]{1,0:T(8,128)(2,1)} %get-tuple-element.250.v_ref, bf16[2048,128]{1,0:T(8,128)(2,1)} %bitcast.22.do_ref), custom_call_target="tpu_custom_call" | custom-call | flops 19549999104 | bytes 1000 | tf_op jit(solution)/shard_map/attend_back/pallas_call | solution.py:134
  331.2 19.1 %attend_back.5.d_ref = bf16[8,3,256,128]{3,2,1,0:T(8,128)(2,1)} custom-call(bf16[2048,128]{1,0:T(8,128)(2,1)} %get-tuple-element.252.q_ref, bf16[2048,128]{1,0:T(8,128)(2,1)} %get-tuple-element.251.k_ref, bf16[2048,128]{1,0:T(8,128)(2,1)} %get-tuple-element.250.v_ref, bf16[2048,128]{1,0:T(8,128)(2,1)} %bitcast.22.do_ref, ...), custom_call_target="tpu_custom_call" | custom-call | flops 19549999104 | bytes 1000 | tf_op jit(solution)/shard_map/attend_back/pallas_call | solution.py:134
  350.2 5.8 %collective-permute-done.25 = bf16[2,2,64,1024]{3,2,1,0:T(8,128)(2,1)S(1)} collective-permute-done((bf16[2,2,64,1024]{3,2,1,0:T(8,128)(2,1)}, bf16[2,2,64,1024]{3,2,1,0:T(8,128)(2,1)S(1)}, u32[]{:S(2)}, u32[]{:S(2)}) %collective-permute-start.25) | collective-permute-done | bytes 524320 | tf_op jit(solution)/shard_map/ppermute | solution.py:588
  364.9 4.3 all-to-all-start.3
  375.7 6.0 %grad_heads.3 = bf16[3,128,1024]{2,1,0:T(8,128)(2,1)} custom-call(bf16[8,3,256,128]{3,2,1,0:T(8,128)(2,1)} %attend_back.5.d_ref, bf16[2048,1024]{1,0:T(8,128)(2,1)} %copy-done, f32[3,128,1024]{2,1,0:T(8,128)} %grad_heads.2.rest_0_), custom_call_target="tpu_custom_call" | custom-call | flops 5750000128 | bytes 1000 | tf_op jit(solution)/shard_map/grad_heads/pallas_call | solution.py:460
  384.9 4.9 all-to-all-done.3.b_ref
  389.8 8.3 %collective-permute-done.30 = bf16[2,2,96,1024]{3,2,1,0:T(8,128)(2,1)} collective-permute-done((bf16[2,2,96,1024]{3,2,1,0:T(8,128)(2,1)}, bf16[2,2,96,1024]{3,2,1,0:T(8,128)(2,1)}, u32[]{:S(2)}, u32[]{:S(2)}) %collective-permute-start.30) | collective-permute-done | bytes 786464 | tf_op jit(solution)/shard_map/ppermute | solution.py:588
  409.0 4.4 all-to-all-start.4
  418.0 8.9 %qkv_backward.3 = (f32[256,1024]{1,0:T(8,128)}, bf16[128,1024]{1,0:T(8,128)(2,1)}, f32[8,1024]{1,0:T(8,128)}, f32[8,1024]{1,0:T(8,128)}) custom-call(bf16[8,3,256,128]{3,2,1,0:T(8,128)(2,1)} %all-to-all-done.3.b_ref, bf16[1024,3072]{1,0:T(8,128)(2,1)} %wv_ref.7, bf16[1024,3072]{1,0:T(8,128)(2,1)} %wv_ref.7, bf16[1024,3072]{1,0:T(8,128)(2,1)} %wv_ref.7, ...), custom_call_target="tpu_custom_call" | custom-call | flops 13799999488 | bytes 1000 | tf_op jit(solution)/shard_map/qkv_backward/pallas_call | solution.py:424
  439.7 5.2 %all-to-all-start.5 = ((f32[16,1,1088]{2,1,0:T(1,128)}), f32[16,1,1088]{2,1,0:T(1,128)S(1)}, u32[]{:S(2)}, u32[]{:S(2)}) async-start(f32[16,1,1088]{2,1,0:T(1,128)} %copy.130), calls=%async_computation.5 | async-start | bytes 147456 | tf_op jit(solution)/shard_map/all_to_all | solution.py:829
  453.7 13.0 %all-to-all-done.5 = f32[16,1,1088]{2,1,0:T(1,128)S(1)} async-done(((f32[16,1,1088]{2,1,0:T(1,128)}), f32[16,1,1088]{2,1,0:T(1,128)S(1)}, u32[]{:S(2)}, u32[]{:S(2)}) %all-to-all-start.5) | async-done | bytes 69664 | tf_op jit(solution)/shard_map/all_to_all | solution.py:829
  466.8 4.6 collective-permute-done.37
  481.9 5.3 %collective-permute-done.41 = bf16[96,1024]{1,0:T(8,128)(2,1)S(1)} collective-permute-done((bf16[96,1024]{1,0:T(8,128)(2,1)S(1)}, bf16[96,1024]{1,0:T(8,128)(2,1)S(1)}, u32[]{:S(2)}, u32[]{:S(2)}) %collective-permute-start.41) | collective-permute-done | bytes 196640 | tf_op jit(solution)/shard_map/ppermute | solution.py:588
  (291 shorter events, 154.8 us)
Async XLA Ops:
  1.8 16.0 %collective-permute-start = (bf16[128,1024]{1,0:T(8,128)(2,1)S(1)}, bf16[128,1024]{1,0:T(8,128)(2,1)S(1)}, u32[]{:S(2)}, u32[]{:S(2)}) collective-permute-start(bf16[128,1024]{1,0:T(8,128)(2,1)S(1)} %get-tuple-element.264), channel_id=1, source_target_pairs={{0,8},{8,0},{1,9},{9,1},{2,10},{10,2},{3,11},{11,3},{4,12},{12,4},... | collective-permute-start | bytes 786440 | tf_op jit(solution)/shard_map/ppermute | solution.py:588
  19.1 13.2 %collective-permute-start.2 = (bf16[256,1024]{1,0:T(8,128)(2,1)S(1)}, bf16[256,1024]{1,0:T(8,128)(2,1)S(1)}, u32[]{:S(2)}, u32[]{:S(2)}) collective-permute-start(bf16[256,1024]{1,0:T(8,128)(2,1)S(1)} %get-tuple-element.243), channel_id=1, source_target_pairs={{0,4},{4,0},{1,5},{5,1},{2,6},{6,2},{3,7},{7,3},{8,12},{12,8},{9,1... | collective-permute-start | bytes 1572872 | tf_op jit(solution)/shard_map/ppermute | solution.py:588
  19.9 13.7 %collective-permute-start.1 = (bf16[256,1024]{1,0:T(8,128)(2,1)S(1)}, bf16[256,1024]{1,0:T(8,128)(2,1)S(1)}, u32[]{:S(2)}, u32[]{:S(2)}) collective-permute-start(bf16[256,1024]{1,0:T(8,128)(2,1)S(1)} %get-tuple-element.243), channel_id=1, source_target_pairs={{0,2},{2,0},{1,3},{3,1},{4,6},{6,4},{5,7},{7,5},{8,10},{10,8},{9,1... | collective-permute-start | bytes 1572872 | tf_op jit(solution)/shard_map/ppermute | solution.py:588
  22.7 18.2 %collective-permute-start.5 = (bf16[256,1024]{1,0:T(8,128)(2,1)S(1)}, bf16[256,1024]{1,0:T(8,128)(2,1)S(1)}, u32[]{:S(2)}, u32[]{:S(2)}) collective-permute-start(bf16[256,1024]{1,0:T(8,128)(2,1)S(1)} %get-tuple-element.243), channel_id=1, source_target_pairs={{0,1},{1,0},{2,3},{3,2},{4,5},{5,4},{6,7},{7,6},{8,9},{9,8},{10,11... | collective-permute-start | bytes 1572872 | tf_op jit(solution)/shard_map/ppermute | solution.py:588
  42.5 27.2 %collective-permute-start.10 = (f32[128,1024]{1,0:T(8,128)S(1)}, f32[128,1024]{1,0:T(8,128)S(1)}, u32[]{:S(2)}, u32[]{:S(2)}) collective-permute-start(f32[128,1024]{1,0:T(8,128)S(1)} %get-tuple-element.254), channel_id=1, source_target_pairs={{0,8},{8,0},{1,9},{9,1},{2,10},{10,2},{3,11},{11,3},{4,12},{12,4},... | collective-permute-start | bytes 1572872 | tf_op jit(solution)/shard_map/ppermute | solution.py:588
  86.5 13.7 %collective-permute-start.12 = (bf16[256,1024]{1,0:T(8,128)(2,1)S(1)}, bf16[256,1024]{1,0:T(8,128)(2,1)S(1)}, u32[]{:S(2)}, u32[]{:S(2)}) collective-permute-start(bf16[256,1024]{1,0:T(8,128)(2,1)S(1)} %get-tuple-element.108), channel_id=1, source_target_pairs={{0,4},{4,0},{1,5},{5,1},{2,6},{6,2},{3,7},{7,3},{8,12},{12,8},{9,1... | collective-permute-start | bytes 1572872 | tf_op jit(solution)/shard_map/ppermute | solution.py:588
  88.0 13.4 %collective-permute-start.11 = (bf16[256,1024]{1,0:T(8,128)(2,1)S(1)}, bf16[256,1024]{1,0:T(8,128)(2,1)S(1)}, u32[]{:S(2)}, u32[]{:S(2)}) collective-permute-start(bf16[256,1024]{1,0:T(8,128)(2,1)S(1)} %get-tuple-element.108), channel_id=1, source_target_pairs={{0,2},{2,0},{1,3},{3,1},{4,6},{6,4},{5,7},{7,5},{8,10},{10,8},{9,1... | collective-permute-start | bytes 1572872 | tf_op jit(solution)/shard_map/ppermute | solution.py:588
  90.0 18.4 %collective-permute-start.15 = (bf16[256,1024]{1,0:T(8,128)(2,1)S(1)}, bf16[256,1024]{1,0:T(8,128)(2,1)S(1)}, u32[]{:S(2)}, u32[]{:S(2)}) collective-permute-start(bf16[256,1024]{1,0:T(8,128)(2,1)S(1)} %get-tuple-element.108), channel_id=1, source_target_pairs={{0,1},{1,0},{2,3},{3,2},{4,5},{5,4},{6,7},{7,6},{8,9},{9,8},{10,11... | collective-permute-start | bytes 1572872 | tf_op jit(solution)/shard_map/ppermute | solution.py:588
  148.5 30.8 %collective-permute-start.20 = (bf16[128,1024]{1,0:T(8,128)(2,1)S(1)}, bf16[128,1024]{1,0:T(8,128)(2,1)S(1)}, u32[]{:S(2)}, u32[]{:S(2)}) collective-permute-start(bf16[128,1024]{1,0:T(8,128)(2,1)S(1)} %get-tuple-element.262), channel_id=1, source_target_pairs={{0,8},{8,0},{1,9},{9,1},{2,10},{10,2},{3,11},{11,3},{4,12},{12,4},... | collective-permute-start | bytes 786440 | tf_op jit(solution)/shard_map/ppermute | solution.py:588
  215.3 24.3 %all-to-all-start.1 = ((bf16[8,3,256,128]{3,2,1,0:T(8,128)(2,1)}), bf16[8,3,256,128]{3,2,1,0:T(8,128)(2,1)S(1)}, u32[]{:S(2)}, u32[]{:S(2)}) async-start(bf16[8,3,256,128]{3,2,1,0:T(8,128)(2,1)} %attend_back.3.d_ref), calls=%async_computation.1 | async-start | bytes 3145728 | tf_op jit(solution)/shard_map/all_to_all | solution.py:785
  288.8 15.8 %collective-permute-start.21 = (bf16[8,192,1024]{2,1,0:T(8,128)(2,1)}, bf16[8,192,1024]{2,1,0:T(8,128)(2,1)S(1)}, u32[]{:S(2)}, u32[]{:S(2)}) collective-permute-start(bf16[8,192,1024]{2,1,0:T(8,128)(2,1)} %get-tuple-element.139), channel_id=1, source_target_pairs={{0,1},{1,0},{2,3},{3,2},{4,5},{5,4},{6,7},{7,6},{8,9},{9,8},{10,11... | collective-permute-start | bytes 9437192 | tf_op jit(solution)/shard_map/ppermute | solution.py:588
  289.3 18.8 %all-to-all-start.2 = ((bf16[8,256,128]{2,1,0:T(8,128)(2,1)}), bf16[8,256,128]{2,1,0:T(8,128)(2,1)}, u32[]{:S(2)}, u32[]{:S(2)}) async-start(bf16[8,256,128]{2,1,0:T(8,128)(2,1)} %get-tuple-element.127), calls=%async_computation.2 | async-start | bytes 1048576 | tf_op jit(solution)/shard_map/all_to_all | solution.py:747
  298.4 57.7 %collective-permute-start.27 = (bf16[2,2,2,32,4096]{4,3,2,1,0:T(8,128)(2,1)}, bf16[2,2,2,32,4096]{4,3,2,1,0:T(8,128)(2,1)}, u32[]{:S(2)}, u32[]{:S(2)}) collective-permute-start(bf16[2,2,2,32,4096]{4,3,2,1,0:T(8,128)(2,1)} %fusion), channel_id=1, source_target_pairs={{0,16},{16,0},{1,17},{17,1},{2,18},{18,2},{3,19},{19,3},{4,20},{20... | collective-permute-start | bytes 6291464 | tf_op jit(solution)/shard_map/ppermute | solution.py:588
  302.5 25.6 %collective-permute-start.24 = (bf16[2,2,2,64,1024]{4,3,2,1,0:T(8,128)(2,1)}, bf16[2,2,2,64,1024]{4,3,2,1,0:T(8,128)(2,1)}, u32[]{:S(2)}, u32[]{:S(2)}) collective-permute-start(bf16[2,2,2,64,1024]{4,3,2,1,0:T(8,128)(2,1)} %fusion.20), channel_id=1, source_target_pairs={{0,4},{4,0},{1,5},{5,1},{2,6},{6,2},{3,7},{7,3},{8,12},{12,8},{9,1... | collective-permute-start | bytes 3145736 | tf_op jit(solution)/shard_map/ppermute | solution.py:588
  306.6 49.4 %collective-permute-start.26 = (bf16[2,2,2,96,1024]{4,3,2,1,0:T(8,128)(2,1)}, bf16[2,2,2,96,1024]{4,3,2,1,0:T(8,128)(2,1)}, u32[]{:S(2)}, u32[]{:S(2)}) collective-permute-start(bf16[2,2,2,96,1024]{4,3,2,1,0:T(8,128)(2,1)} %fusion.6), channel_id=1, source_target_pairs={{0,2},{2,0},{1,3},{3,1},{4,6},{6,4},{5,7},{7,5},{8,10},{10,8},{9,1... | collective-permute-start | bytes 4718600 | tf_op jit(solution)/shard_map/ppermute | solution.py:588
  330.5 25.5 %collective-permute-start.25 = (bf16[2,2,64,1024]{3,2,1,0:T(8,128)(2,1)}, bf16[2,2,64,1024]{3,2,1,0:T(8,128)(2,1)S(1)}, u32[]{:S(2)}, u32[]{:S(2)}) collective-permute-start(bf16[2,2,64,1024]{3,2,1,0:T(8,128)(2,1)} %fusion.22), channel_id=1, source_target_pairs={{0,8},{8,0},{1,9},{9,1},{2,10},{10,2},{3,11},{11,3},{4,12},{12,4},... | collective-permute-start | bytes 1572872 | tf_op jit(solution)/shard_map/ppermute | solution.py:588
  364.9 24.9 %all-to-all-start.3 = ((bf16[8,3,256,128]{3,2,1,0:T(8,128)(2,1)}), bf16[8,3,256,128]{3,2,1,0:T(8,128)(2,1)}, u32[]{:S(2)}, u32[]{:S(2)}) async-start(bf16[8,3,256,128]{3,2,1,0:T(8,128)(2,1)} %attend_back.5.d_ref), calls=%async_computation.3 | async-start | bytes 3145728 | tf_op jit(solution)/shard_map/all_to_all | solution.py:785
  371.8 18.0 %collective-permute-start.31 = (bf16[2,64,1024]{2,1,0:T(8,128)(2,1)}, bf16[2,64,1024]{2,1,0:T(8,128)(2,1)}, u32[]{:S(2)}, u32[]{:S(2)}) collective-permute-start(bf16[2,64,1024]{2,1,0:T(8,128)(2,1)} %fusion.28), channel_id=1, source_target_pairs={{0,16},{16,0},{1,17},{17,1},{2,18},{18,2},{3,19},{19,3},{4,20},{20... | collective-permute-start | bytes 786440 | tf_op jit(solution)/shard_map/ppermute | solution.py:588
  372.3 25.8 %collective-permute-start.30 = (bf16[2,2,96,1024]{3,2,1,0:T(8,128)(2,1)}, bf16[2,2,96,1024]{3,2,1,0:T(8,128)(2,1)}, u32[]{:S(2)}, u32[]{:S(2)}) collective-permute-start(bf16[2,2,96,1024]{3,2,1,0:T(8,128)(2,1)} %fusion.7), channel_id=1, source_target_pairs={{0,16},{16,0},{1,17},{17,1},{2,18},{18,2},{3,19},{19,3},{4,20},{20... | collective-permute-start | bytes 2359304 | tf_op jit(solution)/shard_map/ppermute | solution.py:588
  373.8 39.6 %collective-permute-start.28 = (bf16[2,2,32,4096]{3,2,1,0:T(8,128)(2,1)}, bf16[2,2,32,4096]{3,2,1,0:T(8,128)(2,1)}, u32[]{:S(2)}, u32[]{:S(2)}) collective-permute-start(bf16[2,2,32,4096]{3,2,1,0:T(8,128)(2,1)} %fusion.1), channel_id=1, source_target_pairs={{0,2},{2,0},{1,3},{3,1},{4,6},{6,4},{5,7},{7,5},{8,10},{10,8},{9,1... | collective-permute-start | bytes 3145736 | tf_op jit(solution)/shard_map/ppermute | solution.py:588
  383.7 22.2 %collective-permute-start.29 = (bf16[6,64,512]{2,1,0:T(8,128)(2,1)}, bf16[6,64,512]{2,1,0:T(8,128)(2,1)}, u32[]{:S(2)}, u32[]{:S(2)}) collective-permute-start(bf16[6,64,512]{2,1,0:T(8,128)(2,1)} %get-tuple-element.256), channel_id=1, source_target_pairs={{0,16},{16,0},{1,17},{17,1},{2,18},{18,2},{3,19},{19,3},{4,20},{20... | collective-permute-start | bytes 1179656 | tf_op jit(solution)/shard_map/ppermute | solution.py:588
  400.0 44.9 %collective-permute-start.36 = (bf16[64,1024]{1,0:T(8,128)(2,1)}, bf16[64,1024]{1,0:T(8,128)(2,1)S(1)}, u32[]{:S(2)}, u32[]{:S(2)}) collective-permute-start(bf16[64,1024]{1,0:T(8,128)(2,1)} %fusion.35), channel_id=1, source_target_pairs={{0,2},{2,0},{1,3},{3,1},{4,6},{6,4},{5,7},{7,5},{8,10},{10,8},{9,1... | collective-permute-start | bytes 393224 | tf_op jit(solution)/shard_map/ppermute | solution.py:588
  404.1 25.6 %collective-permute-start.32 = (bf16[2,96,1024]{2,1,0:T(8,128)(2,1)}, bf16[2,96,1024]{2,1,0:T(8,128)(2,1)}, u32[]{:S(2)}, u32[]{:S(2)}) collective-permute-start(bf16[2,96,1024]{2,1,0:T(8,128)(2,1)} %fusion.23), channel_id=1, source_target_pairs={{0,4},{4,0},{1,5},{5,1},{2,6},{6,2},{3,7},{7,3},{8,12},{12,8},{9,1... | collective-permute-start | bytes 1179656 | tf_op jit(solution)/shard_map/ppermute | solution.py:588
  409.0 25.8 %all-to-all-start.4 = ((bf16[16,64,512]{2,1,0:T(8,128)(2,1)}), bf16[16,64,512]{2,1,0:T(8,128)(2,1)}, u32[]{:S(2)}, u32[]{:S(2)}) async-start(bf16[16,64,512]{2,1,0:T(8,128)(2,1)} %take.3), calls=%async_computation.4 | async-start | bytes 2097152 | tf_op jit(solution)/shard_map/all_to_all | solution.py:800
  416.0 31.0 %collective-permute-start.35 = (bf16[2,32,4096]{2,1,0:T(8,128)(2,1)}, bf16[2,32,4096]{2,1,0:T(8,128)(2,1)}, u32[]{:S(2)}, u32[]{:S(2)}) collective-permute-start(bf16[2,32,4096]{2,1,0:T(8,128)(2,1)} %fusion.21), channel_id=1, source_target_pairs={{0,4},{4,0},{1,5},{5,1},{2,6},{6,2},{3,7},{7,3},{8,12},{12,8},{9,1... | collective-permute-start | bytes 1572872 | tf_op jit(solution)/shard_map/ppermute | solution.py:588
  426.8 39.9 %collective-permute-start.33 = (bf16[128,1024]{1,0:T(8,128)(2,1)}, bf16[128,1024]{1,0:T(8,128)(2,1)S(1)}, u32[]{:S(2)}, u32[]{:S(2)}) collective-permute-start(bf16[128,1024]{1,0:T(8,128)(2,1)} %get-tuple-element.178), channel_id=1, source_target_pairs={{0,8},{8,0},{1,9},{9,1},{2,10},{10,2},{3,11},{11,3},{4,12},{12,4},... | collective-permute-start | bytes 786440 | tf_op jit(solution)/shard_map/ppermute | solution.py:588
  431.8 35.0 %collective-permute-start.38 = (bf16[96,1024]{1,0:T(8,128)(2,1)}, bf16[96,1024]{1,0:T(8,128)(2,1)S(1)}, u32[]{:S(2)}, u32[]{:S(2)}) collective-permute-start(bf16[96,1024]{1,0:T(8,128)(2,1)} %fusion.31), channel_id=1, source_target_pairs={{0,8},{8,0},{1,9},{9,1},{2,10},{10,2},{3,11},{11,3},{4,12},{12,4},... | collective-permute-start | bytes 589832 | tf_op jit(solution)/shard_map/ppermute | solution.py:588
  437.3 29.5 %collective-permute-start.34 = (bf16[3,64,512]{2,1,0:T(8,128)(2,1)}, bf16[3,64,512]{2,1,0:T(8,128)(2,1)S(1)}, u32[]{:S(2)}, u32[]{:S(2)}) collective-permute-start(bf16[3,64,512]{2,1,0:T(8,128)(2,1)} %take.4), channel_id=1, source_target_pairs={{0,8},{8,0},{1,9},{9,1},{2,10},{10,2},{3,11},{11,3},{4,12},{12,4},... | collective-permute-start | bytes 589832 | tf_op jit(solution)/shard_map/ppermute | solution.py:588
  439.7 27.0 %all-to-all-start.5 = ((f32[16,1,1088]{2,1,0:T(1,128)}), f32[16,1,1088]{2,1,0:T(1,128)S(1)}, u32[]{:S(2)}, u32[]{:S(2)}) async-start(f32[16,1,1088]{2,1,0:T(1,128)} %copy.130), calls=%async_computation.5 | async-start | bytes 147456 | tf_op jit(solution)/shard_map/all_to_all | solution.py:829
  448.3 18.5 %collective-permute-start.42 = (bf16[64,1024]{1,0:T(8,128)(2,1)S(1)}, bf16[64,1024]{1,0:T(8,128)(2,1)S(1)}, u32[]{:S(2)}, u32[]{:S(2)}) collective-permute-start(bf16[64,1024]{1,0:T(8,128)(2,1)S(1)} %fusion.34), channel_id=1, source_target_pairs={{0,16},{16,0},{1,17},{17,1},{2,18},{18,2},{3,19},{19,3},{4,20},{20... | collective-permute-start | bytes 393224 | tf_op jit(solution)/shard_map/ppermute | solution.py:588
  450.3 21.1 %collective-permute-start.37 = (bf16[32,4096]{1,0:T(8,128)(2,1)S(1)}, bf16[32,4096]{1,0:T(8,128)(2,1)S(1)}, u32[]{:S(2)}, u32[]{:S(2)}) collective-permute-start(bf16[32,4096]{1,0:T(8,128)(2,1)S(1)} %fusion.27), channel_id=1, source_target_pairs={{0,8},{8,0},{1,9},{9,1},{2,10},{10,2},{3,11},{11,3},{4,12},{12,4},... | collective-permute-start | bytes 786440 | tf_op jit(solution)/shard_map/ppermute | solution.py:588
  477.2 13.8 %collective-permute-start.43 = (bf16[32,4096]{1,0:T(8,128)(2,1)S(1)}, bf16[32,4096]{1,0:T(8,128)(2,1)S(1)}, u32[]{:S(2)}, u32[]{:S(2)}) collective-permute-start(bf16[32,4096]{1,0:T(8,128)(2,1)S(1)} %fusion.26), channel_id=1, source_target_pairs={{0,16},{16,0},{1,17},{17,1},{2,18},{18,2},{3,19},{19,3},{4,20},{20... | collective-permute-start | bytes 786440 | tf_op jit(solution)/shard_map/ppermute | solution.py:588
  (67 other events, 787.3 us)

commit v8 on v7

--- a/solution.py
+++ b/solution.py
@@ -384,7 +384,9 @@
     )(core.reshape(1), *left, *right, other, own)
 
 
-def qkv_backward_kernel(b_ref, wq_ref, wk_ref, wv_ref, m_ref, n_ref, r_ref, g_ref, grad_ref, low_ref, sums_ref, qv_ref, total):
+def qkv_backward_kernel(b_ref, wq_ref, wk_ref, wv_ref, m_ref, n_ref, r_ref, g_ref, *rest):
+    grad_ref, low_ref, sums_ref, qv_ref, total = rest[-5:]
+    added = rest[:-5]
     step = pl.program_id(0)
     w = b_ref.shape[3]
     part = None
@@ -392,8 +394,11 @@
         for i, ref in enumerate((wq_ref, wk_ref, wv_ref)):
             x = contract(b_ref[m, i], ref[:, m * w : (m + 1) * w], 1, 1)
             part = x if part is None else part + x
-        qv_ref[0:1, m * w : (m + 1) * w] = column_sum(b_ref[m, 0])
-        qv_ref[1:2, m * w : (m + 1) * w] = column_sum(b_ref[m, 2])
+        for row, i in ((0, 0), (1, 2)):
+            here = column_sum(b_ref[m, i])
+            if added:
+                here = here + added[1][row : row + 1, m * w : (m + 1) * w]
+            qv_ref[row : row + 1, m * w : (m + 1) * w] = here
 
     @pl.when(step == 0)
     def _():
@@ -409,10 +414,13 @@
         grad = m_ref[...] + dv
         grad_ref[...] = grad
         low_ref[...] = grad[grad.shape[0] - low_ref.shape[0] :].astype(bf16)
-        put_sums(sums_ref, gain, bias, column_sum(grad))
-
-
-def qkv_backward(back, w_qkv, middle_grad, n1, r1, gain, low):
+        sums = (gain, bias, column_sum(grad))
+        if added:
+            sums = [v + added[0][i : i + 1, :] for i, v in enumerate(sums)]
+        put_sums(sums_ref, *sums)
+
+
+def qkv_backward(back, w_qkv, middle_grad, n1, r1, gain, low, added=()):
     members, _, t, w = back.shape
     d = members * w
     at_once = max(2, 128 // w)
@@ -426,7 +434,7 @@
         grid=(members // at_once,),
         in_specs=[spec((at_once, 3, t, w), lambda i: (i, 0, 0, 0))] + weight + [
             full, full, spec((t, 1), lambda i: (0, 0)), spec((1, d), lambda i: (0, 0)),
-        ],
+        ] + [spec((8, d), lambda i: (0, 0)), spec((8, block), lambda i: (0, i))][: len(added)],
         out_specs=[
             full, spec((low, d), lambda i: (0, 0)), spec((8, d), lambda i: (0, 0)),
             spec((8, block), lambda i: (0, i)),
@@ -438,7 +446,7 @@
         compiler_params=pltpu.CompilerParams(vmem_limit_bytes=60 * MIB),
         cost_estimate=cost(12),
         name="qkv_backward",
-    )(back, w_qkv, w_qkv, w_qkv, middle_grad, n1, r1, gain.reshape(1, d))
+    )(back, w_qkv, w_qkv, w_qkv, middle_grad, n1, r1, gain.reshape(1, d), *added)
 
 
 def grad_heads_kernel(d_ref, n_ref, *rest):
@@ -711,6 +719,7 @@
 
     grad = out_grad
     small = None
+    added = ()
     core = lax.axis_index("core")
     y = lax.axis_index("samp")
     bands = 2 ** len(axes)
@@ -804,11 +813,13 @@
             owns[0] = own_part(0)
             back = pin(back, w_heads, *owns[0])
         grad, low_grad, sums_one, sums_qv = qkv_backward(
-            back, w_qkv, middle_grad, n1, r1, ln1_gain, half if last else rows
+            back, w_qkv, middle_grad, n1, r1, ln1_gain, half if last else rows, added
         )
+        added = (sums_one, sums_qv)
         down_grad = low_grad
-        step_small = (sums_one[:3], sums_qv[:2], sums_two[:4], hidden_sum)
+        step_small = (sums_two[:4], hidden_sum)
         small = step_small if small is None else tuple(a + b for a, b in zip(small, step_small))
+    small = (sums_one[:3], sums_qv[:2]) + small
     fields_sent = low_grad
     fields_other = swap(fields_sent, "zh")
     x_share.terms[-1] = pin(x_share.terms[-1], fields_sent)

time: 498 us -> 501 us (level)
    unnamed x98 -> x96, local copies, waits for them, and re-layouts: 12.5 us -> 12.5 us
  transfers between devices with their start and end apart: 50 -> 50, of which waited for: 21 -> 20; matrix products, arithmetic and copies ran while one was open for 12% -> 12% of each run, Pallas kernels for 23% -> 23%
where the time goes in v8:
time: 501 us; the launch traced here: 495 us
  Pallas kernels  236 us (47%)
  waiting for transfers between devices  92.6 us (18%)
  starting transfers between devices  74.5 us (15%)
  other arithmetic  43.7 us (9%)
  local copies, waits for them, and re-layouts  32.4 us (6%)
  matrix products  11.4 us (2%)
    pallas_call x3, Pallas kernels, attend_back(): pl.pallas_call(functools.partial(attend_back_kernel, heads=heads, some=so...  69.5 us
    ppermute x44, waiting for transfers between devices, swap(): return lax.ppermute(x, axis, SWAP)  61.2 us
    ppermute x44, starting transfers between devices, swap(): return lax.ppermute(x, axis, SWAP)  48.4 us
    pallas_call x2, Pallas kernels, attend(): pl.pallas_call(attend_kernel, grid=(width // block,), in_specs=[own, spec...  46.5 us
    pallas_call x2, Pallas kernels, block_backward(): pl.pallas_call(functools.partial(block_backward_kernel, grads=bool(grads)...  39.4 us
    convert_element_type x12, other arithmetic, halve(): sent = total(there).astype(bf16)  29.9 us
    pallas_call x2, Pallas kernels, block_forward(): pl.pallas_call(functools.partial(block_forward_kernel, last=last), grid=(...  25.3 us
    pallas_call x2, Pallas kernels, qkv_backward(): pl.pallas_call(qkv_backward_kernel, grid=(members // at_once,), in_specs=...  18.1 us
  transfers between devices with their start and end apart: 50, of which 20 were waited for; matrix products, arithmetic and copies ran while one was open for 12% of the time, Pallas kernels for 23%

profile of v8, /device:TPU:0, one launch (start us, length us, event | category | flops | bytes accessed | tf_op | source)
XLA Modules:
  0.0 494.7 jit_solution(2857290357872219276)
XLA Ops:
  11.3 6.5 %collective-permute-done = bf16[128,1024]{1,0:T(8,128)(2,1)S(1)} collective-permute-done((bf16[128,1024]{1,0:T(8,128)(2,1)S(1)}, bf16[128,1024]{1,0:T(8,128)(2,1)S(1)}, u32[]{:S(2)}, u32[]{:S(2)}) %collective-permute-start) | collective-permute-done | bytes 262176 | tf_op jit(solution)/shard_map/ppermute | solution.py:596
  23.5 8.8 %collective-permute-done.2 = bf16[256,1024]{1,0:T(8,128)(2,1)S(1)} collective-permute-done((bf16[256,1024]{1,0:T(8,128)(2,1)S(1)}, bf16[256,1024]{1,0:T(8,128)(2,1)S(1)}, u32[]{:S(2)}, u32[]{:S(2)}) %collective-permute-start.2) | collective-permute-done | bytes 524320 | tf_op jit(solution)/shard_map/ppermute | solution.py:596
  46.3 23.4 %attend.2.a_ref.r0 = bf16[256,1024]{1,0:T(8,128)(2,1)S(1)} custom-call(bf16[256,1024]{1,0:T(8,128)(2,1)S(1)} %fusion.17.q_ref, bf16[2048,1024]{1,0:T(8,128)(2,1)S(1)} %constant_dynamic-update-slice_fusion.10.n_ref, bf16[1024,3072]{1,0:T(8,128)(2,1)S(1)} %copy-done.2, bf16[1024,3072]{1,0:T(8,128)(2,1)S(1)} %copy-done.2, f32[1,1024]{1,0:T(1,128)S(1)} %bitcast.257), custom_call_target="tpu_custom_call" | custom-call | flops 27599998976 | bytes 1000 | tf_op jit(solution)/shard_map/attend/pallas_call | solution.py:64
  70.0 12.8 %block_forward.2 = (f32[256,1024]{1,0:T(8,128)S(1)}, f32[256,1]{1,0:T(8,128)S(1)}, bf16[256,1024]{1,0:T(8,128)(2,1)S(1)}, f32[256,4096]{1,0:T(8,128)S(1)}, bf16[...) custom-call(f32[256,1024]{1,0:T(8,128)S(1)} %get-tuple-element.258.x, ...), custom_call_target="tpu_custom_call" | custom-call | flops 13799999488 | bytes 1000 | tf_op jit(solution)/shard_map/block_forward/pallas_call | solution.py:235
  90.8 9.4 %collective-permute-done.12 = bf16[256,1024]{1,0:T(8,128)(2,1)S(1)} collective-permute-done((bf16[256,1024]{1,0:T(8,128)(2,1)S(1)}, bf16[256,1024]{1,0:T(8,128)(2,1)S(1)}, u32[]{:S(2)}, u32[]{:S(2)}) %collective-permute-start.12) | collective-permute-done | bytes 524320 | tf_op jit(solution)/shard_map/ppermute | solution.py:596
  110.0 23.0 %attend.3.a_ref.r1 = bf16[256,1024]{1,0:T(8,128)(2,1)S(1)} custom-call(bf16[256,1024]{1,0:T(8,128)(2,1)S(1)} %fusion.14.q_ref, bf16[2048,1024]{1,0:T(8,128)(2,1)S(1)} %constant_dynamic-update-slice_fusion.n_ref, bf16[1024,3072]{1,0:T(8,128)(2,1)S(1)} %copy-done.2, bf16[1024,3072]{1,0:T(8,128)(2,1)S(1)} %copy-done.2, f32[1,1024]{1,0:T(1,128)S(1)} %bitcast.258), custom_call_target="tpu_custom_call" | custom-call | flops 27599998976 | bytes 1000 | tf_op jit(solution)/shard_map/attend/pallas_call | solution.py:64
  133.1 12.6 %block_forward.3 = (f32[256,1024]{1,0:T(8,128)S(1)}, f32[256,1]{1,0:T(8,128)S(1)}, bf16[256,1024]{1,0:T(8,128)(2,1)S(1)}, f32[256,4096]{1,0:T(8,128)S(1)}, bf16[...) custom-call(f32[256,1024]{1,0:T(8,128)S(1)} %copy-done.24, bf16[256,1024]{1,0:T(8,128)(2,1)S(1)} %attend.3.a_ref.r1, ...), custom_call_target="tpu_custom_call" | custom-call | flops 13799999488 | bytes 1000 | tf_op jit(solution)/shard_map/block_forward/pallas_call | solution.py:235
  151.4 16.6 %block_backward.2 = (bf16[256,4096]{1,0:T(8,128)(2,1)}, f32[1,4096]{1,0:T(1,128)S(1)}, f32[256,1024]{1,0:T(8,128)S(1)}, bf16[256,1024]{1,0:T(8,128)(2,1)S(1)}, b...) custom-call(s32[1]{0:T(128)} %bitcast.17.c_ref, f32[256,1024]{1,0:T(8,128)S(1)} %pad_maximum_fusion.grad_ref, ...), custom_call_target="tpu_custom_call" | custom-call | flops 16099999744 | bytes 1000 | tf_op jit(solution)/shard_map/block_backward/pallas_call | solution.py:333
  173.4 4.5 add_convert_fusion.2
  183.4 31.9 %attend_back.3.d_ref = bf16[8,3,256,128]{3,2,1,0:T(8,128)(2,1)} custom-call(bf16[2048,128]{1,0:T(8,128)(2,1)} %get-tuple-element.249.q_ref, bf16[2048,128]{1,0:T(8,128)(2,1)} %get-tuple-element.248.k_ref, bf16[2048,128]{1,0:T(8,128)(2,1)} %get-tuple-element.247.v_ref, bf16[2048,128]{1,0:T(8,128)(2,1)} %bitcast.292), custom_call_target="tpu_custom_call" | custom-call | flops 37950001152 | bytes 1000 | tf_op jit(solution)/shard_map/attend_back/pallas_call | solution.py:134
  219.1 4.5 add_convert_fusion.3
  225.8 5.9 %grad_heads.2.rest_0_ = f32[3,128,1024]{2,1,0:T(8,128)} custom-call(bf16[8,3,256,128]{3,2,1,0:T(8,128)(2,1)} %attend_back.3.d_ref, bf16[2048,1024]{1,0:T(8,128)(2,1)} %copy-done.1), custom_call_target="tpu_custom_call" | custom-call | flops 5750000128 | bytes 1000 | tf_op jit(solution)/shard_map/grad_heads/pallas_call | solution.py:468
  231.7 7.9 %all-to-all-done.1.b_ref = bf16[8,3,256,128]{3,2,1,0:T(8,128)(2,1)S(1)} async-done(((bf16[8,3,256,128]{3,2,1,0:T(8,128)(2,1)}), bf16[8,3,256,128]{3,2,1,0:T(8,128)(2,1)S(1)}, u32[]{:S(2)}, u32[]{:S(2)}) %all-to-all-start.1) | async-done | bytes 1572896 | tf_op jit(solution)/shard_map/all_to_all | solution.py:794
  240.7 9.0 %qkv_backward.2 = (f32[256,1024]{1,0:T(8,128)}, bf16[256,1024]{1,0:T(8,128)(2,1)}, f32[8,1024]{1,0:T(8,128)}, f32[8,1024]{1,0:T(8,128)}) custom-call(bf16[8,3,256,128]{3,2,1,0:T(8,128)(2,1)} %copy-done.32, bf16[1024,3072]{1,0:T(8,128)(2,1)} %wv_ref.7, bf16[1024,3072]{1,0:T(8,128)(2,1)} %wv_ref.7, bf16[1024,3072]{1,0:T(8,128)(2,1)} %wv_ref.7, ...), custom_call_target="tpu_custom_call" | custom-call | flops 13799999488 | bytes 1000 | tf_op jit(solution)/shard_map/qkv_backward/pallas_call | solution.py:432
  249.7 22.8 %block_backward.3 = (bf16[256,4096]{1,0:T(8,128)(2,1)}, f32[1,4096]{1,0:T(1,128)}, f32[256,1024]{1,0:T(8,128)}, bf16[256,1024]{1,0:T(8,128)(2,1)}, bf16[8,256,12...) custom-call(s32[1]{0:T(128)} %bitcast.17.c_ref, ...), custom_call_target="tpu_custom_call" | custom-call | flops 20700000256 | bytes 1000 | tf_op jit(solution)/shard_map/block_backward/pallas_call | solution.py:333
  272.5 10.9 %grad_rows.1 = (bf16[8,64,4096]{2,1,0:T(8,128)(2,1)}, bf16[8,64,4096]{2,1,0:T(8,128)(2,1)}) custom-call(s32[1]{0:T(128)} %bitcast.17.c_ref, bf16[256,1024]{1,0:T(8,128)(2,1)} %convert_element_type.449.l1, bf16[256,1024]{1,0:T(8,128)(2,1)} %get-tuple-element.131.l0, bf16[256,4096]{1,0:T(8,128)(2,1)} %copy-done.19, bf16[256,4096]{1,0:T(8,128)(2,1)} %copy-done.18), custom_call_target="tpu_custom_call" | custom-call | flops 9200000000 | bytes 1000 | tf_op jit(solution)/shard_map/grad_rows/pallas_call | solution.py:167
  283.7 5.0 %grad_out.1 = (bf16[8,192,1024]{2,1,0:T(8,128)(2,1)}, bf16[8,192,1024]{2,1,0:T(8,128)(2,1)}) custom-call(s32[1]{0:T(128)} %bitcast.17.c_ref, bf16[256,1024]{1,0:T(8,128)(2,1)} %copy-done.15, bf16[256,1024]{1,0:T(8,128)(2,1)} %get-tuple-element.135.l0, bf16[256,1024]{1,0:T(8,128)(2,1)} %copy-done.14, ...), custom_call_target="tpu_custom_call", output_to_operand_aliasing={{0}: (5, {}), {1}: (6, {})} | custom-call | flops 3449999872 | bytes 1000 | tf_op jit(solution)/shard_map/grad_out/pallas_call | solution.py:370
  289.2 4.6 all-to-all-start.2
  293.9 4.5 fusion
  308.1 18.5 %attend_back.4.rest_0_ = bf16[8,3,256,128]{3,2,1,0:T(8,128)(2,1)} custom-call(bf16[2048,128]{1,0:T(8,128)(2,1)} %get-tuple-element.252.q_ref, bf16[2048,128]{1,0:T(8,128)(2,1)} %get-tuple-element.251.k_ref, bf16[2048,128]{1,0:T(8,128)(2,1)} %get-tuple-element.250.v_ref, bf16[2048,128]{1,0:T(8,128)(2,1)} %bitcast.22.do_ref), custom_call_target="tpu_custom_call" | custom-call | flops 19549999104 | bytes 1000 | tf_op jit(solution)/shard_map/attend_back/pallas_call | solution.py:134
  331.1 19.1 %attend_back.5.d_ref = bf16[8,3,256,128]{3,2,1,0:T(8,128)(2,1)} custom-call(bf16[2048,128]{1,0:T(8,128)(2,1)} %get-tuple-element.252.q_ref, bf16[2048,128]{1,0:T(8,128)(2,1)} %get-tuple-element.251.k_ref, bf16[2048,128]{1,0:T(8,128)(2,1)} %get-tuple-element.250.v_ref, bf16[2048,128]{1,0:T(8,128)(2,1)} %bitcast.22.do_ref, ...), custom_call_target="tpu_custom_call" | custom-call | flops 19549999104 | bytes 1000 | tf_op jit(solution)/shard_map/attend_back/pallas_call | solution.py:134
  350.2 5.8 %collective-permute-done.25 = bf16[2,2,64,1024]{3,2,1,0:T(8,128)(2,1)S(1)} collective-permute-done((bf16[2,2,64,1024]{3,2,1,0:T(8,128)(2,1)}, bf16[2,2,64,1024]{3,2,1,0:T(8,128)(2,1)S(1)}, u32[]{:S(2)}, u32[]{:S(2)}) %collective-permute-start.25) | collective-permute-done | bytes 524320 | tf_op jit(solution)/shard_map/ppermute | solution.py:596
  364.8 4.3 all-to-all-start.3
  375.6 6.0 %grad_heads.3 = bf16[3,128,1024]{2,1,0:T(8,128)(2,1)} custom-call(bf16[8,3,256,128]{3,2,1,0:T(8,128)(2,1)} %attend_back.5.d_ref, bf16[2048,1024]{1,0:T(8,128)(2,1)} %copy-done, f32[3,128,1024]{2,1,0:T(8,128)} %grad_heads.2.rest_0_), custom_call_target="tpu_custom_call" | custom-call | flops 5750000128 | bytes 1000 | tf_op jit(solution)/shard_map/grad_heads/pallas_call | solution.py:468
  384.8 4.9 all-to-all-done.3.b_ref
  389.7 8.3 %collective-permute-done.30 = bf16[2,2,96,1024]{3,2,1,0:T(8,128)(2,1)} collective-permute-done((bf16[2,2,96,1024]{3,2,1,0:T(8,128)(2,1)}, bf16[2,2,96,1024]{3,2,1,0:T(8,128)(2,1)}, u32[]{:S(2)}, u32[]{:S(2)}) %collective-permute-start.30) | collective-permute-done | bytes 786464 | tf_op jit(solution)/shard_map/ppermute | solution.py:596
  408.9 4.4 all-to-all-start.4
  417.9 9.1 %qkv_backward.3 = (f32[256,1024]{1,0:T(8,128)}, bf16[128,1024]{1,0:T(8,128)(2,1)}, f32[8,1024]{1,0:T(8,128)}, f32[8,1024]{1,0:T(8,128)}) custom-call(bf16[8,3,256,128]{3,2,1,0:T(8,128)(2,1)} %all-to-all-done.3.b_ref, bf16[1024,3072]{1,0:T(8,128)(2,1)} %wv_ref.7, bf16[1024,3072]{1,0:T(8,128)(2,1)} %wv_ref.7, bf16[1024,3072]{1,0:T(8,128)(2,1)} %wv_ref.7, ...), custom_call_target="tpu_custom_call" | custom-call | flops 13799999488 | bytes 1000 | tf_op jit(solution)/shard_map/qkv_backward/pallas_call | solution.py:432
  439.8 5.2 %all-to-all-start.5 = ((f32[16,1,1088]{2,1,0:T(1,128)}), f32[16,1,1088]{2,1,0:T(1,128)S(1)}, u32[]{:S(2)}, u32[]{:S(2)}) async-start(f32[16,1,1088]{2,1,0:T(1,128)} %copy.130), calls=%async_computation.5 | async-start | bytes 147456 | tf_op jit(solution)/shard_map/all_to_all | solution.py:840
  453.8 16.1 %all-to-all-done.5 = f32[16,1,1088]{2,1,0:T(1,128)S(1)} async-done(((f32[16,1,1088]{2,1,0:T(1,128)}), f32[16,1,1088]{2,1,0:T(1,128)S(1)}, u32[]{:S(2)}, u32[]{:S(2)}) %all-to-all-start.5) | async-done | bytes 69664 | tf_op jit(solution)/shard_map/all_to_all | solution.py:840
  470.0 4.3 collective-permute-done.37
  484.7 5.3 %collective-permute-done.41 = bf16[96,1024]{1,0:T(8,128)(2,1)S(1)} collective-permute-done((bf16[96,1024]{1,0:T(8,128)(2,1)S(1)}, bf16[96,1024]{1,0:T(8,128)(2,1)S(1)}, u32[]{:S(2)}, u32[]{:S(2)}) %collective-permute-start.41) | collective-permute-done | bytes 196640 | tf_op jit(solution)/shard_map/ppermute | solution.py:596
  (289 shorter events, 154.4 us)
Async XLA Ops:
  1.8 16.0 %collective-permute-start = (bf16[128,1024]{1,0:T(8,128)(2,1)S(1)}, bf16[128,1024]{1,0:T(8,128)(2,1)S(1)}, u32[]{:S(2)}, u32[]{:S(2)}) collective-permute-start(bf16[128,1024]{1,0:T(8,128)(2,1)S(1)} %get-tuple-element.264), channel_id=1, source_target_pairs={{0,8},{8,0},{1,9},{9,1},{2,10},{10,2},{3,11},{11,3},{4,12},{12,4},... | collective-permute-start | bytes 786440 | tf_op jit(solution)/shard_map/ppermute | solution.py:596
  19.1 13.2 %collective-permute-start.2 = (bf16[256,1024]{1,0:T(8,128)(2,1)S(1)}, bf16[256,1024]{1,0:T(8,128)(2,1)S(1)}, u32[]{:S(2)}, u32[]{:S(2)}) collective-permute-start(bf16[256,1024]{1,0:T(8,128)(2,1)S(1)} %get-tuple-element.243), channel_id=1, source_target_pairs={{0,4},{4,0},{1,5},{5,1},{2,6},{6,2},{3,7},{7,3},{8,12},{12,8},{9,1... | collective-permute-start | bytes 1572872 | tf_op jit(solution)/shard_map/ppermute | solution.py:596
  19.9 13.7 %collective-permute-start.1 = (bf16[256,1024]{1,0:T(8,128)(2,1)S(1)}, bf16[256,1024]{1,0:T(8,128)(2,1)S(1)}, u32[]{:S(2)}, u32[]{:S(2)}) collective-permute-start(bf16[256,1024]{1,0:T(8,128)(2,1)S(1)} %get-tuple-element.243), channel_id=1, source_target_pairs={{0,2},{2,0},{1,3},{3,1},{4,6},{6,4},{5,7},{7,5},{8,10},{10,8},{9,1... | collective-permute-start | bytes 1572872 | tf_op jit(solution)/shard_map/ppermute | solution.py:596
  22.7 18.2 %collective-permute-start.5 = (bf16[256,1024]{1,0:T(8,128)(2,1)S(1)}, bf16[256,1024]{1,0:T(8,128)(2,1)S(1)}, u32[]{:S(2)}, u32[]{:S(2)}) collective-permute-start(bf16[256,1024]{1,0:T(8,128)(2,1)S(1)} %get-tuple-element.243), channel_id=1, source_target_pairs={{0,1},{1,0},{2,3},{3,2},{4,5},{5,4},{6,7},{7,6},{8,9},{9,8},{10,11... | collective-permute-start | bytes 1572872 | tf_op jit(solution)/shard_map/ppermute | solution.py:596
  42.5 27.2 %collective-permute-start.10 = (f32[128,1024]{1,0:T(8,128)S(1)}, f32[128,1024]{1,0:T(8,128)S(1)}, u32[]{:S(2)}, u32[]{:S(2)}) collective-permute-start(f32[128,1024]{1,0:T(8,128)S(1)} %get-tuple-element.254), channel_id=1, source_target_pairs={{0,8},{8,0},{1,9},{9,1},{2,10},{10,2},{3,11},{11,3},{4,12},{12,4},... | collective-permute-start | bytes 1572872 | tf_op jit(solution)/shard_map/ppermute | solution.py:596
  86.5 13.7 %collective-permute-start.12 = (bf16[256,1024]{1,0:T(8,128)(2,1)S(1)}, bf16[256,1024]{1,0:T(8,128)(2,1)S(1)}, u32[]{:S(2)}, u32[]{:S(2)}) collective-permute-start(bf16[256,1024]{1,0:T(8,128)(2,1)S(1)} %get-tuple-element.108), channel_id=1, source_target_pairs={{0,4},{4,0},{1,5},{5,1},{2,6},{6,2},{3,7},{7,3},{8,12},{12,8},{9,1... | collective-permute-start | bytes 1572872 | tf_op jit(solution)/shard_map/ppermute | solution.py:596
  88.0 13.4 %collective-permute-start.11 = (bf16[256,1024]{1,0:T(8,128)(2,1)S(1)}, bf16[256,1024]{1,0:T(8,128)(2,1)S(1)}, u32[]{:S(2)}, u32[]{:S(2)}) collective-permute-start(bf16[256,1024]{1,0:T(8,128)(2,1)S(1)} %get-tuple-element.108), channel_id=1, source_target_pairs={{0,2},{2,0},{1,3},{3,1},{4,6},{6,4},{5,7},{7,5},{8,10},{10,8},{9,1... | collective-permute-start | bytes 1572872 | tf_op jit(solution)/shard_map/ppermute | solution.py:596
  90.0 18.4 %collective-permute-start.15 = (bf16[256,1024]{1,0:T(8,128)(2,1)S(1)}, bf16[256,1024]{1,0:T(8,128)(2,1)S(1)}, u32[]{:S(2)}, u32[]{:S(2)}) collective-permute-start(bf16[256,1024]{1,0:T(8,128)(2,1)S(1)} %get-tuple-element.108), channel_id=1, source_target_pairs={{0,1},{1,0},{2,3},{3,2},{4,5},{5,4},{6,7},{7,6},{8,9},{9,8},{10,11... | collective-permute-start | bytes 1572872 | tf_op jit(solution)/shard_map/ppermute | solution.py:596
  148.5 30.7 %collective-permute-start.20 = (bf16[128,1024]{1,0:T(8,128)(2,1)S(1)}, bf16[128,1024]{1,0:T(8,128)(2,1)S(1)}, u32[]{:S(2)}, u32[]{:S(2)}) collective-permute-start(bf16[128,1024]{1,0:T(8,128)(2,1)S(1)} %get-tuple-element.262), channel_id=1, source_target_pairs={{0,8},{8,0},{1,9},{9,1},{2,10},{10,2},{3,11},{11,3},{4,12},{12,4},... | collective-permute-start | bytes 786440 | tf_op jit(solution)/shard_map/ppermute | solution.py:596
  215.3 24.3 %all-to-all-start.1 = ((bf16[8,3,256,128]{3,2,1,0:T(8,128)(2,1)}), bf16[8,3,256,128]{3,2,1,0:T(8,128)(2,1)S(1)}, u32[]{:S(2)}, u32[]{:S(2)}) async-start(bf16[8,3,256,128]{3,2,1,0:T(8,128)(2,1)} %attend_back.3.d_ref), calls=%async_computation.1 | async-start | bytes 3145728 | tf_op jit(solution)/shard_map/all_to_all | solution.py:794
  288.7 15.8 %collective-permute-start.21 = (bf16[8,192,1024]{2,1,0:T(8,128)(2,1)}, bf16[8,192,1024]{2,1,0:T(8,128)(2,1)S(1)}, u32[]{:S(2)}, u32[]{:S(2)}) collective-permute-start(bf16[8,192,1024]{2,1,0:T(8,128)(2,1)} %get-tuple-element.139), channel_id=1, source_target_pairs={{0,1},{1,0},{2,3},{3,2},{4,5},{5,4},{6,7},{7,6},{8,9},{9,8},{10,11... | collective-permute-start | bytes 9437192 | tf_op jit(solution)/shard_map/ppermute | solution.py:596
  289.2 18.9 %all-to-all-start.2 = ((bf16[8,256,128]{2,1,0:T(8,128)(2,1)}), bf16[8,256,128]{2,1,0:T(8,128)(2,1)}, u32[]{:S(2)}, u32[]{:S(2)}) async-start(bf16[8,256,128]{2,1,0:T(8,128)(2,1)} %get-tuple-element.127), calls=%async_computation.2 | async-start | bytes 1048576 | tf_op jit(solution)/shard_map/all_to_all | solution.py:756
  298.4 57.7 %collective-permute-start.27 = (bf16[2,2,2,32,4096]{4,3,2,1,0:T(8,128)(2,1)}, bf16[2,2,2,32,4096]{4,3,2,1,0:T(8,128)(2,1)}, u32[]{:S(2)}, u32[]{:S(2)}) collective-permute-start(bf16[2,2,2,32,4096]{4,3,2,1,0:T(8,128)(2,1)} %fusion), channel_id=1, source_target_pairs={{0,16},{16,0},{1,17},{17,1},{2,18},{18,2},{3,19},{19,3},{4,20},{20... | collective-permute-start | bytes 6291464 | tf_op jit(solution)/shard_map/ppermute | solution.py:596
  302.5 25.6 %collective-permute-start.24 = (bf16[2,2,2,64,1024]{4,3,2,1,0:T(8,128)(2,1)}, bf16[2,2,2,64,1024]{4,3,2,1,0:T(8,128)(2,1)}, u32[]{:S(2)}, u32[]{:S(2)}) collective-permute-start(bf16[2,2,2,64,1024]{4,3,2,1,0:T(8,128)(2,1)} %fusion.20), channel_id=1, source_target_pairs={{0,4},{4,0},{1,5},{5,1},{2,6},{6,2},{3,7},{7,3},{8,12},{12,8},{9,1... | collective-permute-start | bytes 3145736 | tf_op jit(solution)/shard_map/ppermute | solution.py:596
  306.6 49.4 %collective-permute-start.26 = (bf16[2,2,2,96,1024]{4,3,2,1,0:T(8,128)(2,1)}, bf16[2,2,2,96,1024]{4,3,2,1,0:T(8,128)(2,1)}, u32[]{:S(2)}, u32[]{:S(2)}) collective-permute-start(bf16[2,2,2,96,1024]{4,3,2,1,0:T(8,128)(2,1)} %fusion.6), channel_id=1, source_target_pairs={{0,2},{2,0},{1,3},{3,1},{4,6},{6,4},{5,7},{7,5},{8,10},{10,8},{9,1... | collective-permute-start | bytes 4718600 | tf_op jit(solution)/shard_map/ppermute | solution.py:596
  330.5 25.5 %collective-permute-start.25 = (bf16[2,2,64,1024]{3,2,1,0:T(8,128)(2,1)}, bf16[2,2,64,1024]{3,2,1,0:T(8,128)(2,1)S(1)}, u32[]{:S(2)}, u32[]{:S(2)}) collective-permute-start(bf16[2,2,64,1024]{3,2,1,0:T(8,128)(2,1)} %fusion.22), channel_id=1, source_target_pairs={{0,8},{8,0},{1,9},{9,1},{2,10},{10,2},{3,11},{11,3},{4,12},{12,4},... | collective-permute-start | bytes 1572872 | tf_op jit(solution)/shard_map/ppermute | solution.py:596
  364.8 24.9 %all-to-all-start.3 = ((bf16[8,3,256,128]{3,2,1,0:T(8,128)(2,1)}), bf16[8,3,256,128]{3,2,1,0:T(8,128)(2,1)}, u32[]{:S(2)}, u32[]{:S(2)}) async-start(bf16[8,3,256,128]{3,2,1,0:T(8,128)(2,1)} %attend_back.5.d_ref), calls=%async_computation.3 | async-start | bytes 3145728 | tf_op jit(solution)/shard_map/all_to_all | solution.py:794
  371.7 18.0 %collective-permute-start.31 = (bf16[2,64,1024]{2,1,0:T(8,128)(2,1)}, bf16[2,64,1024]{2,1,0:T(8,128)(2,1)}, u32[]{:S(2)}, u32[]{:S(2)}) collective-permute-start(bf16[2,64,1024]{2,1,0:T(8,128)(2,1)} %fusion.28), channel_id=1, source_target_pairs={{0,16},{16,0},{1,17},{17,1},{2,18},{18,2},{3,19},{19,3},{4,20},{20... | collective-permute-start | bytes 786440 | tf_op jit(solution)/shard_map/ppermute | solution.py:596
  372.3 25.8 %collective-permute-start.30 = (bf16[2,2,96,1024]{3,2,1,0:T(8,128)(2,1)}, bf16[2,2,96,1024]{3,2,1,0:T(8,128)(2,1)}, u32[]{:S(2)}, u32[]{:S(2)}) collective-permute-start(bf16[2,2,96,1024]{3,2,1,0:T(8,128)(2,1)} %fusion.7), channel_id=1, source_target_pairs={{0,16},{16,0},{1,17},{17,1},{2,18},{18,2},{3,19},{19,3},{4,20},{20... | collective-permute-start | bytes 2359304 | tf_op jit(solution)/shard_map/ppermute | solution.py:596
  373.8 39.6 %collective-permute-start.28 = (bf16[2,2,32,4096]{3,2,1,0:T(8,128)(2,1)}, bf16[2,2,32,4096]{3,2,1,0:T(8,128)(2,1)}, u32[]{:S(2)}, u32[]{:S(2)}) collective-permute-start(bf16[2,2,32,4096]{3,2,1,0:T(8,128)(2,1)} %fusion.1), channel_id=1, source_target_pairs={{0,2},{2,0},{1,3},{3,1},{4,6},{6,4},{5,7},{7,5},{8,10},{10,8},{9,1... | collective-permute-start | bytes 3145736 | tf_op jit(solution)/shard_map/ppermute | solution.py:596
  383.7 22.2 %collective-permute-start.29 = (bf16[6,64,512]{2,1,0:T(8,128)(2,1)}, bf16[6,64,512]{2,1,0:T(8,128)(2,1)}, u32[]{:S(2)}, u32[]{:S(2)}) collective-permute-start(bf16[6,64,512]{2,1,0:T(8,128)(2,1)} %get-tuple-element.256), channel_id=1, source_target_pairs={{0,16},{16,0},{1,17},{17,1},{2,18},{18,2},{3,19},{19,3},{4,20},{20... | collective-permute-start | bytes 1179656 | tf_op jit(solution)/shard_map/ppermute | solution.py:596
  399.9 45.0 %collective-permute-start.36 = (bf16[64,1024]{1,0:T(8,128)(2,1)}, bf16[64,1024]{1,0:T(8,128)(2,1)S(1)}, u32[]{:S(2)}, u32[]{:S(2)}) collective-permute-start(bf16[64,1024]{1,0:T(8,128)(2,1)} %fusion.35), channel_id=1, source_target_pairs={{0,2},{2,0},{1,3},{3,1},{4,6},{6,4},{5,7},{7,5},{8,10},{10,8},{9,1... | collective-permute-start | bytes 393224 | tf_op jit(solution)/shard_map/ppermute | solution.py:596
  404.1 25.6 %collective-permute-start.32 = (bf16[2,96,1024]{2,1,0:T(8,128)(2,1)}, bf16[2,96,1024]{2,1,0:T(8,128)(2,1)}, u32[]{:S(2)}, u32[]{:S(2)}) collective-permute-start(bf16[2,96,1024]{2,1,0:T(8,128)(2,1)} %fusion.23), channel_id=1, source_target_pairs={{0,4},{4,0},{1,5},{5,1},{2,6},{6,2},{3,7},{7,3},{8,12},{12,8},{9,1... | collective-permute-start | bytes 1179656 | tf_op jit(solution)/shard_map/ppermute | solution.py:596
  408.9 25.9 %all-to-all-start.4 = ((bf16[16,64,512]{2,1,0:T(8,128)(2,1)}), bf16[16,64,512]{2,1,0:T(8,128)(2,1)}, u32[]{:S(2)}, u32[]{:S(2)}) async-start(bf16[16,64,512]{2,1,0:T(8,128)(2,1)} %take.3), calls=%async_computation.4 | async-start | bytes 2097152 | tf_op jit(solution)/shard_map/all_to_all | solution.py:809
  416.0 29.0 %collective-permute-start.35 = (bf16[2,32,4096]{2,1,0:T(8,128)(2,1)}, bf16[2,32,4096]{2,1,0:T(8,128)(2,1)}, u32[]{:S(2)}, u32[]{:S(2)}) collective-permute-start(bf16[2,32,4096]{2,1,0:T(8,128)(2,1)} %fusion.21), channel_id=1, source_target_pairs={{0,4},{4,0},{1,5},{5,1},{2,6},{6,2},{3,7},{7,3},{8,12},{12,8},{9,1... | collective-permute-start | bytes 1572872 | tf_op jit(solution)/shard_map/ppermute | solution.py:596
  429.7 40.2 %collective-permute-start.33 = (bf16[128,1024]{1,0:T(8,128)(2,1)}, bf16[128,1024]{1,0:T(8,128)(2,1)S(1)}, u32[]{:S(2)}, u32[]{:S(2)}) collective-permute-start(bf16[128,1024]{1,0:T(8,128)(2,1)} %get-tuple-element.178), channel_id=1, source_target_pairs={{0,8},{8,0},{1,9},{9,1},{2,10},{10,2},{3,11},{11,3},{4,12},{12,4},... | collective-permute-start | bytes 786440 | tf_op jit(solution)/shard_map/ppermute | solution.py:596
  431.8 38.1 %collective-permute-start.38 = (bf16[96,1024]{1,0:T(8,128)(2,1)}, bf16[96,1024]{1,0:T(8,128)(2,1)S(1)}, u32[]{:S(2)}, u32[]{:S(2)}) collective-permute-start(bf16[96,1024]{1,0:T(8,128)(2,1)} %fusion.31), channel_id=1, source_target_pairs={{0,8},{8,0},{1,9},{9,1},{2,10},{10,2},{3,11},{11,3},{4,12},{12,4},... | collective-permute-start | bytes 589832 | tf_op jit(solution)/shard_map/ppermute | solution.py:596
  437.4 32.6 %collective-permute-start.34 = (bf16[3,64,512]{2,1,0:T(8,128)(2,1)}, bf16[3,64,512]{2,1,0:T(8,128)(2,1)S(1)}, u32[]{:S(2)}, u32[]{:S(2)}) collective-permute-start(bf16[3,64,512]{2,1,0:T(8,128)(2,1)} %take.4), channel_id=1, source_target_pairs={{0,8},{8,0},{1,9},{9,1},{2,10},{10,2},{3,11},{11,3},{4,12},{12,4},... | collective-permute-start | bytes 589832 | tf_op jit(solution)/shard_map/ppermute | solution.py:596
  439.8 30.1 %all-to-all-start.5 = ((f32[16,1,1088]{2,1,0:T(1,128)}), f32[16,1,1088]{2,1,0:T(1,128)S(1)}, u32[]{:S(2)}, u32[]{:S(2)}) async-start(f32[16,1,1088]{2,1,0:T(1,128)} %copy.130), calls=%async_computation.5 | async-start | bytes 147456 | tf_op jit(solution)/shard_map/all_to_all | solution.py:840
  446.3 23.6 %collective-permute-start.42 = (bf16[64,1024]{1,0:T(8,128)(2,1)S(1)}, bf16[64,1024]{1,0:T(8,128)(2,1)S(1)}, u32[]{:S(2)}, u32[]{:S(2)}) collective-permute-start(bf16[64,1024]{1,0:T(8,128)(2,1)S(1)} %fusion.34), channel_id=1, source_target_pairs={{0,16},{16,0},{1,17},{17,1},{2,18},{18,2},{3,19},{19,3},{4,20},{20... | collective-permute-start | bytes 393224 | tf_op jit(solution)/shard_map/ppermute | solution.py:596
  448.3 26.0 %collective-permute-start.37 = (bf16[32,4096]{1,0:T(8,128)(2,1)S(1)}, bf16[32,4096]{1,0:T(8,128)(2,1)S(1)}, u32[]{:S(2)}, u32[]{:S(2)}) collective-permute-start(bf16[32,4096]{1,0:T(8,128)(2,1)S(1)} %fusion.27), channel_id=1, source_target_pairs={{0,8},{8,0},{1,9},{9,1},{2,10},{10,2},{3,11},{11,3},{4,12},{12,4},... | collective-permute-start | bytes 786440 | tf_op jit(solution)/shard_map/ppermute | solution.py:596
  480.0 13.5 %collective-permute-start.43 = (bf16[32,4096]{1,0:T(8,128)(2,1)S(1)}, bf16[32,4096]{1,0:T(8,128)(2,1)S(1)}, u32[]{:S(2)}, u32[]{:S(2)}) collective-permute-start(bf16[32,4096]{1,0:T(8,128)(2,1)S(1)} %fusion.26), channel_id=1, source_target_pairs={{0,16},{16,0},{1,17},{17,1},{2,18},{18,2},{3,19},{19,3},{4,20},{20... | collective-permute-start | bytes 786440 | tf_op jit(solution)/shard_map/ppermute | solution.py:596
  (66 other events, 782.5 us)

commit v9 on v7

--- a/solution.py
+++ b/solution.py
@@ -775,7 +775,7 @@
             d_heads = waits[0]
             for t, value in zip(shares, waits[1:]):
                 t.terms[-1] = value
-            sent = [x_share.halve("samp"), z_share.halve("samp")] + [down_share.halve(a) for a in x_axes]
+            sent = [x_share.halve("samp"), z_share.halve("samp")] + [down_share.halve("zh")]
             d_heads = pin(d_heads, *sent)
         else:
             own_grad, send_row, keep_rows = pin((own_grad, send_row, keep_rows), result)
@@ -799,7 +799,7 @@
             outgoing = take(units, send_row)
             incoming = lax.all_to_all(outgoing, low, 0, 0, tiled=True)
             down_share.terms[-1] = pin(down_share.terms[-1], outgoing)
-            back = pin(back, down_share.halve("zl"))
+            back = pin(back, *[down_share.halve(a) for a in x_axes])
         else:
             owns[0] = own_part(0)
             back = pin(back, w_heads, *owns[0])
@@ -846,7 +846,7 @@
         return x[:n], x[n:]
 
     incoming, down_share.terms[-1], z_share.terms[-1] = pin((incoming, down_share.terms[-1], z_share.terms[-1]), sums)
-    sent = down_share.halve("zh")
+    sent = down_share.halve("zl")
     own = take([incoming], keep_rows[0])
     up_first = total(z_share.terms).astype(bf16)
     late = (vectors, fields_other, other, down_share.terms[-1], x_share.terms[-1])

time: 498 us -> 499 us (level)
  waiting for transfers between devices: 92.4 us -> 97.8 us
    all_to_all x2, waiting for transfers between devices: 12.8 us -> 25.6 us  [body(): back = lax.all_to_all(d_heads, low, 0, 0, tiled=True)]
    all_to_all x1, waiting for transfers between devices: 13 us -> 5.29 us  [body(): vectors = lax.all_to_all(vectors, band, 0, 0, tiled=True)]
  transfers between devices with their start and end apart: 50 -> 50, of which waited for: 21 -> 20; matrix products, arithmetic and copies ran while one was open for 12% -> 12% of each run, Pallas kernels for 23% -> 23%
where the time goes in v9:
time: 499 us; the launch traced here: 493 us
  Pallas kernels  235 us (47%)
  waiting for transfers between devices  97.8 us (20%)
  starting transfers between devices  67.9 us (14%)
  other arithmetic  46.4 us (9%)
  local copies, waits for them, and re-layouts  29.6 us (6%)
  matrix products  11.4 us (2%)
    pallas_call x3, Pallas kernels, attend_back(): pl.pallas_call(functools.partial(attend_back_kernel, heads=heads, some=so...  69.5 us
    ppermute x44, waiting for transfers between devices, swap(): return lax.ppermute(x, axis, SWAP)  64.4 us
    pallas_call x2, Pallas kernels, attend(): pl.pallas_call(attend_kernel, grid=(width // block,), in_specs=[own, spec...  46.5 us
    ppermute x44, starting transfers between devices, swap(): return lax.ppermute(x, axis, SWAP)  42.8 us
    pallas_call x2, Pallas kernels, block_backward(): pl.pallas_call(functools.partial(block_backward_kernel, grads=bool(grads)...  39.4 us
    convert_element_type x12, other arithmetic, halve(): sent = total(there).astype(bf16)  29.8 us
    all_to_all x2, waiting for transfers between devices, body(): back = lax.all_to_all(d_heads, low, 0, 0, tiled=True)  25.6 us
    pallas_call x2, Pallas kernels, block_forward(): pl.pallas_call(functools.partial(block_forward_kernel, last=last), grid=(...  25.3 us
  transfers between devices with their start and end apart: 50, of which 20 were waited for; matrix products, arithmetic and copies ran while one was open for 12% of the time, Pallas kernels for 23%

profile of v9, /device:TPU:0, one launch (start us, length us, event | category | flops | bytes accessed | tf_op | source)
XLA Modules:
  0.0 493.1 jit_solution(215537814841555145)
XLA Ops:
  11.3 6.5 %collective-permute-done = bf16[128,1024]{1,0:T(8,128)(2,1)S(1)} collective-permute-done((bf16[128,1024]{1,0:T(8,128)(2,1)S(1)}, bf16[128,1024]{1,0:T(8,128)(2,1)S(1)}, u32[]{:S(2)}, u32[]{:S(2)}) %collective-permute-start) | collective-permute-done | bytes 262176 | tf_op jit(solution)/shard_map/ppermute | solution.py:588
  23.5 8.8 %collective-permute-done.2 = bf16[256,1024]{1,0:T(8,128)(2,1)S(1)} collective-permute-done((bf16[256,1024]{1,0:T(8,128)(2,1)S(1)}, bf16[256,1024]{1,0:T(8,128)(2,1)S(1)}, u32[]{:S(2)}, u32[]{:S(2)}) %collective-permute-start.2) | collective-permute-done | bytes 524320 | tf_op jit(solution)/shard_map/ppermute | solution.py:588
  46.3 23.4 %attend.2.a_ref.r0 = bf16[256,1024]{1,0:T(8,128)(2,1)S(1)} custom-call(bf16[256,1024]{1,0:T(8,128)(2,1)S(1)} %fusion.17.q_ref, bf16[2048,1024]{1,0:T(8,128)(2,1)S(1)} %constant_dynamic-update-slice_fusion.10.n_ref, bf16[1024,3072]{1,0:T(8,128)(2,1)S(1)} %copy-done.2, bf16[1024,3072]{1,0:T(8,128)(2,1)S(1)} %copy-done.2, f32[1,1024]{1,0:T(1,128)S(1)} %bitcast.257), custom_call_target="tpu_custom_call" | custom-call | flops 27599998976 | bytes 1000 | tf_op jit(solution)/shard_map/attend/pallas_call | solution.py:64
  70.0 12.8 %block_forward.2 = (f32[256,1024]{1,0:T(8,128)S(1)}, f32[256,1]{1,0:T(8,128)S(1)}, bf16[256,1024]{1,0:T(8,128)(2,1)S(1)}, f32[256,4096]{1,0:T(8,128)S(1)}, bf16[...) custom-call(f32[256,1024]{1,0:T(8,128)S(1)} %get-tuple-element.258.x, ...), custom_call_target="tpu_custom_call" | custom-call | flops 13799999488 | bytes 1000 | tf_op jit(solution)/shard_map/block_forward/pallas_call | solution.py:235
  90.8 9.4 %collective-permute-done.12 = bf16[256,1024]{1,0:T(8,128)(2,1)S(1)} collective-permute-done((bf16[256,1024]{1,0:T(8,128)(2,1)S(1)}, bf16[256,1024]{1,0:T(8,128)(2,1)S(1)}, u32[]{:S(2)}, u32[]{:S(2)}) %collective-permute-start.12) | collective-permute-done | bytes 524320 | tf_op jit(solution)/shard_map/ppermute | solution.py:588
  110.0 23.0 %attend.3.a_ref.r1 = bf16[256,1024]{1,0:T(8,128)(2,1)S(1)} custom-call(bf16[256,1024]{1,0:T(8,128)(2,1)S(1)} %fusion.14.q_ref, bf16[2048,1024]{1,0:T(8,128)(2,1)S(1)} %constant_dynamic-update-slice_fusion.n_ref, bf16[1024,3072]{1,0:T(8,128)(2,1)S(1)} %copy-done.2, bf16[1024,3072]{1,0:T(8,128)(2,1)S(1)} %copy-done.2, f32[1,1024]{1,0:T(1,128)S(1)} %bitcast.258), custom_call_target="tpu_custom_call" | custom-call | flops 27599998976 | bytes 1000 | tf_op jit(solution)/shard_map/attend/pallas_call | solution.py:64
  133.1 12.6 %block_forward.3 = (f32[256,1024]{1,0:T(8,128)S(1)}, f32[256,1]{1,0:T(8,128)S(1)}, bf16[256,1024]{1,0:T(8,128)(2,1)S(1)}, f32[256,4096]{1,0:T(8,128)S(1)}, bf16[...) custom-call(f32[256,1024]{1,0:T(8,128)S(1)} %copy-done.24, bf16[256,1024]{1,0:T(8,128)(2,1)S(1)} %attend.3.a_ref.r1, ...), custom_call_target="tpu_custom_call" | custom-call | flops 13799999488 | bytes 1000 | tf_op jit(solution)/shard_map/block_forward/pallas_call | solution.py:235
  151.4 16.6 %block_backward.2 = (bf16[256,4096]{1,0:T(8,128)(2,1)}, f32[1,4096]{1,0:T(1,128)S(1)}, f32[256,1024]{1,0:T(8,128)S(1)}, bf16[256,1024]{1,0:T(8,128)(2,1)S(1)}, b...) custom-call(s32[1]{0:T(128)} %bitcast.17.c_ref, f32[256,1024]{1,0:T(8,128)S(1)} %pad_maximum_fusion.grad_ref, ...), custom_call_target="tpu_custom_call" | custom-call | flops 16099999744 | bytes 1000 | tf_op jit(solution)/shard_map/block_backward/pallas_call | solution.py:333
  173.4 4.5 add_convert_fusion.2
  183.4 31.9 %attend_back.3.d_ref = bf16[8,3,256,128]{3,2,1,0:T(8,128)(2,1)} custom-call(bf16[2048,128]{1,0:T(8,128)(2,1)} %get-tuple-element.249.q_ref, bf16[2048,128]{1,0:T(8,128)(2,1)} %get-tuple-element.248.k_ref, bf16[2048,128]{1,0:T(8,128)(2,1)} %get-tuple-element.247.v_ref, bf16[2048,128]{1,0:T(8,128)(2,1)} %bitcast.292), custom_call_target="tpu_custom_call" | custom-call | flops 37950001152 | bytes 1000 | tf_op jit(solution)/shard_map/attend_back/pallas_call | solution.py:134
  219.2 4.5 add_convert_fusion.3
  225.8 5.9 %grad_heads.2.rest_0_ = f32[3,128,1024]{2,1,0:T(8,128)} custom-call(bf16[8,3,256,128]{3,2,1,0:T(8,128)(2,1)} %attend_back.3.d_ref, bf16[2048,1024]{1,0:T(8,128)(2,1)} %copy-done.1), custom_call_target="tpu_custom_call" | custom-call | flops 5750000128 | bytes 1000 | tf_op jit(solution)/shard_map/grad_heads/pallas_call | solution.py:460
  231.7 7.9 %all-to-all-done.1.b_ref = bf16[8,3,256,128]{3,2,1,0:T(8,128)(2,1)S(1)} async-done(((bf16[8,3,256,128]{3,2,1,0:T(8,128)(2,1)}), bf16[8,3,256,128]{3,2,1,0:T(8,128)(2,1)S(1)}, u32[]{:S(2)}, u32[]{:S(2)}) %all-to-all-start.1) | async-done | bytes 1572896 | tf_op jit(solution)/shard_map/all_to_all | solution.py:785
  240.8 9.0 %qkv_backward.2 = (f32[256,1024]{1,0:T(8,128)}, bf16[256,1024]{1,0:T(8,128)(2,1)}, f32[8,1024]{1,0:T(8,128)}, f32[8,1024]{1,0:T(8,128)}) custom-call(bf16[8,3,256,128]{3,2,1,0:T(8,128)(2,1)} %copy-done.32, bf16[1024,3072]{1,0:T(8,128)(2,1)} %wv_ref.7, bf16[1024,3072]{1,0:T(8,128)(2,1)} %wv_ref.7, bf16[1024,3072]{1,0:T(8,128)(2,1)} %wv_ref.7, ...), custom_call_target="tpu_custom_call" | custom-call | flops 13799999488 | bytes 1000 | tf_op jit(solution)/shard_map/qkv_backward/pallas_call | solution.py:424
  249.8 22.8 %block_backward.3 = (bf16[256,4096]{1,0:T(8,128)(2,1)}, f32[1,4096]{1,0:T(1,128)}, f32[256,1024]{1,0:T(8,128)}, bf16[256,1024]{1,0:T(8,128)(2,1)}, bf16[8,256,12...) custom-call(s32[1]{0:T(128)} %bitcast.17.c_ref, ...), custom_call_target="tpu_custom_call" | custom-call | flops 20700000256 | bytes 1000 | tf_op jit(solution)/shard_map/block_backward/pallas_call | solution.py:333
  272.6 10.9 %grad_rows.1 = (bf16[8,64,4096]{2,1,0:T(8,128)(2,1)}, bf16[8,64,4096]{2,1,0:T(8,128)(2,1)}) custom-call(s32[1]{0:T(128)} %bitcast.17.c_ref, bf16[256,1024]{1,0:T(8,128)(2,1)} %convert_element_type.449.l1, bf16[256,1024]{1,0:T(8,128)(2,1)} %get-tuple-element.131.l0, bf16[256,4096]{1,0:T(8,128)(2,1)} %copy-done.19, bf16[256,4096]{1,0:T(8,128)(2,1)} %copy-done.18), custom_call_target="tpu_custom_call" | custom-call | flops 9200000000 | bytes 1000 | tf_op jit(solution)/shard_map/grad_rows/pallas_call | solution.py:167
  283.8 5.0 %grad_out.1 = (bf16[8,192,1024]{2,1,0:T(8,128)(2,1)}, bf16[8,192,1024]{2,1,0:T(8,128)(2,1)}) custom-call(s32[1]{0:T(128)} %bitcast.17.c_ref, bf16[256,1024]{1,0:T(8,128)(2,1)} %copy-done.15, bf16[256,1024]{1,0:T(8,128)(2,1)} %get-tuple-element.135.l0, bf16[256,1024]{1,0:T(8,128)(2,1)} %copy-done.14, ...), custom_call_target="tpu_custom_call", output_to_operand_aliasing={{0}: (5, {}), {1}: (6, {})} | custom-call | flops 3449999872 | bytes 1000 | tf_op jit(solution)/shard_map/grad_out/pallas_call | solution.py:370
  289.3 4.6 all-to-all-start.2
  293.9 4.5 fusion
  308.1 18.5 %attend_back.4.rest_0_ = bf16[8,3,256,128]{3,2,1,0:T(8,128)(2,1)} custom-call(bf16[2048,128]{1,0:T(8,128)(2,1)} %get-tuple-element.252.q_ref, bf16[2048,128]{1,0:T(8,128)(2,1)} %get-tuple-element.251.k_ref, bf16[2048,128]{1,0:T(8,128)(2,1)} %get-tuple-element.250.v_ref, bf16[2048,128]{1,0:T(8,128)(2,1)} %bitcast.22.do_ref), custom_call_target="tpu_custom_call" | custom-call | flops 19549999104 | bytes 1000 | tf_op jit(solution)/shard_map/attend_back/pallas_call | solution.py:134
  331.1 19.1 %attend_back.5.d_ref = bf16[8,3,256,128]{3,2,1,0:T(8,128)(2,1)} custom-call(bf16[2048,128]{1,0:T(8,128)(2,1)} %get-tuple-element.252.q_ref, bf16[2048,128]{1,0:T(8,128)(2,1)} %get-tuple-element.251.k_ref, bf16[2048,128]{1,0:T(8,128)(2,1)} %get-tuple-element.250.v_ref, bf16[2048,128]{1,0:T(8,128)(2,1)} %bitcast.22.do_ref, ...), custom_call_target="tpu_custom_call" | custom-call | flops 19549999104 | bytes 1000 | tf_op jit(solution)/shard_map/attend_back/pallas_call | solution.py:134
  350.2 5.8 %collective-permute-done.25 = bf16[2,2,64,1024]{3,2,1,0:T(8,128)(2,1)S(1)} collective-permute-done((bf16[2,2,64,1024]{3,2,1,0:T(8,128)(2,1)}, bf16[2,2,64,1024]{3,2,1,0:T(8,128)(2,1)S(1)}, u32[]{:S(2)}, u32[]{:S(2)}) %collective-permute-start.25) | collective-permute-done | bytes 524320 | tf_op jit(solution)/shard_map/ppermute | solution.py:588
  364.9 4.3 all-to-all-start.3
  373.8 6.0 %grad_heads.3 = bf16[3,128,1024]{2,1,0:T(8,128)(2,1)} custom-call(bf16[8,3,256,128]{3,2,1,0:T(8,128)(2,1)} %attend_back.5.d_ref, bf16[2048,1024]{1,0:T(8,128)(2,1)} %copy-done, f32[3,128,1024]{2,1,0:T(8,128)} %grad_heads.2.rest_0_), custom_call_target="tpu_custom_call" | custom-call | flops 5750000128 | bytes 1000 | tf_op jit(solution)/shard_map/grad_heads/pallas_call | solution.py:460
  383.0 17.7 %all-to-all-done.3.b_ref = bf16[8,3,256,128]{3,2,1,0:T(8,128)(2,1)} async-done(((bf16[8,3,256,128]{3,2,1,0:T(8,128)(2,1)}), bf16[8,3,256,128]{3,2,1,0:T(8,128)(2,1)}, u32[]{:S(2)}, u32[]{:S(2)}) %all-to-all-start.3) | async-done | bytes 1572896 | tf_op jit(solution)/shard_map/all_to_all | solution.py:785
  409.0 4.4 all-to-all-start.4
  413.4 9.1 %collective-permute-done.28 = bf16[2,2,32,4096]{3,2,1,0:T(8,128)(2,1)} collective-permute-done((bf16[2,2,32,4096]{3,2,1,0:T(8,128)(2,1)}, bf16[2,2,32,4096]{3,2,1,0:T(8,128)(2,1)}, u32[]{:S(2)}, u32[]{:S(2)}) %collective-permute-start.28) | collective-permute-done | bytes 1048608 | tf_op jit(solution)/shard_map/ppermute | solution.py:588
  426.7 8.9 %qkv_backward.3 = (f32[256,1024]{1,0:T(8,128)}, bf16[128,1024]{1,0:T(8,128)(2,1)}, f32[8,1024]{1,0:T(8,128)}, f32[8,1024]{1,0:T(8,128)}) custom-call(bf16[8,3,256,128]{3,2,1,0:T(8,128)(2,1)} %all-to-all-done.3.b_ref, bf16[1024,3072]{1,0:T(8,128)(2,1)} %wv_ref.7, bf16[1024,3072]{1,0:T(8,128)(2,1)} %wv_ref.7, bf16[1024,3072]{1,0:T(8,128)(2,1)} %wv_ref.7, ...), custom_call_target="tpu_custom_call" | custom-call | flops 13799999488 | bytes 1000 | tf_op jit(solution)/shard_map/qkv_backward/pallas_call | solution.py:424
  448.5 4.3 all-to-all-start.5
  460.7 5.3 %all-to-all-done.5 = f32[16,1,1088]{2,1,0:T(1,128)S(1)} async-done(((f32[16,1,1088]{2,1,0:T(1,128)}), f32[16,1,1088]{2,1,0:T(1,128)S(1)}, u32[]{:S(2)}, u32[]{:S(2)}) %all-to-all-start.5) | async-done | bytes 69664 | tf_op jit(solution)/shard_map/all_to_all | solution.py:829
  466.1 5.5 %collective-permute-done.37 = bf16[32,4096]{1,0:T(8,128)(2,1)S(1)} collective-permute-done((bf16[32,4096]{1,0:T(8,128)(2,1)S(1)}, bf16[32,4096]{1,0:T(8,128)(2,1)S(1)}, u32[]{:S(2)}, u32[]{:S(2)}) %collective-permute-start.37) | collective-permute-done | bytes 262176 | tf_op jit(solution)/shard_map/ppermute | solution.py:588
  482.0 5.3 %collective-permute-done.41 = bf16[96,1024]{1,0:T(8,128)(2,1)S(1)} collective-permute-done((bf16[96,1024]{1,0:T(8,128)(2,1)S(1)}, bf16[96,1024]{1,0:T(8,128)(2,1)S(1)}, u32[]{:S(2)}, u32[]{:S(2)}) %collective-permute-start.41) | collective-permute-done | bytes 196640 | tf_op jit(solution)/shard_map/ppermute | solution.py:588
  (291 shorter events, 149.8 us)
Async XLA Ops:
  1.8 16.0 %collective-permute-start = (bf16[128,1024]{1,0:T(8,128)(2,1)S(1)}, bf16[128,1024]{1,0:T(8,128)(2,1)S(1)}, u32[]{:S(2)}, u32[]{:S(2)}) collective-permute-start(bf16[128,1024]{1,0:T(8,128)(2,1)S(1)} %get-tuple-element.264), channel_id=1, source_target_pairs={{0,8},{8,0},{1,9},{9,1},{2,10},{10,2},{3,11},{11,3},{4,12},{12,4},... | collective-permute-start | bytes 786440 | tf_op jit(solution)/shard_map/ppermute | solution.py:588
  19.1 13.2 %collective-permute-start.2 = (bf16[256,1024]{1,0:T(8,128)(2,1)S(1)}, bf16[256,1024]{1,0:T(8,128)(2,1)S(1)}, u32[]{:S(2)}, u32[]{:S(2)}) collective-permute-start(bf16[256,1024]{1,0:T(8,128)(2,1)S(1)} %get-tuple-element.243), channel_id=1, source_target_pairs={{0,4},{4,0},{1,5},{5,1},{2,6},{6,2},{3,7},{7,3},{8,12},{12,8},{9,1... | collective-permute-start | bytes 1572872 | tf_op jit(solution)/shard_map/ppermute | solution.py:588
  19.9 13.7 %collective-permute-start.1 = (bf16[256,1024]{1,0:T(8,128)(2,1)S(1)}, bf16[256,1024]{1,0:T(8,128)(2,1)S(1)}, u32[]{:S(2)}, u32[]{:S(2)}) collective-permute-start(bf16[256,1024]{1,0:T(8,128)(2,1)S(1)} %get-tuple-element.243), channel_id=1, source_target_pairs={{0,2},{2,0},{1,3},{3,1},{4,6},{6,4},{5,7},{7,5},{8,10},{10,8},{9,1... | collective-permute-start | bytes 1572872 | tf_op jit(solution)/shard_map/ppermute | solution.py:588
  22.7 18.2 %collective-permute-start.5 = (bf16[256,1024]{1,0:T(8,128)(2,1)S(1)}, bf16[256,1024]{1,0:T(8,128)(2,1)S(1)}, u32[]{:S(2)}, u32[]{:S(2)}) collective-permute-start(bf16[256,1024]{1,0:T(8,128)(2,1)S(1)} %get-tuple-element.243), channel_id=1, source_target_pairs={{0,1},{1,0},{2,3},{3,2},{4,5},{5,4},{6,7},{7,6},{8,9},{9,8},{10,11... | collective-permute-start | bytes 1572872 | tf_op jit(solution)/shard_map/ppermute | solution.py:588
  42.5 27.2 %collective-permute-start.10 = (f32[128,1024]{1,0:T(8,128)S(1)}, f32[128,1024]{1,0:T(8,128)S(1)}, u32[]{:S(2)}, u32[]{:S(2)}) collective-permute-start(f32[128,1024]{1,0:T(8,128)S(1)} %get-tuple-element.254), channel_id=1, source_target_pairs={{0,8},{8,0},{1,9},{9,1},{2,10},{10,2},{3,11},{11,3},{4,12},{12,4},... | collective-permute-start | bytes 1572872 | tf_op jit(solution)/shard_map/ppermute | solution.py:588
  86.5 13.7 %collective-permute-start.12 = (bf16[256,1024]{1,0:T(8,128)(2,1)S(1)}, bf16[256,1024]{1,0:T(8,128)(2,1)S(1)}, u32[]{:S(2)}, u32[]{:S(2)}) collective-permute-start(bf16[256,1024]{1,0:T(8,128)(2,1)S(1)} %get-tuple-element.108), channel_id=1, source_target_pairs={{0,4},{4,0},{1,5},{5,1},{2,6},{6,2},{3,7},{7,3},{8,12},{12,8},{9,1... | collective-permute-start | bytes 1572872 | tf_op jit(solution)/shard_map/ppermute | solution.py:588
  88.0 13.4 %collective-permute-start.11 = (bf16[256,1024]{1,0:T(8,128)(2,1)S(1)}, bf16[256,1024]{1,0:T(8,128)(2,1)S(1)}, u32[]{:S(2)}, u32[]{:S(2)}) collective-permute-start(bf16[256,1024]{1,0:T(8,128)(2,1)S(1)} %get-tuple-element.108), channel_id=1, source_target_pairs={{0,2},{2,0},{1,3},{3,1},{4,6},{6,4},{5,7},{7,5},{8,10},{10,8},{9,1... | collective-permute-start | bytes 1572872 | tf_op jit(solution)/shard_map/ppermute | solution.py:588
  90.0 18.4 %collective-permute-start.15 = (bf16[256,1024]{1,0:T(8,128)(2,1)S(1)}, bf16[256,1024]{1,0:T(8,128)(2,1)S(1)}, u32[]{:S(2)}, u32[]{:S(2)}) collective-permute-start(bf16[256,1024]{1,0:T(8,128)(2,1)S(1)} %get-tuple-element.108), channel_id=1, source_target_pairs={{0,1},{1,0},{2,3},{3,2},{4,5},{5,4},{6,7},{7,6},{8,9},{9,8},{10,11... | collective-permute-start | bytes 1572872 | tf_op jit(solution)/shard_map/ppermute | solution.py:588
  148.5 30.8 %collective-permute-start.20 = (bf16[128,1024]{1,0:T(8,128)(2,1)S(1)}, bf16[128,1024]{1,0:T(8,128)(2,1)S(1)}, u32[]{:S(2)}, u32[]{:S(2)}) collective-permute-start(bf16[128,1024]{1,0:T(8,128)(2,1)S(1)} %get-tuple-element.262), channel_id=1, source_target_pairs={{0,8},{8,0},{1,9},{9,1},{2,10},{10,2},{3,11},{11,3},{4,12},{12,4},... | collective-permute-start | bytes 786440 | tf_op jit(solution)/shard_map/ppermute | solution.py:588
  169.7 12.9 %all-to-all-start = ((bf16[8,256,128]{2,1,0:T(8,128)(2,1)}), bf16[8,256,128]{2,1,0:T(8,128)(2,1)S(1)}, u32[]{:S(2)}, u32[]{:S(2)}) async-start(bf16[8,256,128]{2,1,0:T(8,128)(2,1)} %get-tuple-element.114), calls=%async_computation | async-start | bytes 1048576 | tf_op jit(solution)/shard_map/all_to_all | solution.py:747
  215.3 24.3 %all-to-all-start.1 = ((bf16[8,3,256,128]{3,2,1,0:T(8,128)(2,1)}), bf16[8,3,256,128]{3,2,1,0:T(8,128)(2,1)S(1)}, u32[]{:S(2)}, u32[]{:S(2)}) async-start(bf16[8,3,256,128]{3,2,1,0:T(8,128)(2,1)} %attend_back.3.d_ref), calls=%async_computation.1 | async-start | bytes 3145728 | tf_op jit(solution)/shard_map/all_to_all | solution.py:785
  288.8 15.7 %collective-permute-start.21 = (bf16[8,192,1024]{2,1,0:T(8,128)(2,1)}, bf16[8,192,1024]{2,1,0:T(8,128)(2,1)S(1)}, u32[]{:S(2)}, u32[]{:S(2)}) collective-permute-start(bf16[8,192,1024]{2,1,0:T(8,128)(2,1)} %get-tuple-element.139), channel_id=1, source_target_pairs={{0,1},{1,0},{2,3},{3,2},{4,5},{5,4},{6,7},{7,6},{8,9},{9,8},{10,11... | collective-permute-start | bytes 9437192 | tf_op jit(solution)/shard_map/ppermute | solution.py:588
  289.3 18.8 %all-to-all-start.2 = ((bf16[8,256,128]{2,1,0:T(8,128)(2,1)}), bf16[8,256,128]{2,1,0:T(8,128)(2,1)}, u32[]{:S(2)}, u32[]{:S(2)}) async-start(bf16[8,256,128]{2,1,0:T(8,128)(2,1)} %get-tuple-element.127), calls=%async_computation.2 | async-start | bytes 1048576 | tf_op jit(solution)/shard_map/all_to_all | solution.py:747
  298.4 57.7 %collective-permute-start.27 = (bf16[2,2,2,32,4096]{4,3,2,1,0:T(8,128)(2,1)}, bf16[2,2,2,32,4096]{4,3,2,1,0:T(8,128)(2,1)}, u32[]{:S(2)}, u32[]{:S(2)}) collective-permute-start(bf16[2,2,2,32,4096]{4,3,2,1,0:T(8,128)(2,1)} %fusion), channel_id=1, source_target_pairs={{0,16},{16,0},{1,17},{17,1},{2,18},{18,2},{3,19},{19,3},{4,20},{20... | collective-permute-start | bytes 6291464 | tf_op jit(solution)/shard_map/ppermute | solution.py:588
  302.5 25.6 %collective-permute-start.24 = (bf16[2,2,2,64,1024]{4,3,2,1,0:T(8,128)(2,1)}, bf16[2,2,2,64,1024]{4,3,2,1,0:T(8,128)(2,1)}, u32[]{:S(2)}, u32[]{:S(2)}) collective-permute-start(bf16[2,2,2,64,1024]{4,3,2,1,0:T(8,128)(2,1)} %fusion.20), channel_id=1, source_target_pairs={{0,4},{4,0},{1,5},{5,1},{2,6},{6,2},{3,7},{7,3},{8,12},{12,8},{9,1... | collective-permute-start | bytes 3145736 | tf_op jit(solution)/shard_map/ppermute | solution.py:588
  306.6 49.4 %collective-permute-start.26 = (bf16[2,2,2,96,1024]{4,3,2,1,0:T(8,128)(2,1)}, bf16[2,2,2,96,1024]{4,3,2,1,0:T(8,128)(2,1)}, u32[]{:S(2)}, u32[]{:S(2)}) collective-permute-start(bf16[2,2,2,96,1024]{4,3,2,1,0:T(8,128)(2,1)} %fusion.6), channel_id=1, source_target_pairs={{0,2},{2,0},{1,3},{3,1},{4,6},{6,4},{5,7},{7,5},{8,10},{10,8},{9,1... | collective-permute-start | bytes 4718600 | tf_op jit(solution)/shard_map/ppermute | solution.py:588
  330.5 25.5 %collective-permute-start.25 = (bf16[2,2,64,1024]{3,2,1,0:T(8,128)(2,1)}, bf16[2,2,64,1024]{3,2,1,0:T(8,128)(2,1)S(1)}, u32[]{:S(2)}, u32[]{:S(2)}) collective-permute-start(bf16[2,2,64,1024]{3,2,1,0:T(8,128)(2,1)} %fusion.22), channel_id=1, source_target_pairs={{0,8},{8,0},{1,9},{9,1},{2,10},{10,2},{3,11},{11,3},{4,12},{12,4},... | collective-permute-start | bytes 1572872 | tf_op jit(solution)/shard_map/ppermute | solution.py:588
  364.9 35.8 %all-to-all-start.3 = ((bf16[8,3,256,128]{3,2,1,0:T(8,128)(2,1)}), bf16[8,3,256,128]{3,2,1,0:T(8,128)(2,1)}, u32[]{:S(2)}, u32[]{:S(2)}) async-start(bf16[8,3,256,128]{3,2,1,0:T(8,128)(2,1)} %attend_back.5.d_ref), calls=%async_computation.3 | async-start | bytes 3145728 | tf_op jit(solution)/shard_map/all_to_all | solution.py:785
  371.8 28.9 %collective-permute-start.31 = (bf16[2,64,1024]{2,1,0:T(8,128)(2,1)}, bf16[2,64,1024]{2,1,0:T(8,128)(2,1)}, u32[]{:S(2)}, u32[]{:S(2)}) collective-permute-start(bf16[2,64,1024]{2,1,0:T(8,128)(2,1)} %fusion.28), channel_id=1, source_target_pairs={{0,16},{16,0},{1,17},{17,1},{2,18},{18,2},{3,19},{19,3},{4,20},{20... | collective-permute-start | bytes 786440 | tf_op jit(solution)/shard_map/ppermute | solution.py:588
  372.3 28.4 %collective-permute-start.30 = (bf16[2,2,96,1024]{3,2,1,0:T(8,128)(2,1)}, bf16[2,2,96,1024]{3,2,1,0:T(8,128)(2,1)}, u32[]{:S(2)}, u32[]{:S(2)}) collective-permute-start(bf16[2,2,96,1024]{3,2,1,0:T(8,128)(2,1)} %fusion.7), channel_id=1, source_target_pairs={{0,16},{16,0},{1,17},{17,1},{2,18},{18,2},{3,19},{19,3},{4,20},{20... | collective-permute-start | bytes 2359304 | tf_op jit(solution)/shard_map/ppermute | solution.py:588
  373.8 48.7 %collective-permute-start.28 = (bf16[2,2,32,4096]{3,2,1,0:T(8,128)(2,1)}, bf16[2,2,32,4096]{3,2,1,0:T(8,128)(2,1)}, u32[]{:S(2)}, u32[]{:S(2)}) collective-permute-start(bf16[2,2,32,4096]{3,2,1,0:T(8,128)(2,1)} %fusion.1), channel_id=1, source_target_pairs={{0,8},{8,0},{1,9},{9,1},{2,10},{10,2},{3,11},{11,3},{4,12},{12,4},... | collective-permute-start | bytes 3145736 | tf_op jit(solution)/shard_map/ppermute | solution.py:588
  381.9 24.1 %collective-permute-start.29 = (bf16[6,64,512]{2,1,0:T(8,128)(2,1)}, bf16[6,64,512]{2,1,0:T(8,128)(2,1)}, u32[]{:S(2)}, u32[]{:S(2)}) collective-permute-start(bf16[6,64,512]{2,1,0:T(8,128)(2,1)} %get-tuple-element.256), channel_id=1, source_target_pairs={{0,16},{16,0},{1,17},{17,1},{2,18},{18,2},{3,19},{19,3},{4,20},{20... | collective-permute-start | bytes 1179656 | tf_op jit(solution)/shard_map/ppermute | solution.py:588
  402.6 50.2 %collective-permute-start.36 = (bf16[64,1024]{1,0:T(8,128)(2,1)}, bf16[64,1024]{1,0:T(8,128)(2,1)S(1)}, u32[]{:S(2)}, u32[]{:S(2)}) collective-permute-start(bf16[64,1024]{1,0:T(8,128)(2,1)} %fusion.35), channel_id=1, source_target_pairs={{0,2},{2,0},{1,3},{3,1},{4,6},{6,4},{5,7},{7,5},{8,10},{10,8},{9,1... | collective-permute-start | bytes 393224 | tf_op jit(solution)/shard_map/ppermute | solution.py:588
  404.9 33.6 %collective-permute-start.32 = (bf16[2,96,1024]{2,1,0:T(8,128)(2,1)}, bf16[2,96,1024]{2,1,0:T(8,128)(2,1)}, u32[]{:S(2)}, u32[]{:S(2)}) collective-permute-start(bf16[2,96,1024]{2,1,0:T(8,128)(2,1)} %fusion.23), channel_id=1, source_target_pairs={{0,4},{4,0},{1,5},{5,1},{2,6},{6,2},{3,7},{7,3},{8,12},{12,8},{9,1... | collective-permute-start | bytes 1179656 | tf_op jit(solution)/shard_map/ppermute | solution.py:588
  409.0 34.6 %all-to-all-start.4 = ((bf16[16,64,512]{2,1,0:T(8,128)(2,1)}), bf16[16,64,512]{2,1,0:T(8,128)(2,1)}, u32[]{:S(2)}, u32[]{:S(2)}) async-start(bf16[16,64,512]{2,1,0:T(8,128)(2,1)} %take.3), calls=%async_computation.4 | async-start | bytes 2097152 | tf_op jit(solution)/shard_map/all_to_all | solution.py:800
  425.1 27.7 %collective-permute-start.35 = (bf16[2,32,4096]{2,1,0:T(8,128)(2,1)}, bf16[2,32,4096]{2,1,0:T(8,128)(2,1)}, u32[]{:S(2)}, u32[]{:S(2)}) collective-permute-start(bf16[2,32,4096]{2,1,0:T(8,128)(2,1)} %fusion.21), channel_id=1, source_target_pairs={{0,2},{2,0},{1,3},{3,1},{4,6},{6,4},{5,7},{7,5},{8,10},{10,8},{9,1... | collective-permute-start | bytes 1572872 | tf_op jit(solution)/shard_map/ppermute | solution.py:588
  435.6 30.4 %collective-permute-start.33 = (bf16[128,1024]{1,0:T(8,128)(2,1)}, bf16[128,1024]{1,0:T(8,128)(2,1)S(1)}, u32[]{:S(2)}, u32[]{:S(2)}) collective-permute-start(bf16[128,1024]{1,0:T(8,128)(2,1)} %get-tuple-element.178), channel_id=1, source_target_pairs={{0,8},{8,0},{1,9},{9,1},{2,10},{10,2},{3,11},{11,3},{4,12},{12,4},... | collective-permute-start | bytes 786440 | tf_op jit(solution)/shard_map/ppermute | solution.py:588
  440.6 25.5 %collective-permute-start.38 = (bf16[96,1024]{1,0:T(8,128)(2,1)}, bf16[96,1024]{1,0:T(8,128)(2,1)S(1)}, u32[]{:S(2)}, u32[]{:S(2)}) collective-permute-start(bf16[96,1024]{1,0:T(8,128)(2,1)} %fusion.31), channel_id=1, source_target_pairs={{0,8},{8,0},{1,9},{9,1},{2,10},{10,2},{3,11},{11,3},{4,12},{12,4},... | collective-permute-start | bytes 589832 | tf_op jit(solution)/shard_map/ppermute | solution.py:588
  446.1 19.9 %collective-permute-start.34 = (bf16[3,64,512]{2,1,0:T(8,128)(2,1)}, bf16[3,64,512]{2,1,0:T(8,128)(2,1)S(1)}, u32[]{:S(2)}, u32[]{:S(2)}) collective-permute-start(bf16[3,64,512]{2,1,0:T(8,128)(2,1)} %take.4), channel_id=1, source_target_pairs={{0,8},{8,0},{1,9},{9,1},{2,10},{10,2},{3,11},{11,3},{4,12},{12,4},... | collective-permute-start | bytes 589832 | tf_op jit(solution)/shard_map/ppermute | solution.py:588
  448.5 17.5 %all-to-all-start.5 = ((f32[16,1,1088]{2,1,0:T(1,128)}), f32[16,1,1088]{2,1,0:T(1,128)S(1)}, u32[]{:S(2)}, u32[]{:S(2)}) async-start(f32[16,1,1088]{2,1,0:T(1,128)} %copy.127), calls=%async_computation.5 | async-start | bytes 147456 | tf_op jit(solution)/shard_map/all_to_all | solution.py:829
  456.1 15.5 %collective-permute-start.37 = (bf16[32,4096]{1,0:T(8,128)(2,1)S(1)}, bf16[32,4096]{1,0:T(8,128)(2,1)S(1)}, u32[]{:S(2)}, u32[]{:S(2)}) collective-permute-start(bf16[32,4096]{1,0:T(8,128)(2,1)S(1)} %fusion.27), channel_id=1, source_target_pairs={{0,4},{4,0},{1,5},{5,1},{2,6},{6,2},{3,7},{7,3},{8,12},{12,8},{9,1... | collective-permute-start | bytes 786440 | tf_op jit(solution)/shard_map/ppermute | solution.py:588
  477.4 14.5 %collective-permute-start.43 = (bf16[32,4096]{1,0:T(8,128)(2,1)S(1)}, bf16[32,4096]{1,0:T(8,128)(2,1)S(1)}, u32[]{:S(2)}, u32[]{:S(2)}) collective-permute-start(bf16[32,4096]{1,0:T(8,128)(2,1)S(1)} %fusion.26), channel_id=1, source_target_pairs={{0,16},{16,0},{1,17},{17,1},{2,18},{18,2},{3,19},{19,3},{4,20},{20... | collective-permute-start | bytes 786440 | tf_op jit(solution)/shard_map/ppermute | solution.py:588
  (67 other events, 777.8 us)
